TPU v7x, 512 devices: a whole 4x4x16 slice. The times are simulated.
512 devices in a mesh: gx: 8 (over y, core), gy: 4 (over x), gz: 16 (over z).
Axes of the slice: x: 4, y: 4, z: 16, core: 2. Of those that a mesh axis runs over, the one named last changes fastest.
Arguments:
- jump_rhs: float32 [8, 4, 16, 3, 16, 128], P('gx', 'gy', 'gz'), may hold values from -40 to 40
- flex_diag: float32 [8, 4, 16, 6, 128, 128], P('gx', 'gy', 'gz'), may hold values from -0.5 to 4.5, as said below
- flex_couple: float32 [8, 4, 16, 6, 128, 128], P('gx', 'gy', 'gz'), may hold values from -0.2 to 0.2
- dirichlet_diag: float32 [8, 4, 16, 6, 128, 128], P('gx', 'gy', 'gz'), may hold values from -0.5 to 4.5, as said below
- dirichlet_couple: float32 [8, 4, 16, 6, 128, 128], P('gx', 'gy', 'gz'), may hold values from -0.2 to 0.2
- face_pairs: int32 [8, 4, 16, 6, 2], P('gx', 'gy', 'gz'), may hold values from 0 to 5, as said below
- corner_coupling: float32 [8, 4, 16, 24, 768], P('gx', 'gy', 'gz'), may hold values from -0.21875 to 0.21875
- coarse_ids: int32 [8, 4, 16, 8], P('gx', 'gy', 'gz'), may hold values from 0 to 191, as said below
- partner: int32 [8, 4, 16, 3, 128], P('gx', 'gy', 'gz'), may hold values from 0 to 127, as said below
- coarse_inverse: float32 [576, 576], replicated, may hold values from -0.5 to 3.5, as said below
Outputs:
- multipliers: float32 [8, 4, 16, 3, 16, 128], P('gx', 'gy', 'gz')
- residual: float32 [8, 4, 16, 3, 16, 128], P('gx', 'gy', 'gz')
Inputs may be any that keep to these rules, and one draw needn't show every extreme that they name: Each row of 128 entries is a permutation: dof k of a subdomain's upper face along d matches dof partner[k] of the next subdomain's lower face. `face_pairs`: each subdomain lists 6 different pairs of its 6 faces, the first number below the second. `coarse_ids`: corners of neighbouring subdomains that coincide carry the same aggregate. `flex_diag`: each block is symmetric, and each subdomain's assembled face operator is symmetric positive definite. `dirichlet_diag`: each block is symmetric, and each subdomain's assembled face operator is symmetric positive definite. `coarse_inverse`: symmetric positive definite.
All inputs are finite; a program needn't handle non-finite values.
Results may differ from a plain program's by a relative error of at most 0.0003.
Values sent between devices are 32-bit elements; how exact they have to be, the bound alone decides.
No kernel may reach another device: no remote copies, remote signals or barrier semaphores. Data moves between devices by JAX's collectives and lax.ppermute only.
A program may use at most 64 MiB of HBM per device.

v0:
```python
import jax
import jax.numpy as jnp
from jax import lax
from jax.sharding import PartitionSpec as P

ITERS = 3


HIGHEST = lax.Precision.HIGHEST


def passed_along(shard, axis, by):
    peers = lax.axis_size(axis)
    pairs = [(i, i + by) for i in range(peers) if 0 <= i + by < peers]
    return lax.ppermute(shard, axis, pairs)


def apply_blocks(face_loads, diagonal, couple, hit_first, hit_second):
    result = jnp.einsum("nfcm,nfmk->nfck", face_loads, diagonal, precision=HIGHEST)
    take_first = jnp.einsum("nkf,nfcm->nkcm", hit_first, face_loads, precision=HIGHEST)
    take_second = jnp.einsum("nkf,nfcm->nkcm", hit_second, face_loads, precision=HIGHEST)
    to_first = jnp.einsum("nkcm,nkml->nkcl", take_second, couple, precision=HIGHEST)
    to_second = jnp.einsum("nkcl,nkml->nkcm", take_first, couple, precision=HIGHEST)
    result = result + jnp.einsum("nkf,nkcl->nfcl", hit_first, to_first, precision=HIGHEST)
    result = result + jnp.einsum("nkf,nkcl->nfcl", hit_second, to_second, precision=HIGHEST)
    return result


def case_sums(left, right):
    return jnp.sum(left * right, axis=(0, 1, 2, 3, 5))


def boundary_mask(depth):
    last_x = (lax.axis_index("gx") < lax.axis_size("gx") - 1).astype(jnp.float32)
    last_y = (lax.axis_index("gy") < lax.axis_size("gy") - 1).astype(jnp.float32)
    total_z = depth * lax.axis_size("gz")
    layers = lax.axis_index("gz") * depth + jnp.arange(depth)
    inner_z = (layers < total_z - 1).astype(jnp.float32)
    unit_row = jnp.ones((depth,), jnp.float32)
    stacked = jnp.stack([unit_row * last_x, unit_row * last_y, inner_z], axis=1)
    return stacked[None, None, :, :, None, None]


def spread(field, matching):
    depth = field.shape[2]
    flat = field.reshape((depth,) + field.shape[3:])
    permuted = jnp.einsum("ndck,ndkj->ndcj", flat, matching, precision=HIGHEST).reshape(field.shape)
    from_x = passed_along(permuted[:, :, :, 0], "gx", 1)
    from_y = passed_along(permuted[:, :, :, 1], "gy", 1)
    below_z = passed_along(permuted[:, :, -1:, 2], "gz", 1)
    from_z = jnp.concatenate([below_z, permuted[:, :, :-1, 2]], axis=2)
    return jnp.stack(
        [-from_x, field[:, :, :, 0], -from_y, field[:, :, :, 1], -from_z, field[:, :, :, 2]], axis=3
    )


def jump_trace(displaced, matching):
    depth = displaced.shape[2]
    above_x = passed_along(displaced[:, :, :, 0], "gx", -1)
    above_y = passed_along(displaced[:, :, :, 2], "gy", -1)
    first_z = passed_along(displaced[:, :, :1, 4], "gz", -1)
    above_z = jnp.concatenate([displaced[:, :, 1:, 4], first_z], axis=2)
    jump_parts = []
    for direction, from_above in enumerate((above_x, above_y, above_z)):
        flat_above = from_above.reshape((depth,) + from_above.shape[3:])
        matched = jnp.einsum(
            "ncm,nkm->nck", flat_above, matching[:, direction], precision=HIGHEST
        ).reshape(from_above.shape)
        jump_parts.append(displaced[:, :, :, 2 * direction + 1] - matched)
    return jnp.stack(jump_parts, axis=3)


def body(
    jump_rhs,
    flex_diag,
    flex_couple,
    dirichlet_diag,
    dirichlet_couple,
    face_pairs,
    corner_coupling,
    coarse_ids,
    partner,
    coarse_inverse,
):
    depth = jump_rhs.shape[2]
    case_count = jump_rhs.shape[4]
    face_width = jump_rhs.shape[5]
    corner_count = corner_coupling.shape[3]
    inner = boundary_mask(depth)
    pair_list = face_pairs.reshape((depth,) + face_pairs.shape[3:])
    face_range = jnp.arange(6)
    hit_first = (pair_list[:, :, 0][:, :, None] == face_range[None, None, :]).astype(jnp.float32)
    hit_second = (pair_list[:, :, 1][:, :, None] == face_range[None, None, :]).astype(jnp.float32)
    partner_rows = partner.reshape(depth, 3, face_width)
    matching = (partner_rows[:, :, :, None] == jnp.arange(face_width)[None, None, None, :]).astype(
        jnp.float32
    )
    flex_main = flex_diag.reshape((depth,) + flex_diag.shape[3:])
    flex_side = flex_couple.reshape((depth,) + flex_couple.shape[3:])
    schur_main = dirichlet_diag.reshape((depth,) + dirichlet_diag.shape[3:])
    schur_side = dirichlet_couple.reshape((depth,) + dirichlet_couple.shape[3:])
    coupling = corner_coupling.reshape(depth, corner_count, 6, face_width)
    point_count = coarse_inverse.shape[0] // 3
    corner_ids = coarse_ids.reshape(depth, 8)
    one_hot = (corner_ids[:, :, None] == jnp.arange(point_count)[None, None, :]).astype(jnp.float32)

    def dirichlet(field):
        face_loads = spread(field, matching)
        flat_loads = face_loads.reshape((depth,) + face_loads.shape[3:])
        answer = apply_blocks(flat_loads, schur_main, schur_side, hit_first, hit_second)
        return 0.25 * jump_trace(answer.reshape(face_loads.shape), matching) * inner

    def precond_product(residual, preconditioned):
        return lax.psum(case_sums(residual, preconditioned), ("gx", "gy", "gz"))

    residual = jump_rhs * inner
    multipliers = jnp.zeros_like(residual)
    preconditioned = dirichlet(residual)
    search = preconditioned
    norm_now = precond_product(residual, preconditioned)
    for iteration in range(ITERS):
        flexibility_face_loads = spread(search, matching)
        flexibility_flat_loads = flexibility_face_loads.reshape(
            (depth,) + flexibility_face_loads.shape[3:]
        )
        displaced = apply_blocks(
            flexibility_flat_loads, flex_main, flex_side, hit_first, hit_second
        )
        corner_load = jnp.einsum(
            "nrfm,nfcm->nrc", coupling, flexibility_flat_loads, precision=HIGHEST
        )
        grouped = corner_load.reshape(depth, 8, 3, case_count)
        flexibility_local_sum = jnp.einsum(
            "njdc,njp->cdp", grouped, one_hot, precision=HIGHEST
        ).reshape(case_count, 3 * point_count)
        total_sum = lax.psum(flexibility_local_sum, ("gx", "gy", "gz"))
        coarse_values = jnp.dot(total_sum, coarse_inverse, precision=HIGHEST).reshape(
            case_count, 3, point_count
        )
        picked = jnp.einsum("cqp,njp->njqc", coarse_values, one_hot, precision=HIGHEST)
        corner_values = picked.reshape(depth, corner_count, case_count)
        displaced = displaced + jnp.einsum(
            "nrc,nrfm->nfcm", corner_values, coupling, precision=HIGHEST
        )
        applied = jump_trace(displaced.reshape(flexibility_face_loads.shape), matching) * inner
        step_size = (norm_now / lax.psum(case_sums(search, applied), ("gx", "gy", "gz")))[:, None]
        multipliers = multipliers + step_size * search
        residual = residual - step_size * applied
        if iteration + 1 < ITERS:
            preconditioned = dirichlet(residual)
            norm_next = precond_product(residual, preconditioned)
            search = preconditioned + (norm_next / norm_now)[:, None] * search
            norm_now = norm_next
    return (multipliers, residual)


def solution(mesh):
    placed = (
        P("gx", "gy", "gz", None, None, None),
        P("gx", "gy", "gz", None, None, None),
        P("gx", "gy", "gz", None, None, None),
        P("gx", "gy", "gz", None, None, None),
        P("gx", "gy", "gz", None, None, None),
        P("gx", "gy", "gz", None, None),
        P("gx", "gy", "gz", None, None),
        P("gx", "gy", "gz", None),
        P("gx", "gy", "gz", None, None),
        P(),
    )
    return jax.shard_map(
        body,
        mesh=mesh,
        in_specs=placed,
        out_specs=(P("gx", "gy", "gz", None, None, None), P("gx", "gy", "gz", None, None, None)),
        check_vma=False,
    )
```

profile of v0, /device:TPU:1, one launch (start us, length us, event | category | flops | bytes accessed | tf_op | source)
XLA Modules:
  0.0 979.1 jit_solution(910736296158399458)
XLA Ops:
  2.7 4.4 collective-permute-start.2
  7.1 3.1 collective-permute-start.1
  10.2 4.3 collective-permute-start
  15.8 1.5 fusion.52
  18.9 1.9 collective-permute-start.3
  21.0 1.3 collective-permute-start.5
  22.3 1.3 collective-permute-start.4
  23.6 0.9 collective-permute-done.3
  24.6 1.2 collective-permute-done.5
  27.2 4.2 collective-permute-start.8
  31.3 3.1 collective-permute-start.7
  34.5 6.0 collective-permute-start.6
  44.5 109.5 %psum.64 = f32[16,576]{1,0:T(8,128)S(1)} all-reduce(f32[16,576]{1,0:T(8,128)} %reshape.2034), channel_id=1, replica_groups=mesh['gx'=8,'gy'=4,'gz'=16] {'gx','gy','gz'}, use_global_device_ids=true, to_apply=%region_2.0 | all-reduce | flops 9216 | bytes 73728 | tf_op jit(solution)/shard_map/psum | solution.py:136
  154.0 1.4 fusion.246
  157.9 3.0 collective-permute-start.9
  160.9 1.3 collective-permute-start.11
  162.2 1.3 collective-permute-start.10
  164.4 1.1 collective-permute-done.11
  167.8 100.3 %all-reduce = (f32[16]{0:T(128)S(1)}, f32[16]{0:T(128)S(1)}) all-reduce(f32[16]{0:T(128)S(1)} %get-tuple-element.3, f32[16]{0:T(128)S(1)} %get-tuple-element.2), channel_id=1, replica_groups=mesh['gx'=8,'gy'=4,'gz'=16] {'gx','gy','gz'}, use_global_device_ids=true, to_apply=%region_1.0 | all-reduce | flops 32 | bytes 256 | tf_op jit(solution)/shard_map/psum | solution.py:114
  268.2 1.0 convolution_bitcast_fusion.9
  269.2 1.9 collective-permute-start.12
  271.1 2.8 collective-permute-start.14
  273.9 2.4 collective-permute-start.13
  279.5 2.5 collective-permute-start.15
  282.1 1.3 collective-permute-start.17
  283.4 1.3 collective-permute-start.16
  284.8 1.8 collective-permute-done.17
  286.7 1.6 collective-permute-done.16
  288.7 102.9 %psum.66 = f32[16]{0:T(128)S(1)} all-reduce(f32[16]{0:T(128)S(1)} %multiply_reduce_fusion.3), channel_id=1, replica_groups=mesh['gx'=8,'gy'=4,'gz'=16] {'gx','gy','gz'}, use_global_device_ids=true, to_apply=%region_6.0 | all-reduce | flops 16 | bytes 128 | tf_op jit(solution)/shard_map/psum | solution.py:114
  392.5 1.9 collective-permute-start.18
  394.5 3.2 collective-permute-start.20
  397.7 2.2 collective-permute-start.19
  403.0 102.4 %psum.67 = f32[16,576]{1,0:T(8,128)} all-reduce(f32[16,576]{1,0:T(8,128)} %reshape.2051), channel_id=1, replica_groups=mesh['gx'=8,'gy'=4,'gz'=16] {'gx','gy','gz'}, use_global_device_ids=true, to_apply=%region_7.0 | all-reduce | flops 9216 | bytes 73728 | tf_op jit(solution)/shard_map/psum | solution.py:136
  505.5 2.2 fusion.247
  507.7 1.5 reshape.2052
  509.2 1.0 convolution_bitcast_fusion.14
  510.9 1.0 convolution_bitcast_fusion.2
  513.8 2.6 collective-permute-start.21
  516.4 1.3 collective-permute-start.23
  517.7 1.3 collective-permute-start.22
  519.2 1.8 collective-permute-done.23
  521.1 1.2 collective-permute-done.22
  522.4 0.9 multiply_reduce_fusion.2
  523.3 103.2 %psum.68 = f32[16]{0:T(128)S(1)} all-reduce(f32[16]{0:T(128)S(1)} %multiply_reduce_fusion.2), channel_id=1, replica_groups=mesh['gx'=8,'gy'=4,'gz'=16] {'gx','gy','gz'}, use_global_device_ids=true, to_apply=%region_9.0 | all-reduce | flops 16 | bytes 128 | tf_op jit(solution)/shard_map/psum | solution.py:146
  627.8 1.0 convolution_bitcast_fusion.7
  628.8 2.5 collective-permute-start.24
  631.3 3.7 collective-permute-start.26
  635.0 1.8 collective-permute-start.25
  640.0 3.1 collective-permute-start.27
  643.1 1.3 collective-permute-start.29
  644.4 1.3 collective-permute-start.28
  645.9 1.8 collective-permute-done.29
  647.8 1.6 collective-permute-done.28
  649.8 101.5 %psum.69 = f32[16]{0:T(128)S(1)} all-reduce(f32[16]{0:T(128)S(1)} %multiply_reduce_fusion.1), channel_id=1, replica_groups=mesh['gx'=8,'gy'=4,'gz'=16] {'gx','gy','gz'}, use_global_device_ids=true, to_apply=%region_11.0 | all-reduce | flops 16 | bytes 128 | tf_op jit(solution)/shard_map/psum | solution.py:114
  752.3 2.0 collective-permute-start.30
  754.4 3.1 collective-permute-start.32
  757.5 1.9 collective-permute-start.31
  761.3 102.0 %psum.70 = f32[16,576]{1,0:T(8,128)S(1)} all-reduce(f32[16,576]{1,0:T(8,128)S(1)} %reshape.2067), channel_id=1, replica_groups=mesh['gx'=8,'gy'=4,'gz'=16] {'gx','gy','gz'}, use_global_device_ids=true, to_apply=%region_12.0 | all-reduce | flops 9216 | bytes 73728 | tf_op jit(solution)/shard_map/psum | solution.py:136
  866.7 2.6 collective-permute-start.33
  869.3 1.3 collective-permute-start.35
  870.6 1.3 collective-permute-start.34
  872.0 1.8 collective-permute-done.35
  874.0 1.2 collective-permute-done.34
  875.5 102.8 %psum.71 = f32[16]{0:T(128)S(1)} all-reduce(f32[16]{0:T(128)S(1)} %multiply_reduce_fusion), channel_id=1, replica_groups=mesh['gx'=8,'gy'=4,'gz'=16] {'gx','gy','gz'}, use_global_device_ids=true, to_apply=%region_14.0 | all-reduce | flops 16 | bytes 128 | tf_op jit(solution)/shard_map/psum | solution.py:146
  (240 shorter events, 39.4 us)
Async XLA Ops:
  0.6 153.4 %copy-start = (f32[576,576]{1,0:T(8,128)S(1)}, f32[576,576]{1,0:T(8,128)}, u32[]{:S(2)}) copy-start(f32[576,576]{1,0:T(8,128)} %param.19) | copy-start | bytes 3981316
  0.6 16.8 %copy-start.1 = (f32[1,1,1,6,128,128]{5,4,3,2,1,0:T(8,128)S(1)}, f32[1,1,1,6,128,128]{5,4,3,2,1,0:T(8,128)}, u32[]{:S(2)}) copy-start(f32[1,1,1,6,128,128]{5,4,3,2,1,0:T(8,128)} %param.14) | copy-start | bytes 1179652
  0.7 17.7 %copy-start.3 = (f32[1,1,1,6,128,128]{5,4,3,2,1,0:T(8,128)S(1)}, f32[1,1,1,6,128,128]{5,4,3,2,1,0:T(8,128)}, u32[]{:S(2)}) copy-start(f32[1,1,1,6,128,128]{5,4,3,2,1,0:T(8,128)} %param.13) | copy-start | bytes 1179652
  0.7 20.2 %copy-start.6 = (f32[1,1,1,24,768]{4,3,2,1,0:T(8,128)S(1)}, f32[1,1,1,24,768]{4,3,2,1,0:T(8,128)}, u32[]{:S(2)}) copy-start(f32[1,1,1,24,768]{4,3,2,1,0:T(8,128)} %param.16) | copy-start | bytes 221188
  1.6 25.2 %copy-start.18 = (s32[1,1,1,3,128]{4,3,2,1,0:T(4,128)}, s32[1,1,1,3,128]{4,3,2,1,0:T(4,128)S(1)}, u32[]{:S(2)}) copy-start(s32[1,1,1,3,128]{4,3,2,1,0:T(4,128)S(1)} %copy.201) | copy-start | bytes 4612
  2.7 12.6 %collective-permute-start.2 = (f32[1,1,1,16,128]{4,3,2,1,0:T(8,128)S(1)}, f32[1,1,1,16,128]{4,3,2,1,0:T(8,128)S(1)}, u32[]{:S(2)}, u32[]{:S(2)}) collective-permute-start(f32[1,1,1,16,128]{4,3,2,1,0:T(8,128)S(1)} %get-tuple-element.41), channel_id=1, source_target_pairs={{0,1},{1,2},{2,3},{3,4},{4,5},{5,6},{6,7},{7,8},{8,9},{9,10},{10,1... | collective-permute-start | bytes 24584 | tf_op jit(solution)/shard_map/ppermute | solution.py:15
  7.1 8.2 collective-permute-start.1
  10.2 5.1 collective-permute-start
  15.8 25.9 %copy-start.2 = (f32[1,1,1,6,128,128]{5,4,3,2,1,0:T(8,128)S(1)}, f32[1,1,1,6,128,128]{5,4,3,2,1,0:T(8,128)}, u32[]{:S(2)}) copy-start(f32[1,1,1,6,128,128]{5,4,3,2,1,0:T(8,128)} %param.12) | copy-start | bytes 1179652
  18.4 25.1 %copy-start.23 = (s32[1,1,1,8]{3,2,1,0:T(1,128)S(1)}, s32[1,1,1,8]{3,2,1,0:T(1,128)}, u32[]{:S(2)}) copy-start(s32[1,1,1,8]{3,2,1,0:T(1,128)} %param.17) | copy-start | bytes 100
  18.9 5.6 collective-permute-start.3
  20.9 20.4 %copy-start.8 = (pred[1,3,128,128]{3,2,1,0:T(32,128)(4,1)}, pred[1,3,128,128]{3,2,1,0:T(32,128)(4,1)S(1)}, u32[]{:S(2)}) copy-start(pred[1,3,128,128]{3,2,1,0:T(32,128)(4,1)S(1)} %iota_compare_fusion) | copy-start | bytes 147460
  21.0 4.8 collective-permute-start.5
  22.3 4.4 collective-permute-start.4
  27.2 14.1 %collective-permute-start.8 = (f32[1,1,1,16,128]{4,3,2,1,0:T(8,128)S(1)}, f32[1,1,1,16,128]{4,3,2,1,0:T(8,128)S(1)}, u32[]{:S(2)}, u32[]{:S(2)}) collective-permute-start(f32[1,1,1,16,128]{4,3,2,1,0:T(8,128)S(1)} %get-tuple-element.38), channel_id=1, source_target_pairs={{0,1},{1,2},{2,3},{3,4},{4,5},{5,6},{6,7},{7,8},{8,9},{9,10},{10,1... | collective-permute-start | bytes 24584 | tf_op jit(solution)/shard_map/ppermute | solution.py:15
  31.3 9.9 %collective-permute-start.7 = (f32[1,1,1,16,128]{4,3,2,1,0:T(8,128)S(1)}, f32[1,1,1,16,128]{4,3,2,1,0:T(8,128)S(1)}, u32[]{:S(2)}, u32[]{:S(2)}) collective-permute-start(f32[1,1,1,16,128]{4,3,2,1,0:T(8,128)S(1)} %get-tuple-element.39), channel_id=1, source_target_pairs={{0,16},{16,32},{32,48},{1,17},{17,33},{33,49},{2,18},{18,34},{34,5... | collective-permute-start | bytes 24584 | tf_op jit(solution)/shard_map/ppermute | solution.py:15
  34.5 6.8 collective-permute-start.6
  42.4 115.1 %copy-start.4 = (f32[1,1,1,6,128,128]{5,4,3,2,1,0:T(8,128)S(1)}, f32[1,1,1,6,128,128]{5,4,3,2,1,0:T(8,128)}, u32[]{:S(2)}) copy-start(f32[1,1,1,6,128,128]{5,4,3,2,1,0:T(8,128)} %param.11) | copy-start | bytes 1179652
  43.8 123.8 %copy-start.5 = (f32[1,1,1,3,16,128]{5,4,3,2,1,0:T(8,128)S(1)}, f32[1,1,1,3,16,128]{5,4,3,2,1,0:T(8,128)}, u32[]{:S(2)}) copy-start(f32[1,1,1,3,16,128]{5,4,3,2,1,0:T(8,128)} %param.10) | copy-start | bytes 73732
  157.9 126.8 %copy-start.9 = (pred[1,3,128,128]{3,2,1,0:T(32,128)(4,1)S(1)}, pred[1,3,128,128]{3,2,1,0:T(32,128)(4,1)}, u32[]{:S(2)}) copy-start(pred[1,3,128,128]{3,2,1,0:T(32,128)(4,1)} %copy-done.8) | copy-start | bytes 147460
  157.9 234.3 %copy-start.19 = (s32[1,1,1,3,128]{4,3,2,1,0:T(4,128)S(1)}, s32[1,1,1,3,128]{4,3,2,1,0:T(4,128)}, u32[]{:S(2)}) copy-start(s32[1,1,1,3,128]{4,3,2,1,0:T(4,128)} %copy-done.18) | copy-start | bytes 4612
  157.9 5.6 collective-permute-start.9
  160.9 4.5 collective-permute-start.11
  162.2 4.5 collective-permute-start.10
  268.2 126.3 %copy-start.12 = (f32[16]{0:T(128)}, f32[16]{0:T(128)S(1)}, u32[]{:S(2)}) copy-start(f32[16]{0:T(128)S(1)} %div.15) | copy-start | bytes 196
  269.2 7.1 collective-permute-start.12
  271.1 6.0 collective-permute-start.14
  273.9 3.2 collective-permute-start.13
  277.6 124.5 %copy-start.24 = (s32[1,1,1,8]{3,2,1,0:T(1,128)S(1)}, s32[1,1,1,8]{3,2,1,0:T(1,128)}, u32[]{:S(2)}) copy-start(s32[1,1,1,8]{3,2,1,0:T(1,128)} %param.17) | copy-start | bytes 100
  279.5 5.1 collective-permute-start.15
  282.1 4.5 collective-permute-start.17
  283.4 5.0 collective-permute-start.16
  391.6 0.6 copy-start.27
  391.6 8.3 copy-start.15
  392.5 7.5 collective-permute-start.18
  394.5 6.2 collective-permute-start.20
  397.7 3.0 collective-permute-start.19
  403.0 108.8 %copy-start.7 = (f32[6,16,128]{2,0,1:T(8,128)S(1)}, f32[6,16,128]{2,0,1:T(8,128)}, u32[]{:S(2)}) copy-start(f32[6,16,128]{2,0,1:T(8,128)} %fusion.73) | copy-start | bytes 147460
  510.9 8.2 copy-start.10
  513.8 132.0 %copy-start.11 = (pred[1,3,128,128]{3,2,1,0:T(32,128)(4,1)S(1)}, pred[1,3,128,128]{3,2,1,0:T(32,128)(4,1)}, u32[]{:S(2)}) copy-start(pred[1,3,128,128]{3,2,1,0:T(32,128)(4,1)} %copy-done.8) | copy-start | bytes 147460
  513.8 135.7 %copy-start.13 = (f32[16]{0:T(128)S(1)}, f32[16]{0:T(128)}, u32[]{:S(2)}) copy-start(f32[16]{0:T(128)} %copy-done.12) | copy-start | bytes 196
  513.8 5.2 collective-permute-start.21
  516.4 4.5 collective-permute-start.23
  517.7 234.3 %copy-start.16 = (f32[16]{0:T(128)S(1)}, f32[16]{0:T(128)}, u32[]{:S(2)}) copy-start(f32[16]{0:T(128)} %copy-done.15) | copy-start | bytes 196
  517.7 234.3 %copy-start.20 = (s32[1,1,1,3,128]{4,3,2,1,0:T(4,128)S(1)}, s32[1,1,1,3,128]{4,3,2,1,0:T(4,128)}, u32[]{:S(2)}) copy-start(s32[1,1,1,3,128]{4,3,2,1,0:T(4,128)} %copy-done.18) | copy-start | bytes 4612
  517.7 4.5 collective-permute-start.22
  627.1 125.2 %copy-start.21 = (f32[16]{0:T(128)}, f32[16]{0:T(128)S(1)}, u32[]{:S(2)}) copy-start(f32[16]{0:T(128)S(1)} %div.17) | copy-start | bytes 196
  628.8 8.0 collective-permute-start.24
  631.3 6.3 collective-permute-start.26
  635.0 2.6 collective-permute-start.25
  638.0 122.9 %copy-start.25 = (s32[1,1,1,8]{3,2,1,0:T(1,128)S(1)}, s32[1,1,1,8]{3,2,1,0:T(1,128)}, u32[]{:S(2)}) copy-start(s32[1,1,1,8]{3,2,1,0:T(1,128)} %param.17) | copy-start | bytes 100
  640.0 5.7 collective-permute-start.27
  643.1 4.5 collective-permute-start.29
  644.4 5.0 collective-permute-start.28
  752.0 112.2 %copy-start.26 = (s32[1,1,1,8]{3,2,1,0:T(1,128)S(1)}, s32[1,1,1,8]{3,2,1,0:T(1,128)}, u32[]{:S(2)}) copy-start(s32[1,1,1,8]{3,2,1,0:T(1,128)} %param.17) | copy-start | bytes 100
  752.3 7.2 collective-permute-start.30
  754.4 5.8 collective-permute-start.32
  757.5 2.7 collective-permute-start.31
  864.1 11.1 %copy-start.17 = (f32[16]{0:T(128)S(1)}, f32[16]{0:T(128)}, u32[]{:S(2)}) copy-start(f32[16]{0:T(128)} %copy-done.15) | copy-start | bytes 196
  864.1 114.2 %copy-start.14 = (f32[16]{0:T(128)S(1)}, f32[16]{0:T(128)}, u32[]{:S(2)}) copy-start(f32[16]{0:T(128)} %copy-done.12) | copy-start | bytes 196
  864.1 114.2 %copy-start.22 = (f32[16]{0:T(128)S(1)}, f32[16]{0:T(128)}, u32[]{:S(2)}) copy-start(f32[16]{0:T(128)} %copy-done.21) | copy-start | bytes 196
  866.7 5.2 collective-permute-start.33
  869.3 4.5 collective-permute-start.35
  870.6 4.5 collective-permute-start.34
where the time goes:
time: 982 us; the launch traced here: 979 us
  blocking collectives  825 us (84%)
  starting transfers between devices  85.8 us (9%)
  matrix products  32.7 us (3%)
  waiting for transfers between devices  20.8 us (2%)
    psum x3, blocking collectives, body(): total_sum = lax.psum(flexibility_local_sum, ('gx', 'gy', 'gz'))  314 us
    psum x3, blocking collectives, precond_product(): return lax.psum(case_sums(residual, preconditioned), ('gx', 'gy', 'gz'))  305 us
    psum x2, blocking collectives, body(): lax.psum(case_sums(search, applied), ('gx', 'gy', 'gz'))  206 us
    ppermute x36, starting transfers between devices, passed_along(): return lax.ppermute(shard, axis, pairs)  85.8 us
    ppermute x36, waiting for transfers between devices, passed_along(): return lax.ppermute(shard, axis, pairs)  20.8 us
  transfers between devices with their start and end apart: 36, of which 18 were waited for; matrix products, arithmetic and copies ran while one was open for 0% of the time, Pallas kernels for 0%

commit v1 on v0

v1 whole, which is shorter than its diff:
```python
import functools

import jax
import jax.numpy as jnp
from jax import lax
from jax.experimental import pallas as pl
from jax.experimental.pallas import tpu as pltpu
from jax.sharding import PartitionSpec as P

ITERS = 3
CASES = 16
FD = 128
WIDE = 6 * FD
QPAD = 256
SUBS = 32
PLANE = ("gx", "gy")
F32 = jnp.float32
BF16 = jnp.bfloat16
VMEM = pl.BlockSpec(memory_space=pltpu.VMEM)
SMEM = pl.BlockSpec(memory_space=pltpu.SMEM)


def call(kernel, outs, *args, smem=0, scratch=()):
    return pl.pallas_call(
        kernel,
        out_shape=[jax.ShapeDtypeStruct(shape, dtype) for shape, dtype in outs],
        in_specs=[SMEM] * smem + [VMEM] * (len(args) - smem),
        out_specs=[VMEM] * len(outs),
        scratch_shapes=list(scratch),
        compiler_params=pltpu.CompilerParams(vmem_limit_bytes=40 * 1024 * 1024),
    )(*args)


def halves(x):
    high = x.astype(BF16)
    return high, (x - high.astype(F32)).astype(BF16)


def dot_exact(x, selector):
    rows = x.shape[0]
    high, low = halves(x)
    both = jnp.dot(jnp.concatenate([high, low], 0), selector, preferred_element_type=F32)
    return both[:rows] + both[rows:]


def dot_split(x, high_ref, low_ref):
    rows = x.shape[0]
    high, low = halves(x)
    both = jnp.dot(jnp.concatenate([high, low], 0), high_ref[...], preferred_element_type=F32)
    rest = jnp.dot(high, low_ref[...], preferred_element_type=F32)
    return both[:rows] + both[rows:] + rest


def face(x, f):
    return x[:, f * FD:(f + 1) * FD]


def take(x, row):
    index = jnp.broadcast_to(row.astype(jnp.int32), x.shape)
    return jnp.take_along_axis(x, index, axis=1, mode="promise_in_bounds")


def lower_changed(x, rows):
    parts = []
    for d in range(3):
        parts.append(-take(face(x, 2 * d), rows[d]))
        parts.append(face(x, 2 * d + 1))
    return jnp.concatenate(parts, axis=1)


def partner_rows(messages):
    return [m[CASES:CASES + 1, :] for m in messages]


def inverse_rows(messages):
    return [m[CASES + 1:CASES + 2, :] for m in messages]


def apply_dense(field, messages, high_ref, low_ref):
    loads = lower_changed(field, inverse_rows(messages))
    return loads, lower_changed(dot_split(loads, high_ref, low_ref), partner_rows(messages))


def put_plane(spots, slots_ref, piece, gy):
    here = spots[0]
    for f, by in ((0, -gy), (1, gy), (2, -1), (3, 1)):
        @pl.when(spots[2 + f] > 0)
        def _():
            value = piece(f)
            slots_ref[here + by, 0:value.shape[0], :] = value


def take_plane(spots, slots_ref, f, gy, rows):
    here = spots[0]
    by = (-gy, gy, -1, 1)[f]
    spot = jnp.where(spots[2 + f] > 0, here + by, here)
    return slots_ref[spot, rows, :]


def prep_kernel(spots, rhs_ref, partner_ref, message_ref):
    for d in range(3):
        inner = spots[3 + 2 * d].astype(F32)
        row = partner_ref[d:d + 1, :]
        message_ref[d, 0:CASES, :] = rhs_ref[d] * inner
        wanted = lax.broadcasted_iota(jnp.int32, (FD, FD), 0)
        hits = (wanted == jnp.broadcast_to(row, (FD, FD))).astype(F32).astype(BF16)
        count = lax.broadcasted_iota(jnp.int32, (16, FD), 1).astype(F32).astype(BF16)
        inverse = lax.dot_general(
            count, hits, (((1,), (1,)), ((), ())), preferred_element_type=F32
        )
        message_ref[d, CASES:CASES + 1, :] = row.astype(F32)
        message_ref[d, CASES + 1:CASES + 2, :] = inverse[0:1, :]
        message_ref[d, CASES + 2:CASES + 8, :] = jnp.zeros((6, FD), F32)


def build_kernel(pairs, diag_ref, couple_ref, high_ref, low_ref):
    high_ref[...] = jnp.zeros_like(high_ref)
    low_ref[...] = jnp.zeros_like(low_ref)

    def put(row_face, col_face, block):
        high, low = halves(block)
        if isinstance(row_face, int):
            rows, cols = row_face * FD, col_face * FD
        else:
            rows = pl.multiple_of(row_face * FD, FD)
            cols = pl.multiple_of(col_face * FD, FD)
        high_ref[pl.ds(rows, FD), pl.ds(cols, FD)] = high
        low_ref[pl.ds(rows, FD), pl.ds(cols, FD)] = low

    for f in range(6):
        put(f, f, diag_ref[f])
    for k in range(6):
        first, second = pairs[2 * k], pairs[2 * k + 1]
        block = couple_ref[k]
        put(second, first, block)
        put(first, second, block.T)


def split_kernel(matrix_ref, high_ref, low_ref):
    high, low = halves(matrix_ref[...])
    high_ref[...] = high
    low_ref[...] = low


def corner_kernel(ids, coupling_ref, wh_ref, wl_ref, expand_ref, pad):
    pad[...] = jnp.zeros_like(pad)
    pad[0:24, :] = coupling_ref[...]
    for f in range(6):
        high, low = halves(pad[:, f * FD:(f + 1) * FD].T)
        wh_ref[f * FD:(f + 1) * FD, :] = high
        wl_ref[f * FD:(f + 1) * FD, :] = low
    pad[...] = jnp.zeros_like(pad)
    lanes = lax.broadcasted_iota(jnp.int32, (1, 3 * QPAD), 1)
    for r in range(24):
        spot = (r % 3) * QPAD + ids[r // 3]
        pad[r:r + 1, :] = (lanes == spot).astype(F32)
    expand_ref[...] = pad[...].astype(BF16)


def start_kernel(gy, spots, ids, rhs_ref, mx_ref, my_ref, mz_ref, dh_ref, dl_ref, coupling_ref,
                 field_ref, shown_ref, own_ref, slots_ref, up_ref, down_ref):
    messages = (mx_ref, my_ref, mz_ref)
    parts = []
    for d in range(3):
        parts.append(messages[d][0:CASES, :])
        parts.append(rhs_ref[d] * spots[3 + 2 * d].astype(F32))
    field = jnp.concatenate(parts, axis=1)
    field_ref[...] = field
    _, shown = apply_dense(field, messages, dh_ref, dl_ref)
    shown_ref[...] = shown
    own = lower_changed(coupling_ref[...], partner_rows(messages))
    own_ref[...] = own
    lanes = lax.broadcasted_iota(jnp.int32, (8, FD), 1) % SUBS
    target = jnp.full((8, FD), -1, jnp.int32)
    for r in range(24):
        target = jnp.where(lanes == r, (r % 3) * QPAD + ids[r // 3], target)
    target = target.astype(F32)

    def piece(f):
        return jnp.concatenate([face(shown, f), face(own, f), target], axis=0)

    slots_ref[...] = jnp.zeros_like(slots_ref)
    put_plane(spots, slots_ref, piece, gy)
    down_ref[...] = piece(4)
    up_ref[...] = piece(5)


def joint_kernel(gy, spots, ids, own_ref, slots_ref, low_ref, top_ref, gh_ref, gl_ref, pick_ref, whole):
    whole[...] = jnp.zeros_like(whole)
    whole[0:24, :] = own_ref[...]
    lanes = lax.broadcasted_iota(jnp.int32, (8, FD), 1)
    target = jnp.full((8, FD), -1, jnp.int32)
    for r in range(24):
        target = jnp.where(lanes % SUBS == r, (r % 3) * QPAD + ids[r // 3], target)
    targets = [target.astype(F32)]
    for f in range(6):
        if f < 4:
            other = take_plane(spots, slots_ref, f, gy, slice(CASES, CASES + 32))
        else:
            other = (low_ref, top_ref)[f - 4][CASES:CASES + 32, :]
        there = spots[2 + f].astype(F32)
        whole[SUBS * (f + 1):SUBS * (f + 1) + 24, f * FD:(f + 1) * FD] = other[0:24, :] * there
        targets.append(other[24:32, :] * there)
    high, low = halves(whole[...])
    gh_ref[...] = high
    gl_ref[...] = low
    rows = lax.broadcasted_iota(jnp.int32, (3 * QPAD, FD), 0)
    for half in range(2):
        wanted = jnp.full((8, FD), -1.0, F32)
        for n in range(4 * half, min(4 * half + 4, 7)):
            wanted = jnp.where(lanes // SUBS == n % 4, targets[n], wanted)
        wanted = jnp.broadcast_to(wanted[0:1, :].astype(jnp.int32), (3 * QPAD, FD))
        pick_ref[:, half * FD:(half + 1) * FD] = (rows == wanted).astype(F32).astype(BF16)


def load_kernel(gy, first, spots, mask_ref, mx_ref, my_ref, mz_ref, shown_ref, slots_ref, low_ref,
                top_ref, residual_ref, fh_ref, fl_ref, wh_ref, wl_ref, expand_ref, *rest):
    if first:
        z_ref, flexed_ref, out_ref = rest
    else:
        search_ref, applied_ref, z_ref, flexed_ref, out_ref = rest
    messages = (mx_ref, my_ref, mz_ref)
    head = slice(0, CASES)
    across = [take_plane(spots, slots_ref, f, gy, head) for f in range(4)]
    across += [low_ref[head, :], top_ref[head, :]]
    mask = mask_ref[...]
    z = 0.25 * (shown_ref[...] + jnp.concatenate(across, axis=1)) * mask
    z_ref[...] = z
    loads, flexed = apply_dense(z, messages, fh_ref, fl_ref)
    flexed_ref[...] = flexed
    corner = dot_split(loads, wh_ref, wl_ref)
    gathered = dot_exact(corner, expand_ref[...])

    def upper_sum(a):
        return jnp.sum(face(a, 1) + face(a, 3) + face(a, 5), axis=1, keepdims=True)

    sums = [upper_sum(z * residual_ref[...]), jnp.sum(z * flexed, axis=1, keepdims=True)]
    if not first:
        sums.append(
            upper_sum(z * applied_ref[...])
            + jnp.sum(search_ref[...] * flexed, axis=1, keepdims=True)
        )
    lanes = lax.broadcasted_iota(jnp.int32, (CASES, FD), 1)
    out_ref[...] = jnp.zeros_like(out_ref)
    for b in range(6):
        block = face(gathered, b)
        if b == 1:
            for t, value in enumerate(sums):
                block = jnp.where(lanes == 64 + t, value, block)
        for h in range(2):
            out_ref[2 * b + h, CASES:CASES + 8, :] = block[8 * h:8 * h + 8, :]
    put_plane(spots, out_ref, lambda f: face(flexed, f), gy)


def layer_kernel(spots, slots_ref, flexed_ref, out_ref):
    total = jnp.sum(slots_ref[:, CASES:CASES + 8, :], axis=0)
    out_ref[...] = jnp.zeros_like(out_ref)
    for i in range(out_ref.shape[0]):
        out_ref[i, CASES:CASES + 8, :] = total
    for f, by in ((4, -1), (5, 1)):
        @pl.when(spots[2 + f] > 0)
        def _():
            out_ref[spots[1] + by, 0:CASES, :] = flexed_ref[:, f * FD:(f + 1) * FD]


def spread_kernel(slots_ref, out_ref):
    total = jnp.sum(slots_ref[:, CASES:CASES + 8, :], axis=0)
    for i in range(out_ref.shape[0]):
        out_ref[i] = total


def step_kernel(gy, first, last, spots, mask_ref, total_ref, slots_ref, layers_ref, flexed_ref,
                z_ref, residual_ref, kh_ref, kl_ref, gh_ref, gl_ref, pick_ref, *rest):
    rest = list(rest)
    if not last:
        mx_ref, my_ref, mz_ref, dh_ref, dl_ref = rest[:5]
        rest = rest[5:]
    if not first:
        search_ref, applied_ref, load_ref, scale_ref, iterate_ref = rest[:5]
        rest = rest[5:]
    head = slice(0, CASES)
    across = [take_plane(spots, slots_ref, f, gy, head) for f in range(4)]
    for f, by in ((4, -1), (5, 1)):
        spot = jnp.where(spots[2 + f] > 0, spots[1] + by, spots[1])
        across.append(layers_ref[spot, head, :])
    mask = mask_ref[...]
    applied = (flexed_ref[...] + jnp.concatenate(across, axis=1)) * mask
    search = z_ref[...]
    blocks = []
    for b in range(6):
        blocks.append(jnp.concatenate([total_ref[2 * b], total_ref[2 * b + 1]], axis=0))
    norm = blocks[1][:, 64:65]
    energy = blocks[1][:, 65:66]
    load = jnp.concatenate(blocks, axis=1)
    lanes = lax.broadcasted_iota(jnp.int32, load.shape, 1) % QPAD
    load = jnp.where(lanes < 192, load, 0.0)
    if not first:
        beta = norm / scale_ref[:, 0:1]
        cross = blocks[1][:, 66:67]
        energy = energy + beta * cross + beta * beta * scale_ref[:, 1:2]
        applied = applied + beta * applied_ref[...]
        search = search + beta * search_ref[...]
        load = load + beta * load_ref[...]
    coarse = dot_split(load, kh_ref, kl_ref)
    step = norm / (energy + jnp.sum(load * coarse, axis=1, keepdims=True))
    corner = dot_exact(coarse, pick_ref[...])
    correction = dot_split(corner, gh_ref, gl_ref) * mask
    residual = residual_ref[...] - step * (applied + correction)
    moved = step * search
    if last:
        multipliers_ref, left_ref = rest
        for d in range(3):
            multipliers_ref[d] = iterate_ref[d] + face(moved, 2 * d + 1)
            left_ref[d] = face(residual, 2 * d + 1)
        return
    (search_out, applied_out, load_out, scale_out, iterate_out, residual_out, shown_ref, out_ref,
     up_ref, down_ref) = rest
    search_out[...] = search
    applied_out[...] = applied
    load_out[...] = load
    residual_out[...] = residual
    lanes = lax.broadcasted_iota(jnp.int32, (CASES, FD), 1)
    scale_out[...] = jnp.where(lanes == 0, norm, energy)
    for d in range(3):
        moved_face = face(moved, 2 * d + 1)
        iterate_out[d] = moved_face if first else iterate_ref[d] + moved_face
    _, shown = apply_dense(residual, (mx_ref, my_ref, mz_ref), dh_ref, dl_ref)
    shown_ref[...] = shown
    out_ref[...] = jnp.zeros_like(out_ref)
    put_plane(spots, out_ref, lambda f: face(shown, f), gy)
    down_ref[...] = face(shown, 4)
    up_ref[...] = face(shown, 5)


def passed_along(shard, axis, by):
    peers = lax.axis_size(axis)
    pairs = [(i, i + by) for i in range(peers) if 0 <= i + by < peers]
    return lax.ppermute(shard, axis, pairs)


def swapped(slots, axes):
    return lax.all_to_all(slots, axes, 0, 0)


def body(
    jump_rhs,
    flex_diag,
    flex_couple,
    dirichlet_diag,
    dirichlet_couple,
    face_pairs,
    corner_coupling,
    coarse_ids,
    partner,
    coarse_inverse,
):
    gx, gy, gz = (lax.axis_size(a) for a in ("gx", "gy", "gz"))
    ix, iy, iz = (lax.axis_index(a) for a in ("gx", "gy", "gz"))
    plane = gx * gy
    spots = jnp.stack(
        [ix * gy + iy, iz]
        + [v.astype(jnp.int32) for v in (ix > 0, ix < gx - 1, iy > 0, iy < gy - 1, iz > 0, iz < gz - 1)]
    ).astype(jnp.int32)
    mask = jnp.repeat(spots[2:].astype(F32), FD)[None, :]
    rhs = jump_rhs.reshape(3, CASES, FD)
    pairs = face_pairs.reshape(12)
    coupling = corner_coupling.reshape(24, WIDE)
    ids = coarse_ids.reshape(8)
    square = (WIDE, WIDE)
    wide = (CASES, WIDE)

    (message,) = call(
        prep_kernel, [((3, CASES + 8, FD), F32)], spots, rhs, partner.reshape(3, FD), smem=1
    )
    messages = [passed_along(message[d], a, 1) for d, a in enumerate(("gx", "gy", "gz"))]

    def build(diag, couple):
        return call(
            build_kernel, [(square, BF16)] * 2, pairs, diag.reshape(6, FD, FD),
            couple.reshape(6, FD, FD), smem=1
        )

    dirichlet = build(dirichlet_diag, dirichlet_couple)
    flex = build(flex_diag, flex_couple)
    padded = jnp.pad(
        coarse_inverse.reshape(3, 192, 3, 192), ((0, 0), (0, 64), (0, 0), (0, 64))
    ).reshape(square)
    inverse = call(split_kernel, [(square, BF16)] * 2, padded)
    weight_high, weight_low, expand = call(
        corner_kernel,
        [((WIDE, FD), BF16), ((WIDE, FD), BF16), ((FD, WIDE), BF16)],
        ids, coupling, smem=1, scratch=[pltpu.VMEM((FD, WIDE), F32)],
    )

    long = CASES + 32
    residual, shown, own, slots, up, down = call(
        functools.partial(start_kernel, gy),
        [(wide, F32), (wide, F32), ((24, WIDE), F32), ((plane, long, FD), F32), ((long, FD), F32),
         ((long, FD), F32)],
        spots, ids, rhs, *messages, *dirichlet, coupling, smem=2,
    )
    top = passed_along(down, "gz", -1)
    low = passed_along(up, "gz", 1)
    slots = swapped(slots, PLANE)
    joint = call(
        functools.partial(joint_kernel, gy),
        [((QPAD, WIDE), BF16), ((QPAD, WIDE), BF16), ((3 * QPAD, QPAD), BF16)],
        spots, ids, own, slots, low, top, smem=2, scratch=[pltpu.VMEM((QPAD, WIDE), F32)],
    )

    kept = ()
    for iteration in range(ITERS):
        first, last = iteration == 0, iteration + 1 == ITERS
        z, flexed, out = call(
            functools.partial(load_kernel, gy, first),
            [(wide, F32), (wide, F32), ((plane, CASES + 8, FD), F32)],
            spots, mask, *messages, shown, slots, low, top, residual, *flex, weight_high,
            weight_low, expand, *kept[:2], smem=1,
        )
        across = swapped(out, PLANE)
        (layers,) = call(
            layer_kernel, [((gz, CASES + 8, FD), F32)], spots, across, flexed, smem=1
        )
        layers = swapped(layers, "gz")
        (total,) = call(spread_kernel, [((plane, 8, FD), F32)], layers)
        total = swapped(total, PLANE)
        common = (spots, mask, total, across, layers, flexed, z, residual, *inverse, *joint)
        kernel = functools.partial(step_kernel, gy, first, last)
        if last:
            multipliers, left = call(
                kernel, [((3, CASES, FD), F32)] * 2, *common, *kept, smem=1
            )
            break
        search, applied, load, scale, iterate, residual, shown, slots, up, down = call(
            kernel,
            [(wide, F32)] * 3 + [((CASES, FD), F32), ((3, CASES, FD), F32), (wide, F32), (wide, F32),
             ((plane, CASES, FD), F32), ((CASES, FD), F32), ((CASES, FD), F32)],
            *common, *messages, *dirichlet, *kept, smem=1,
        )
        kept = (search, applied, load, scale, iterate)
        top = passed_along(down, "gz", -1)
        low = passed_along(up, "gz", 1)
        slots = swapped(slots, PLANE)
    return multipliers.reshape(jump_rhs.shape), left.reshape(jump_rhs.shape)


def solution(mesh):
    placed = (
        P("gx", "gy", "gz", None, None, None),
        P("gx", "gy", "gz", None, None, None),
        P("gx", "gy", "gz", None, None, None),
        P("gx", "gy", "gz", None, None, None),
        P("gx", "gy", "gz", None, None, None),
        P("gx", "gy", "gz", None, None),
        P("gx", "gy", "gz", None, None),
        P("gx", "gy", "gz", None),
        P("gx", "gy", "gz", None, None),
        P(),
    )
    return jax.shard_map(
        body,
        mesh=mesh,
        in_specs=placed,
        out_specs=(P("gx", "gy", "gz", None, None, None), P("gx", "gy", "gz", None, None, None)),
        check_vma=False,
    )
```

time: 982 us -> 316 us (0.32)
  blocking collectives: 825 us -> 149 us
  local copies, waits for them, and re-layouts: 7.17 us -> 78.7 us
  matrix products: 32.7 us -> 0 us
  starting transfers between devices: 85.8 us -> 53.4 us
  Pallas kernels: 0 us -> 20.7 us
  waiting for transfers between devices: 20.8 us -> 8.41 us
    psum x8 -> x0, blocking collectives: 825 us -> none  [the longest x3 314 us: body(): total_sum = lax.psum(flexibility_local_sum, ('gx', 'gy', 'gz'))]
    all_to_all x0 -> x8, blocking collectives: none -> 149 us  [swapped(): return lax.all_to_all(slots, axes, 0, 0)]
    unnamed x69 -> x275, local copies, waits for them, and re-layouts: 1.56 us -> 72.3 us
    ppermute x36 -> x9, starting transfers between devices: 85.8 us -> 26.6 us  [passed_along(): return lax.ppermute(shard, axis, pairs)]
    dot_general x81 -> x0, matrix products: 32.7 us -> none  [the longest x3 4.49 us: body(): jnp.dot(total_sum, coarse_inverse, precision=HIGHEST)]
    all_to_all x0 -> x4, starting transfers between devices: none -> 26.9 us  [swapped(): return lax.all_to_all(slots, axes, 0, 0)]
    pallas_call x0 -> x19, Pallas kernels: none -> 20.7 us  [call(): pl.pallas_call(kernel, out_shape=[jax.ShapeDtypeStruct(shape, dtype) for...]
    ppermute x36 -> x9, waiting for transfers between devices: 20.8 us -> 6.1 us  [passed_along(): return lax.ppermute(shard, axis, pairs)]
  transfers between devices with their start and end apart: 36 -> 13, of which waited for: 18 -> 3; matrix products, arithmetic and copies ran while one was open for 0% -> 2% of each run, Pallas kernels for 0% -> 1%
where the time goes in v1:
time: 316 us; the launch traced here: 312 us
  blocking collectives  149 us (47%)
  local copies, waits for them, and re-layouts  78.7 us (25%)
  starting transfers between devices  53.4 us (17%)
  Pallas kernels  20.7 us (7%)
  waiting for transfers between devices  8.41 us (3%)
    all_to_all x8, blocking collectives, swapped(): return lax.all_to_all(slots, axes, 0, 0)  149 us
    unnamed x275, local copies, waits for them, and re-layouts  72.3 us
    all_to_all x4, starting transfers between devices, swapped(): return lax.all_to_all(slots, axes, 0, 0)  26.9 us
    ppermute x9, starting transfers between devices, passed_along(): return lax.ppermute(shard, axis, pairs)  26.6 us
    pallas_call x19, Pallas kernels, call(): pl.pallas_call(kernel, out_shape=[jax.ShapeDtypeStruct(shape, dtype) for...  20.7 us
  transfers between devices with their start and end apart: 13, of which 3 were waited for; matrix products, arithmetic and copies ran while one was open for 2% of the time, Pallas kernels for 1%

profile of v1, /device:TPU:1, one launch (start us, length us, event | category | flops | bytes accessed | tf_op | source)
XLA Modules:
  0.0 312.2 jit_solution(15502207009020404753)
XLA Ops:
  2.9 4.4 %collective-permute-start.2 = (f32[24,128]{1,0:T(8,128)S(1)}, f32[24,128]{1,0:T(8,128)S(1)}, u32[]{:S(2)}, u32[]{:S(2)}) collective-permute-start(f32[24,128]{1,0:T(8,128)S(1)} %get-tuple-element.100), channel_id=1, source_target_pairs={{0,1},{1,2},{2,3},{3,4},{4,5},{5,6},{6,7},{7,8},{8,9},{9,10},{10,1... | collective-permute-start | bytes 36872 | tf_op jit(solution)/shard_map/ppermute | solution.py:338
  7.3 3.1 collective-permute-start.1
  10.4 4.3 %collective-permute-start = (f32[24,128]{1,0:T(8,128)S(1)}, f32[24,128]{1,0:T(8,128)S(1)}, u32[]{:S(2)}, u32[]{:S(2)}) collective-permute-start(f32[24,128]{1,0:T(8,128)S(1)} %get-tuple-element.102), channel_id=1, source_target_pairs={{0,64},{64,128},{128,192},{192,256},{256,320},{320,384},{384,448},... | collective-permute-start | bytes 36872 | tf_op jit(solution)/shard_map/ppermute | solution.py:338
  15.6 1.0 copy-done.49
  16.6 1.0 copy-done.50
  17.6 1.0 shard_map.114
  18.6 1.0 copy-done.53
  21.0 2.0 shard_map.115
  24.9 6.8 %all-to-all-start = ((f32[32,48,128]{2,1,0:T(8,128)}), f32[32,48,128]{2,1,0:T(8,128)S(1)}, u32[]{:S(2)}, u32[]{:S(2)}) async-start(f32[32,48,128]{2,1,0:T(8,128)} %get-tuple-element.54), calls=%async_computation | async-start | bytes 1572864 | tf_op jit(solution)/shard_map/all_to_all | solution.py:342
  31.8 3.5 %collective-permute-start.3 = (f32[48,128]{1,0:T(8,128)}, f32[48,128]{1,0:T(8,128)S(1)}, u32[]{:S(2)}, u32[]{:S(2)}) collective-permute-start(f32[48,128]{1,0:T(8,128)} %get-tuple-element.55), channel_id=1, source_target_pairs={{0,1},{1,2},{2,3},{3,4},{4,5},{5,6},{6,7},{7,8},{8,9},{9,10},{10,1... | collective-permute-start | bytes 73736 | tf_op jit(solution)/shard_map/ppermute | solution.py:338
  35.3 1.3 collective-permute-start.4
  38.1 1.1 copy-done.51
  39.2 1.0 copy-done.52
  40.8 1.0 shard_map.116
  43.0 2.3 all-to-all-done.slots_ref
  45.3 1.1 copy-done.33
  47.9 0.8 copy-done.58
  50.8 0.8 copy-done.103
  51.6 1.3 shard_map.118
  53.5 15.3 %all_to_all.60.slots_ref = f32[32,24,128]{2,1,0:T(8,128)S(1)} all-to-all(f32[32,24,128]{2,1,0:T(8,128)S(1)} %get-tuple-element.63), channel_id=1, replica_groups=mesh['gx'=8,'gy'=4,'gz'=16] {'gx','gy'}, dimensions={0} | all-to-all | bytes 786432 | tf_op jit(solution)/shard_map/all_to_all | solution.py:342
  70.2 28.6 %all_to_all.61.slots_ref.layers_ref = f32[16,24,128]{2,1,0:T(8,128)S(1)} all-to-all(f32[16,24,128]{2,1,0:T(8,128)S(1)} %shard_map.119), channel_id=1, replica_groups=mesh['gx'=8,'gy'=4,'gz'=16] {'gz'}, dimensions={0} | all-to-all | bytes 393216 | tf_op jit(solution)/shard_map/all_to_all | solution.py:342
  100.2 8.0 %all-to-all-start.3 = ((f32[32,8,128]{2,1,0:T(8,128)}), f32[32,8,128]{2,1,0:T(8,128)}, u32[]{:S(2)}, u32[]{:S(2)}) async-start(f32[32,8,128]{2,1,0:T(8,128)} %shard_map.120), calls=%async_computation.3 | async-start | bytes 262144 | tf_op jit(solution)/shard_map/all_to_all | solution.py:342
  108.1 4.0 %reshape.52 = f32[3,192,3,192]{3,2,1,0:T(4,128)} reshape(f32[576,576]{1,0:T(8,128)} %param.19) | data formatting | bytes 2654208 | tf_op jit(solution)/shard_map/reshape | solution.py:386
  112.2 2.2 pad.4
  115.3 1.0 copy-done
  119.4 1.3 copy-done.1
  120.6 1.3 copy-done.5
  121.9 1.3 copy-done.8
  123.2 1.0 copy-done.13
  124.2 1.0 copy-done.17
  125.2 1.0 copy-done.21
  126.2 1.0 copy-done.25
  127.2 0.9 copy-done.37
  129.5 0.8 copy-done.59
  130.3 0.8 copy-done.61
  131.8 0.8 copy-done.105
  132.6 2.4 shard_map.123
  141.2 7.5 %all-to-all-start.4 = ((f32[32,16,128]{2,1,0:T(8,128)}), f32[32,16,128]{2,1,0:T(8,128)}, u32[]{:S(2)}, u32[]{:S(2)}) async-start(f32[32,16,128]{2,1,0:T(8,128)} %copy-done.56), calls=%async_computation.4 | async-start | bytes 524288 | tf_op jit(solution)/shard_map/all_to_all | solution.py:342
  148.7 3.8 %collective-permute-start.5 = (f32[16,128]{1,0:T(8,128)}, f32[16,128]{1,0:T(8,128)S(1)}, u32[]{:S(2)}, u32[]{:S(2)}) collective-permute-start(f32[16,128]{1,0:T(8,128)} %copy-done.134), channel_id=1, source_target_pairs={{0,1},{1,2},{2,3},{3,4},{4,5},{5,6},{6,7},{7,8},{8,9},{9,10},{10,1... | collective-permute-start | bytes 24584 | tf_op jit(solution)/shard_map/ppermute | solution.py:338
  152.5 1.3 collective-permute-start.6
  154.4 3.0 collective-permute-done.6.top_ref
  158.0 0.9 copy-done.27
  159.0 0.9 copy-done.30
  159.9 0.9 copy-done.34
  162.2 0.8 copy-done.72
  163.0 0.8 copy-done.75
  165.3 0.8 copy-done.109
  167.6 1.9 shard_map.124
  169.5 18.6 %all_to_all.62.slots_ref = f32[32,24,128]{2,1,0:T(8,128)S(1)} all-to-all(f32[32,24,128]{2,1,0:T(8,128)S(1)} %get-tuple-element.79), channel_id=1, replica_groups=mesh['gx'=8,'gy'=4,'gz'=16] {'gx','gy'}, dimensions={0} | all-to-all | bytes 786432 | tf_op jit(solution)/shard_map/all_to_all | solution.py:342
  188.7 19.2 %all_to_all.63.slots_ref.layers_ref = f32[16,24,128]{2,1,0:T(8,128)S(1)} all-to-all(f32[16,24,128]{2,1,0:T(8,128)S(1)} %shard_map.125), channel_id=1, replica_groups=mesh['gx'=8,'gy'=4,'gz'=16] {'gz'}, dimensions={0} | all-to-all | bytes 393216 | tf_op jit(solution)/shard_map/all_to_all | solution.py:342
  207.9 15.2 %all_to_all.64.total_ref = f32[32,8,128]{2,1,0:T(8,128)S(1)} all-to-all(f32[32,8,128]{2,1,0:T(8,128)S(1)} %shard_map.126), channel_id=1, replica_groups=mesh['gx'=8,'gy'=4,'gz'=16] {'gx','gy'}, dimensions={0} | all-to-all | bytes 262144 | tf_op jit(solution)/shard_map/all_to_all | solution.py:342
  223.2 2.2 shard_map.127
  231.6 4.7 %all-to-all-start.8 = ((f32[32,16,128]{2,1,0:T(8,128)}), f32[32,16,128]{2,1,0:T(8,128)}, u32[]{:S(2)}, u32[]{:S(2)}) async-start(f32[32,16,128]{2,1,0:T(8,128)} %copy-done.55), calls=%async_computation.8 | async-start | bytes 524288 | tf_op jit(solution)/shard_map/all_to_all | solution.py:342
  236.3 3.5 %collective-permute-start.7 = (f32[16,128]{1,0:T(8,128)}, f32[16,128]{1,0:T(8,128)S(1)}, u32[]{:S(2)}, u32[]{:S(2)}) collective-permute-start(f32[16,128]{1,0:T(8,128)} %copy-done.132), channel_id=1, source_target_pairs={{0,1},{1,2},{2,3},{3,4},{4,5},{5,6},{6,7},{7,8},{8,9},{9,10},{10,1... | collective-permute-start | bytes 24584 | tf_op jit(solution)/shard_map/ppermute | solution.py:338
  239.8 1.3 collective-permute-start.8
  241.7 3.1 collective-permute-done.8.top_ref
  245.4 0.9 copy-done.28
  246.4 0.9 copy-done.31
  247.3 0.9 copy-done.35
  254.9 1.8 shard_map.128
  256.8 18.6 %all_to_all.65.slots_ref = f32[32,24,128]{2,1,0:T(8,128)S(1)} all-to-all(f32[32,24,128]{2,1,0:T(8,128)S(1)} %get-tuple-element.92), channel_id=1, replica_groups=mesh['gx'=8,'gy'=4,'gz'=16] {'gx','gy'}, dimensions={0} | all-to-all | bytes 786432 | tf_op jit(solution)/shard_map/all_to_all | solution.py:342
  275.9 18.6 %all_to_all.66.slots_ref.layers_ref = f32[16,24,128]{2,1,0:T(8,128)S(1)} all-to-all(f32[16,24,128]{2,1,0:T(8,128)S(1)} %shard_map.129), channel_id=1, replica_groups=mesh['gx'=8,'gy'=4,'gz'=16] {'gz'}, dimensions={0} | all-to-all | bytes 393216 | tf_op jit(solution)/shard_map/all_to_all | solution.py:342
  294.6 15.2 %all_to_all.67.total_ref = f32[32,8,128]{2,1,0:T(8,128)S(1)} all-to-all(f32[32,8,128]{2,1,0:T(8,128)S(1)} %shard_map.130), channel_id=1, replica_groups=mesh['gx'=8,'gy'=4,'gz'=16] {'gx','gy'}, dimensions={0} | all-to-all | bytes 262144 | tf_op jit(solution)/shard_map/all_to_all | solution.py:342
  309.9 2.3 shard_map.131
  (271 shorter events, 49.7 us)
Async XLA Ops:
  1.4 17.2 %copy-start.88 = (s32[8]{0:T(128)}, s32[8]{0:T(128)S(1)}, u32[]{:S(2)}) copy-start(s32[8]{0:T(128)S(1)} %stack.61.spots) | copy-start | bytes 100
  2.9 15.7 %collective-permute-start.2 = (f32[24,128]{1,0:T(8,128)S(1)}, f32[24,128]{1,0:T(8,128)S(1)}, u32[]{:S(2)}, u32[]{:S(2)}) collective-permute-start(f32[24,128]{1,0:T(8,128)S(1)} %get-tuple-element.100), channel_id=1, source_target_pairs={{0,1},{1,2},{2,3},{3,4},{4,5},{5,6},{6,7},{7,8},{8,9},{9,10},{10,1... | collective-permute-start | bytes 36872 | tf_op jit(solution)/shard_map/ppermute | solution.py:338
  7.3 11.3 %collective-permute-start.1 = (f32[24,128]{1,0:T(8,128)S(1)}, f32[24,128]{1,0:T(8,128)S(1)}, u32[]{:S(2)}, u32[]{:S(2)}) collective-permute-start(f32[24,128]{1,0:T(8,128)S(1)} %get-tuple-element.101), channel_id=1, source_target_pairs={{0,16},{16,32},{32,48},{1,17},{17,33},{33,49},{2,18},{18,34},{34,5... | collective-permute-start | bytes 36872 | tf_op jit(solution)/shard_map/ppermute | solution.py:338
  10.4 8.2 %collective-permute-start = (f32[24,128]{1,0:T(8,128)S(1)}, f32[24,128]{1,0:T(8,128)S(1)}, u32[]{:S(2)}, u32[]{:S(2)}) collective-permute-start(f32[24,128]{1,0:T(8,128)S(1)} %get-tuple-element.102), channel_id=1, source_target_pairs={{0,64},{64,128},{128,192},{192,256},{256,320},{320,384},{384,448},... | collective-permute-start | bytes 36872 | tf_op jit(solution)/shard_map/ppermute | solution.py:338
  15.6 3.0 copy-start.129
  15.6 1.0 copy-start.49
  18.5 4.5 %copy-start.4 = (bf16[768,768]{1,0:T(8,128)(2,1)}, bf16[768,768]{1,0:T(8,128)(2,1)S(1)}, u32[]{:S(2)}) copy-start(bf16[768,768]{1,0:T(8,128)(2,1)S(1)} %get-tuple-element.51.dh_ref.rest_3_) | copy-start | bytes 3538948
  18.5 4.5 %copy-start.7 = (bf16[768,768]{1,0:T(8,128)(2,1)}, bf16[768,768]{1,0:T(8,128)(2,1)S(1)}, u32[]{:S(2)}) copy-start(bf16[768,768]{1,0:T(8,128)(2,1)S(1)} %get-tuple-element.52.dl_ref.rest_4_) | copy-start | bytes 3538948
  18.6 4.4 %copy-start.38 = (f32[24,128]{1,0:T(8,128)}, f32[24,128]{1,0:T(8,128)S(1)}, u32[]{:S(2)}) copy-start(f32[24,128]{1,0:T(8,128)S(1)} %collective-permute-done.1.my_ref.rest_1_) | copy-start | bytes 36868
  18.6 4.4 %copy-start.43 = (f32[24,128]{1,0:T(8,128)}, f32[24,128]{1,0:T(8,128)S(1)}, u32[]{:S(2)}) copy-start(f32[24,128]{1,0:T(8,128)S(1)} %collective-permute-done.mx_ref.rest_0_) | copy-start | bytes 36868
  24.9 11.8 %copy-start.54 = (f32[1,1,1,24,768]{4,3,2,1,0:T(8,128)S(1)}, f32[1,1,1,24,768]{4,3,2,1,0:T(8,128)}, u32[]{:S(2)}) copy-start(f32[1,1,1,24,768]{4,3,2,1,0:T(8,128)} %param.16) | copy-start | bytes 221188
  24.9 11.8 %copy-start.127 = (s32[1,1,1,8]{3,2,1,0:T(1,128)S(1)}, s32[1,1,1,8]{3,2,1,0:T(1,128)}, u32[]{:S(2)}) copy-start(s32[1,1,1,8]{3,2,1,0:T(1,128)} %param.17) | copy-start | bytes 100
  24.9 20.4 %all-to-all-start = ((f32[32,48,128]{2,1,0:T(8,128)}), f32[32,48,128]{2,1,0:T(8,128)S(1)}, u32[]{:S(2)}, u32[]{:S(2)}) async-start(f32[32,48,128]{2,1,0:T(8,128)} %get-tuple-element.54), calls=%async_computation | async-start | bytes 1572864 | tf_op jit(solution)/shard_map/all_to_all | solution.py:342
  31.8 10.0 %collective-permute-start.3 = (f32[48,128]{1,0:T(8,128)}, f32[48,128]{1,0:T(8,128)S(1)}, u32[]{:S(2)}, u32[]{:S(2)}) collective-permute-start(f32[48,128]{1,0:T(8,128)} %get-tuple-element.55), channel_id=1, source_target_pairs={{0,1},{1,2},{2,3},{3,4},{4,5},{5,6},{6,7},{7,8},{8,9},{9,10},{10,1... | collective-permute-start | bytes 73736 | tf_op jit(solution)/shard_map/ppermute | solution.py:338
  35.3 7.1 %collective-permute-start.4 = (f32[48,128]{1,0:T(8,128)}, f32[48,128]{1,0:T(8,128)S(1)}, u32[]{:S(2)}, u32[]{:S(2)}) collective-permute-start(f32[48,128]{1,0:T(8,128)} %get-tuple-element.56), channel_id=1, source_target_pairs={{1,0},{2,1},{3,2},{4,3},{5,4},{6,5},{7,6},{8,7},{9,8},{10,9},{11,1... | collective-permute-start | bytes 73736 | tf_op jit(solution)/shard_map/ppermute | solution.py:338
  38.1 14.8 %copy-start.26 = (bf16[768,128]{1,0:T(8,128)(2,1)}, bf16[768,128]{1,0:T(8,128)(2,1)S(1)}, u32[]{:S(2)}) copy-start(bf16[768,128]{1,0:T(8,128)(2,1)S(1)} %get-tuple-element.60.wh_ref) | copy-start | bytes 589828
  38.1 14.8 %copy-start.29 = (bf16[768,128]{1,0:T(8,128)(2,1)}, bf16[768,128]{1,0:T(8,128)(2,1)S(1)}, u32[]{:S(2)}) copy-start(bf16[768,128]{1,0:T(8,128)(2,1)S(1)} %get-tuple-element.61.wl_ref) | copy-start | bytes 589828
  38.1 1.1 copy-start.51
  39.2 1.0 copy-start.52
  45.3 7.6 %copy-start.10 = (f32[32,48,128]{2,1,0:T(8,128)}, f32[32,48,128]{2,1,0:T(8,128)S(1)}, u32[]{:S(2)}) copy-start(f32[32,48,128]{2,1,0:T(8,128)S(1)} %all-to-all-done.slots_ref) | copy-start | bytes 2359300
  45.3 1.1 copy-start.33
  53.5 45.3 %copy-start.60 = (f32[16,768]{1,0:T(8,128)}, f32[16,768]{1,0:T(8,128)S(1)}, u32[]{:S(2)}) copy-start(f32[16,768]{1,0:T(8,128)S(1)} %get-tuple-element.64.flexed_ref) | copy-start | bytes 147460
  100.2 19.2 %all-to-all-start.3 = ((f32[32,8,128]{2,1,0:T(8,128)}), f32[32,8,128]{2,1,0:T(8,128)}, u32[]{:S(2)}, u32[]{:S(2)}) async-start(f32[32,8,128]{2,1,0:T(8,128)} %shard_map.120), calls=%async_computation.3 | async-start | bytes 262144 | tf_op jit(solution)/shard_map/all_to_all | solution.py:342
  114.9 1.5 copy-start.11
  114.9 1.5 copy-start.84
  114.9 1.4 copy-start.87
  114.9 1.4 copy-start.90
  114.9 1.4 copy-start.97
  115.0 1.4 copy-start.128
  115.3 1.0 copy-start
  119.4 1.3 copy-start.1
  120.6 1.3 copy-start.5
  121.9 1.3 copy-start.8
  141.2 16.8 %all-to-all-start.4 = ((f32[32,16,128]{2,1,0:T(8,128)}), f32[32,16,128]{2,1,0:T(8,128)}, u32[]{:S(2)}, u32[]{:S(2)}) async-start(f32[32,16,128]{2,1,0:T(8,128)} %copy-done.56), calls=%async_computation.4 | async-start | bytes 524288 | tf_op jit(solution)/shard_map/all_to_all | solution.py:342
  148.7 5.1 %collective-permute-start.5 = (f32[16,128]{1,0:T(8,128)}, f32[16,128]{1,0:T(8,128)S(1)}, u32[]{:S(2)}, u32[]{:S(2)}) collective-permute-start(f32[16,128]{1,0:T(8,128)} %copy-done.134), channel_id=1, source_target_pairs={{0,1},{1,2},{2,3},{3,4},{4,5},{5,6},{6,7},{7,8},{8,9},{9,10},{10,1... | collective-permute-start | bytes 24584 | tf_op jit(solution)/shard_map/ppermute | solution.py:338
  152.5 4.9 %collective-permute-start.6 = (f32[16,128]{1,0:T(8,128)}, f32[16,128]{1,0:T(8,128)S(1)}, u32[]{:S(2)}, u32[]{:S(2)}) collective-permute-start(f32[16,128]{1,0:T(8,128)} %copy-done.133), channel_id=1, source_target_pairs={{1,0},{2,1},{3,2},{4,3},{5,4},{6,5},{7,6},{8,7},{9,8},{10,9},{11,1... | collective-permute-start | bytes 24584 | tf_op jit(solution)/shard_map/ppermute | solution.py:338
  167.5 20.6 %copy-start.93 = (s32[8]{0:T(128)S(1)}, s32[8]{0:T(128)}, u32[]{:S(2)}) copy-start(s32[8]{0:T(128)} %copy-done.88) | copy-start | bytes 100
  167.5 55.6 %copy-start.9 = (bf16[768,768]{1,0:T(8,128)(2,1)S(1)}, bf16[768,768]{1,0:T(8,128)(2,1)}, u32[]{:S(2)}) copy-start(bf16[768,768]{1,0:T(8,128)(2,1)} %copy-done.7) | copy-start | bytes 3538948
  167.5 55.6 %copy-start.14 = (bf16[256,768]{1,0:T(8,128)(2,1)S(1)}, bf16[256,768]{1,0:T(8,128)(2,1)}, u32[]{:S(2)}) copy-start(bf16[256,768]{1,0:T(8,128)(2,1)} %copy-done.12) | copy-start | bytes 1179652
  167.5 55.6 %copy-start.18 = (bf16[256,768]{1,0:T(8,128)(2,1)S(1)}, bf16[256,768]{1,0:T(8,128)(2,1)}, u32[]{:S(2)}) copy-start(bf16[256,768]{1,0:T(8,128)(2,1)} %copy-done.16) | copy-start | bytes 1179652
  167.5 55.6 %copy-start.22 = (bf16[768,256]{1,0:T(8,128)(2,1)S(1)}, bf16[768,256]{1,0:T(8,128)(2,1)}, u32[]{:S(2)}) copy-start(bf16[768,256]{1,0:T(8,128)(2,1)} %copy-done.20) | copy-start | bytes 1179652
  167.5 55.6 %copy-start.73 = (f32[16,768]{1,0:T(8,128)S(1)}, f32[16,768]{1,0:T(8,128)}, u32[]{:S(2)}) copy-start(f32[16,768]{1,0:T(8,128)} %copy-done.71) | copy-start | bytes 147460
  167.5 55.6 %copy-start.76 = (f32[16,768]{1,0:T(8,128)S(1)}, f32[16,768]{1,0:T(8,128)}, u32[]{:S(2)}) copy-start(f32[16,768]{1,0:T(8,128)} %copy-done.74) | copy-start | bytes 147460
  167.5 55.6 %copy-start.79 = (f32[16,768]{1,0:T(8,128)S(1)}, f32[16,768]{1,0:T(8,128)}, u32[]{:S(2)}) copy-start(f32[16,768]{1,0:T(8,128)} %copy-done.77) | copy-start | bytes 147460
  167.5 55.6 %copy-start.101 = (f32[16,768]{1,0:T(8,128)S(1)}, f32[16,768]{1,0:T(8,128)}, u32[]{:S(2)}) copy-start(f32[16,768]{1,0:T(8,128)} %copy-done.100) | copy-start | bytes 147460
  169.4 53.8 %copy-start.2 = (bf16[768,768]{1,0:T(8,128)(2,1)S(1)}, bf16[768,768]{1,0:T(8,128)(2,1)}, u32[]{:S(2)}) copy-start(bf16[768,768]{1,0:T(8,128)(2,1)} %copy-done) | copy-start | bytes 3538948
  169.4 53.8 %copy-start.6 = (bf16[768,768]{1,0:T(8,128)(2,1)S(1)}, bf16[768,768]{1,0:T(8,128)(2,1)}, u32[]{:S(2)}) copy-start(bf16[768,768]{1,0:T(8,128)(2,1)} %copy-done.4) | copy-start | bytes 3538948
  169.4 53.8 %copy-start.47 = (f32[24,128]{1,0:T(8,128)S(1)}, f32[24,128]{1,0:T(8,128)}, u32[]{:S(2)}) copy-start(f32[24,128]{1,0:T(8,128)} %copy-done.43) | copy-start | bytes 36868
  169.4 53.8 %copy-start.113 = (f32[3,16,128]{2,1,0:T(8,128)S(1)}, f32[3,16,128]{2,1,0:T(8,128)}, u32[]{:S(2)}) copy-start(f32[3,16,128]{2,1,0:T(8,128)} %copy-done.112) | copy-start | bytes 73732
  169.5 53.8 %copy-start.117 = (f32[16,128]{1,0:T(8,128)S(1)}, f32[16,128]{1,0:T(8,128)}, u32[]{:S(2)}) copy-start(f32[16,128]{1,0:T(8,128)} %copy-done.116) | copy-start | bytes 24580
  231.6 13.8 %all-to-all-start.8 = ((f32[32,16,128]{2,1,0:T(8,128)}), f32[32,16,128]{2,1,0:T(8,128)}, u32[]{:S(2)}, u32[]{:S(2)}) async-start(f32[32,16,128]{2,1,0:T(8,128)} %copy-done.55), calls=%async_computation.8 | async-start | bytes 524288 | tf_op jit(solution)/shard_map/all_to_all | solution.py:342
  236.3 4.8 %collective-permute-start.7 = (f32[16,128]{1,0:T(8,128)}, f32[16,128]{1,0:T(8,128)S(1)}, u32[]{:S(2)}, u32[]{:S(2)}) collective-permute-start(f32[16,128]{1,0:T(8,128)} %copy-done.132), channel_id=1, source_target_pairs={{0,1},{1,2},{2,3},{3,4},{4,5},{5,6},{6,7},{7,8},{8,9},{9,10},{10,1... | collective-permute-start | bytes 24584 | tf_op jit(solution)/shard_map/ppermute | solution.py:338
  239.8 5.0 %collective-permute-start.8 = (f32[16,128]{1,0:T(8,128)}, f32[16,128]{1,0:T(8,128)S(1)}, u32[]{:S(2)}, u32[]{:S(2)}) collective-permute-start(f32[16,128]{1,0:T(8,128)} %copy-done.131), channel_id=1, source_target_pairs={{1,0},{2,1},{3,2},{4,3},{5,4},{6,5},{7,6},{8,7},{9,8},{10,9},{11,1... | collective-permute-start | bytes 24584 | tf_op jit(solution)/shard_map/ppermute | solution.py:338
  254.9 20.4 %copy-start.95 = (s32[8]{0:T(128)S(1)}, s32[8]{0:T(128)}, u32[]{:S(2)}) copy-start(s32[8]{0:T(128)} %copy-done.88) | copy-start | bytes 100
  254.9 54.9 %copy-start.67 = (f32[16,768]{1,0:T(8,128)S(1)}, f32[16,768]{1,0:T(8,128)}, u32[]{:S(2)}) copy-start(f32[16,768]{1,0:T(8,128)} %copy-done.65) | copy-start | bytes 147460
  254.9 54.9 %copy-start.70 = (f32[16,768]{1,0:T(8,128)S(1)}, f32[16,768]{1,0:T(8,128)}, u32[]{:S(2)}) copy-start(f32[16,768]{1,0:T(8,128)} %copy-done.68) | copy-start | bytes 147460
  254.9 54.9 %copy-start.99 = (f32[16,768]{1,0:T(8,128)S(1)}, f32[16,768]{1,0:T(8,128)}, u32[]{:S(2)}) copy-start(f32[16,768]{1,0:T(8,128)} %copy-done.98) | copy-start | bytes 147460
  254.9 54.9 %copy-start.111 = (f32[3,16,128]{2,1,0:T(8,128)S(1)}, f32[3,16,128]{2,1,0:T(8,128)}, u32[]{:S(2)}) copy-start(f32[3,16,128]{2,1,0:T(8,128)} %copy-done.110) | copy-start | bytes 73732
  256.7 53.1 %copy-start.3 = (bf16[768,768]{1,0:T(8,128)(2,1)S(1)}, bf16[768,768]{1,0:T(8,128)(2,1)}, u32[]{:S(2)}) copy-start(bf16[768,768]{1,0:T(8,128)(2,1)} %copy-done) | copy-start | bytes 3538948
  256.7 53.1 %copy-start.15 = (bf16[256,768]{1,0:T(8,128)(2,1)S(1)}, bf16[256,768]{1,0:T(8,128)(2,1)}, u32[]{:S(2)}) copy-start(bf16[256,768]{1,0:T(8,128)(2,1)} %copy-done.12) | copy-start | bytes 1179652
  256.7 53.1 %copy-start.19 = (bf16[256,768]{1,0:T(8,128)(2,1)S(1)}, bf16[256,768]{1,0:T(8,128)(2,1)}, u32[]{:S(2)}) copy-start(bf16[256,768]{1,0:T(8,128)(2,1)} %copy-done.16) | copy-start | bytes 1179652
  256.7 53.1 %copy-start.23 = (bf16[768,256]{1,0:T(8,128)(2,1)S(1)}, bf16[768,256]{1,0:T(8,128)(2,1)}, u32[]{:S(2)}) copy-start(bf16[768,256]{1,0:T(8,128)(2,1)} %copy-done.20) | copy-start | bytes 1179652
  256.7 53.1 %copy-start.64 = (f32[16,768]{1,0:T(8,128)S(1)}, f32[16,768]{1,0:T(8,128)}, u32[]{:S(2)}) copy-start(f32[16,768]{1,0:T(8,128)} %copy-done.62) | copy-start | bytes 147460
  256.7 53.1 %copy-start.115 = (f32[16,128]{1,0:T(8,128)S(1)}, f32[16,128]{1,0:T(8,128)}, u32[]{:S(2)}) copy-start(f32[16,128]{1,0:T(8,128)} %copy-done.114) | copy-start | bytes 24580
  (84 other events, 61.1 us)

commit v2 on v1

--- a/solution.py
+++ b/solution.py
@@ -136,8 +136,14 @@
         put(first, second, block.T)
 
 
-def split_kernel(matrix_ref, high_ref, low_ref):
-    high, low = halves(matrix_ref[...])
+def split_kernel(matrix_ref, high_ref, low_ref, pad):
+    pad[...] = jnp.zeros_like(pad)
+    for p in range(3):
+        for q in range(3):
+            pad[p * QPAD:p * QPAD + 192, q * QPAD:q * QPAD + 192] = matrix_ref[
+                p * 192:(p + 1) * 192, q * 192:(q + 1) * 192
+            ]
+    high, low = halves(pad[...])
     high_ref[...] = high
     low_ref[...] = low
 
@@ -382,16 +388,17 @@
 
     dirichlet = build(dirichlet_diag, dirichlet_couple)
     flex = build(flex_diag, flex_couple)
-    padded = jnp.pad(
-        coarse_inverse.reshape(3, 192, 3, 192), ((0, 0), (0, 64), (0, 0), (0, 64))
-    ).reshape(square)
-    inverse = call(split_kernel, [(square, BF16)] * 2, padded)
+    inverse = call(
+        split_kernel, [(square, BF16)] * 2, coarse_inverse, scratch=[pltpu.VMEM(square, F32)]
+    )
     weight_high, weight_low, expand = call(
         corner_kernel,
         [((WIDE, FD), BF16), ((WIDE, FD), BF16), ((FD, WIDE), BF16)],
         ids, coupling, smem=1, scratch=[pltpu.VMEM((FD, WIDE), F32)],
     )
 
+    setup = (messages, dirichlet, flex, inverse, weight_high, weight_low, expand)
+    messages, dirichlet, flex, inverse, weight_high, weight_low, expand = lax.optimization_barrier(setup)
     long = CASES + 32
     residual, shown, own, slots, up, down = call(
         functools.partial(start_kernel, gy),
@@ -401,6 +408,7 @@
     )
     top = passed_along(down, "gz", -1)
     low = passed_along(up, "gz", 1)
+    slots, low, top = lax.optimization_barrier((slots, low, top))
     slots = swapped(slots, PLANE)
     joint = call(
         functools.partial(joint_kernel, gy),
@@ -408,6 +416,7 @@
         spots, ids, own, slots, low, top, smem=2, scratch=[pltpu.VMEM((QPAD, WIDE), F32)],
     )
 
+    slots, low, top, joint = lax.optimization_barrier((slots, low, top, joint))
     kept = ()
     for iteration in range(ITERS):
         first, last = iteration == 0, iteration + 1 == ITERS
@@ -440,6 +449,7 @@
         kept = (search, applied, load, scale, iterate)
         top = passed_along(down, "gz", -1)
         low = passed_along(up, "gz", 1)
+        slots, low, top = lax.optimization_barrier((slots, low, top))
         slots = swapped(slots, PLANE)
     return multipliers.reshape(jump_rhs.shape), left.reshape(jump_rhs.shape)
 

time: 316 us -> 285 us (0.902)
  local copies, waits for them, and re-layouts: 78.7 us -> 25.1 us
  blocking collectives: 149 us -> 181 us
  starting transfers between devices: 53.4 us -> 33.2 us
  waiting for transfers between devices: 8.41 us -> 22.6 us
    unnamed x275 -> x94, local copies, waits for them, and re-layouts: 72.3 us -> 23.6 us
    all_to_all x8 -> x11, blocking collectives: 149 us -> 181 us  [swapped(): return lax.all_to_all(slots, axes, 0, 0)]
    all_to_all x4 -> x1, starting transfers between devices: 26.9 us -> 6.35 us  [swapped(): return lax.all_to_all(slots, axes, 0, 0)]
    all_to_all x4 -> x1, waiting for transfers between devices: 2.31 us -> 13.5 us  [swapped(): return lax.all_to_all(slots, axes, 0, 0)]
    reshape x1 -> x0, local copies, waits for them, and re-layouts: 4.02 us -> none  [body(): coarse_inverse.reshape(3, 192, 3, 192)]
  transfers between devices with their start and end apart: 13 -> 10, of which waited for: 3 -> 4; matrix products, arithmetic and copies ran while one was open for 2% -> 1% of each run, Pallas kernels for 1% -> 1%
where the time goes in v2:
time: 285 us; the launch traced here: 283 us
  blocking collectives  181 us (64%)
  starting transfers between devices  33.2 us (12%)
  local copies, waits for them, and re-layouts  25.1 us (9%)
  waiting for transfers between devices  22.6 us (8%)
  Pallas kernels  20.3 us (7%)
    all_to_all x11, blocking collectives, swapped(): return lax.all_to_all(slots, axes, 0, 0)  181 us
    ppermute x9, starting transfers between devices, passed_along(): return lax.ppermute(shard, axis, pairs)  26.9 us
    unnamed x94, local copies, waits for them, and re-layouts  23.6 us
    pallas_call x19, Pallas kernels, call(): pl.pallas_call(kernel, out_shape=[jax.ShapeDtypeStruct(shape, dtype) for...  20.3 us
    all_to_all x1, waiting for transfers between devices, swapped(): return lax.all_to_all(slots, axes, 0, 0)  13.5 us
    ppermute x9, waiting for transfers between devices, passed_along(): return lax.ppermute(shard, axis, pairs)  9.02 us
    all_to_all x1, starting transfers between devices, swapped(): return lax.all_to_all(slots, axes, 0, 0)  6.35 us
  transfers between devices with their start and end apart: 10, of which 4 were waited for; matrix products, arithmetic and copies ran while one was open for 1% of the time, Pallas kernels for 1%

profile of v2, /device:TPU:1, one launch (start us, length us, event | category | flops | bytes accessed | tf_op | source)
XLA Modules:
  0.0 283.2 jit_solution(3655636709452627666)
XLA Ops:
  0.7 0.7 copy.19
  1.5 0.7 copy-done.24
  2.2 0.7 shard_map.113
  2.9 0.6 slice_bitcast_fusion
  3.5 4.4 %collective-permute-start.2 = (f32[24,128]{1,0:T(8,128)}, f32[24,128]{1,0:T(8,128)S(1)}, u32[]{:S(2)}, u32[]{:S(2)}) collective-permute-start(f32[24,128]{1,0:T(8,128)} %get-tuple-element.154), channel_id=1, source_target_pairs={{0,1},{1,2},{2,3},{3,4},{4,5},{5,6},{6,7},{7,8},{8,9},{9,10},{10,1... | collective-permute-start | bytes 36872 | tf_op jit(solution)/shard_map/ppermute | solution.py:344
  7.9 3.7 %collective-permute-start.1 = (f32[24,128]{1,0:T(8,128)}, f32[24,128]{1,0:T(8,128)}, u32[]{:S(2)}, u32[]{:S(2)}) collective-permute-start(f32[24,128]{1,0:T(8,128)} %get-tuple-element.155), channel_id=1, source_target_pairs={{0,16},{16,32},{32,48},{1,17},{17,33},{33,49},{2,18},{18,34},{34,5... | collective-permute-start | bytes 36872 | tf_op jit(solution)/shard_map/ppermute | solution.py:344
  11.6 4.3 %collective-permute-start = (f32[24,128]{1,0:T(8,128)}, f32[24,128]{1,0:T(8,128)}, u32[]{:S(2)}, u32[]{:S(2)}) collective-permute-start(f32[24,128]{1,0:T(8,128)} %get-tuple-element.156), channel_id=1, source_target_pairs={{0,64},{64,128},{128,192},{192,256},{256,320},{320,384},{384,448},... | collective-permute-start | bytes 36872 | tf_op jit(solution)/shard_map/ppermute | solution.py:344
  15.9 0.8 copy.13
  16.7 0.7 reshape.39.pairs
  17.4 1.4 copy-done.13
  19.4 0.7 shard_map.117
  20.2 0.7 copy-done.7
  20.8 0.7 copy-done.9
  21.5 0.7 copy-done.11
  22.2 0.7 copy-done.43
  22.8 1.0 shard_map.115
  23.8 1.0 copy-done
  24.9 0.7 copy-done.44
  25.5 1.0 shard_map.114
  26.6 1.4 shard_map.118
  28.0 0.9 copy-done.14
  30.8 3.5 %collective-permute-start.3 = (f32[48,128]{1,0:T(8,128)S(1)}, f32[48,128]{1,0:T(8,128)S(1)}, u32[]{:S(2)}, u32[]{:S(2)}) collective-permute-start(f32[48,128]{1,0:T(8,128)S(1)} %get-tuple-element.94), channel_id=1, source_target_pairs={{0,1},{1,2},{2,3},{3,4},{4,5},{5,6},{6,7},{7,8},{8,9},{9,10},{10,1... | collective-permute-start | bytes 73736 | tf_op jit(solution)/shard_map/ppermute | solution.py:344
  34.4 1.3 collective-permute-start.4
  36.3 2.8 %collective-permute-done.4.top_ref = f32[48,128]{1,0:T(8,128)S(1)} collective-permute-done((f32[48,128]{1,0:T(8,128)S(1)}, f32[48,128]{1,0:T(8,128)S(1)}, u32[]{:S(2)}, u32[]{:S(2)}) %collective-permute-start.4) | collective-permute-done | bytes 24608 | tf_op jit(solution)/shard_map/ppermute | solution.py:344
  39.7 6.3 %all-to-all-start = ((f32[32,48,128]{2,1,0:T(8,128)}), f32[32,48,128]{2,1,0:T(8,128)}, u32[]{:S(2)}, u32[]{:S(2)}) async-start(f32[32,48,128]{2,1,0:T(8,128)} %copy-done.14), calls=%async_computation | async-start | bytes 1572864 | tf_op jit(solution)/shard_map/all_to_all | solution.py:348
  46.3 13.5 %all-to-all-done.slots_ref = f32[32,48,128]{2,1,0:T(8,128)} async-done(((f32[32,48,128]{2,1,0:T(8,128)}), f32[32,48,128]{2,1,0:T(8,128)}, u32[]{:S(2)}, u32[]{:S(2)}) %all-to-all-start) | async-done | bytes 786464 | tf_op jit(solution)/shard_map/all_to_all | solution.py:348
  59.8 0.7 copy-done.27
  60.6 0.7 copy-done.30
  61.3 0.7 copy-done.33
  62.0 0.9 copy-done.37
  62.8 0.7 copy-done.42
  63.5 1.3 shard_map.119
  64.8 1.3 copy-done.1
  66.1 0.9 copy-done.8
  67.0 0.9 copy-done.10
  67.9 0.9 copy-done.12
  68.9 0.8 copy-done.22
  69.6 0.7 copy-done.28
  70.4 0.7 copy-done.31
  71.1 0.7 copy-done.34
  71.8 0.8 copy-done.39
  72.6 1.9 shard_map.120
  74.5 14.9 %all_to_all.60.slots_ref = f32[32,24,128]{2,1,0:T(8,128)S(1)} all-to-all(f32[32,24,128]{2,1,0:T(8,128)S(1)} %get-tuple-element.112), channel_id=1, replica_groups=mesh['gx'=8,'gy'=4,'gz'=16] {'gx','gy'}, dimensions={0} | all-to-all | bytes 786432 | tf_op jit(solution)/shard_map/all_to_all | solution.py:348
  90.0 26.6 %all_to_all.61.slots_ref.layers_ref = f32[16,24,128]{2,1,0:T(8,128)S(1)} all-to-all(f32[16,24,128]{2,1,0:T(8,128)S(1)} %shard_map.121), channel_id=1, replica_groups=mesh['gx'=8,'gy'=4,'gz'=16] {'gz'}, dimensions={0} | all-to-all | bytes 393216 | tf_op jit(solution)/shard_map/all_to_all | solution.py:348
  116.7 15.2 %all_to_all.62.total_ref = f32[32,8,128]{2,1,0:T(8,128)S(1)} all-to-all(f32[32,8,128]{2,1,0:T(8,128)S(1)} %shard_map.122), channel_id=1, replica_groups=mesh['gx'=8,'gy'=4,'gz'=16] {'gx','gy'}, dimensions={0} | all-to-all | bytes 262144 | tf_op jit(solution)/shard_map/all_to_all | solution.py:348
  131.9 2.4 shard_map.123
  134.3 3.5 %collective-permute-start.5 = (f32[16,128]{1,0:T(8,128)S(1)}, f32[16,128]{1,0:T(8,128)S(1)}, u32[]{:S(2)}, u32[]{:S(2)}) collective-permute-start(f32[16,128]{1,0:T(8,128)S(1)} %get-tuple-element.122), channel_id=1, source_target_pairs={{0,1},{1,2},{2,3},{3,4},{4,5},{5,6},{6,7},{7,8},{8,9},{9,10},{10,1... | collective-permute-start | bytes 24584 | tf_op jit(solution)/shard_map/ppermute | solution.py:344
  137.8 1.3 collective-permute-start.6
  139.2 3.1 %collective-permute-done.6.top_ref = f32[16,128]{1,0:T(8,128)S(1)} collective-permute-done((f32[16,128]{1,0:T(8,128)S(1)}, f32[16,128]{1,0:T(8,128)S(1)}, u32[]{:S(2)}, u32[]{:S(2)}) %collective-permute-start.6) | collective-permute-done | bytes 8224 | tf_op jit(solution)/shard_map/ppermute | solution.py:344
  142.2 14.1 %all_to_all.63.slots_ref = f32[32,16,128]{2,1,0:T(8,128)S(1)} all-to-all(f32[32,16,128]{2,1,0:T(8,128)S(1)} %get-tuple-element.124), channel_id=1, replica_groups=mesh['gx'=8,'gy'=4,'gz'=16] {'gx','gy'}, dimensions={0} | all-to-all | bytes 524288 | tf_op jit(solution)/shard_map/all_to_all | solution.py:348
  156.4 1.5 shard_map.124
  157.9 14.1 %all_to_all.64.slots_ref = f32[32,24,128]{2,1,0:T(8,128)S(1)} all-to-all(f32[32,24,128]{2,1,0:T(8,128)S(1)} %get-tuple-element.130), channel_id=1, replica_groups=mesh['gx'=8,'gy'=4,'gz'=16] {'gx','gy'}, dimensions={0} | all-to-all | bytes 786432 | tf_op jit(solution)/shard_map/all_to_all | solution.py:348
  172.5 18.6 %all_to_all.65.slots_ref.layers_ref = f32[16,24,128]{2,1,0:T(8,128)S(1)} all-to-all(f32[16,24,128]{2,1,0:T(8,128)S(1)} %shard_map.125), channel_id=1, replica_groups=mesh['gx'=8,'gy'=4,'gz'=16] {'gz'}, dimensions={0} | all-to-all | bytes 393216 | tf_op jit(solution)/shard_map/all_to_all | solution.py:348
  191.2 15.2 %all_to_all.66.total_ref = f32[32,8,128]{2,1,0:T(8,128)S(1)} all-to-all(f32[32,8,128]{2,1,0:T(8,128)S(1)} %shard_map.126), channel_id=1, replica_groups=mesh['gx'=8,'gy'=4,'gz'=16] {'gx','gy'}, dimensions={0} | all-to-all | bytes 262144 | tf_op jit(solution)/shard_map/all_to_all | solution.py:348
  206.4 2.4 shard_map.127
  208.8 3.5 %collective-permute-start.7 = (f32[16,128]{1,0:T(8,128)S(1)}, f32[16,128]{1,0:T(8,128)S(1)}, u32[]{:S(2)}, u32[]{:S(2)}) collective-permute-start(f32[16,128]{1,0:T(8,128)S(1)} %get-tuple-element.138), channel_id=1, source_target_pairs={{0,1},{1,2},{2,3},{3,4},{4,5},{5,6},{6,7},{7,8},{8,9},{9,10},{10,1... | collective-permute-start | bytes 24584 | tf_op jit(solution)/shard_map/ppermute | solution.py:344
  212.3 1.3 collective-permute-start.8
  213.6 3.1 %collective-permute-done.8.top_ref = f32[16,128]{1,0:T(8,128)S(1)} collective-permute-done((f32[16,128]{1,0:T(8,128)S(1)}, f32[16,128]{1,0:T(8,128)S(1)}, u32[]{:S(2)}, u32[]{:S(2)}) %collective-permute-start.8) | collective-permute-done | bytes 8224 | tf_op jit(solution)/shard_map/ppermute | solution.py:344
  216.7 14.1 %all_to_all.67.slots_ref = f32[32,16,128]{2,1,0:T(8,128)S(1)} all-to-all(f32[32,16,128]{2,1,0:T(8,128)S(1)} %get-tuple-element.140), channel_id=1, replica_groups=mesh['gx'=8,'gy'=4,'gz'=16] {'gx','gy'}, dimensions={0} | all-to-all | bytes 524288 | tf_op jit(solution)/shard_map/all_to_all | solution.py:348
  230.9 1.5 shard_map.128
  232.3 14.1 %all_to_all.68.slots_ref = f32[32,24,128]{2,1,0:T(8,128)S(1)} all-to-all(f32[32,24,128]{2,1,0:T(8,128)S(1)} %get-tuple-element.146), channel_id=1, replica_groups=mesh['gx'=8,'gy'=4,'gz'=16] {'gx','gy'}, dimensions={0} | all-to-all | bytes 786432 | tf_op jit(solution)/shard_map/all_to_all | solution.py:348
  247.0 18.6 %all_to_all.69.slots_ref.layers_ref = f32[16,24,128]{2,1,0:T(8,128)S(1)} all-to-all(f32[16,24,128]{2,1,0:T(8,128)S(1)} %shard_map.129), channel_id=1, replica_groups=mesh['gx'=8,'gy'=4,'gz'=16] {'gz'}, dimensions={0} | all-to-all | bytes 393216 | tf_op jit(solution)/shard_map/all_to_all | solution.py:348
  265.7 15.2 %all_to_all.70.total_ref = f32[32,8,128]{2,1,0:T(8,128)S(1)} all-to-all(f32[32,8,128]{2,1,0:T(8,128)S(1)} %shard_map.130), channel_id=1, replica_groups=mesh['gx'=8,'gy'=4,'gz'=16] {'gx','gy'}, dimensions={0} | all-to-all | bytes 262144 | tf_op jit(solution)/shard_map/all_to_all | solution.py:348
  280.9 2.3 shard_map.131
  (85 shorter events, 5.9 us)
Async XLA Ops:
  0.6 18.8 %copy-start.19 = (f32[1,1,1,24,768]{4,3,2,1,0:T(8,128)S(1)}, f32[1,1,1,24,768]{4,3,2,1,0:T(8,128)}, u32[]{:S(2)}) copy-start(f32[1,1,1,24,768]{4,3,2,1,0:T(8,128)} %param.16) | copy-start | bytes 221188
  1.5 25.1 %copy-start.32 = (s32[8]{0:T(128)}, s32[8]{0:T(128)S(1)}, u32[]{:S(2)}) copy-start(s32[8]{0:T(128)S(1)} %stack.61.spots) | copy-start | bytes 100
  1.5 0.7 copy-start.24
  2.2 17.2 %copy-start.40 = (s32[1,1,1,8]{3,2,1,0:T(1,128)S(1)}, s32[1,1,1,8]{3,2,1,0:T(1,128)}, u32[]{:S(2)}) copy-start(s32[1,1,1,8]{3,2,1,0:T(1,128)} %param.17) | copy-start | bytes 100
  3.5 23.0 %collective-permute-start.2 = (f32[24,128]{1,0:T(8,128)}, f32[24,128]{1,0:T(8,128)S(1)}, u32[]{:S(2)}, u32[]{:S(2)}) collective-permute-start(f32[24,128]{1,0:T(8,128)} %get-tuple-element.154), channel_id=1, source_target_pairs={{0,1},{1,2},{2,3},{3,4},{4,5},{5,6},{6,7},{7,8},{8,9},{9,10},{10,1... | collective-permute-start | bytes 36872 | tf_op jit(solution)/shard_map/ppermute | solution.py:344
  7.9 18.6 %collective-permute-start.1 = (f32[24,128]{1,0:T(8,128)}, f32[24,128]{1,0:T(8,128)}, u32[]{:S(2)}, u32[]{:S(2)}) collective-permute-start(f32[24,128]{1,0:T(8,128)} %get-tuple-element.155), channel_id=1, source_target_pairs={{0,16},{16,32},{32,48},{1,17},{17,33},{33,49},{2,18},{18,34},{34,5... | collective-permute-start | bytes 36872 | tf_op jit(solution)/shard_map/ppermute | solution.py:344
  11.6 14.9 %collective-permute-start = (f32[24,128]{1,0:T(8,128)}, f32[24,128]{1,0:T(8,128)}, u32[]{:S(2)}, u32[]{:S(2)}) collective-permute-start(f32[24,128]{1,0:T(8,128)} %get-tuple-element.156), channel_id=1, source_target_pairs={{0,64},{64,128},{128,192},{192,256},{256,320},{320,384},{384,448},... | collective-permute-start | bytes 36872 | tf_op jit(solution)/shard_map/ppermute | solution.py:344
  17.4 1.4 copy-start.13
  18.7 3.4 %copy-start.15 = (f32[1,1,1,6,128,128]{5,4,3,2,1,0:T(8,128)S(1)}, f32[1,1,1,6,128,128]{5,4,3,2,1,0:T(8,128)}, u32[]{:S(2)}) copy-start(f32[1,1,1,6,128,128]{5,4,3,2,1,0:T(8,128)} %param.11) | copy-start | bytes 1179652
  18.7 3.4 %copy-start.16 = (f32[1,1,1,6,128,128]{5,4,3,2,1,0:T(8,128)S(1)}, f32[1,1,1,6,128,128]{5,4,3,2,1,0:T(8,128)}, u32[]{:S(2)}) copy-start(f32[1,1,1,6,128,128]{5,4,3,2,1,0:T(8,128)} %param.12) | copy-start | bytes 1179652
  18.7 6.1 %copy-start.17 = (f32[1,1,1,6,128,128]{5,4,3,2,1,0:T(8,128)S(1)}, f32[1,1,1,6,128,128]{5,4,3,2,1,0:T(8,128)}, u32[]{:S(2)}) copy-start(f32[1,1,1,6,128,128]{5,4,3,2,1,0:T(8,128)} %param.13) | copy-start | bytes 1179652
  18.7 6.1 %copy-start.18 = (f32[1,1,1,6,128,128]{5,4,3,2,1,0:T(8,128)S(1)}, f32[1,1,1,6,128,128]{5,4,3,2,1,0:T(8,128)}, u32[]{:S(2)}) copy-start(f32[1,1,1,6,128,128]{5,4,3,2,1,0:T(8,128)} %param.14) | copy-start | bytes 1179652
  19.4 7.2 %copy-start.20 = (f32[1,1,1,24,768]{4,3,2,1,0:T(8,128)S(1)}, f32[1,1,1,24,768]{4,3,2,1,0:T(8,128)}, u32[]{:S(2)}) copy-start(f32[1,1,1,24,768]{4,3,2,1,0:T(8,128)} %param.16) | copy-start | bytes 221188
  19.4 7.2 %copy-start.25 = (f32[1,1,1,3,16,128]{5,4,3,2,1,0:T(8,128)S(1)}, f32[1,1,1,3,16,128]{5,4,3,2,1,0:T(8,128)}, u32[]{:S(2)}) copy-start(f32[1,1,1,3,16,128]{5,4,3,2,1,0:T(8,128)} %param.10) | copy-start | bytes 73732
  19.4 7.2 %copy-start.41 = (s32[1,1,1,8]{3,2,1,0:T(1,128)S(1)}, s32[1,1,1,8]{3,2,1,0:T(1,128)}, u32[]{:S(2)}) copy-start(s32[1,1,1,8]{3,2,1,0:T(1,128)} %param.17) | copy-start | bytes 100
  20.2 0.7 copy-start.7
  20.8 0.7 copy-start.9
  21.5 0.7 copy-start.11
  22.2 0.7 copy-start.43
  23.8 1.1 copy-start
  24.9 0.7 copy-start.44
  26.5 1.5 copy-start.3
  26.5 1.5 copy-start.5
  28.0 0.9 copy-start.14
  29.0 0.6 copy-start.21
  29.6 0.6 copy-start.36
  30.2 0.6 copy-start.38
  30.8 4.8 %collective-permute-start.3 = (f32[48,128]{1,0:T(8,128)S(1)}, f32[48,128]{1,0:T(8,128)S(1)}, u32[]{:S(2)}, u32[]{:S(2)}) collective-permute-start(f32[48,128]{1,0:T(8,128)S(1)} %get-tuple-element.94), channel_id=1, source_target_pairs={{0,1},{1,2},{2,3},{3,4},{4,5},{5,6},{6,7},{7,8},{8,9},{9,10},{10,1... | collective-permute-start | bytes 73736 | tf_op jit(solution)/shard_map/ppermute | solution.py:344
  34.4 4.8 %collective-permute-start.4 = (f32[48,128]{1,0:T(8,128)S(1)}, f32[48,128]{1,0:T(8,128)S(1)}, u32[]{:S(2)}, u32[]{:S(2)}) collective-permute-start(f32[48,128]{1,0:T(8,128)S(1)} %get-tuple-element.95), channel_id=1, source_target_pairs={{1,0},{2,1},{3,2},{4,3},{5,4},{6,5},{7,6},{8,7},{9,8},{10,9},{11,1... | collective-permute-start | bytes 73736 | tf_op jit(solution)/shard_map/ppermute | solution.py:344
  35.7 0.6 copy-start.26
  39.1 0.6 copy-start.29
  39.7 20.1 %all-to-all-start = ((f32[32,48,128]{2,1,0:T(8,128)}), f32[32,48,128]{2,1,0:T(8,128)}, u32[]{:S(2)}, u32[]{:S(2)}) async-start(f32[32,48,128]{2,1,0:T(8,128)} %copy-done.14), calls=%async_computation | async-start | bytes 1572864 | tf_op jit(solution)/shard_map/all_to_all | solution.py:348
  59.8 0.7 copy-start.27
  60.6 0.7 copy-start.30
  61.3 0.7 copy-start.33
  61.9 0.9 copy-start.37
  62.8 0.7 copy-start.42
  64.8 1.3 copy-start.1
  66.1 0.9 copy-start.8
  67.0 0.9 copy-start.10
  67.9 0.9 copy-start.12
  68.8 0.8 copy-start.22
  69.6 0.7 copy-start.28
  70.4 0.7 copy-start.31
  71.1 0.7 copy-start.34
  71.8 0.8 copy-start.39
  72.6 16.8 %copy-start.35 = (s32[8]{0:T(128)S(1)}, s32[8]{0:T(128)}, u32[]{:S(2)}) copy-start(s32[8]{0:T(128)} %copy-done.32) | copy-start | bytes 100
  74.5 57.4 %copy-start.4 = (bf16[768,768]{1,0:T(8,128)(2,1)S(1)}, bf16[768,768]{1,0:T(8,128)(2,1)}, u32[]{:S(2)}) copy-start(bf16[768,768]{1,0:T(8,128)(2,1)} %copy-done.3) | copy-start | bytes 3538948
  74.5 57.4 %copy-start.6 = (bf16[768,768]{1,0:T(8,128)(2,1)S(1)}, bf16[768,768]{1,0:T(8,128)(2,1)}, u32[]{:S(2)}) copy-start(bf16[768,768]{1,0:T(8,128)(2,1)} %copy-done.5) | copy-start | bytes 3538948
  74.5 57.4 %copy-start.23 = (f32[16,768]{1,0:T(8,128)S(1)}, f32[16,768]{1,0:T(8,128)}, u32[]{:S(2)}) copy-start(f32[16,768]{1,0:T(8,128)} %copy-done.21) | copy-start | bytes 147460
  131.9 24.5 %copy-start.2 = (bf16[768,768]{1,0:T(8,128)(2,1)S(1)}, bf16[768,768]{1,0:T(8,128)(2,1)}, u32[]{:S(2)}) copy-start(bf16[768,768]{1,0:T(8,128)(2,1)} %copy-done) | copy-start | bytes 3538948
  134.3 4.8 %collective-permute-start.5 = (f32[16,128]{1,0:T(8,128)S(1)}, f32[16,128]{1,0:T(8,128)S(1)}, u32[]{:S(2)}, u32[]{:S(2)}) collective-permute-start(f32[16,128]{1,0:T(8,128)S(1)} %get-tuple-element.122), channel_id=1, source_target_pairs={{0,1},{1,2},{2,3},{3,4},{4,5},{5,6},{6,7},{7,8},{8,9},{9,10},{10,1... | collective-permute-start | bytes 24584 | tf_op jit(solution)/shard_map/ppermute | solution.py:344
  137.8 4.4 %collective-permute-start.6 = (f32[16,128]{1,0:T(8,128)S(1)}, f32[16,128]{1,0:T(8,128)S(1)}, u32[]{:S(2)}, u32[]{:S(2)}) collective-permute-start(f32[16,128]{1,0:T(8,128)S(1)} %get-tuple-element.123), channel_id=1, source_target_pairs={{1,0},{2,1},{3,2},{4,3},{5,4},{6,5},{7,6},{8,7},{9,8},{10,9},{11,1... | collective-permute-start | bytes 24584 | tf_op jit(solution)/shard_map/ppermute | solution.py:344
  208.8 4.8 %collective-permute-start.7 = (f32[16,128]{1,0:T(8,128)S(1)}, f32[16,128]{1,0:T(8,128)S(1)}, u32[]{:S(2)}, u32[]{:S(2)}) collective-permute-start(f32[16,128]{1,0:T(8,128)S(1)} %get-tuple-element.138), channel_id=1, source_target_pairs={{0,1},{1,2},{2,3},{3,4},{4,5},{5,6},{6,7},{7,8},{8,9},{9,10},{10,1... | collective-permute-start | bytes 24584 | tf_op jit(solution)/shard_map/ppermute | solution.py:344
  212.3 4.4 %collective-permute-start.8 = (f32[16,128]{1,0:T(8,128)S(1)}, f32[16,128]{1,0:T(8,128)S(1)}, u32[]{:S(2)}, u32[]{:S(2)}) collective-permute-start(f32[16,128]{1,0:T(8,128)S(1)} %get-tuple-element.139), channel_id=1, source_target_pairs={{1,0},{2,1},{3,2},{4,3},{5,4},{6,5},{7,6},{8,7},{9,8},{10,9},{11,1... | collective-permute-start | bytes 24584 | tf_op jit(solution)/shard_map/ppermute | solution.py:344

commit v3 on v2

v3 whole, which is shorter than its diff:
```python
import functools

import jax
import jax.numpy as jnp
from jax import lax
from jax.experimental import pallas as pl
from jax.experimental.pallas import tpu as pltpu
from jax.sharding import PartitionSpec as P

ITERS = 3
CASES = 16
FD = 128
WIDE = 6 * FD
QPAD = 256
SUBS = 32
AXES = ("gx", "gy", "gz")
PLANE = ("gx", "gy")
F32 = jnp.float32
BF16 = jnp.bfloat16
VMEM = pl.BlockSpec(memory_space=pltpu.VMEM)
SMEM = pl.BlockSpec(memory_space=pltpu.SMEM)


def call(kernel, outs, args, specs=(), scratch=()):
    return pl.pallas_call(
        kernel,
        out_shape=[jax.ShapeDtypeStruct(shape, dtype) for shape, dtype in outs],
        in_specs=list(specs) + [VMEM] * (len(args) - len(specs)),
        out_specs=[VMEM] * len(outs),
        scratch_shapes=list(scratch),
        compiler_params=pltpu.CompilerParams(vmem_limit_bytes=40 * 1024 * 1024),
    )(*args)


def halves(x):
    high = x.astype(BF16)
    return high, (x - high.astype(F32)).astype(BF16)


def dot_exact(x, selector):
    rows = x.shape[0]
    high, low = halves(x)
    both = jnp.dot(jnp.concatenate([high, low], 0), selector, preferred_element_type=F32)
    return both[:rows] + both[rows:]


def dot_split(x, high_ref, low_ref):
    rows = x.shape[0]
    high, low = halves(x)
    both = jnp.dot(jnp.concatenate([high, low], 0), high_ref[...], preferred_element_type=F32)
    rest = jnp.dot(high, low_ref[...], preferred_element_type=F32)
    return both[:rows] + both[rows:] + rest


def face(x, f):
    return x[:, f * FD:(f + 1) * FD]


def take(x, row):
    index = jnp.broadcast_to(row.astype(jnp.int32), x.shape)
    return jnp.take_along_axis(x, index, axis=1, mode="promise_in_bounds")


def lower_changed(x, rows):
    parts = []
    for d in range(3):
        parts.append(-take(face(x, 2 * d), rows[d]))
        parts.append(face(x, 2 * d + 1))
    return jnp.concatenate(parts, axis=1)


def partner_rows(messages):
    return [m[CASES:CASES + 1, :] for m in messages]


def inverse_rows(messages):
    return [m[CASES + 1:CASES + 2, :] for m in messages]


def apply_dense(field, messages, high_ref, low_ref):
    loads = lower_changed(field, inverse_rows(messages))
    return loads, lower_changed(dot_split(loads, high_ref, low_ref), partner_rows(messages))


def position():
    gy = lax.axis_size("gy")
    places = [(lax.axis_index(a), lax.axis_size(a)) for a in ("gx", "gy", "gz")]
    there = []
    for place, size in places:
        there += [place > 0, place < size - 1]
    return places[0][0] * gy + places[1][0], places[2][0], there


def steps():
    gy = lax.axis_size("gy")
    return (-gy, gy, -1, 1)


def mask_row(there):
    return jnp.concatenate([jnp.full((1, FD), t.astype(F32)) for t in there], axis=1)


def put_rows(slots_ref, spot, rows):
    for q in range(4):
        slots_ref[spot, q] = rows[4 * q:4 * q + 4, :]


def take_rows(slots_ref, spot):
    return jnp.concatenate([slots_ref[spot, q] for q in range(4)], axis=0)


def prep_kernel(rhs_ref, partner_ref, *message_refs):
    _, _, there = position()
    for d in range(3):
        message_ref = message_refs[d]
        row = partner_ref[d:d + 1, :]
        message_ref[0:CASES, :] = rhs_ref[d] * there[2 * d + 1].astype(F32)
        wanted = lax.broadcasted_iota(jnp.int32, (FD, FD), 0)
        hits = (wanted == jnp.broadcast_to(row, (FD, FD))).astype(F32).astype(BF16)
        count = lax.broadcasted_iota(jnp.int32, (16, FD), 1).astype(F32).astype(BF16)
        inverse = lax.dot_general(
            count, hits, (((1,), (1,)), ((), ())), preferred_element_type=F32
        )
        message_ref[CASES:CASES + 1, :] = row.astype(F32)
        message_ref[CASES + 1:CASES + 2, :] = inverse[0:1, :]
        message_ref[CASES + 2:CASES + 8, :] = jnp.zeros((6, FD), F32)


def put_dense(pairs, diag_ref, couple_ref, high_ref, low_ref):
    high_ref[...] = jnp.zeros_like(high_ref)
    low_ref[...] = jnp.zeros_like(low_ref)

    def put(rows, cols, block):
        high, low = halves(block)
        high_ref[pl.ds(rows, FD), pl.ds(cols, FD)] = high
        low_ref[pl.ds(rows, FD), pl.ds(cols, FD)] = low

    for f in range(6):
        put(f * FD, f * FD, diag_ref[f])
    for k in range(6):
        first = pl.multiple_of(pairs[k, 0] * FD, FD)
        second = pl.multiple_of(pairs[k, 1] * FD, FD)
        block = couple_ref[k]
        put(second, first, block)
        put(first, second, block.T)


def setup_kernel(pairs, ids, *rest):
    sources, rest = rest[:6], rest[6:]
    (dh_ref, dl_ref, fh_ref, fl_ref, kh_ref, kl_ref, wh_ref, wl_ref, expand_ref, target_ref) = rest[:10]
    held, (pad, square, sems) = rest[10:16], rest[16:]
    copies = [
        pltpu.make_async_copy(source, target, sems.at[i])
        for i, (source, target) in enumerate(zip(sources, held))
    ]
    for copy in copies:
        copy.start()
    lanes = lax.broadcasted_iota(jnp.int32, (8, FD), 1) % SUBS
    target = jnp.full((8, FD), -1, jnp.int32)
    for r in range(24):
        target = jnp.where(lanes == r, (r % 3) * QPAD + ids[0, r // 3], target)
    target_ref[...] = target.astype(F32)
    pad[...] = jnp.zeros_like(pad)
    lanes = lax.broadcasted_iota(jnp.int32, (1, 3 * QPAD), 1)
    for r in range(24):
        spot = (r % 3) * QPAD + ids[0, r // 3]
        pad[r:r + 1, :] = (lanes == spot).astype(F32)
    expand_ref[...] = pad[...].astype(BF16)
    copies[0].wait()
    copies[1].wait()
    put_dense(pairs, held[0], held[1], dh_ref, dl_ref)
    copies[2].wait()
    copies[3].wait()
    put_dense(pairs, held[2], held[3], fh_ref, fl_ref)
    square[...] = jnp.zeros_like(square)
    copies[4].wait()
    for p in range(3):
        for q in range(3):
            square[p * QPAD:p * QPAD + 192, q * QPAD:q * QPAD + 192] = held[4][
                p * 192:(p + 1) * 192, q * 192:(q + 1) * 192
            ]
    high, low = halves(square[...])
    kh_ref[...] = high
    kl_ref[...] = low
    pad[...] = jnp.zeros_like(pad)
    copies[5].wait()
    pad[0:24, :] = held[5][...]
    for f in range(6):
        high, low = halves(pad[:, f * FD:(f + 1) * FD].T)
        wh_ref[f * FD:(f + 1) * FD, :] = high
        wl_ref[f * FD:(f + 1) * FD, :] = low


def start_kernel(rhs_ref, mx_ref, my_ref, mz_ref, dh_ref, dl_ref, coupling_ref, target_ref,
                 field_ref, shown_ref, own_ref, *piece_refs):
    _, _, there = position()
    messages = (mx_ref, my_ref, mz_ref)
    parts = []
    for d in range(3):
        parts.append(messages[d][0:CASES, :])
        parts.append(rhs_ref[d] * there[2 * d + 1].astype(F32))
    field = jnp.concatenate(parts, axis=1)
    field_ref[...] = field
    _, shown = apply_dense(field, messages, dh_ref, dl_ref)
    shown_ref[...] = shown
    own = lower_changed(coupling_ref[...], partner_rows(messages))
    own_ref[...] = own
    for f in range(6):
        piece_refs[f][0:CASES, :] = face(shown, f)
        piece_refs[f][CASES:CASES + 24, :] = face(own, f)
        piece_refs[f][CASES + 24:CASES + 32, :] = target_ref[...]


def joint_kernel(own_ref, target_ref, *rest):
    others, (gh_ref, gl_ref, pick_ref, whole) = rest[:6], rest[6:]
    _, _, there = position()
    whole[...] = jnp.zeros_like(whole)
    whole[0:24, :] = own_ref[...]
    lanes = lax.broadcasted_iota(jnp.int32, (8, FD), 1)
    targets = [target_ref[...]]
    for f in range(6):
        exists = there[f].astype(F32)
        whole[SUBS * (f + 1):SUBS * (f + 1) + 24, f * FD:(f + 1) * FD] = (
            others[f][CASES:CASES + 24, :] * exists
        )
        targets.append(others[f][CASES + 24:CASES + 32, :] * exists)
    high, low = halves(whole[...])
    gh_ref[...] = high
    gl_ref[...] = low
    rows = lax.broadcasted_iota(jnp.int32, (3 * QPAD, FD), 0)
    for half in range(2):
        wanted = jnp.full((8, FD), -1.0, F32)
        for n in range(4 * half, min(4 * half + 4, 7)):
            wanted = jnp.where(lanes // SUBS == n % 4, targets[n], wanted)
        wanted = jnp.broadcast_to(wanted[0:1, :].astype(jnp.int32), (3 * QPAD, FD))
        pick_ref[:, half * FD:(half + 1) * FD] = (rows == wanted).astype(F32).astype(BF16)


def load_kernel(first, mx_ref, my_ref, mz_ref, shown_ref, *rest):
    others, rest = rest[:6], rest[6:]
    residual_ref, fh_ref, fl_ref, wh_ref, wl_ref, expand_ref = rest[:6]
    rest = rest[6:]
    if first:
        z_ref, flexed_ref, out_ref = rest
    else:
        search_ref, applied_ref, z_ref, flexed_ref, out_ref = rest
    messages = (mx_ref, my_ref, mz_ref)
    here, _, there = position()
    across = jnp.concatenate([other[0:CASES, :] for other in others], axis=1)
    z = 0.25 * (shown_ref[...] + across) * mask_row(there)
    z_ref[...] = z
    loads, flexed = apply_dense(z, messages, fh_ref, fl_ref)
    flexed_ref[...] = flexed
    corner = dot_split(loads, wh_ref, wl_ref)
    gathered = dot_exact(corner, expand_ref[...])

    def upper_sum(a):
        return jnp.sum(face(a, 1) + face(a, 3) + face(a, 5), axis=1, keepdims=True)

    sums = [upper_sum(z * residual_ref[...]), jnp.sum(z * flexed, axis=1, keepdims=True)]
    if not first:
        sums.append(
            upper_sum(z * applied_ref[...])
            + jnp.sum(search_ref[...] * flexed, axis=1, keepdims=True)
        )
    lanes = lax.broadcasted_iota(jnp.int32, (CASES, FD), 1)
    out_ref[...] = jnp.zeros_like(out_ref)
    for b in range(6):
        block = face(gathered, b)
        if b == 1:
            for t, value in enumerate(sums):
                block = jnp.where(lanes == 64 + t, value, block)
        for q in range(4):
            out_ref[4 * b + q, 4] = block[4 * q:4 * q + 4, :]
    for f, by in enumerate(steps()):
        @pl.when(there[f])
        def _():
            put_rows(out_ref, here + by, face(flexed, f))


def layer_kernel(slots_ref, flexed_ref, out_ref):
    _, layer, there = position()
    total = jnp.sum(slots_ref[:, 4], axis=0)
    out_ref[...] = jnp.zeros_like(out_ref)
    for i in range(out_ref.shape[0]):
        out_ref[i, 4] = total
    for f, by in ((4, -1), (5, 1)):
        @pl.when(there[f])
        def _():
            put_rows(out_ref, layer + by, flexed_ref[:, f * FD:(f + 1) * FD])


def spread_kernel(slots_ref, out_ref):
    total = jnp.sum(slots_ref[:, 4], axis=0)
    for i in range(out_ref.shape[0]):
        out_ref[i] = total


def step_kernel(first, last, total_ref, slots_ref, layers_ref, flexed_ref,
                z_ref, residual_ref, kh_ref, kl_ref, gh_ref, gl_ref, pick_ref, *rest):
    rest = list(rest)
    if not last:
        mx_ref, my_ref, mz_ref, dh_ref, dl_ref = rest[:5]
        rest = rest[5:]
    if not first:
        search_ref, applied_ref, load_ref, scale_ref, iterate_ref = rest[:5]
        rest = rest[5:]
    here, layer, there = position()
    across = []
    for f, by in enumerate(steps()):
        across.append(take_rows(slots_ref, jnp.where(there[f], here + by, here)))
    for f, by in ((4, -1), (5, 1)):
        across.append(take_rows(layers_ref, jnp.where(there[f], layer + by, layer)))
    mask = mask_row(there)
    applied = (flexed_ref[...] + jnp.concatenate(across, axis=1)) * mask
    search = z_ref[...]
    blocks = []
    for b in range(6):
        blocks.append(jnp.concatenate([total_ref[4 * b + q] for q in range(4)], axis=0))
    norm = blocks[1][:, 64:65]
    energy = blocks[1][:, 65:66]
    load = jnp.concatenate(blocks, axis=1)
    lanes = lax.broadcasted_iota(jnp.int32, load.shape, 1) % QPAD
    load = jnp.where(lanes < 192, load, 0.0)
    if not first:
        beta = norm / scale_ref[:, 0:1]
        cross = blocks[1][:, 66:67]
        energy = energy + beta * cross + beta * beta * scale_ref[:, 1:2]
        applied = applied + beta * applied_ref[...]
        search = search + beta * search_ref[...]
        load = load + beta * load_ref[...]
    coarse = dot_split(load, kh_ref, kl_ref)
    step = norm / (energy + jnp.sum(load * coarse, axis=1, keepdims=True))
    corner = dot_exact(coarse, pick_ref[...])
    correction = dot_split(corner, gh_ref, gl_ref) * mask
    residual = residual_ref[...] - step * (applied + correction)
    moved = step * search
    if last:
        multipliers_ref, left_ref = rest
        for d in range(3):
            multipliers_ref[d] = iterate_ref[d] + face(moved, 2 * d + 1)
            left_ref[d] = face(residual, 2 * d + 1)
        return
    search_out, applied_out, load_out, scale_out, iterate_out, residual_out, shown_ref = rest[:7]
    piece_refs = rest[7:]
    search_out[...] = search
    applied_out[...] = applied
    load_out[...] = load
    residual_out[...] = residual
    lanes = lax.broadcasted_iota(jnp.int32, (CASES, FD), 1)
    scale_out[...] = jnp.where(lanes == 0, norm, energy)
    for d in range(3):
        moved_face = face(moved, 2 * d + 1)
        iterate_out[d] = moved_face if first else iterate_ref[d] + moved_face
    _, shown = apply_dense(residual, (mx_ref, my_ref, mz_ref), dh_ref, dl_ref)
    shown_ref[...] = shown
    for f in range(6):
        piece_refs[f][...] = face(shown, f)


def passed_along(shard, axis, by):
    peers = lax.axis_size(axis)
    pairs = [(i, i + by) for i in range(peers) if 0 <= i + by < peers]
    return lax.ppermute(shard, axis, pairs)


def swapped(slots, axes):
    return lax.all_to_all(slots, axes, 0, 0)


def across_faces(pieces):
    got = [None] * 6
    for d in (2, 1, 0):
        got[2 * d] = passed_along(pieces[2 * d + 1], AXES[d], 1)
        got[2 * d + 1] = passed_along(pieces[2 * d], AXES[d], -1)
    return got


def body(
    jump_rhs,
    flex_diag,
    flex_couple,
    dirichlet_diag,
    dirichlet_couple,
    face_pairs,
    corner_coupling,
    coarse_ids,
    partner,
    coarse_inverse,
):
    gx, gy, gz = (lax.axis_size(a) for a in AXES)
    plane = gx * gy
    rhs = jump_rhs.reshape(3, CASES, FD)
    pairs = face_pairs.reshape(6, 2)
    coupling = corner_coupling.reshape(24, WIDE)
    ids = coarse_ids.reshape(1, 8)
    square = (WIDE, WIDE)
    wide = (CASES, WIDE)
    long = CASES + 32

    messages = call(
        prep_kernel, [((CASES + 8, FD), F32)] * 3, [rhs, partner.reshape(3, FD)]
    )
    messages = [passed_along(m, a, 1) for m, a in zip(messages, AXES)]
    blocks = [b.reshape(6, FD, FD) for b in (dirichlet_diag, dirichlet_couple, flex_diag, flex_couple)]
    sources = blocks + [coarse_inverse, coupling]
    *dense, target = call(
        setup_kernel,
        [(square, BF16)] * 6 + [((WIDE, FD), BF16)] * 2 + [((FD, WIDE), BF16), ((8, FD), F32)],
        [pairs, ids] + sources,
        specs=[SMEM] * 2 + [pl.BlockSpec(memory_space=pl.ANY)] * 6,
        scratch=[pltpu.VMEM(source.shape, F32) for source in sources]
        + [pltpu.VMEM((FD, WIDE), F32), pltpu.VMEM(square, F32), pltpu.SemaphoreType.DMA((6,))],
    )
    dirichlet, flex, inverse, weights = dense[0:2], dense[2:4], dense[4:6], dense[6:9]
    residual, shown, own, *pieces = call(
        start_kernel,
        [(wide, F32), (wide, F32), ((24, WIDE), F32)] + [((long, FD), F32)] * 6,
        [rhs, *messages, *dirichlet, coupling, target],
    )
    others = across_faces(pieces)
    joint = call(
        joint_kernel,
        [((QPAD, WIDE), BF16), ((QPAD, WIDE), BF16), ((3 * QPAD, QPAD), BF16)],
        [own, target, *others],
        scratch=[pltpu.VMEM((QPAD, WIDE), F32)],
    )
    joint, others = lax.optimization_barrier((joint, others))

    kept = []
    for iteration in range(ITERS):
        first, last = iteration == 0, iteration + 1 == ITERS
        z, flexed, out = call(
            functools.partial(load_kernel, first),
            [(wide, F32), (wide, F32), ((plane, 5, 4, FD), F32)],
            [*messages, shown, *others, residual, *flex, *weights, *kept[:2]],
        )
        slots = swapped(out, PLANE)
        (layers,) = call(layer_kernel, [((gz, 5, 4, FD), F32)], [slots, flexed])
        layers = swapped(layers, "gz")
        (total,) = call(spread_kernel, [((plane, 4, FD), F32)], [layers])
        total = swapped(total, PLANE)
        common = [total, slots, layers, flexed, z, residual, *inverse, *joint]
        kernel = functools.partial(step_kernel, first, last)
        if last:
            multipliers, left = call(kernel, [((3, CASES, FD), F32)] * 2, common + kept)
            break
        *kept, residual, shown, p0, p1, p2, p3, p4, p5 = call(
            kernel,
            [(wide, F32)] * 3 + [((CASES, FD), F32), ((3, CASES, FD), F32), (wide, F32), (wide, F32)]
            + [((CASES, FD), F32)] * 6,
            common + [*messages, *dirichlet] + kept,
        )
        others = across_faces((p0, p1, p2, p3, p4, p5))
    return multipliers.reshape(jump_rhs.shape), left.reshape(jump_rhs.shape)


def solution(mesh):
    placed = (
        P("gx", "gy", "gz", None, None, None),
        P("gx", "gy", "gz", None, None, None),
        P("gx", "gy", "gz", None, None, None),
        P("gx", "gy", "gz", None, None, None),
        P("gx", "gy", "gz", None, None, None),
        P("gx", "gy", "gz", None, None),
        P("gx", "gy", "gz", None, None),
        P("gx", "gy", "gz", None),
        P("gx", "gy", "gz", None, None),
        P(),
    )
    return jax.shard_map(
        body,
        mesh=mesh,
        in_specs=placed,
        out_specs=(P("gx", "gy", "gz", None, None, None), P("gx", "gy", "gz", None, None, None)),
        check_vma=False,
    )
```

time: 285 us -> 243 us (0.85)
  blocking collectives: 181 us -> 161 us
  local copies, waits for them, and re-layouts: 25.1 us -> 9.08 us
  starting transfers between devices: 33.2 us -> 49.1 us
  waiting for transfers between devices: 22.6 us -> 9.98 us
  Pallas kernels: 20.3 us -> 11.8 us
    ppermute x9 -> x21, starting transfers between devices: 26.9 us -> 49.1 us  [passed_along(): return lax.ppermute(shard, axis, pairs)]
    all_to_all x11 -> x9, blocking collectives: 181 us -> 161 us  [swapped(): return lax.all_to_all(slots, axes, 0, 0)]
    unnamed x94 -> x19, local copies, waits for them, and re-layouts: 23.6 us -> 8.32 us
    all_to_all x1 -> x0, waiting for transfers between devices: 13.5 us -> none  [swapped(): return lax.all_to_all(slots, axes, 0, 0)]
    pallas_call x19 -> x16, Pallas kernels: 20.3 us -> 11.8 us  [call(): pl.pallas_call(kernel, out_shape=[jax.ShapeDtypeStruct(shape, dtype) for...]
    all_to_all x1 -> x0, starting transfers between devices: 6.35 us -> none  [swapped(): return lax.all_to_all(slots, axes, 0, 0)]
    ppermute x9 -> x21, waiting for transfers between devices: 9.02 us -> 9.98 us  [passed_along(): return lax.ppermute(shard, axis, pairs)]
  transfers between devices with their start and end apart: 10 -> 21, of which waited for: 4 -> 3; matrix products, arithmetic and copies ran while one was open for 1% -> 0% of each run, Pallas kernels for 1% -> 1%
where the time goes in v3:
time: 243 us; the launch traced here: 242 us
  blocking collectives  161 us (66%)
  starting transfers between devices  49.1 us (20%)
  Pallas kernels  11.8 us (5%)
  waiting for transfers between devices  9.98 us (4%)
  local copies, waits for them, and re-layouts  9.08 us (4%)
    all_to_all x9, blocking collectives, swapped(): return lax.all_to_all(slots, axes, 0, 0)  161 us
    ppermute x21, starting transfers between devices, passed_along(): return lax.ppermute(shard, axis, pairs)  49.1 us
    pallas_call x16, Pallas kernels, call(): pl.pallas_call(kernel, out_shape=[jax.ShapeDtypeStruct(shape, dtype) for...  11.8 us
    ppermute x21, waiting for transfers between devices, passed_along(): return lax.ppermute(shard, axis, pairs)  9.98 us
    unnamed x19, local copies, waits for them, and re-layouts  8.32 us
  transfers between devices with their start and end apart: 21, of which 3 were waited for; matrix products, arithmetic and copies ran while one was open for 0% of the time, Pallas kernels for 1%

profile of v3, /device:TPU:1, one launch (start us, length us, event | category | flops | bytes accessed | tf_op | source)
XLA Modules:
  0.0 241.8 jit_solution(3206962944794915314)
XLA Ops:
  0.6 0.7 copy.15
  1.3 0.7 copy-done.6
  2.0 0.2 shard_map.113
  2.2 4.6 %collective-permute-start = (f32[24,128]{1,0:T(8,128)S(1)}, f32[24,128]{1,0:T(8,128)S(1)}, u32[]{:S(2)}, u32[]{:S(2)}) collective-permute-start(f32[24,128]{1,0:T(8,128)S(1)} %get-tuple-element.73), channel_id=1, source_target_pairs={{0,64},{64,128},{128,192},{192,256},{256,320},{320,384},{384,448},... | collective-permute-start | bytes 36872 | tf_op jit(solution)/shard_map/ppermute | solution.py:364
  6.8 3.1 %collective-permute-start.1 = (f32[24,128]{1,0:T(8,128)S(1)}, f32[24,128]{1,0:T(8,128)S(1)}, u32[]{:S(2)}, u32[]{:S(2)}) collective-permute-start(f32[24,128]{1,0:T(8,128)S(1)} %get-tuple-element.74), channel_id=1, source_target_pairs={{0,16},{16,32},{32,48},{1,17},{17,33},{33,49},{2,18},{18,34},{34,5... | collective-permute-start | bytes 36872 | tf_op jit(solution)/shard_map/ppermute | solution.py:364
  10.0 3.5 %collective-permute-start.2 = (f32[24,128]{1,0:T(8,128)S(1)}, f32[24,128]{1,0:T(8,128)S(1)}, u32[]{:S(2)}, u32[]{:S(2)}) collective-permute-start(f32[24,128]{1,0:T(8,128)S(1)} %get-tuple-element.75), channel_id=1, source_target_pairs={{0,1},{1,2},{2,3},{3,4},{4,5},{5,6},{6,7},{7,8},{8,9},{9,10},{10,1... | collective-permute-start | bytes 36872 | tf_op jit(solution)/shard_map/ppermute | solution.py:364
  13.5 0.8 copy.12.pairs
  14.3 1.4 copy-done
  15.6 1.0 copy-done.1
  16.6 1.0 copy-done.2
  17.6 1.0 copy-done.3
  18.6 1.0 copy-done.4
  19.6 0.9 copy-done.5
  20.5 0.7 copy-done.8
  21.2 3.6 %shard_map.114 = (bf16[768,768]{1,0:T(8,128)(2,1)S(1)}, bf16[768,768]{1,0:T(8,128)(2,1)S(1)}, bf16[768,768]{1,0:T(8,128)(2,1)S(1)}, bf16[768,768]{1,0:T(8,128)(2...) custom-call(s32[6,2]{1,0:T(8,128)S(1)} %copy.12.pairs, ...), custom_call_target="tpu_custom_call" | custom-call | tf_op jit(solution)/shard_map/pallas_call | solution.py:25
  24.8 0.0 collective-permute-done.2.mz_ref.rest_2_
  24.8 0.6 shard_map.115
  25.4 2.5 %collective-permute-start.3 = (f32[48,128]{1,0:T(8,128)S(1)}, f32[48,128]{1,0:T(8,128)S(1)}, u32[]{:S(2)}, u32[]{:S(2)}) collective-permute-start(f32[48,128]{1,0:T(8,128)S(1)} %get-tuple-element.81), channel_id=1, source_target_pairs={{0,64},{64,128},{128,192},{192,256},{256,320},{320,384},{384,448},... | collective-permute-start | bytes 73736 | tf_op jit(solution)/shard_map/ppermute | solution.py:364
  27.9 1.9 collective-permute-start.4
  29.8 3.1 %collective-permute-start.5 = (f32[48,128]{1,0:T(8,128)S(1)}, f32[48,128]{1,0:T(8,128)S(1)}, u32[]{:S(2)}, u32[]{:S(2)}) collective-permute-start(f32[48,128]{1,0:T(8,128)S(1)} %get-tuple-element.83), channel_id=1, source_target_pairs={{0,16},{16,32},{32,48},{1,17},{17,33},{33,49},{2,18},{18,34},{34,5... | collective-permute-start | bytes 73736 | tf_op jit(solution)/shard_map/ppermute | solution.py:364
  33.0 1.3 collective-permute-start.6
  34.3 3.5 %collective-permute-start.7 = (f32[48,128]{1,0:T(8,128)S(1)}, f32[48,128]{1,0:T(8,128)S(1)}, u32[]{:S(2)}, u32[]{:S(2)}) collective-permute-start(f32[48,128]{1,0:T(8,128)S(1)} %get-tuple-element.85), channel_id=1, source_target_pairs={{0,1},{1,2},{2,3},{3,4},{4,5},{5,6},{6,7},{7,8},{8,9},{9,10},{10,1... | collective-permute-start | bytes 73736 | tf_op jit(solution)/shard_map/ppermute | solution.py:364
  37.8 0.0 collective-permute-done.3.rest_0_
  37.8 1.3 collective-permute-start.8
  39.1 0.0 collective-permute-done.4.rest_1_
  39.1 0.0 collective-permute-done.6.rest_3_
  39.2 0.0 collective-permute-done.7.rest_4_
  39.2 3.8 %collective-permute-done.8.rest_5_ = f32[48,128]{1,0:T(8,128)S(1)} collective-permute-done((f32[48,128]{1,0:T(8,128)S(1)}, f32[48,128]{1,0:T(8,128)S(1)}, u32[]{:S(2)}, u32[]{:S(2)}) %collective-permute-start.8) | collective-permute-done | bytes 24608 | tf_op jit(solution)/shard_map/ppermute | solution.py:364
  43.0 0.1 shard_map.116
  43.2 0.7 shard_map.117
  43.9 18.9 %all_to_all.45.slots_ref = f32[32,5,4,128]{3,2,1,0:T(4,128)S(1)} all-to-all(f32[32,5,4,128]{3,2,1,0:T(4,128)S(1)} %get-tuple-element.102), channel_id=1, replica_groups=mesh['gx'=8,'gy'=4,'gz'=16] {'gx','gy'}, dimensions={0} | all-to-all | bytes 655360 | tf_op jit(solution)/shard_map/all_to_all | solution.py:368
  62.9 26.1 %all_to_all.46.slots_ref.layers_ref = f32[16,5,4,128]{3,2,1,0:T(4,128)S(1)} all-to-all(f32[16,5,4,128]{3,2,1,0:T(4,128)S(1)} %shard_map.118), channel_id=1, replica_groups=mesh['gx'=8,'gy'=4,'gz'=16] {'gz'}, dimensions={0} | all-to-all | bytes 327680 | tf_op jit(solution)/shard_map/all_to_all | solution.py:368
  89.0 14.5 %all_to_all.47.total_ref = f32[32,4,128]{2,1,0:T(4,128)S(1)} all-to-all(f32[32,4,128]{2,1,0:T(4,128)S(1)} %shard_map.119), channel_id=1, replica_groups=mesh['gx'=8,'gy'=4,'gz'=16] {'gx','gy'}, dimensions={0} | all-to-all | bytes 131072 | tf_op jit(solution)/shard_map/all_to_all | solution.py:368
  103.5 1.5 shard_map.120
  105.0 2.5 %collective-permute-start.9 = (f32[16,128]{1,0:T(8,128)S(1)}, f32[16,128]{1,0:T(8,128)S(1)}, u32[]{:S(2)}, u32[]{:S(2)}) collective-permute-start(f32[16,128]{1,0:T(8,128)S(1)} %get-tuple-element.111), channel_id=1, source_target_pairs={{0,64},{64,128},{128,192},{192,256},{256,320},{320,384},{384,448},... | collective-permute-start | bytes 24584 | tf_op jit(solution)/shard_map/ppermute | solution.py:364
  107.5 1.9 collective-permute-start.10
  109.5 2.2 collective-permute-start.11
  111.7 1.3 collective-permute-start.12
  113.0 2.8 %collective-permute-start.13 = (f32[16,128]{1,0:T(8,128)S(1)}, f32[16,128]{1,0:T(8,128)S(1)}, u32[]{:S(2)}, u32[]{:S(2)}) collective-permute-start(f32[16,128]{1,0:T(8,128)S(1)} %get-tuple-element.115), channel_id=1, source_target_pairs={{0,1},{1,2},{2,3},{3,4},{4,5},{5,6},{6,7},{7,8},{8,9},{9,10},{10,1... | collective-permute-start | bytes 24584 | tf_op jit(solution)/shard_map/ppermute | solution.py:364
  115.8 0.0 collective-permute-done.9.rest_0_
  115.8 1.3 collective-permute-start.14
  117.1 0.0 collective-permute-done.10.rest_1_
  117.2 0.0 collective-permute-done.13.rest_4_
  117.2 3.1 %collective-permute-done.14.rest_5_ = f32[16,128]{1,0:T(8,128)S(1)} collective-permute-done((f32[16,128]{1,0:T(8,128)S(1)}, f32[16,128]{1,0:T(8,128)S(1)}, u32[]{:S(2)}, u32[]{:S(2)}) %collective-permute-start.14) | collective-permute-done | bytes 8224 | tf_op jit(solution)/shard_map/ppermute | solution.py:364
  120.2 0.7 shard_map.121
  121.0 18.1 %all_to_all.48.slots_ref = f32[32,5,4,128]{3,2,1,0:T(4,128)S(1)} all-to-all(f32[32,5,4,128]{3,2,1,0:T(4,128)S(1)} %get-tuple-element.120), channel_id=1, replica_groups=mesh['gx'=8,'gy'=4,'gz'=16] {'gx','gy'}, dimensions={0} | all-to-all | bytes 655360 | tf_op jit(solution)/shard_map/all_to_all | solution.py:368
  139.1 18.1 %all_to_all.49.slots_ref.layers_ref = f32[16,5,4,128]{3,2,1,0:T(4,128)S(1)} all-to-all(f32[16,5,4,128]{3,2,1,0:T(4,128)S(1)} %shard_map.122), channel_id=1, replica_groups=mesh['gx'=8,'gy'=4,'gz'=16] {'gz'}, dimensions={0} | all-to-all | bytes 327680 | tf_op jit(solution)/shard_map/all_to_all | solution.py:368
  157.3 14.5 %all_to_all.50.total_ref = f32[32,4,128]{2,1,0:T(4,128)S(1)} all-to-all(f32[32,4,128]{2,1,0:T(4,128)S(1)} %shard_map.123), channel_id=1, replica_groups=mesh['gx'=8,'gy'=4,'gz'=16] {'gx','gy'}, dimensions={0} | all-to-all | bytes 131072 | tf_op jit(solution)/shard_map/all_to_all | solution.py:368
  171.7 1.6 shard_map.124
  173.4 2.5 %collective-permute-start.15 = (f32[16,128]{1,0:T(8,128)S(1)}, f32[16,128]{1,0:T(8,128)S(1)}, u32[]{:S(2)}, u32[]{:S(2)}) collective-permute-start(f32[16,128]{1,0:T(8,128)S(1)} %get-tuple-element.127), channel_id=1, source_target_pairs={{0,64},{64,128},{128,192},{192,256},{256,320},{320,384},{384,448},... | collective-permute-start | bytes 24584 | tf_op jit(solution)/shard_map/ppermute | solution.py:364
  175.9 1.9 collective-permute-start.16
  177.8 2.2 collective-permute-start.17
  180.1 1.3 collective-permute-start.18
  181.4 2.8 %collective-permute-start.19 = (f32[16,128]{1,0:T(8,128)S(1)}, f32[16,128]{1,0:T(8,128)S(1)}, u32[]{:S(2)}, u32[]{:S(2)}) collective-permute-start(f32[16,128]{1,0:T(8,128)S(1)} %get-tuple-element.131), channel_id=1, source_target_pairs={{0,1},{1,2},{2,3},{3,4},{4,5},{5,6},{6,7},{7,8},{8,9},{9,10},{10,1... | collective-permute-start | bytes 24584 | tf_op jit(solution)/shard_map/ppermute | solution.py:364
  184.2 1.3 collective-permute-start.20
  185.5 0.0 collective-permute-done.16.rest_1_
  185.5 0.0 collective-permute-done.17.rest_2_
  185.5 0.0 collective-permute-done.19.rest_4_
  185.6 3.1 %collective-permute-done.20.rest_5_ = f32[16,128]{1,0:T(8,128)S(1)} collective-permute-done((f32[16,128]{1,0:T(8,128)S(1)}, f32[16,128]{1,0:T(8,128)S(1)}, u32[]{:S(2)}, u32[]{:S(2)}) %collective-permute-start.20) | collective-permute-done | bytes 8224 | tf_op jit(solution)/shard_map/ppermute | solution.py:364
  188.6 0.7 shard_map.125
  189.4 18.1 %all_to_all.51.slots_ref = f32[32,5,4,128]{3,2,1,0:T(4,128)S(1)} all-to-all(f32[32,5,4,128]{3,2,1,0:T(4,128)S(1)} %get-tuple-element.136), channel_id=1, replica_groups=mesh['gx'=8,'gy'=4,'gz'=16] {'gx','gy'}, dimensions={0} | all-to-all | bytes 655360 | tf_op jit(solution)/shard_map/all_to_all | solution.py:368
  207.5 18.1 %all_to_all.52.slots_ref.layers_ref = f32[16,5,4,128]{3,2,1,0:T(4,128)S(1)} all-to-all(f32[16,5,4,128]{3,2,1,0:T(4,128)S(1)} %shard_map.126), channel_id=1, replica_groups=mesh['gx'=8,'gy'=4,'gz'=16] {'gz'}, dimensions={0} | all-to-all | bytes 327680 | tf_op jit(solution)/shard_map/all_to_all | solution.py:368
  225.6 14.5 %all_to_all.53.total_ref = f32[32,4,128]{2,1,0:T(4,128)S(1)} all-to-all(f32[32,4,128]{2,1,0:T(4,128)S(1)} %shard_map.127), channel_id=1, replica_groups=mesh['gx'=8,'gy'=4,'gz'=16] {'gx','gy'}, dimensions={0} | all-to-all | bytes 131072 | tf_op jit(solution)/shard_map/all_to_all | solution.py:368
  240.1 1.7 shard_map.128
  (23 shorter events, 0.2 us)
Async XLA Ops:
  1.3 0.7 copy-start.6
  2.2 22.6 %collective-permute-start = (f32[24,128]{1,0:T(8,128)S(1)}, f32[24,128]{1,0:T(8,128)S(1)}, u32[]{:S(2)}, u32[]{:S(2)}) collective-permute-start(f32[24,128]{1,0:T(8,128)S(1)} %get-tuple-element.73), channel_id=1, source_target_pairs={{0,64},{64,128},{128,192},{192,256},{256,320},{320,384},{384,448},... | collective-permute-start | bytes 36872 | tf_op jit(solution)/shard_map/ppermute | solution.py:364
  6.8 18.0 %collective-permute-start.1 = (f32[24,128]{1,0:T(8,128)S(1)}, f32[24,128]{1,0:T(8,128)S(1)}, u32[]{:S(2)}, u32[]{:S(2)}) collective-permute-start(f32[24,128]{1,0:T(8,128)S(1)} %get-tuple-element.74), channel_id=1, source_target_pairs={{0,16},{16,32},{32,48},{1,17},{17,33},{33,49},{2,18},{18,34},{34,5... | collective-permute-start | bytes 36872 | tf_op jit(solution)/shard_map/ppermute | solution.py:364
  10.0 14.9 %collective-permute-start.2 = (f32[24,128]{1,0:T(8,128)S(1)}, f32[24,128]{1,0:T(8,128)S(1)}, u32[]{:S(2)}, u32[]{:S(2)}) collective-permute-start(f32[24,128]{1,0:T(8,128)S(1)} %get-tuple-element.75), channel_id=1, source_target_pairs={{0,1},{1,2},{2,3},{3,4},{4,5},{5,6},{6,7},{7,8},{8,9},{9,10},{10,1... | collective-permute-start | bytes 36872 | tf_op jit(solution)/shard_map/ppermute | solution.py:364
  14.3 1.4 copy-start
  15.6 1.0 copy-start.1
  16.6 1.0 copy-start.2
  17.6 1.0 copy-start.3
  18.6 1.0 copy-start.4
  19.6 0.9 copy-start.5
  20.5 0.7 copy-start.8
  21.2 3.7 %copy-start.7 = (f32[1,1,1,3,16,128]{5,4,3,2,1,0:T(8,128)S(1)}, f32[1,1,1,3,16,128]{5,4,3,2,1,0:T(8,128)}, u32[]{:S(2)}) copy-start(f32[1,1,1,3,16,128]{5,4,3,2,1,0:T(8,128)} %param.10) | copy-start | bytes 73732
  25.4 12.4 %collective-permute-start.3 = (f32[48,128]{1,0:T(8,128)S(1)}, f32[48,128]{1,0:T(8,128)S(1)}, u32[]{:S(2)}, u32[]{:S(2)}) collective-permute-start(f32[48,128]{1,0:T(8,128)S(1)} %get-tuple-element.81), channel_id=1, source_target_pairs={{0,64},{64,128},{128,192},{192,256},{256,320},{320,384},{384,448},... | collective-permute-start | bytes 73736 | tf_op jit(solution)/shard_map/ppermute | solution.py:364
  27.9 11.2 %collective-permute-start.4 = (f32[48,128]{1,0:T(8,128)S(1)}, f32[48,128]{1,0:T(8,128)S(1)}, u32[]{:S(2)}, u32[]{:S(2)}) collective-permute-start(f32[48,128]{1,0:T(8,128)S(1)} %get-tuple-element.82), channel_id=1, source_target_pairs={{64,0},{128,64},{192,128},{256,192},{320,256},{384,320},{448,384},... | collective-permute-start | bytes 73736 | tf_op jit(solution)/shard_map/ppermute | solution.py:364
  29.8 9.3 %collective-permute-start.5 = (f32[48,128]{1,0:T(8,128)S(1)}, f32[48,128]{1,0:T(8,128)S(1)}, u32[]{:S(2)}, u32[]{:S(2)}) collective-permute-start(f32[48,128]{1,0:T(8,128)S(1)} %get-tuple-element.83), channel_id=1, source_target_pairs={{0,16},{16,32},{32,48},{1,17},{17,33},{33,49},{2,18},{18,34},{34,5... | collective-permute-start | bytes 73736 | tf_op jit(solution)/shard_map/ppermute | solution.py:364
  33.0 6.2 %collective-permute-start.6 = (f32[48,128]{1,0:T(8,128)S(1)}, f32[48,128]{1,0:T(8,128)S(1)}, u32[]{:S(2)}, u32[]{:S(2)}) collective-permute-start(f32[48,128]{1,0:T(8,128)S(1)} %get-tuple-element.84), channel_id=1, source_target_pairs={{16,0},{32,16},{48,32},{17,1},{33,17},{49,33},{18,2},{34,18},{50,3... | collective-permute-start | bytes 73736 | tf_op jit(solution)/shard_map/ppermute | solution.py:364
  34.3 4.9 %collective-permute-start.7 = (f32[48,128]{1,0:T(8,128)S(1)}, f32[48,128]{1,0:T(8,128)S(1)}, u32[]{:S(2)}, u32[]{:S(2)}) collective-permute-start(f32[48,128]{1,0:T(8,128)S(1)} %get-tuple-element.85), channel_id=1, source_target_pairs={{0,1},{1,2},{2,3},{3,4},{4,5},{5,6},{6,7},{7,8},{8,9},{9,10},{10,1... | collective-permute-start | bytes 73736 | tf_op jit(solution)/shard_map/ppermute | solution.py:364
  37.8 5.2 %collective-permute-start.8 = (f32[48,128]{1,0:T(8,128)S(1)}, f32[48,128]{1,0:T(8,128)S(1)}, u32[]{:S(2)}, u32[]{:S(2)}) collective-permute-start(f32[48,128]{1,0:T(8,128)S(1)} %get-tuple-element.86), channel_id=1, source_target_pairs={{1,0},{2,1},{3,2},{4,3},{5,4},{6,5},{7,6},{8,7},{9,8},{10,9},{11,1... | collective-permute-start | bytes 73736 | tf_op jit(solution)/shard_map/ppermute | solution.py:364
  105.0 10.8 %collective-permute-start.9 = (f32[16,128]{1,0:T(8,128)S(1)}, f32[16,128]{1,0:T(8,128)S(1)}, u32[]{:S(2)}, u32[]{:S(2)}) collective-permute-start(f32[16,128]{1,0:T(8,128)S(1)} %get-tuple-element.111), channel_id=1, source_target_pairs={{0,64},{64,128},{128,192},{192,256},{256,320},{320,384},{384,448},... | collective-permute-start | bytes 24584 | tf_op jit(solution)/shard_map/ppermute | solution.py:364
  107.5 9.6 %collective-permute-start.10 = (f32[16,128]{1,0:T(8,128)S(1)}, f32[16,128]{1,0:T(8,128)S(1)}, u32[]{:S(2)}, u32[]{:S(2)}) collective-permute-start(f32[16,128]{1,0:T(8,128)S(1)} %get-tuple-element.112), channel_id=1, source_target_pairs={{64,0},{128,64},{192,128},{256,192},{320,256},{384,320},{448,384},... | collective-permute-start | bytes 24584 | tf_op jit(solution)/shard_map/ppermute | solution.py:364
  109.5 7.7 %collective-permute-start.11 = (f32[16,128]{1,0:T(8,128)S(1)}, f32[16,128]{1,0:T(8,128)S(1)}, u32[]{:S(2)}, u32[]{:S(2)}) collective-permute-start(f32[16,128]{1,0:T(8,128)S(1)} %get-tuple-element.113), channel_id=1, source_target_pairs={{0,16},{16,32},{32,48},{1,17},{17,33},{33,49},{2,18},{18,34},{34,5... | collective-permute-start | bytes 24584 | tf_op jit(solution)/shard_map/ppermute | solution.py:364
  111.7 5.5 %collective-permute-start.12 = (f32[16,128]{1,0:T(8,128)S(1)}, f32[16,128]{1,0:T(8,128)S(1)}, u32[]{:S(2)}, u32[]{:S(2)}) collective-permute-start(f32[16,128]{1,0:T(8,128)S(1)} %get-tuple-element.114), channel_id=1, source_target_pairs={{16,0},{32,16},{48,32},{17,1},{33,17},{49,33},{18,2},{34,18},{50,3... | collective-permute-start | bytes 24584 | tf_op jit(solution)/shard_map/ppermute | solution.py:364
  113.0 4.2 %collective-permute-start.13 = (f32[16,128]{1,0:T(8,128)S(1)}, f32[16,128]{1,0:T(8,128)S(1)}, u32[]{:S(2)}, u32[]{:S(2)}) collective-permute-start(f32[16,128]{1,0:T(8,128)S(1)} %get-tuple-element.115), channel_id=1, source_target_pairs={{0,1},{1,2},{2,3},{3,4},{4,5},{5,6},{6,7},{7,8},{8,9},{9,10},{10,1... | collective-permute-start | bytes 24584 | tf_op jit(solution)/shard_map/ppermute | solution.py:364
  115.8 4.4 %collective-permute-start.14 = (f32[16,128]{1,0:T(8,128)S(1)}, f32[16,128]{1,0:T(8,128)S(1)}, u32[]{:S(2)}, u32[]{:S(2)}) collective-permute-start(f32[16,128]{1,0:T(8,128)S(1)} %get-tuple-element.116), channel_id=1, source_target_pairs={{1,0},{2,1},{3,2},{4,3},{5,4},{6,5},{7,6},{8,7},{9,8},{10,9},{11,1... | collective-permute-start | bytes 24584 | tf_op jit(solution)/shard_map/ppermute | solution.py:364
  173.4 10.8 %collective-permute-start.15 = (f32[16,128]{1,0:T(8,128)S(1)}, f32[16,128]{1,0:T(8,128)S(1)}, u32[]{:S(2)}, u32[]{:S(2)}) collective-permute-start(f32[16,128]{1,0:T(8,128)S(1)} %get-tuple-element.127), channel_id=1, source_target_pairs={{0,64},{64,128},{128,192},{192,256},{256,320},{320,384},{384,448},... | collective-permute-start | bytes 24584 | tf_op jit(solution)/shard_map/ppermute | solution.py:364
  175.9 9.6 %collective-permute-start.16 = (f32[16,128]{1,0:T(8,128)S(1)}, f32[16,128]{1,0:T(8,128)S(1)}, u32[]{:S(2)}, u32[]{:S(2)}) collective-permute-start(f32[16,128]{1,0:T(8,128)S(1)} %get-tuple-element.128), channel_id=1, source_target_pairs={{64,0},{128,64},{192,128},{256,192},{320,256},{384,320},{448,384},... | collective-permute-start | bytes 24584 | tf_op jit(solution)/shard_map/ppermute | solution.py:364
  177.8 7.7 %collective-permute-start.17 = (f32[16,128]{1,0:T(8,128)S(1)}, f32[16,128]{1,0:T(8,128)S(1)}, u32[]{:S(2)}, u32[]{:S(2)}) collective-permute-start(f32[16,128]{1,0:T(8,128)S(1)} %get-tuple-element.129), channel_id=1, source_target_pairs={{0,16},{16,32},{32,48},{1,17},{17,33},{33,49},{2,18},{18,34},{34,5... | collective-permute-start | bytes 24584 | tf_op jit(solution)/shard_map/ppermute | solution.py:364
  180.1 5.5 %collective-permute-start.18 = (f32[16,128]{1,0:T(8,128)S(1)}, f32[16,128]{1,0:T(8,128)S(1)}, u32[]{:S(2)}, u32[]{:S(2)}) collective-permute-start(f32[16,128]{1,0:T(8,128)S(1)} %get-tuple-element.130), channel_id=1, source_target_pairs={{16,0},{32,16},{48,32},{17,1},{33,17},{49,33},{18,2},{34,18},{50,3... | collective-permute-start | bytes 24584 | tf_op jit(solution)/shard_map/ppermute | solution.py:364
  181.4 4.2 %collective-permute-start.19 = (f32[16,128]{1,0:T(8,128)S(1)}, f32[16,128]{1,0:T(8,128)S(1)}, u32[]{:S(2)}, u32[]{:S(2)}) collective-permute-start(f32[16,128]{1,0:T(8,128)S(1)} %get-tuple-element.131), channel_id=1, source_target_pairs={{0,1},{1,2},{2,3},{3,4},{4,5},{5,6},{6,7},{7,8},{8,9},{9,10},{10,1... | collective-permute-start | bytes 24584 | tf_op jit(solution)/shard_map/ppermute | solution.py:364
  184.2 4.4 %collective-permute-start.20 = (f32[16,128]{1,0:T(8,128)S(1)}, f32[16,128]{1,0:T(8,128)S(1)}, u32[]{:S(2)}, u32[]{:S(2)}) collective-permute-start(f32[16,128]{1,0:T(8,128)S(1)} %get-tuple-element.132), channel_id=1, source_target_pairs={{1,0},{2,1},{3,2},{4,3},{5,4},{6,5},{7,6},{8,7},{9,8},{10,9},{11,1... | collective-permute-start | bytes 24584 | tf_op jit(solution)/shard_map/ppermute | solution.py:364

commit v4 on v3

--- a/solution.py
+++ b/solution.py
@@ -96,6 +96,47 @@
     return (-gy, gy, -1, 1)
 
 
+def cube_groups(start):
+    gx, gy, gz = (lax.axis_size(a) for a in AXES)
+    return [
+        [
+            (i + a) % gx * gy * gz + (j + b) % gy * gz + (k + c) % gz
+            for a in range(2) for b in range(2) for c in range(2)
+        ]
+        for i in range(start, gx + start, 2)
+        for j in range(start, gy + start, 2)
+        for k in range(start, gz + start, 2)
+    ]
+
+
+def cube_places():
+    odd = [lax.rem(lax.axis_index(a), 2) for a in AXES]
+    first = odd[0] * 4 + odd[1] * 2 + odd[2]
+    found = []
+    for d in range(3):
+        bit = 4 >> d
+        other = first + bit * (1 - 2 * odd[d])
+        found.append((odd[d] == 0, other, 7 - other))
+    return found
+
+
+def put_cubes(first_ref, second_ref, piece):
+    first_ref[...] = jnp.zeros_like(first_ref)
+    second_ref[...] = jnp.zeros_like(second_ref)
+    for d, (even, one, two) in enumerate(cube_places()):
+        lower, upper = piece(2 * d), piece(2 * d + 1)
+        first_ref[one] = jnp.where(even, upper, lower)
+        second_ref[two] = jnp.where(even, lower, upper)
+
+
+def take_cubes(first_ref, second_ref, rows):
+    got = []
+    for even, one, two in cube_places():
+        a, b = first_ref[one, rows, :], second_ref[two, rows, :]
+        got += [jnp.where(even, b, a), jnp.where(even, a, b)]
+    return got
+
+
 def mask_row(there):
     return jnp.concatenate([jnp.full((1, FD), t.astype(F32)) for t in there], axis=1)
 
@@ -113,7 +154,7 @@
     _, _, there = position()
     for d in range(3):
         message_ref = message_refs[d]
-        row = partner_ref[d:d + 1, :]
+        row = partner_ref[0, 0, 0, d:d + 1, :]
         message_ref[0:CASES, :] = rhs_ref[d] * there[2 * d + 1].astype(F32)
         wanted = lax.broadcasted_iota(jnp.int32, (FD, FD), 0)
         hits = (wanted == jnp.broadcast_to(row, (FD, FD))).astype(F32).astype(BF16)
@@ -138,8 +179,8 @@
     for f in range(6):
         put(f * FD, f * FD, diag_ref[f])
     for k in range(6):
-        first = pl.multiple_of(pairs[k, 0] * FD, FD)
-        second = pl.multiple_of(pairs[k, 1] * FD, FD)
+        first = pl.multiple_of(pairs[0, 0, 0, k, 0] * FD, FD)
+        second = pl.multiple_of(pairs[0, 0, 0, k, 1] * FD, FD)
         block = couple_ref[k]
         put(second, first, block)
         put(first, second, block.T)
@@ -158,12 +199,12 @@
     lanes = lax.broadcasted_iota(jnp.int32, (8, FD), 1) % SUBS
     target = jnp.full((8, FD), -1, jnp.int32)
     for r in range(24):
-        target = jnp.where(lanes == r, (r % 3) * QPAD + ids[0, r // 3], target)
+        target = jnp.where(lanes == r, (r % 3) * QPAD + ids[0, 0, 0, r // 3], target)
     target_ref[...] = target.astype(F32)
     pad[...] = jnp.zeros_like(pad)
     lanes = lax.broadcasted_iota(jnp.int32, (1, 3 * QPAD), 1)
     for r in range(24):
-        spot = (r % 3) * QPAD + ids[0, r // 3]
+        spot = (r % 3) * QPAD + ids[0, 0, 0, r // 3]
         pad[r:r + 1, :] = (lanes == spot).astype(F32)
     expand_ref[...] = pad[...].astype(BF16)
     copies[0].wait()
@@ -192,7 +233,7 @@
 
 
 def start_kernel(rhs_ref, mx_ref, my_ref, mz_ref, dh_ref, dl_ref, coupling_ref, target_ref,
-                 field_ref, shown_ref, own_ref, *piece_refs):
+                 field_ref, shown_ref, own_ref, first_ref, second_ref):
     _, _, there = position()
     messages = (mx_ref, my_ref, mz_ref)
     parts = []
@@ -205,15 +246,16 @@
     shown_ref[...] = shown
     own = lower_changed(coupling_ref[...], partner_rows(messages))
     own_ref[...] = own
-    for f in range(6):
-        piece_refs[f][0:CASES, :] = face(shown, f)
-        piece_refs[f][CASES:CASES + 24, :] = face(own, f)
-        piece_refs[f][CASES + 24:CASES + 32, :] = target_ref[...]
-
-
-def joint_kernel(own_ref, target_ref, *rest):
-    others, (gh_ref, gl_ref, pick_ref, whole) = rest[:6], rest[6:]
+    target = target_ref[...]
+    put_cubes(
+        first_ref, second_ref,
+        lambda f: jnp.concatenate([face(shown, f), face(own, f), target], axis=0),
+    )
+
+
+def joint_kernel(own_ref, target_ref, first_ref, second_ref, gh_ref, gl_ref, pick_ref, whole):
     _, _, there = position()
+    others = take_cubes(first_ref, second_ref, slice(CASES, CASES + 32))
     whole[...] = jnp.zeros_like(whole)
     whole[0:24, :] = own_ref[...]
     lanes = lax.broadcasted_iota(jnp.int32, (8, FD), 1)
@@ -221,9 +263,9 @@
     for f in range(6):
         exists = there[f].astype(F32)
         whole[SUBS * (f + 1):SUBS * (f + 1) + 24, f * FD:(f + 1) * FD] = (
-            others[f][CASES:CASES + 24, :] * exists
+            others[f][0:24, :] * exists
         )
-        targets.append(others[f][CASES + 24:CASES + 32, :] * exists)
+        targets.append(others[f][24:32, :] * exists)
     high, low = halves(whole[...])
     gh_ref[...] = high
     gl_ref[...] = low
@@ -236,17 +278,15 @@
         pick_ref[:, half * FD:(half + 1) * FD] = (rows == wanted).astype(F32).astype(BF16)
 
 
-def load_kernel(first, mx_ref, my_ref, mz_ref, shown_ref, *rest):
-    others, rest = rest[:6], rest[6:]
-    residual_ref, fh_ref, fl_ref, wh_ref, wl_ref, expand_ref = rest[:6]
-    rest = rest[6:]
+def load_kernel(first, mx_ref, my_ref, mz_ref, shown_ref, one_ref, two_ref, residual_ref, fh_ref,
+                fl_ref, wh_ref, wl_ref, expand_ref, *rest):
     if first:
         z_ref, flexed_ref, out_ref = rest
     else:
         search_ref, applied_ref, z_ref, flexed_ref, out_ref = rest
     messages = (mx_ref, my_ref, mz_ref)
     here, _, there = position()
-    across = jnp.concatenate([other[0:CASES, :] for other in others], axis=1)
+    across = jnp.concatenate(take_cubes(one_ref, two_ref, slice(0, CASES)), axis=1)
     z = 0.25 * (shown_ref[...] + across) * mask_row(there)
     z_ref[...] = z
     loads, flexed = apply_dense(z, messages, fh_ref, fl_ref)
@@ -342,7 +382,7 @@
             left_ref[d] = face(residual, 2 * d + 1)
         return
     search_out, applied_out, load_out, scale_out, iterate_out, residual_out, shown_ref = rest[:7]
-    piece_refs = rest[7:]
+    first_ref, second_ref = rest[7:]
     search_out[...] = search
     applied_out[...] = applied
     load_out[...] = load
@@ -354,8 +394,7 @@
         iterate_out[d] = moved_face if first else iterate_ref[d] + moved_face
     _, shown = apply_dense(residual, (mx_ref, my_ref, mz_ref), dh_ref, dl_ref)
     shown_ref[...] = shown
-    for f in range(6):
-        piece_refs[f][...] = face(shown, f)
+    put_cubes(first_ref, second_ref, lambda f: face(shown, f))
 
 
 def passed_along(shard, axis, by):
@@ -368,12 +407,10 @@
     return lax.all_to_all(slots, axes, 0, 0)
 
 
-def across_faces(pieces):
-    got = [None] * 6
-    for d in (2, 1, 0):
-        got[2 * d] = passed_along(pieces[2 * d + 1], AXES[d], 1)
-        got[2 * d + 1] = passed_along(pieces[2 * d], AXES[d], -1)
-    return got
+def across_faces(one, two):
+    one = lax.all_to_all(one, AXES, 0, 0, axis_index_groups=cube_groups(0))
+    one, two = lax.optimization_barrier((one, two))
+    return [one, lax.all_to_all(two, AXES, 0, 0, axis_index_groups=cube_groups(1))]
 
 
 def body(
@@ -391,15 +428,13 @@
     gx, gy, gz = (lax.axis_size(a) for a in AXES)
     plane = gx * gy
     rhs = jump_rhs.reshape(3, CASES, FD)
-    pairs = face_pairs.reshape(6, 2)
     coupling = corner_coupling.reshape(24, WIDE)
-    ids = coarse_ids.reshape(1, 8)
     square = (WIDE, WIDE)
     wide = (CASES, WIDE)
     long = CASES + 32
 
     messages = call(
-        prep_kernel, [((CASES + 8, FD), F32)] * 3, [rhs, partner.reshape(3, FD)]
+        prep_kernel, [((CASES + 8, FD), F32)] * 3, [rhs, partner]
     )
     messages = [passed_along(m, a, 1) for m, a in zip(messages, AXES)]
     blocks = [b.reshape(6, FD, FD) for b in (dirichlet_diag, dirichlet_couple, flex_diag, flex_couple)]
@@ -407,18 +442,18 @@
     *dense, target = call(
         setup_kernel,
         [(square, BF16)] * 6 + [((WIDE, FD), BF16)] * 2 + [((FD, WIDE), BF16), ((8, FD), F32)],
-        [pairs, ids] + sources,
-        specs=[SMEM] * 2 + [pl.BlockSpec(memory_space=pl.ANY)] * 6,
+        [face_pairs, coarse_ids] + sources,
+        specs=[SMEM] * 2 + [pl.BlockSpec(memory_space=pltpu.HBM)] * 6,
         scratch=[pltpu.VMEM(source.shape, F32) for source in sources]
         + [pltpu.VMEM((FD, WIDE), F32), pltpu.VMEM(square, F32), pltpu.SemaphoreType.DMA((6,))],
     )
     dirichlet, flex, inverse, weights = dense[0:2], dense[2:4], dense[4:6], dense[6:9]
-    residual, shown, own, *pieces = call(
+    residual, shown, own, one, two = call(
         start_kernel,
-        [(wide, F32), (wide, F32), ((24, WIDE), F32)] + [((long, FD), F32)] * 6,
+        [(wide, F32), (wide, F32), ((24, WIDE), F32)] + [((8, long, FD), F32)] * 2,
         [rhs, *messages, *dirichlet, coupling, target],
     )
-    others = across_faces(pieces)
+    others = across_faces(one, two)
     joint = call(
         joint_kernel,
         [((QPAD, WIDE), BF16), ((QPAD, WIDE), BF16), ((3 * QPAD, QPAD), BF16)],
@@ -445,13 +480,13 @@
         if last:
             multipliers, left = call(kernel, [((3, CASES, FD), F32)] * 2, common + kept)
             break
-        *kept, residual, shown, p0, p1, p2, p3, p4, p5 = call(
+        *kept, residual, shown, one, two = call(
             kernel,
             [(wide, F32)] * 3 + [((CASES, FD), F32), ((3, CASES, FD), F32), (wide, F32), (wide, F32)]
-            + [((CASES, FD), F32)] * 6,
+            + [((8, CASES, FD), F32)] * 2,
             common + [*messages, *dirichlet] + kept,
         )
-        others = across_faces((p0, p1, p2, p3, p4, p5))
+        others = across_faces(one, two)
     return multipliers.reshape(jump_rhs.shape), left.reshape(jump_rhs.shape)
 
 

time: 243 us -> 243 us (level)
  blocking collectives: 161 us -> 209 us
  starting transfers between devices: 49.1 us -> 11.3 us
  waiting for transfers between devices: 9.98 us -> 0.01 us
    all_to_all x0 -> x6, blocking collectives: none -> 59 us  [the longest x3 34.8 us: across_faces(): lax.all_to_all(two, AXES, 0, 0, axis_index_groups=cube_groups(1))]
    ppermute x21 -> x3, starting transfers between devices: 49.1 us -> 11.3 us  [passed_along(): return lax.ppermute(shard, axis, pairs)]
    all_to_all x9, blocking collectives: 161 us -> 150 us  [swapped(): return lax.all_to_all(slots, axes, 0, 0)]
    ppermute x21 -> x3, waiting for transfers between devices: 9.98 us -> 0.01 us  [passed_along(): return lax.ppermute(shard, axis, pairs)]
    unnamed x19 -> x20, local copies, waits for them, and re-layouts: 8.32 us -> 9.08 us
  transfers between devices with their start and end apart: 21 -> 3, of which waited for: 3 -> 0; matrix products, arithmetic and copies ran while one was open for 0% -> 0% of each run, Pallas kernels for 1% -> 1%
where the time goes in v4:
time: 243 us; the launch traced here: 242 us
  blocking collectives  209 us (86%)
  Pallas kernels  11.9 us (5%)
  starting transfers between devices  11.3 us (5%)
  local copies, waits for them, and re-layouts  9.08 us (4%)
    all_to_all x9, blocking collectives, swapped(): return lax.all_to_all(slots, axes, 0, 0)  150 us
    all_to_all x3, blocking collectives, across_faces(): lax.all_to_all(two, AXES, 0, 0, axis_index_groups=cube_groups(1))  34.8 us
    all_to_all x3, blocking collectives, across_faces(): one = lax.all_to_all(one, AXES, 0, 0, axis_index_groups=cube_groups(0))  24.2 us
    pallas_call x16, Pallas kernels, call(): pl.pallas_call(kernel, out_shape=[jax.ShapeDtypeStruct(shape, dtype) for...  11.9 us
    ppermute x3, starting transfers between devices, passed_along(): return lax.ppermute(shard, axis, pairs)  11.3 us
    unnamed x20, local copies, waits for them, and re-layouts  9.08 us
  transfers between devices with their start and end apart: 3, of which 0 were waited for; matrix products, arithmetic and copies ran while one was open for 0% of the time, Pallas kernels for 1%

profile of v4, /device:TPU:1, one launch (start us, length us, event | category | flops | bytes accessed | tf_op | source)
XLA Modules:
  0.0 242.1 jit_solution(17275053169304972047)
XLA Ops:
  0.6 0.7 copy.12.partner_ref
  1.3 0.0 copy-start.6
  1.3 0.7 copy-done.6
  2.0 0.2 shard_map.113
  2.2 4.6 %collective-permute-start = (f32[24,128]{1,0:T(8,128)S(1)}, f32[24,128]{1,0:T(8,128)S(1)}, u32[]{:S(2)}, u32[]{:S(2)}) collective-permute-start(f32[24,128]{1,0:T(8,128)S(1)} %get-tuple-element.63), channel_id=1, source_target_pairs={{0,64},{64,128},{128,192},{192,256},{256,320},{320,384},{384,448},... | collective-permute-start | bytes 36872 | tf_op jit(solution)/shard_map/ppermute | solution.py:403
  6.8 3.1 %collective-permute-start.1 = (f32[24,128]{1,0:T(8,128)S(1)}, f32[24,128]{1,0:T(8,128)S(1)}, u32[]{:S(2)}, u32[]{:S(2)}) collective-permute-start(f32[24,128]{1,0:T(8,128)S(1)} %get-tuple-element.64), channel_id=1, source_target_pairs={{0,16},{16,32},{32,48},{1,17},{17,33},{33,49},{2,18},{18,34},{34,5... | collective-permute-start | bytes 36872 | tf_op jit(solution)/shard_map/ppermute | solution.py:403
  10.0 3.5 %collective-permute-start.2 = (f32[24,128]{1,0:T(8,128)S(1)}, f32[24,128]{1,0:T(8,128)S(1)}, u32[]{:S(2)}, u32[]{:S(2)}) collective-permute-start(f32[24,128]{1,0:T(8,128)S(1)} %get-tuple-element.65), channel_id=1, source_target_pairs={{0,1},{1,2},{2,3},{3,4},{4,5},{5,6},{6,7},{7,8},{8,9},{9,10},{10,1... | collective-permute-start | bytes 36872 | tf_op jit(solution)/shard_map/ppermute | solution.py:403
  13.5 0.8 copy.13.pairs
  14.3 0.0 copy-start
  14.3 1.4 copy-done
  15.6 0.0 copy-start.1
  15.6 1.0 copy-done.1
  16.6 0.0 copy-start.2
  16.6 1.0 copy-done.2
  17.6 0.0 copy-start.3
  17.6 1.0 copy-done.3
  18.6 0.0 copy-start.4
  18.6 1.0 copy-done.4
  19.6 0.0 copy-start.5
  19.6 0.9 copy-done.5
  20.5 0.0 copy-start.8
  20.5 0.7 copy-done.8
  21.2 0.0 copy-start.7
  21.2 3.6 %shard_map.114 = (bf16[768,768]{1,0:T(8,128)(2,1)S(1)}, bf16[768,768]{1,0:T(8,128)(2,1)S(1)}, bf16[768,768]{1,0:T(8,128)(2,1)S(1)}, bf16[768,768]{1,0:T(8,128)(2...) custom-call(s32[1,1,1,6,2]{4,3,2,1,0:T(8,128)S(1)} %copy.13.pairs, ...), custom_call_target="tpu_custom_call" | custom-call | tf_op jit(solution)/shard_map/pallas_call | solution.py:25
  24.8 0.0 collective-permute-done.mx_ref.rest_0_
  24.8 0.0 collective-permute-done.1.my_ref.rest_1_
  24.8 0.0 collective-permute-done.2.mz_ref.rest_2_
  24.8 0.0 copy-done.7
  24.8 0.6 shard_map.115
  25.4 9.6 %all_to_all.75.first_ref.one_ref = f32[8,48,128]{2,1,0:T(8,128)S(1)} all-to-all(f32[8,48,128]{2,1,0:T(8,128)S(1)} %get-tuple-element.71), channel_id=1, replica_groups={{0,1,16,17,64,65,80,81},{2,3,18,19,66,67,82,83},{4,5,20,21,68,69,84,85}..., dimensions={0} | all-to-all | bytes 393216 | tf_op jit(solution)/shard_map/all_to_all | solution.py:411
  35.0 15.5 %all_to_all.76.second_ref.two_ref = f32[8,48,128]{2,1,0:T(8,128)S(1)} all-to-all(f32[8,48,128]{2,1,0:T(8,128)S(1)} %get-tuple-element.74), channel_id=1, replica_groups={{81,82,97,98,145,146,161,162},{83,84,99,100,147,148,163,164},{85,86,101..., dimensions={0} | all-to-all | bytes 393216 | tf_op jit(solution)/shard_map/all_to_all | solution.py:413
  50.5 0.2 shard_map.116
  50.7 0.7 shard_map.117
  51.4 15.8 %all_to_all.77.slots_ref = f32[32,5,4,128]{3,2,1,0:T(4,128)S(1)} all-to-all(f32[32,5,4,128]{3,2,1,0:T(4,128)S(1)} %get-tuple-element.86), channel_id=1, replica_groups=mesh['gx'=8,'gy'=4,'gz'=16] {'gx','gy'}, dimensions={0} | all-to-all | bytes 655360 | tf_op jit(solution)/shard_map/all_to_all | solution.py:407
  67.3 21.0 %all_to_all.78.slots_ref.layers_ref = f32[16,5,4,128]{3,2,1,0:T(4,128)S(1)} all-to-all(f32[16,5,4,128]{3,2,1,0:T(4,128)S(1)} %shard_map.118), channel_id=1, replica_groups=mesh['gx'=8,'gy'=4,'gz'=16] {'gz'}, dimensions={0} | all-to-all | bytes 327680 | tf_op jit(solution)/shard_map/all_to_all | solution.py:407
  88.3 14.5 %all_to_all.79.total_ref = f32[32,4,128]{2,1,0:T(4,128)S(1)} all-to-all(f32[32,4,128]{2,1,0:T(4,128)S(1)} %shard_map.119), channel_id=1, replica_groups=mesh['gx'=8,'gy'=4,'gz'=16] {'gx','gy'}, dimensions={0} | all-to-all | bytes 131072 | tf_op jit(solution)/shard_map/all_to_all | solution.py:407
  102.8 1.5 shard_map.120
  104.3 7.3 %all_to_all.80.one_ref = f32[8,16,128]{2,1,0:T(8,128)S(1)} all-to-all(f32[8,16,128]{2,1,0:T(8,128)S(1)} %get-tuple-element.95), channel_id=1, replica_groups={{0,1,16,17,64,65,80,81},{2,3,18,19,66,67,82,83},{4,5,20,21,68,69,84,85}..., dimensions={0} | all-to-all | bytes 131072 | tf_op jit(solution)/shard_map/all_to_all | solution.py:411
  111.6 9.7 %all_to_all.81.two_ref = f32[8,16,128]{2,1,0:T(8,128)S(1)} all-to-all(f32[8,16,128]{2,1,0:T(8,128)S(1)} %get-tuple-element.98), channel_id=1, replica_groups={{81,82,97,98,145,146,161,162},{83,84,99,100,147,148,163,164},{85,86,101..., dimensions={0} | all-to-all | bytes 131072 | tf_op jit(solution)/shard_map/all_to_all | solution.py:413
  121.3 0.8 shard_map.121
  122.1 16.6 %all_to_all.82.slots_ref = f32[32,5,4,128]{3,2,1,0:T(4,128)S(1)} all-to-all(f32[32,5,4,128]{3,2,1,0:T(4,128)S(1)} %get-tuple-element.102), channel_id=1, replica_groups=mesh['gx'=8,'gy'=4,'gz'=16] {'gx','gy'}, dimensions={0} | all-to-all | bytes 655360 | tf_op jit(solution)/shard_map/all_to_all | solution.py:407
  138.7 18.3 %all_to_all.83.slots_ref.layers_ref = f32[16,5,4,128]{3,2,1,0:T(4,128)S(1)} all-to-all(f32[16,5,4,128]{3,2,1,0:T(4,128)S(1)} %shard_map.122), channel_id=1, replica_groups=mesh['gx'=8,'gy'=4,'gz'=16] {'gz'}, dimensions={0} | all-to-all | bytes 327680 | tf_op jit(solution)/shard_map/all_to_all | solution.py:407
  157.1 14.5 %all_to_all.84.total_ref = f32[32,4,128]{2,1,0:T(4,128)S(1)} all-to-all(f32[32,4,128]{2,1,0:T(4,128)S(1)} %shard_map.123), channel_id=1, replica_groups=mesh['gx'=8,'gy'=4,'gz'=16] {'gx','gy'}, dimensions={0} | all-to-all | bytes 131072 | tf_op jit(solution)/shard_map/all_to_all | solution.py:407
  171.5 1.6 shard_map.124
  173.2 7.3 %all_to_all.85.one_ref = f32[8,16,128]{2,1,0:T(8,128)S(1)} all-to-all(f32[8,16,128]{2,1,0:T(8,128)S(1)} %get-tuple-element.109), channel_id=1, replica_groups={{0,1,16,17,64,65,80,81},{2,3,18,19,66,67,82,83},{4,5,20,21,68,69,84,85}..., dimensions={0} | all-to-all | bytes 131072 | tf_op jit(solution)/shard_map/all_to_all | solution.py:411
  180.5 9.7 %all_to_all.86.two_ref = f32[8,16,128]{2,1,0:T(8,128)S(1)} all-to-all(f32[8,16,128]{2,1,0:T(8,128)S(1)} %get-tuple-element.112), channel_id=1, replica_groups={{81,82,97,98,145,146,161,162},{83,84,99,100,147,148,163,164},{85,86,101..., dimensions={0} | all-to-all | bytes 131072 | tf_op jit(solution)/shard_map/all_to_all | solution.py:413
  190.2 0.8 shard_map.125
  190.9 16.6 %all_to_all.87.slots_ref = f32[32,5,4,128]{3,2,1,0:T(4,128)S(1)} all-to-all(f32[32,5,4,128]{3,2,1,0:T(4,128)S(1)} %get-tuple-element.116), channel_id=1, replica_groups=mesh['gx'=8,'gy'=4,'gz'=16] {'gx','gy'}, dimensions={0} | all-to-all | bytes 655360 | tf_op jit(solution)/shard_map/all_to_all | solution.py:407
  207.5 18.3 %all_to_all.88.slots_ref.layers_ref = f32[16,5,4,128]{3,2,1,0:T(4,128)S(1)} all-to-all(f32[16,5,4,128]{3,2,1,0:T(4,128)S(1)} %shard_map.126), channel_id=1, replica_groups=mesh['gx'=8,'gy'=4,'gz'=16] {'gz'}, dimensions={0} | all-to-all | bytes 327680 | tf_op jit(solution)/shard_map/all_to_all | solution.py:407
  225.9 14.5 %all_to_all.89.total_ref = f32[32,4,128]{2,1,0:T(4,128)S(1)} all-to-all(f32[32,4,128]{2,1,0:T(4,128)S(1)} %shard_map.127), channel_id=1, replica_groups=mesh['gx'=8,'gy'=4,'gz'=16] {'gx','gy'}, dimensions={0} | all-to-all | bytes 131072 | tf_op jit(solution)/shard_map/all_to_all | solution.py:407
  240.4 1.7 shard_map.128
  (6 shorter events, 0.2 us)
Async XLA Ops:
  1.3 0.7 copy-start.6
  2.2 22.6 %collective-permute-start = (f32[24,128]{1,0:T(8,128)S(1)}, f32[24,128]{1,0:T(8,128)S(1)}, u32[]{:S(2)}, u32[]{:S(2)}) collective-permute-start(f32[24,128]{1,0:T(8,128)S(1)} %get-tuple-element.63), channel_id=1, source_target_pairs={{0,64},{64,128},{128,192},{192,256},{256,320},{320,384},{384,448},... | collective-permute-start | bytes 36872 | tf_op jit(solution)/shard_map/ppermute | solution.py:403
  6.8 18.0 %collective-permute-start.1 = (f32[24,128]{1,0:T(8,128)S(1)}, f32[24,128]{1,0:T(8,128)S(1)}, u32[]{:S(2)}, u32[]{:S(2)}) collective-permute-start(f32[24,128]{1,0:T(8,128)S(1)} %get-tuple-element.64), channel_id=1, source_target_pairs={{0,16},{16,32},{32,48},{1,17},{17,33},{33,49},{2,18},{18,34},{34,5... | collective-permute-start | bytes 36872 | tf_op jit(solution)/shard_map/ppermute | solution.py:403
  10.0 14.9 %collective-permute-start.2 = (f32[24,128]{1,0:T(8,128)S(1)}, f32[24,128]{1,0:T(8,128)S(1)}, u32[]{:S(2)}, u32[]{:S(2)}) collective-permute-start(f32[24,128]{1,0:T(8,128)S(1)} %get-tuple-element.65), channel_id=1, source_target_pairs={{0,1},{1,2},{2,3},{3,4},{4,5},{5,6},{6,7},{7,8},{8,9},{9,10},{10,1... | collective-permute-start | bytes 36872 | tf_op jit(solution)/shard_map/ppermute | solution.py:403
  14.3 1.4 copy-start
  15.6 1.0 copy-start.1
  16.6 1.0 copy-start.2
  17.6 1.0 copy-start.3
  18.6 1.0 copy-start.4
  19.6 0.9 copy-start.5
  20.5 0.7 copy-start.8
  21.2 3.7 %copy-start.7 = (f32[1,1,1,3,16,128]{5,4,3,2,1,0:T(8,128)S(1)}, f32[1,1,1,3,16,128]{5,4,3,2,1,0:T(8,128)}, u32[]{:S(2)}) copy-start(f32[1,1,1,3,16,128]{5,4,3,2,1,0:T(8,128)} %param.10) | copy-start | bytes 73732

commit v5 on v4

--- a/solution.py
+++ b/solution.py
@@ -42,6 +42,10 @@
     high, low = halves(x)
     both = jnp.dot(jnp.concatenate([high, low], 0), selector, preferred_element_type=F32)
     return both[:rows] + both[rows:]
+
+
+def dot_across(x, matrix):
+    return lax.dot_general(x, matrix, (((1,), (1,)), ((), ())), preferred_element_type=F32)
 
 
 def dot_split(x, high_ref, low_ref):
@@ -186,50 +190,17 @@
         put(first, second, block.T)
 
 
-def setup_kernel(pairs, ids, *rest):
-    sources, rest = rest[:6], rest[6:]
-    (dh_ref, dl_ref, fh_ref, fl_ref, kh_ref, kl_ref, wh_ref, wl_ref, expand_ref, target_ref) = rest[:10]
-    held, (pad, square, sems) = rest[10:16], rest[16:]
-    copies = [
-        pltpu.make_async_copy(source, target, sems.at[i])
-        for i, (source, target) in enumerate(zip(sources, held))
-    ]
-    for copy in copies:
-        copy.start()
+def target_rows(ids):
     lanes = lax.broadcasted_iota(jnp.int32, (8, FD), 1) % SUBS
     target = jnp.full((8, FD), -1, jnp.int32)
     for r in range(24):
         target = jnp.where(lanes == r, (r % 3) * QPAD + ids[0, 0, 0, r // 3], target)
-    target_ref[...] = target.astype(F32)
-    pad[...] = jnp.zeros_like(pad)
-    lanes = lax.broadcasted_iota(jnp.int32, (1, 3 * QPAD), 1)
-    for r in range(24):
-        spot = (r % 3) * QPAD + ids[0, 0, 0, r // 3]
-        pad[r:r + 1, :] = (lanes == spot).astype(F32)
-    expand_ref[...] = pad[...].astype(BF16)
-    copies[0].wait()
-    copies[1].wait()
-    put_dense(pairs, held[0], held[1], dh_ref, dl_ref)
-    copies[2].wait()
-    copies[3].wait()
-    put_dense(pairs, held[2], held[3], fh_ref, fl_ref)
-    square[...] = jnp.zeros_like(square)
-    copies[4].wait()
-    for p in range(3):
-        for q in range(3):
-            square[p * QPAD:p * QPAD + 192, q * QPAD:q * QPAD + 192] = held[4][
-                p * 192:(p + 1) * 192, q * 192:(q + 1) * 192
-            ]
-    high, low = halves(square[...])
-    kh_ref[...] = high
-    kl_ref[...] = low
-    pad[...] = jnp.zeros_like(pad)
-    copies[5].wait()
-    pad[0:24, :] = held[5][...]
-    for f in range(6):
-        high, low = halves(pad[:, f * FD:(f + 1) * FD].T)
-        wh_ref[f * FD:(f + 1) * FD, :] = high
-        wl_ref[f * FD:(f + 1) * FD, :] = low
+    return target.astype(F32)
+
+
+def dense_kernel(pairs, ids, diag_ref, couple_ref, high_ref, low_ref, target_ref):
+    put_dense(pairs, diag_ref, couple_ref, high_ref, low_ref)
+    target_ref[...] = target_rows(ids)
 
 
 def start_kernel(rhs_ref, mx_ref, my_ref, mz_ref, dh_ref, dl_ref, coupling_ref, target_ref,
@@ -253,20 +224,40 @@
     )
 
 
-def joint_kernel(own_ref, target_ref, first_ref, second_ref, gh_ref, gl_ref, pick_ref, whole):
+def setup_kernel(pairs, ids, diag_ref, couple_ref, inverse_ref, coupling_ref, own_ref, target_ref,
+                 first_ref, second_ref, fh_ref, fl_ref, kh_ref, kl_ref, wh_ref, wl_ref, expand_ref,
+                 gh_ref, gl_ref, pick_ref, pad, square):
     _, _, there = position()
+    put_dense(pairs, diag_ref, couple_ref, fh_ref, fl_ref)
+    square[...] = jnp.zeros_like(square)
+    for p in range(3):
+        for q in range(3):
+            square[p * QPAD:p * QPAD + 192, q * QPAD:q * QPAD + 192] = inverse_ref[
+                p * 192:(p + 1) * 192, q * 192:(q + 1) * 192
+            ]
+    high, low = halves(square[...])
+    kh_ref[...] = high
+    kl_ref[...] = low
+    pad[...] = jnp.zeros_like(pad)
+    pad[0:24, :] = coupling_ref[...]
+    for f in range(6):
+        high, low = halves(pad[0:FD, f * FD:(f + 1) * FD].T)
+        wh_ref[f * FD:(f + 1) * FD, :] = high
+        wl_ref[f * FD:(f + 1) * FD, :] = low
+    lanes = lax.broadcasted_iota(jnp.int32, (1, 3 * QPAD), 1)
+    for r in range(24):
+        spot = (r % 3) * QPAD + ids[0, 0, 0, r // 3]
+        pad[r:r + 1, :] = (lanes == spot).astype(F32)
+    expand_ref[...] = pad[0:FD, :].astype(BF16)
     others = take_cubes(first_ref, second_ref, slice(CASES, CASES + 32))
-    whole[...] = jnp.zeros_like(whole)
-    whole[0:24, :] = own_ref[...]
+    pad[0:24, :] = own_ref[...]
     lanes = lax.broadcasted_iota(jnp.int32, (8, FD), 1)
     targets = [target_ref[...]]
     for f in range(6):
         exists = there[f].astype(F32)
-        whole[SUBS * (f + 1):SUBS * (f + 1) + 24, f * FD:(f + 1) * FD] = (
-            others[f][0:24, :] * exists
-        )
+        pad[SUBS * (f + 1):SUBS * (f + 1) + 24, f * FD:(f + 1) * FD] = others[f][0:24, :] * exists
         targets.append(others[f][24:32, :] * exists)
-    high, low = halves(whole[...])
+    high, low = halves(pad[...])
     gh_ref[...] = high
     gl_ref[...] = low
     rows = lax.broadcasted_iota(jnp.int32, (3 * QPAD, FD), 0)
@@ -278,49 +269,44 @@
         pick_ref[:, half * FD:(half + 1) * FD] = (rows == wanted).astype(F32).astype(BF16)
 
 
-def load_kernel(first, mx_ref, my_ref, mz_ref, shown_ref, one_ref, two_ref, residual_ref, fh_ref,
-                fl_ref, wh_ref, wl_ref, expand_ref, *rest):
-    if first:
-        z_ref, flexed_ref, out_ref = rest
-    else:
-        search_ref, applied_ref, z_ref, flexed_ref, out_ref = rest
-    messages = (mx_ref, my_ref, mz_ref)
+def face_sum(x, faces=range(6)):
+    total = None
+    for f in faces:
+        total = face(x, f) if total is None else total + face(x, f)
+    return total
+
+
+def put_payload(out_ref, gathered, extras):
+    lanes = lax.broadcasted_iota(jnp.int32, (CASES, FD), 1)
+    for b in range(6):
+        block = face(gathered, b)
+        if b == 1:
+            for t, value in enumerate(extras):
+                block = jnp.where(lanes == 64 + t, value, block)
+        for c in range(CASES):
+            out_ref[2 * c + b // 3, 4, b % 3:b % 3 + 1, :] = block[c:c + 1, :]
+
+
+def load_kernel(mx_ref, my_ref, mz_ref, shown_ref, one_ref, two_ref, residual_ref, fh_ref,
+                fl_ref, wh_ref, wl_ref, expand_ref, z_ref, flexed_ref, out_ref):
     here, _, there = position()
     across = jnp.concatenate(take_cubes(one_ref, two_ref, slice(0, CASES)), axis=1)
     z = 0.25 * (shown_ref[...] + across) * mask_row(there)
     z_ref[...] = z
-    loads, flexed = apply_dense(z, messages, fh_ref, fl_ref)
+    loads, flexed = apply_dense(z, (mx_ref, my_ref, mz_ref), fh_ref, fl_ref)
     flexed_ref[...] = flexed
-    corner = dot_split(loads, wh_ref, wl_ref)
-    gathered = dot_exact(corner, expand_ref[...])
-
-    def upper_sum(a):
-        return jnp.sum(face(a, 1) + face(a, 3) + face(a, 5), axis=1, keepdims=True)
-
-    sums = [upper_sum(z * residual_ref[...]), jnp.sum(z * flexed, axis=1, keepdims=True)]
-    if not first:
-        sums.append(
-            upper_sum(z * applied_ref[...])
-            + jnp.sum(search_ref[...] * flexed, axis=1, keepdims=True)
-        )
-    lanes = lax.broadcasted_iota(jnp.int32, (CASES, FD), 1)
+    gathered = dot_exact(dot_split(loads, wh_ref, wl_ref), expand_ref[...])
+    norm = jnp.sum(face_sum(z * residual_ref[...], (1, 3, 5)), axis=1, keepdims=True)
+    energy = jnp.sum(face_sum(z * flexed), axis=1, keepdims=True)
     out_ref[...] = jnp.zeros_like(out_ref)
-    for b in range(6):
-        block = face(gathered, b)
-        if b == 1:
-            for t, value in enumerate(sums):
-                block = jnp.where(lanes == 64 + t, value, block)
-        for q in range(4):
-            out_ref[4 * b + q, 4] = block[4 * q:4 * q + 4, :]
+    put_payload(out_ref, gathered, [norm, energy])
     for f, by in enumerate(steps()):
         @pl.when(there[f])
         def _():
             put_rows(out_ref, here + by, face(flexed, f))
 
 
-def layer_kernel(slots_ref, flexed_ref, out_ref):
-    _, layer, there = position()
-    total = jnp.sum(slots_ref[:, 4], axis=0)
+def put_layers(out_ref, total, flexed_ref, layer, there):
     out_ref[...] = jnp.zeros_like(out_ref)
     for i in range(out_ref.shape[0]):
         out_ref[i, 4] = total
@@ -330,15 +316,55 @@
             put_rows(out_ref, layer + by, flexed_ref[:, f * FD:(f + 1) * FD])
 
 
+def layer_kernel(slots_ref, flexed_ref, out_ref):
+    _, layer, there = position()
+    put_layers(out_ref, jnp.sum(slots_ref[:, 4], axis=0), flexed_ref, layer, there)
+
+
 def spread_kernel(slots_ref, out_ref):
     total = jnp.sum(slots_ref[:, 4], axis=0)
     for i in range(out_ref.shape[0]):
         out_ref[i] = total
 
 
+def flex_kernel(mx_ref, my_ref, mz_ref, shown_ref, slots_ref, below_ref, above_ref, fh_ref, fl_ref,
+                search_ref, applied_ref, z_ref, flexed_ref, out_ref, turn):
+    here, layer, there = position()
+    across = []
+    for f, by in enumerate(steps()):
+        across.append(take_rows(slots_ref, jnp.where(there[f], here + by, here)))
+    across += [below_ref[...], above_ref[...]]
+    z = 0.25 * (shown_ref[...] + jnp.concatenate(across, axis=1)) * mask_row(there)
+    z_ref[...] = z
+    _, flexed = apply_dense(z, (mx_ref, my_ref, mz_ref), fh_ref, fl_ref)
+    flexed_ref[...] = flexed
+    turn[...] = jnp.zeros_like(turn)
+    turn[0:CASES, :] = face_sum(z * flexed)
+    turn[CASES:2 * CASES, :] = (
+        face_sum(z * applied_ref[...], (1, 3, 5)) + face_sum(search_ref[...] * flexed)
+    )
+    sums = jnp.sum(turn[...].T, axis=0, keepdims=True)
+    total = jnp.sum(slots_ref[:, 4], axis=0)
+    rows = lax.broadcasted_iota(jnp.int32, total.shape, 0)
+    total = jnp.where(rows == 3, jnp.broadcast_to(sums, total.shape), total)
+    put_layers(out_ref, total, flexed_ref, layer, there)
+
+
+def share_kernel(layers_ref, flexed_ref, out_ref):
+    here, _, there = position()
+    total = jnp.sum(layers_ref[:, 4], axis=0)
+    out_ref[...] = jnp.zeros_like(out_ref)
+    for i in range(out_ref.shape[0]):
+        out_ref[i, 4] = total
+    for f, by in enumerate(steps()):
+        @pl.when(there[f])
+        def _():
+            put_rows(out_ref, here + by, flexed_ref[:, f * FD:(f + 1) * FD])
+
+
 def step_kernel(first, last, total_ref, slots_ref, layers_ref, flexed_ref,
                 z_ref, residual_ref, kh_ref, kl_ref, gh_ref, gl_ref, pick_ref, *rest):
-    rest = list(rest)
+    rest, whole = list(rest[:-1]), rest[-1]
     if not last:
         mx_ref, my_ref, mz_ref, dh_ref, dl_ref = rest[:5]
         rest = rest[5:]
@@ -354,17 +380,24 @@
     mask = mask_row(there)
     applied = (flexed_ref[...] + jnp.concatenate(across, axis=1)) * mask
     search = z_ref[...]
-    blocks = []
-    for b in range(6):
-        blocks.append(jnp.concatenate([total_ref[4 * b + q] for q in range(4)], axis=0))
-    norm = blocks[1][:, 64:65]
-    energy = blocks[1][:, 65:66]
-    load = jnp.concatenate(blocks, axis=1)
+    for c in range(CASES):
+        for b in range(6):
+            slot, row = 2 * c + b // 3, slice(b % 3, b % 3 + 1)
+            whole[c:c + 1, b * FD:(b + 1) * FD] = (
+                total_ref[slot, row, :] if first else total_ref[slot, 4, row, :]
+            )
+    load = whole[...]
+    norm = load[:, FD + 64:FD + 65]
+    if first:
+        energy = load[:, FD + 65:FD + 66]
+    else:
+        sums = jnp.sum(total_ref[:, 4], axis=0)[3:4, :]
+        sums = jnp.broadcast_to(sums, (FD, FD)).T
+        energy, cross = sums[0:CASES, 0:1], sums[CASES:2 * CASES, 0:1]
     lanes = lax.broadcasted_iota(jnp.int32, load.shape, 1) % QPAD
     load = jnp.where(lanes < 192, load, 0.0)
     if not first:
         beta = norm / scale_ref[:, 0:1]
-        cross = blocks[1][:, 66:67]
         energy = energy + beta * cross + beta * beta * scale_ref[:, 1:2]
         applied = applied + beta * applied_ref[...]
         search = search + beta * search_ref[...]
@@ -382,7 +415,7 @@
             left_ref[d] = face(residual, 2 * d + 1)
         return
     search_out, applied_out, load_out, scale_out, iterate_out, residual_out, shown_ref = rest[:7]
-    first_ref, second_ref = rest[7:]
+    out_ref, down_ref, up_ref = rest[7:]
     search_out[...] = search
     applied_out[...] = applied
     load_out[...] = load
@@ -394,7 +427,21 @@
         iterate_out[d] = moved_face if first else iterate_ref[d] + moved_face
     _, shown = apply_dense(residual, (mx_ref, my_ref, mz_ref), dh_ref, dl_ref)
     shown_ref[...] = shown
-    put_cubes(first_ref, second_ref, lambda f: face(shown, f))
+    down_ref[...] = face(shown, 4)
+    up_ref[...] = face(shown, 5)
+    share = 0.25 * shown * mask
+    high, low = halves(share)
+    both = dot_across(jnp.concatenate([high, low], 0), gh_ref[...])
+    corner = both[:CASES] + both[CASES:] + dot_across(high, gl_ref[...])
+    high, low = halves(corner)
+    both = dot_across(jnp.concatenate([high, low], 0), pick_ref[...])
+    next_norm = jnp.sum(face_sum(share * residual), axis=1, keepdims=True)
+    out_ref[...] = jnp.zeros_like(out_ref)
+    put_payload(out_ref, both[:CASES] + both[CASES:], [next_norm])
+    for f, by in enumerate(steps()):
+        @pl.when(there[f])
+        def _():
+            put_rows(out_ref, here + by, face(shown, f))
 
 
 def passed_along(shard, axis, by):
@@ -438,55 +485,69 @@
     )
     messages = [passed_along(m, a, 1) for m, a in zip(messages, AXES)]
     blocks = [b.reshape(6, FD, FD) for b in (dirichlet_diag, dirichlet_couple, flex_diag, flex_couple)]
-    sources = blocks + [coarse_inverse, coupling]
-    *dense, target = call(
-        setup_kernel,
-        [(square, BF16)] * 6 + [((WIDE, FD), BF16)] * 2 + [((FD, WIDE), BF16), ((8, FD), F32)],
-        [face_pairs, coarse_ids] + sources,
-        specs=[SMEM] * 2 + [pl.BlockSpec(memory_space=pltpu.HBM)] * 6,
-        scratch=[pltpu.VMEM(source.shape, F32) for source in sources]
-        + [pltpu.VMEM((FD, WIDE), F32), pltpu.VMEM(square, F32), pltpu.SemaphoreType.DMA((6,))],
-    )
-    dirichlet, flex, inverse, weights = dense[0:2], dense[2:4], dense[4:6], dense[6:9]
+    *dirichlet, target = call(
+        dense_kernel, [(square, BF16)] * 2 + [((8, FD), F32)],
+        [face_pairs, coarse_ids] + blocks[:2], specs=[SMEM] * 2,
+    )
     residual, shown, own, one, two = call(
         start_kernel,
         [(wide, F32), (wide, F32), ((24, WIDE), F32)] + [((8, long, FD), F32)] * 2,
         [rhs, *messages, *dirichlet, coupling, target],
     )
-    others = across_faces(one, two)
-    joint = call(
-        joint_kernel,
-        [((QPAD, WIDE), BF16), ((QPAD, WIDE), BF16), ((3 * QPAD, QPAD), BF16)],
-        [own, target, *others],
-        scratch=[pltpu.VMEM((QPAD, WIDE), F32)],
-    )
-    joint, others = lax.optimization_barrier((joint, others))
+    one, two = across_faces(one, two)
+    dense = call(
+        setup_kernel,
+        [(square, BF16)] * 4 + [((WIDE, FD), BF16)] * 2
+        + [((FD, WIDE), BF16), ((QPAD, WIDE), BF16), ((QPAD, WIDE), BF16), ((3 * QPAD, QPAD), BF16)],
+        [face_pairs, coarse_ids] + blocks[2:] + [coarse_inverse, coupling, own, target, one, two],
+        specs=[SMEM] * 2,
+        scratch=[pltpu.VMEM((QPAD, WIDE), F32), pltpu.VMEM(square, F32)],
+    )
+    flex, inverse, weights, joint = dense[0:2], dense[2:4], dense[4:7], dense[7:10]
+    stacked = (plane, 5, 4, FD)
 
     kept = []
     for iteration in range(ITERS):
         first, last = iteration == 0, iteration + 1 == ITERS
-        z, flexed, out = call(
-            functools.partial(load_kernel, first),
-            [(wide, F32), (wide, F32), ((plane, 5, 4, FD), F32)],
-            [*messages, shown, *others, residual, *flex, *weights, *kept[:2]],
-        )
-        slots = swapped(out, PLANE)
-        (layers,) = call(layer_kernel, [((gz, 5, 4, FD), F32)], [slots, flexed])
-        layers = swapped(layers, "gz")
-        (total,) = call(spread_kernel, [((plane, 4, FD), F32)], [layers])
-        total = swapped(total, PLANE)
+        if first:
+            z, flexed, slots = call(
+                load_kernel,
+                [(wide, F32), (wide, F32), (stacked, F32)],
+                [*messages, shown, one, two, residual, *flex, *weights],
+            )
+            slots = swapped(slots, PLANE)
+            (layers,) = call(layer_kernel, [((gz, 5, 4, FD), F32)], [slots, flexed])
+            layers = swapped(layers, "gz")
+            (total,) = call(spread_kernel, [((plane, 4, FD), F32)], [layers])
+            total = swapped(total, PLANE)
+        else:
+            z, flexed, layers = call(
+                flex_kernel,
+                [(wide, F32), (wide, F32), ((gz, 5, 4, FD), F32)],
+                [*messages, shown, slots, below, above, *flex, *kept[:2]],
+                scratch=[pltpu.VMEM((FD, FD), F32)],
+            )
+            layers = swapped(layers, "gz")
+            (total,) = call(share_kernel, [(stacked, F32)], [layers, flexed])
+            slots = total = swapped(total, PLANE)
         common = [total, slots, layers, flexed, z, residual, *inverse, *joint]
         kernel = functools.partial(step_kernel, first, last)
+        scratch = [pltpu.VMEM(wide, F32)]
         if last:
-            multipliers, left = call(kernel, [((3, CASES, FD), F32)] * 2, common + kept)
+            multipliers, left = call(
+                kernel, [((3, CASES, FD), F32)] * 2, common + kept, scratch=scratch
+            )
             break
-        *kept, residual, shown, one, two = call(
+        *kept, residual, shown, slots, down, up = call(
             kernel,
             [(wide, F32)] * 3 + [((CASES, FD), F32), ((3, CASES, FD), F32), (wide, F32), (wide, F32)]
-            + [((8, CASES, FD), F32)] * 2,
-            common + [*messages, *dirichlet] + kept,
+            + [(stacked, F32)] + [((CASES, FD), F32)] * 2,
+            common + [*messages, *dirichlet] + kept, scratch=scratch,
         )
-        others = across_faces(one, two)
+        below = passed_along(up, "gz", 1)
+        above = passed_along(down, "gz", -1)
+        slots, below, above = lax.optimization_barrier((slots, below, above))
+        slots = swapped(slots, PLANE)
     return multipliers.reshape(jump_rhs.shape), left.reshape(jump_rhs.shape)
 
 

time: 243 us -> 222 us (0.914)
  blocking collectives: 209 us -> 176 us
  starting transfers between devices: 11.3 us -> 19.5 us
  waiting for transfers between devices: 0.01 us -> 6.18 us
  local copies, waits for them, and re-layouts: 9.08 us -> 6.46 us
    all_to_all x3 -> x1, blocking collectives: 34.8 us -> 15.5 us  [across_faces(): lax.all_to_all(two, AXES, 0, 0, axis_index_groups=cube_groups(1))]
    all_to_all x3 -> x1, blocking collectives: 24.2 us -> 9.75 us  [across_faces(): one = lax.all_to_all(one, AXES, 0, 0, axis_index_groups=cube_groups(0))]
    ppermute x3 -> x7, starting transfers between devices: 11.3 us -> 19.5 us  [passed_along(): return lax.ppermute(shard, axis, pairs)]
    ppermute x3 -> x7, waiting for transfers between devices: 0.01 us -> 6.18 us  [passed_along(): return lax.ppermute(shard, axis, pairs)]
    unnamed x20 -> x22, local copies, waits for them, and re-layouts: 9.08 us -> 6.46 us
    pallas_call x16 -> x14, Pallas kernels: 11.9 us -> 12.5 us  [call(): pl.pallas_call(kernel, out_shape=[jax.ShapeDtypeStruct(shape, dtype) for...]
  transfers between devices with their start and end apart: 3 -> 7, of which waited for: 0 -> 2; matrix products, arithmetic and copies ran while one was open for 0% -> 0% of each run, Pallas kernels for 1% -> 0%
where the time goes in v5:
time: 222 us; the launch traced here: 221 us
  blocking collectives  176 us (79%)
  starting transfers between devices  19.5 us (9%)
  Pallas kernels  12.5 us (6%)
  local copies, waits for them, and re-layouts  6.46 us (3%)
  waiting for transfers between devices  6.18 us (3%)
    all_to_all x9, blocking collectives, swapped(): return lax.all_to_all(slots, axes, 0, 0)  151 us
    ppermute x7, starting transfers between devices, passed_along(): return lax.ppermute(shard, axis, pairs)  19.5 us
    all_to_all x1, blocking collectives, across_faces(): lax.all_to_all(two, AXES, 0, 0, axis_index_groups=cube_groups(1))  15.5 us
    pallas_call x14, Pallas kernels, call(): pl.pallas_call(kernel, out_shape=[jax.ShapeDtypeStruct(shape, dtype) for...  12.5 us
    all_to_all x1, blocking collectives, across_faces(): one = lax.all_to_all(one, AXES, 0, 0, axis_index_groups=cube_groups(0))  9.75 us
    unnamed x22, local copies, waits for them, and re-layouts  6.46 us
    ppermute x7, waiting for transfers between devices, passed_along(): return lax.ppermute(shard, axis, pairs)  6.18 us
  transfers between devices with their start and end apart: 7, of which 2 were waited for; matrix products, arithmetic and copies ran while one was open for 0% of the time, Pallas kernels for 0%

profile of v5, /device:TPU:1, one launch (start us, length us, event | category | flops | bytes accessed | tf_op | source)
XLA Modules:
  0.0 221.2 jit_solution(8648617179171388167)
XLA Ops:
  0.6 0.7 copy.12.partner_ref
  1.3 0.0 copy-start.7
  1.3 0.7 copy-done.7
  2.0 0.2 shard_map.113
  2.2 4.6 %collective-permute-start = (f32[24,128]{1,0:T(8,128)S(1)}, f32[24,128]{1,0:T(8,128)S(1)}, u32[]{:S(2)}, u32[]{:S(2)}) collective-permute-start(f32[24,128]{1,0:T(8,128)S(1)} %get-tuple-element.62), channel_id=1, source_target_pairs={{0,64},{64,128},{128,192},{192,256},{256,320},{320,384},{384,448},... | collective-permute-start | bytes 36872 | tf_op jit(solution)/shard_map/ppermute | solution.py:450
  6.8 3.1 %collective-permute-start.1 = (f32[24,128]{1,0:T(8,128)S(1)}, f32[24,128]{1,0:T(8,128)S(1)}, u32[]{:S(2)}, u32[]{:S(2)}) collective-permute-start(f32[24,128]{1,0:T(8,128)S(1)} %get-tuple-element.63), channel_id=1, source_target_pairs={{0,16},{16,32},{32,48},{1,17},{17,33},{33,49},{2,18},{18,34},{34,5... | collective-permute-start | bytes 36872 | tf_op jit(solution)/shard_map/ppermute | solution.py:450
  10.0 3.5 %collective-permute-start.2 = (f32[24,128]{1,0:T(8,128)S(1)}, f32[24,128]{1,0:T(8,128)S(1)}, u32[]{:S(2)}, u32[]{:S(2)}) collective-permute-start(f32[24,128]{1,0:T(8,128)S(1)} %get-tuple-element.64), channel_id=1, source_target_pairs={{0,1},{1,2},{2,3},{3,4},{4,5},{5,6},{6,7},{7,8},{8,9},{9,10},{10,1... | collective-permute-start | bytes 36872 | tf_op jit(solution)/shard_map/ppermute | solution.py:450
  13.5 0.8 copy.13.pairs
  14.3 0.0 copy-start.3
  14.3 1.0 copy-done.3
  15.3 0.0 copy-start.4
  15.3 1.0 copy-done.4
  16.3 0.0 copy-start.9
  16.3 0.7 copy-done.9
  16.9 1.0 shard_map.114
  17.9 0.0 collective-permute-done.mx_ref.rest_0_
  18.0 0.0 collective-permute-done.1.my_ref.rest_1_
  18.0 0.0 collective-permute-done.2.mz_ref.rest_2_
  18.0 0.0 copy-start.5
  18.0 0.9 copy-done.5
  18.9 0.0 copy-start.8
  18.9 0.7 copy-done.8
  19.6 0.0 copy-start
  19.6 0.0 copy-start.1
  19.6 0.0 copy-start.2
  19.6 0.0 copy-start.6
  19.6 0.6 shard_map.115
  20.2 9.7 %all_to_all.55.first_ref.one_ref = f32[8,48,128]{2,1,0:T(8,128)S(1)} all-to-all(f32[8,48,128]{2,1,0:T(8,128)S(1)} %get-tuple-element.69), channel_id=1, replica_groups={{0,1,16,17,64,65,80,81},{2,3,18,19,66,67,82,83},{4,5,20,21,68,69,84,85}..., dimensions={0} | all-to-all | bytes 393216 | tf_op jit(solution)/shard_map/all_to_all | solution.py:458
  29.9 15.5 %all_to_all.56.second_ref.two_ref = f32[8,48,128]{2,1,0:T(8,128)S(1)} all-to-all(f32[8,48,128]{2,1,0:T(8,128)S(1)} %get-tuple-element.72), channel_id=1, replica_groups={{81,82,97,98,145,146,161,162},{83,84,99,100,147,148,163,164},{85,86,101..., dimensions={0} | all-to-all | bytes 393216 | tf_op jit(solution)/shard_map/all_to_all | solution.py:460
  45.4 0.0 copy-done
  45.4 0.0 copy-done.1
  45.4 0.0 copy-done.2
  45.4 0.0 copy-done.6
  45.4 2.0 shard_map.116
  47.4 0.8 shard_map.117
  48.2 15.8 %all_to_all.57.slots_ref = f32[32,5,4,128]{3,2,1,0:T(4,128)S(1)} all-to-all(f32[32,5,4,128]{3,2,1,0:T(4,128)S(1)} %get-tuple-element.80), channel_id=1, replica_groups=mesh['gx'=8,'gy'=4,'gz'=16] {'gx','gy'}, dimensions={0} | all-to-all | bytes 655360 | tf_op jit(solution)/shard_map/all_to_all | solution.py:454
  64.1 21.0 %all_to_all.58.slots_ref.layers_ref = f32[16,5,4,128]{3,2,1,0:T(4,128)S(1)} all-to-all(f32[16,5,4,128]{3,2,1,0:T(4,128)S(1)} %shard_map.118), channel_id=1, replica_groups=mesh['gx'=8,'gy'=4,'gz'=16] {'gz'}, dimensions={0} | all-to-all | bytes 327680 | tf_op jit(solution)/shard_map/all_to_all | solution.py:454
  85.1 14.5 %all_to_all.59.total_ref = f32[32,4,128]{2,1,0:T(4,128)S(1)} all-to-all(f32[32,4,128]{2,1,0:T(4,128)S(1)} %shard_map.119), channel_id=1, replica_groups=mesh['gx'=8,'gy'=4,'gz'=16] {'gx','gy'}, dimensions={0} | all-to-all | bytes 131072 | tf_op jit(solution)/shard_map/all_to_all | solution.py:454
  99.6 2.3 %shard_map.120 = (f32[16,768]{1,0:T(8,128)S(1)}, f32[16,768]{1,0:T(8,128)S(1)}, f32[16,768]{1,0:T(8,128)S(1)}, f32[16,128]{1,0:T(8,128)S(1)}, f32[3,16,128]{2,1,...) custom-call(f32[32,4,128]{2,1,0:T(4,128)S(1)} %all_to_all.59.total_r, ...), custom_call_target="tpu_custom_call" | custom-call | tf_op jit(solution)/shard_map/pallas_call | solution.py:25
  101.9 2.8 %collective-permute-start.3 = (f32[16,128]{1,0:T(8,128)S(1)}, f32[16,128]{1,0:T(8,128)S(1)}, u32[]{:S(2)}, u32[]{:S(2)}) collective-permute-start(f32[16,128]{1,0:T(8,128)S(1)} %get-tuple-element.90), channel_id=1, source_target_pairs={{0,1},{1,2},{2,3},{3,4},{4,5},{5,6},{6,7},{7,8},{8,9},{9,10},{10,1... | collective-permute-start | bytes 24584 | tf_op jit(solution)/shard_map/ppermute | solution.py:450
  104.7 1.3 collective-permute-start.4
  106.0 0.0 collective-permute-done.3.below_ref
  106.0 3.1 %collective-permute-done.4.above_ref = f32[16,128]{1,0:T(8,128)S(1)} collective-permute-done((f32[16,128]{1,0:T(8,128)S(1)}, f32[16,128]{1,0:T(8,128)S(1)}, u32[]{:S(2)}, u32[]{:S(2)}) %collective-permute-start.4) | collective-permute-done | bytes 8224 | tf_op jit(solution)/shard_map/ppermute | solution.py:450
  109.1 14.6 %all_to_all.60.slots_ref = f32[32,5,4,128]{3,2,1,0:T(4,128)S(1)} all-to-all(f32[32,5,4,128]{3,2,1,0:T(4,128)S(1)} %get-tuple-element.92), channel_id=1, replica_groups=mesh['gx'=8,'gy'=4,'gz'=16] {'gx','gy'}, dimensions={0} | all-to-all | bytes 655360 | tf_op jit(solution)/shard_map/all_to_all | solution.py:454
  123.7 0.7 shard_map.121
  124.4 18.1 %all_to_all.61.layers_ref = f32[16,5,4,128]{3,2,1,0:T(4,128)S(1)} all-to-all(f32[16,5,4,128]{3,2,1,0:T(4,128)S(1)} %get-tuple-element.97), channel_id=1, replica_groups=mesh['gx'=8,'gy'=4,'gz'=16] {'gz'}, dimensions={0} | all-to-all | bytes 327680 | tf_op jit(solution)/shard_map/all_to_all | solution.py:454
  142.5 0.1 shard_map.122
  142.6 16.8 %all_to_all.62.total_ref.slots_ref = f32[32,5,4,128]{3,2,1,0:T(4,128)S(1)} all-to-all(f32[32,5,4,128]{3,2,1,0:T(4,128)S(1)} %shard_map.122), channel_id=1, replica_groups=mesh['gx'=8,'gy'=4,'gz'=16] {'gx','gy'}, dimensions={0} | all-to-all | bytes 655360 | tf_op jit(solution)/shard_map/all_to_all | solution.py:454
  159.4 2.4 %shard_map.123 = (f32[16,768]{1,0:T(8,128)S(1)}, f32[16,768]{1,0:T(8,128)S(1)}, f32[16,768]{1,0:T(8,128)S(1)}, f32[16,128]{1,0:T(8,128)S(1)}, f32[3,16,128]{2,1,...) custom-call(f32[32,5,4,128]{3,2,1,0:T(4,128)S(1)} %all_to_all.62.tot, ...), custom_call_target="tpu_custom_call" | custom-call | tf_op jit(solution)/shard_map/pallas_call | solution.py:25
  161.7 2.8 %collective-permute-start.5 = (f32[16,128]{1,0:T(8,128)S(1)}, f32[16,128]{1,0:T(8,128)S(1)}, u32[]{:S(2)}, u32[]{:S(2)}) collective-permute-start(f32[16,128]{1,0:T(8,128)S(1)} %get-tuple-element.106), channel_id=1, source_target_pairs={{0,1},{1,2},{2,3},{3,4},{4,5},{5,6},{6,7},{7,8},{8,9},{9,10},{10,1... | collective-permute-start | bytes 24584 | tf_op jit(solution)/shard_map/ppermute | solution.py:450
  164.6 1.3 collective-permute-start.6
  165.9 0.0 collective-permute-done.5.below_ref
  165.9 3.1 %collective-permute-done.6.above_ref = f32[16,128]{1,0:T(8,128)S(1)} collective-permute-done((f32[16,128]{1,0:T(8,128)S(1)}, f32[16,128]{1,0:T(8,128)S(1)}, u32[]{:S(2)}, u32[]{:S(2)}) %collective-permute-start.6) | collective-permute-done | bytes 8224 | tf_op jit(solution)/shard_map/ppermute | solution.py:450
  169.0 14.9 %all_to_all.63.slots_ref = f32[32,5,4,128]{3,2,1,0:T(4,128)S(1)} all-to-all(f32[32,5,4,128]{3,2,1,0:T(4,128)S(1)} %get-tuple-element.108), channel_id=1, replica_groups=mesh['gx'=8,'gy'=4,'gz'=16] {'gx','gy'}, dimensions={0} | all-to-all | bytes 655360 | tf_op jit(solution)/shard_map/all_to_all | solution.py:454
  183.9 0.7 shard_map.124
  184.6 18.1 %all_to_all.64.layers_ref = f32[16,5,4,128]{3,2,1,0:T(4,128)S(1)} all-to-all(f32[16,5,4,128]{3,2,1,0:T(4,128)S(1)} %get-tuple-element.113), channel_id=1, replica_groups=mesh['gx'=8,'gy'=4,'gz'=16] {'gz'}, dimensions={0} | all-to-all | bytes 327680 | tf_op jit(solution)/shard_map/all_to_all | solution.py:454
  202.7 0.1 shard_map.125
  202.8 16.7 %all_to_all.65.total_ref.slots_ref = f32[32,5,4,128]{3,2,1,0:T(4,128)S(1)} all-to-all(f32[32,5,4,128]{3,2,1,0:T(4,128)S(1)} %shard_map.125), channel_id=1, replica_groups=mesh['gx'=8,'gy'=4,'gz'=16] {'gx','gy'}, dimensions={0} | all-to-all | bytes 655360 | tf_op jit(solution)/shard_map/all_to_all | solution.py:454
  219.5 1.7 shard_map.126
  (2 shorter events, 0.1 us)
Async XLA Ops:
  1.3 0.7 copy-start.7
  2.2 15.7 %collective-permute-start = (f32[24,128]{1,0:T(8,128)S(1)}, f32[24,128]{1,0:T(8,128)S(1)}, u32[]{:S(2)}, u32[]{:S(2)}) collective-permute-start(f32[24,128]{1,0:T(8,128)S(1)} %get-tuple-element.62), channel_id=1, source_target_pairs={{0,64},{64,128},{128,192},{192,256},{256,320},{320,384},{384,448},... | collective-permute-start | bytes 36872 | tf_op jit(solution)/shard_map/ppermute | solution.py:450
  6.8 11.1 %collective-permute-start.1 = (f32[24,128]{1,0:T(8,128)S(1)}, f32[24,128]{1,0:T(8,128)S(1)}, u32[]{:S(2)}, u32[]{:S(2)}) collective-permute-start(f32[24,128]{1,0:T(8,128)S(1)} %get-tuple-element.63), channel_id=1, source_target_pairs={{0,16},{16,32},{32,48},{1,17},{17,33},{33,49},{2,18},{18,34},{34,5... | collective-permute-start | bytes 36872 | tf_op jit(solution)/shard_map/ppermute | solution.py:450
  10.0 8.0 %collective-permute-start.2 = (f32[24,128]{1,0:T(8,128)S(1)}, f32[24,128]{1,0:T(8,128)S(1)}, u32[]{:S(2)}, u32[]{:S(2)}) collective-permute-start(f32[24,128]{1,0:T(8,128)S(1)} %get-tuple-element.64), channel_id=1, source_target_pairs={{0,1},{1,2},{2,3},{3,4},{4,5},{5,6},{6,7},{7,8},{8,9},{9,10},{10,1... | collective-permute-start | bytes 36872 | tf_op jit(solution)/shard_map/ppermute | solution.py:450
  14.3 1.0 copy-start.3
  15.3 1.0 copy-start.4
  16.3 0.7 copy-start.9
  18.0 0.9 copy-start.5
  18.9 0.7 copy-start.8
  19.6 25.8 %copy-start = (f32[576,576]{1,0:T(8,128)S(1)}, f32[576,576]{1,0:T(8,128)}, u32[]{:S(2)}) copy-start(f32[576,576]{1,0:T(8,128)} %inverse_ref.1) | copy-start | bytes 3981316
  19.6 25.8 %copy-start.1 = (f32[1,1,1,6,128,128]{5,4,3,2,1,0:T(8,128)S(1)}, f32[1,1,1,6,128,128]{5,4,3,2,1,0:T(8,128)}, u32[]{:S(2)}) copy-start(f32[1,1,1,6,128,128]{5,4,3,2,1,0:T(8,128)} %param.11) | copy-start | bytes 1179652
  19.6 25.8 %copy-start.2 = (f32[1,1,1,6,128,128]{5,4,3,2,1,0:T(8,128)S(1)}, f32[1,1,1,6,128,128]{5,4,3,2,1,0:T(8,128)}, u32[]{:S(2)}) copy-start(f32[1,1,1,6,128,128]{5,4,3,2,1,0:T(8,128)} %param.12) | copy-start | bytes 1179652
  19.6 25.8 %copy-start.6 = (f32[1,1,1,24,768]{4,3,2,1,0:T(8,128)S(1)}, f32[1,1,1,24,768]{4,3,2,1,0:T(8,128)}, u32[]{:S(2)}) copy-start(f32[1,1,1,24,768]{4,3,2,1,0:T(8,128)} %param.16) | copy-start | bytes 221188
  101.9 4.2 %collective-permute-start.3 = (f32[16,128]{1,0:T(8,128)S(1)}, f32[16,128]{1,0:T(8,128)S(1)}, u32[]{:S(2)}, u32[]{:S(2)}) collective-permute-start(f32[16,128]{1,0:T(8,128)S(1)} %get-tuple-element.90), channel_id=1, source_target_pairs={{0,1},{1,2},{2,3},{3,4},{4,5},{5,6},{6,7},{7,8},{8,9},{9,10},{10,1... | collective-permute-start | bytes 24584 | tf_op jit(solution)/shard_map/ppermute | solution.py:450
  104.7 4.4 %collective-permute-start.4 = (f32[16,128]{1,0:T(8,128)S(1)}, f32[16,128]{1,0:T(8,128)S(1)}, u32[]{:S(2)}, u32[]{:S(2)}) collective-permute-start(f32[16,128]{1,0:T(8,128)S(1)} %get-tuple-element.91), channel_id=1, source_target_pairs={{1,0},{2,1},{3,2},{4,3},{5,4},{6,5},{7,6},{8,7},{9,8},{10,9},{11,1... | collective-permute-start | bytes 24584 | tf_op jit(solution)/shard_map/ppermute | solution.py:450
  161.7 4.2 %collective-permute-start.5 = (f32[16,128]{1,0:T(8,128)S(1)}, f32[16,128]{1,0:T(8,128)S(1)}, u32[]{:S(2)}, u32[]{:S(2)}) collective-permute-start(f32[16,128]{1,0:T(8,128)S(1)} %get-tuple-element.106), channel_id=1, source_target_pairs={{0,1},{1,2},{2,3},{3,4},{4,5},{5,6},{6,7},{7,8},{8,9},{9,10},{10,1... | collective-permute-start | bytes 24584 | tf_op jit(solution)/shard_map/ppermute | solution.py:450
  164.6 4.4 %collective-permute-start.6 = (f32[16,128]{1,0:T(8,128)S(1)}, f32[16,128]{1,0:T(8,128)S(1)}, u32[]{:S(2)}, u32[]{:S(2)}) collective-permute-start(f32[16,128]{1,0:T(8,128)S(1)} %get-tuple-element.107), channel_id=1, source_target_pairs={{1,0},{2,1},{3,2},{4,3},{5,4},{6,5},{7,6},{8,7},{9,8},{10,9},{11,1... | collective-permute-start | bytes 24584 | tf_op jit(solution)/shard_map/ppermute | solution.py:450

commit v6 on v5

v6 whole, which is shorter than its diff:
```python
import functools

import jax
import jax.numpy as jnp
from jax import lax
from jax.experimental import pallas as pl
from jax.experimental.pallas import tpu as pltpu
from jax.sharding import PartitionSpec as P

ITERS = 3
CASES = 16
FD = 128
WIDE = 6 * FD
QPAD = 256
SUBS = 32
AXES = ("gx", "gy", "gz")
PLANE = ("gx", "gy")
F32 = jnp.float32
BF16 = jnp.bfloat16
VMEM = pl.BlockSpec(memory_space=pltpu.VMEM)
SMEM = pl.BlockSpec(memory_space=pltpu.SMEM)


def call(kernel, outs, args, specs=(), scratch=()):
    return pl.pallas_call(
        kernel,
        out_shape=[jax.ShapeDtypeStruct(shape, dtype) for shape, dtype in outs],
        in_specs=list(specs) + [VMEM] * (len(args) - len(specs)),
        out_specs=[VMEM] * len(outs),
        scratch_shapes=list(scratch),
        compiler_params=pltpu.CompilerParams(vmem_limit_bytes=40 * 1024 * 1024),
    )(*args)


def halves(x):
    high = x.astype(BF16)
    return high, (x - high.astype(F32)).astype(BF16)


def dot_exact(x, selector):
    rows = x.shape[0]
    high, low = halves(x)
    both = jnp.dot(jnp.concatenate([high, low], 0), selector, preferred_element_type=F32)
    return both[:rows] + both[rows:]


def dot_across(x, matrix):
    return lax.dot_general(x, matrix, (((1,), (1,)), ((), ())), preferred_element_type=F32)


def dot_split(x, high_ref, low_ref):
    rows = x.shape[0]
    high, low = halves(x)
    both = jnp.dot(jnp.concatenate([high, low], 0), high_ref[...], preferred_element_type=F32)
    rest = jnp.dot(high, low_ref[...], preferred_element_type=F32)
    return both[:rows] + both[rows:] + rest


def face(x, f):
    return x[:, f * FD:(f + 1) * FD]


def take(x, row):
    index = jnp.broadcast_to(row.astype(jnp.int32), x.shape)
    return jnp.take_along_axis(x, index, axis=1, mode="promise_in_bounds")


def lower_changed(x, rows):
    parts = []
    for d in range(3):
        parts.append(-take(face(x, 2 * d), rows[d]))
        parts.append(face(x, 2 * d + 1))
    return jnp.concatenate(parts, axis=1)


def partner_rows(messages):
    return [m[CASES:CASES + 1, :] for m in messages]


def inverse_rows(messages):
    return [m[CASES + 1:CASES + 2, :] for m in messages]


def apply_dense(field, messages, high_ref, low_ref):
    loads = lower_changed(field, inverse_rows(messages))
    return loads, lower_changed(dot_split(loads, high_ref, low_ref), partner_rows(messages))


def position():
    gy = lax.axis_size("gy")
    places = [(lax.axis_index(a), lax.axis_size(a)) for a in ("gx", "gy", "gz")]
    there = []
    for place, size in places:
        there += [place > 0, place < size - 1]
    return places[0][0] * gy + places[1][0], places[2][0], there


def steps():
    gy = lax.axis_size("gy")
    return (-gy, gy, -1, 1)


def mask_row(there):
    return jnp.concatenate([jnp.full((1, FD), t.astype(F32)) for t in there], axis=1)


def put_rows(slots_ref, spot, rows):
    for q in range(4):
        slots_ref[spot, q] = rows[4 * q:4 * q + 4, :]


def take_rows(slots_ref, spot):
    return jnp.concatenate([slots_ref[spot, q] for q in range(4)], axis=0)


def target_rows(ids):
    lanes = lax.broadcasted_iota(jnp.int32, (8, FD), 1) % SUBS
    target = jnp.full((8, FD), -1, jnp.int32)
    for r in range(24):
        target = jnp.where(lanes == r, (r % 3) * QPAD + ids[0, 0, 0, r // 3], target)
    return target.astype(F32)


def prep_kernel(ids, rhs_ref, partner_ref, coupling_ref, *message_refs):
    _, _, there = position()
    target = target_rows(ids)
    for d in range(3):
        up_ref, down_ref = message_refs[d], message_refs[3 + d]
        row = partner_ref[0, 0, 0, d:d + 1, :]
        up_ref[0:CASES, :] = rhs_ref[d] * there[2 * d + 1].astype(F32)
        wanted = lax.broadcasted_iota(jnp.int32, (FD, FD), 0)
        hits = (wanted == jnp.broadcast_to(row, (FD, FD))).astype(F32).astype(BF16)
        count = lax.broadcasted_iota(jnp.int32, (16, FD), 1).astype(F32).astype(BF16)
        up_ref[CASES:CASES + 8, :] = jnp.zeros((8, FD), F32)
        up_ref[CASES:CASES + 1, :] = row.astype(F32)
        up_ref[CASES + 1:CASES + 2, :] = dot_across(count, hits)[0:1, :]
        up_ref[24:48, :] = coupling_ref[:, (2 * d + 1) * FD:(2 * d + 2) * FD]
        up_ref[48:56, :] = target
        down_ref[0:24, :] = coupling_ref[:, 2 * d * FD:(2 * d + 1) * FD]
        down_ref[24:32, :] = target


def put_dense(pairs, diag_ref, couple_ref, high_ref, low_ref):
    high_ref[...] = jnp.zeros_like(high_ref)
    low_ref[...] = jnp.zeros_like(low_ref)

    def put(rows, cols, block):
        high, low = halves(block)
        high_ref[pl.ds(rows, FD), pl.ds(cols, FD)] = high
        low_ref[pl.ds(rows, FD), pl.ds(cols, FD)] = low

    for f in range(6):
        put(f * FD, f * FD, diag_ref[f])
    for k in range(6):
        first = pl.multiple_of(pairs[0, 0, 0, k, 0] * FD, FD)
        second = pl.multiple_of(pairs[0, 0, 0, k, 1] * FD, FD)
        block = couple_ref[k]
        put(second, first, block)
        put(first, second, block.T)


def dense_kernel(pairs, diag_ref, couple_ref, high_ref, low_ref):
    put_dense(pairs, diag_ref, couple_ref, high_ref, low_ref)


def start_kernel(ux_ref, uy_ref, uz_ref, mx_ref, my_ref, mz_ref, nx_ref, ny_ref, nz_ref, dh_ref,
                 dl_ref, coupling_ref, field_ref, shown_ref, gh_ref, gl_ref, pick_ref, down_ref,
                 up_ref, pad):
    _, _, there = position()
    own, messages, above = (ux_ref, uy_ref, uz_ref), (mx_ref, my_ref, mz_ref), (nx_ref, ny_ref, nz_ref)
    parts = []
    for d in range(3):
        parts += [messages[d][0:CASES, :], own[d][0:CASES, :]]
    field = jnp.concatenate(parts, axis=1)
    field_ref[...] = field
    _, shown = apply_dense(field, messages, dh_ref, dl_ref)
    shown_ref[...] = shown
    down_ref[...] = face(shown, 4)
    up_ref[...] = face(shown, 5)
    pad[...] = jnp.zeros_like(pad)
    pad[0:24, :] = lower_changed(coupling_ref[...], partner_rows(messages))
    targets = [own[0][48:56, :]]
    for d in range(3):
        row = own[d][CASES:CASES + 1, :]
        sides = (
            (messages[d][24:48, :], messages[d][48:56, :]),
            (-take(above[d][0:24, :], row), above[d][24:32, :]),
        )
        for f, (rows, target) in zip((2 * d, 2 * d + 1), sides):
            exists = there[f].astype(F32)
            pad[SUBS * (f + 1):SUBS * (f + 1) + 24, f * FD:(f + 1) * FD] = rows * exists
            targets.append(target * exists)
    high, low = halves(pad[...])
    gh_ref[...] = high
    gl_ref[...] = low
    lanes = lax.broadcasted_iota(jnp.int32, (8, FD), 1)
    rows = lax.broadcasted_iota(jnp.int32, (3 * QPAD, FD), 0)
    for half in range(2):
        wanted = jnp.full((8, FD), -1.0, F32)
        for n in range(4 * half, min(4 * half + 4, 7)):
            wanted = jnp.where(lanes // SUBS == n % 4, targets[n], wanted)
        wanted = jnp.broadcast_to(wanted[0:1, :].astype(jnp.int32), (3 * QPAD, FD))
        pick_ref[:, half * FD:(half + 1) * FD] = (rows == wanted).astype(F32).astype(BF16)


def late_kernel(pairs, diag_ref, couple_ref, inverse_ref, _, fh_ref, fl_ref, kh_ref, kl_ref, square):
    put_dense(pairs, diag_ref, couple_ref, fh_ref, fl_ref)
    square[...] = jnp.zeros_like(square)
    for p in range(3):
        for q in range(3):
            square[p * QPAD:p * QPAD + 192, q * QPAD:q * QPAD + 192] = inverse_ref[
                p * 192:(p + 1) * 192, q * 192:(q + 1) * 192
            ]
    high, low = halves(square[...])
    kh_ref[...] = high
    kl_ref[...] = low


def face_sum(x, faces=range(6)):
    total = None
    for f in faces:
        total = face(x, f) if total is None else total + face(x, f)
    return total


def put_payload(out_ref, gathered, extras):
    lanes = lax.broadcasted_iota(jnp.int32, (CASES, FD), 1)
    for b in range(6):
        block = face(gathered, b)
        if b == 1:
            for t, value in enumerate(extras):
                block = jnp.where(lanes == 64 + t, value, block)
        for c in range(CASES):
            out_ref[2 * c + b // 3, 4, b % 3:b % 3 + 1, :] = block[c:c + 1, :]


def sum_kernel(shown_ref, residual_ref, gh_ref, gl_ref, pick_ref, out_ref):
    here, _, there = position()
    shown = shown_ref[...]
    share = 0.25 * shown * mask_row(there)
    high, low = halves(share)
    both = dot_across(jnp.concatenate([high, low], 0), gh_ref[...])
    corner = both[:CASES] + both[CASES:] + dot_across(high, gl_ref[...])
    high, low = halves(corner)
    both = dot_across(jnp.concatenate([high, low], 0), pick_ref[...])
    norm = jnp.sum(face_sum(share * residual_ref[...]), axis=1, keepdims=True)
    out_ref[...] = jnp.zeros_like(out_ref)
    put_payload(out_ref, both[:CASES] + both[CASES:], [norm])
    for f, by in enumerate(steps()):
        @pl.when(there[f])
        def _():
            put_rows(out_ref, here + by, face(shown, f))


def put_layers(out_ref, total, flexed_ref, layer, there):
    out_ref[...] = jnp.zeros_like(out_ref)
    for i in range(out_ref.shape[0]):
        out_ref[i, 4] = total
    for f, by in ((4, -1), (5, 1)):
        @pl.when(there[f])
        def _():
            put_rows(out_ref, layer + by, flexed_ref[:, f * FD:(f + 1) * FD])


def flex_kernel(first, mx_ref, my_ref, mz_ref, shown_ref, slots_ref, below_ref, above_ref, fh_ref,
                fl_ref, *rest):
    rest = list(rest)
    if not first:
        search_ref, applied_ref = rest[:2]
        rest = rest[2:]
    z_ref, flexed_ref, out_ref, turn = rest
    here, layer, there = position()
    across = []
    for f, by in enumerate(steps()):
        across.append(take_rows(slots_ref, jnp.where(there[f], here + by, here)))
    across += [below_ref[...], above_ref[...]]
    z = 0.25 * (shown_ref[...] + jnp.concatenate(across, axis=1)) * mask_row(there)
    z_ref[...] = z
    _, flexed = apply_dense(z, (mx_ref, my_ref, mz_ref), fh_ref, fl_ref)
    flexed_ref[...] = flexed
    turn[...] = jnp.zeros_like(turn)
    turn[0:CASES, :] = face_sum(z * flexed)
    if not first:
        turn[CASES:2 * CASES, :] = (
            face_sum(z * applied_ref[...], (1, 3, 5)) + face_sum(search_ref[...] * flexed)
        )
    sums = jnp.sum(turn[...].T, axis=0, keepdims=True)
    total = jnp.sum(slots_ref[:, 4], axis=0)
    rows = lax.broadcasted_iota(jnp.int32, total.shape, 0)
    total = jnp.where(rows == 3, jnp.broadcast_to(sums, total.shape), total)
    put_layers(out_ref, total, flexed_ref, layer, there)


def share_kernel(layers_ref, flexed_ref, out_ref):
    here, _, there = position()
    total = jnp.sum(layers_ref[:, 4], axis=0)
    out_ref[...] = jnp.zeros_like(out_ref)
    for i in range(out_ref.shape[0]):
        out_ref[i, 4] = total
    for f, by in enumerate(steps()):
        @pl.when(there[f])
        def _():
            put_rows(out_ref, here + by, flexed_ref[:, f * FD:(f + 1) * FD])


def step_kernel(first, last, slots_ref, layers_ref, flexed_ref, z_ref,
                residual_ref, kh_ref, kl_ref, gh_ref, gl_ref, pick_ref, *rest):
    rest, whole = list(rest[:-1]), rest[-1]
    if not last:
        mx_ref, my_ref, mz_ref, dh_ref, dl_ref = rest[:5]
        rest = rest[5:]
    if not first:
        search_ref, applied_ref, load_ref, scale_ref, iterate_ref = rest[:5]
        rest = rest[5:]
    here, layer, there = position()
    across = []
    for f, by in enumerate(steps()):
        across.append(take_rows(slots_ref, jnp.where(there[f], here + by, here)))
    for f, by in ((4, -1), (5, 1)):
        across.append(take_rows(layers_ref, jnp.where(there[f], layer + by, layer)))
    mask = mask_row(there)
    applied = (flexed_ref[...] + jnp.concatenate(across, axis=1)) * mask
    search = z_ref[...]
    for c in range(CASES):
        for b in range(6):
            row = slice(b % 3, b % 3 + 1)
            whole[c:c + 1, b * FD:(b + 1) * FD] = slots_ref[2 * c + b // 3, 4, row, :]
    load = whole[...]
    norm = load[:, FD + 64:FD + 65]
    sums = jnp.sum(slots_ref[:, 4], axis=0)[3:4, :]
    sums = jnp.broadcast_to(sums, (FD, FD)).T
    energy, cross = sums[0:CASES, 0:1], sums[CASES:2 * CASES, 0:1]
    lanes = lax.broadcasted_iota(jnp.int32, load.shape, 1) % QPAD
    load = jnp.where(lanes < 192, load, 0.0)
    if not first:
        beta = norm / scale_ref[:, 0:1]
        energy = energy + beta * cross + beta * beta * scale_ref[:, 1:2]
        applied = applied + beta * applied_ref[...]
        search = search + beta * search_ref[...]
        load = load + beta * load_ref[...]
    coarse = dot_split(load, kh_ref, kl_ref)
    step = norm / (energy + jnp.sum(load * coarse, axis=1, keepdims=True))
    corner = dot_exact(coarse, pick_ref[...])
    correction = dot_split(corner, gh_ref, gl_ref) * mask
    residual = residual_ref[...] - step * (applied + correction)
    moved = step * search
    if last:
        multipliers_ref, left_ref = rest
        for d in range(3):
            multipliers_ref[d] = iterate_ref[d] + face(moved, 2 * d + 1)
            left_ref[d] = face(residual, 2 * d + 1)
        return
    search_out, applied_out, load_out, scale_out, iterate_out, residual_out, shown_ref = rest[:7]
    down_ref, up_ref = rest[7:]
    search_out[...] = search
    applied_out[...] = applied
    load_out[...] = load
    residual_out[...] = residual
    lanes = lax.broadcasted_iota(jnp.int32, (CASES, FD), 1)
    scale_out[...] = jnp.where(lanes == 0, norm, energy)
    for d in range(3):
        moved_face = face(moved, 2 * d + 1)
        iterate_out[d] = moved_face if first else iterate_ref[d] + moved_face
    _, shown = apply_dense(residual, (mx_ref, my_ref, mz_ref), dh_ref, dl_ref)
    shown_ref[...] = shown
    down_ref[...] = face(shown, 4)
    up_ref[...] = face(shown, 5)


def passed_along(shard, axis, by):
    peers = lax.axis_size(axis)
    pairs = [(i, i + by) for i in range(peers) if 0 <= i + by < peers]
    return lax.ppermute(shard, axis, pairs)


def swapped(slots, axes):
    return lax.all_to_all(slots, axes, 0, 0)


def body(
    jump_rhs,
    flex_diag,
    flex_couple,
    dirichlet_diag,
    dirichlet_couple,
    face_pairs,
    corner_coupling,
    coarse_ids,
    partner,
    coarse_inverse,
):
    gx, gy, gz = (lax.axis_size(a) for a in AXES)
    plane = gx * gy
    rhs = jump_rhs.reshape(3, CASES, FD)
    coupling = corner_coupling.reshape(24, WIDE)
    square = (WIDE, WIDE)
    wide = (CASES, WIDE)

    *ups, dx, dy, dz = call(
        prep_kernel, [((56, FD), F32)] * 3 + [((32, FD), F32)] * 3,
        [coarse_ids, rhs, partner, coupling], specs=[SMEM],
    )
    messages = [passed_along(m, a, 1) for m, a in zip(ups, AXES)]
    above = [passed_along(m, a, -1) for m, a in zip((dx, dy, dz), AXES)]
    blocks = [b.reshape(6, FD, FD) for b in (dirichlet_diag, dirichlet_couple, flex_diag, flex_couple)]
    dirichlet = call(
        dense_kernel, [(square, BF16)] * 2, [face_pairs] + blocks[:2], specs=[SMEM]
    )
    residual, shown, *joint, down, up = call(
        start_kernel,
        [(wide, F32)] * 2 + [((QPAD, WIDE), BF16)] * 2 + [((3 * QPAD, QPAD), BF16)]
        + [((CASES, FD), F32)] * 2,
        [*ups, *messages, *above, *dirichlet, coupling],
        scratch=[pltpu.VMEM((QPAD, WIDE), F32)],
    )
    stacked = (plane, 5, 4, FD)

    kept = []
    for iteration in range(ITERS):
        first, last = iteration == 0, iteration + 1 == ITERS
        below = passed_along(up, "gz", 1)
        over = passed_along(down, "gz", -1)
        (slots,) = call(sum_kernel, [(stacked, F32)], [shown, residual, *joint])
        slots, below, over = lax.optimization_barrier((slots, below, over))
        slots = swapped(slots, PLANE)
        if first:
            late = call(
                late_kernel, [(square, BF16)] * 4,
                [face_pairs] + blocks[2:] + [coarse_inverse, slots],
                specs=[SMEM] + [VMEM] * 3 + [pl.BlockSpec(memory_space=pl.ANY)],
                scratch=[pltpu.VMEM(square, F32)],
            )
            flex, inverse = late[:2], late[2:]
        z, flexed, layers = call(
            functools.partial(flex_kernel, first),
            [(wide, F32), (wide, F32), ((gz, 5, 4, FD), F32)],
            [*messages, shown, slots, below, over, *flex, *kept[:2]],
            scratch=[pltpu.VMEM((FD, FD), F32)],
        )
        layers = swapped(layers, "gz")
        (slots,) = call(share_kernel, [(stacked, F32)], [layers, flexed])
        slots = swapped(slots, PLANE)
        common = [slots, layers, flexed, z, residual, *inverse, *joint]
        kernel = functools.partial(step_kernel, first, last)
        scratch = [pltpu.VMEM(wide, F32)]
        if last:
            multipliers, left = call(
                kernel, [((3, CASES, FD), F32)] * 2, common + kept, scratch=scratch
            )
            break
        *kept, residual, shown, down, up = call(
            kernel,
            [(wide, F32)] * 3 + [((CASES, FD), F32), ((3, CASES, FD), F32), (wide, F32), (wide, F32)]
            + [((CASES, FD), F32)] * 2,
            common + [*messages, *dirichlet] + kept, scratch=scratch,
        )
    return multipliers.reshape(jump_rhs.shape), left.reshape(jump_rhs.shape)


def solution(mesh):
    placed = (
        P("gx", "gy", "gz", None, None, None),
        P("gx", "gy", "gz", None, None, None),
        P("gx", "gy", "gz", None, None, None),
        P("gx", "gy", "gz", None, None, None),
        P("gx", "gy", "gz", None, None, None),
        P("gx", "gy", "gz", None, None),
        P("gx", "gy", "gz", None, None),
        P("gx", "gy", "gz", None),
        P("gx", "gy", "gz", None, None),
        P(),
    )
    return jax.shard_map(
        body,
        mesh=mesh,
        in_specs=placed,
        out_specs=(P("gx", "gy", "gz", None, None, None), P("gx", "gy", "gz", None, None, None)),
        check_vma=False,
    )
```

time: 222 us -> 222 us (level)
  blocking collectives: 176 us -> 163 us
  starting transfers between devices: 19.5 us -> 29.6 us
    all_to_all x2 -> x0, blocking collectives: 25.2 us -> none  [the longest x1 15.5 us: across_faces(): lax.all_to_all(two, AXES, 0, 0, axis_index_groups=cube_groups(1))]
    all_to_all x9, blocking collectives: 151 us -> 163 us  [swapped(): return lax.all_to_all(slots, axes, 0, 0)]
    ppermute x7 -> x12, starting transfers between devices: 19.5 us -> 29.6 us  [passed_along(): return lax.ppermute(shard, axis, pairs)]
    ppermute x7 -> x12, waiting for transfers between devices: 6.18 us -> 7.79 us  [passed_along(): return lax.ppermute(shard, axis, pairs)]
    pallas_call x14 -> x16, Pallas kernels: 12.5 us -> 13.3 us  [call(): pl.pallas_call(kernel, out_shape=[jax.ShapeDtypeStruct(shape, dtype) for...]
    unnamed x22 -> x20, local copies, waits for them, and re-layouts: 6.46 us -> 6.61 us
  transfers between devices with their start and end apart: 7 -> 12, of which waited for: 2 -> 3; matrix products, arithmetic and copies ran while one was open for 0% -> 0% of each run, Pallas kernels for 0% -> 1%
where the time goes in v6:
time: 222 us; the launch traced here: 221 us
  blocking collectives  163 us (73%)
  starting transfers between devices  29.6 us (13%)
  Pallas kernels  13.3 us (6%)
  waiting for transfers between devices  7.79 us (4%)
  local copies, waits for them, and re-layouts  6.61 us (3%)
    all_to_all x9, blocking collectives, swapped(): return lax.all_to_all(slots, axes, 0, 0)  163 us
    ppermute x12, starting transfers between devices, passed_along(): return lax.ppermute(shard, axis, pairs)  29.6 us
    pallas_call x16, Pallas kernels, call(): pl.pallas_call(kernel, out_shape=[jax.ShapeDtypeStruct(shape, dtype) for...  13.3 us
    ppermute x12, waiting for transfers between devices, passed_along(): return lax.ppermute(shard, axis, pairs)  7.79 us
    unnamed x20, local copies, waits for them, and re-layouts  6.61 us
  transfers between devices with their start and end apart: 12, of which 3 were waited for; matrix products, arithmetic and copies ran while one was open for 0% of the time, Pallas kernels for 1%

profile of v6, /device:TPU:1, one launch (start us, length us, event | category | flops | bytes accessed | tf_op | source)
XLA Modules:
  0.0 220.9 jit_solution(5678495757253729750)
XLA Ops:
  0.6 0.7 copy.12.partner_ref
  1.3 0.0 copy-start.5
  1.3 0.9 copy-done.5
  2.2 0.7 copy-done.7
  2.9 0.7 copy-done.8
  3.6 0.7 shard_map.113
  4.3 8.8 %collective-permute-start.3 = (f32[32,128]{1,0:T(8,128)S(1)}, f32[32,128]{1,0:T(8,128)S(1)}, u32[]{:S(2)}, u32[]{:S(2)}) collective-permute-start(f32[32,128]{1,0:T(8,128)S(1)} %get-tuple-element.62), channel_id=1, source_target_pairs={{64,0},{128,64},{192,128},{256,192},{320,256},{384,320},{448,384},... | collective-permute-start | bytes 49160 | tf_op jit(solution)/shard_map/ppermute | solution.py:373
  13.1 1.9 collective-permute-start
  15.0 1.3 collective-permute-start.1
  16.3 1.3 collective-permute-start.2
  17.6 1.3 collective-permute-start.4
  18.9 0.0 collective-permute-done.3.nx_ref
  18.9 1.3 collective-permute-start.5
  20.2 0.8 copy.13.pairs
  21.0 1.0 copy-done.3
  22.0 1.0 copy-done.4
  23.0 1.0 shard_map.114
  24.0 0.0 collective-permute-done.4.ny_ref
  24.0 0.0 collective-permute-done.5.nz_ref
  24.0 0.0 collective-permute-done.mx_ref.rest_0_
  24.1 0.0 collective-permute-done.1.my_ref.rest_1_
  24.1 0.0 collective-permute-done.2.mz_ref.rest_2_
  24.1 0.0 copy-start.6
  24.1 0.9 copy-done.6
  25.0 0.6 shard_map.115
  25.6 0.0 copy-start.1
  25.6 0.0 copy-start.2
  25.6 4.2 %collective-permute-start.6 = (f32[16,128]{1,0:T(8,128)S(1)}, f32[16,128]{1,0:T(8,128)S(1)}, u32[]{:S(2)}, u32[]{:S(2)}) collective-permute-start(f32[16,128]{1,0:T(8,128)S(1)} %get-tuple-element.72), channel_id=1, source_target_pairs={{0,1},{1,2},{2,3},{3,4},{4,5},{5,6},{6,7},{7,8},{8,9},{9,10},{10,1... | collective-permute-start | bytes 24584 | tf_op jit(solution)/shard_map/ppermute | solution.py:373
  29.8 1.3 collective-permute-start.7
  31.1 0.7 shard_map.116
  31.8 0.0 collective-permute-done.6.below_ref
  31.8 3.1 %collective-permute-done.7.above_ref = f32[16,128]{1,0:T(8,128)S(1)} collective-permute-done((f32[16,128]{1,0:T(8,128)S(1)}, f32[16,128]{1,0:T(8,128)S(1)}, u32[]{:S(2)}, u32[]{:S(2)}) %collective-permute-start.7) | collective-permute-done | bytes 8224 | tf_op jit(solution)/shard_map/ppermute | solution.py:373
  34.9 19.0 %all_to_all.45._.slots_ref = f32[32,5,4,128]{3,2,1,0:T(4,128)S(1)} all-to-all(f32[32,5,4,128]{3,2,1,0:T(4,128)S(1)} %shard_map.116), channel_id=1, replica_groups=mesh['gx'=8,'gy'=4,'gz'=16] {'gx','gy'}, dimensions={0} | all-to-all | bytes 655360 | tf_op jit(solution)/shard_map/all_to_all | solution.py:377
  54.0 0.0 copy-done
  54.0 0.0 copy-done.1
  54.0 0.0 copy-done.2
  54.0 1.6 shard_map.117
  55.6 0.7 shard_map.118
  56.3 27.4 %all_to_all.46.layers_ref = f32[16,5,4,128]{3,2,1,0:T(4,128)S(1)} all-to-all(f32[16,5,4,128]{3,2,1,0:T(4,128)S(1)} %get-tuple-element.79), channel_id=1, replica_groups=mesh['gx'=8,'gy'=4,'gz'=16] {'gz'}, dimensions={0} | all-to-all | bytes 327680 | tf_op jit(solution)/shard_map/all_to_all | solution.py:377
  83.7 0.1 shard_map.119
  83.7 16.7 %all_to_all.47.slots_ref = f32[32,5,4,128]{3,2,1,0:T(4,128)S(1)} all-to-all(f32[32,5,4,128]{3,2,1,0:T(4,128)S(1)} %shard_map.119), channel_id=1, replica_groups=mesh['gx'=8,'gy'=4,'gz'=16] {'gx','gy'}, dimensions={0} | all-to-all | bytes 655360 | tf_op jit(solution)/shard_map/all_to_all | solution.py:377
  100.5 1.5 shard_map.120
  102.0 2.8 %collective-permute-start.8 = (f32[16,128]{1,0:T(8,128)S(1)}, f32[16,128]{1,0:T(8,128)S(1)}, u32[]{:S(2)}, u32[]{:S(2)}) collective-permute-start(f32[16,128]{1,0:T(8,128)S(1)} %get-tuple-element.86), channel_id=1, source_target_pairs={{0,1},{1,2},{2,3},{3,4},{4,5},{5,6},{6,7},{7,8},{8,9},{9,10},{10,1... | collective-permute-start | bytes 24584 | tf_op jit(solution)/shard_map/ppermute | solution.py:373
  104.9 1.3 collective-permute-start.9
  106.2 0.7 shard_map.121
  106.9 0.0 collective-permute-done.8.below_ref
  106.9 2.3 %collective-permute-done.9.above_ref = f32[16,128]{1,0:T(8,128)S(1)} collective-permute-done((f32[16,128]{1,0:T(8,128)S(1)}, f32[16,128]{1,0:T(8,128)S(1)}, u32[]{:S(2)}, u32[]{:S(2)}) %collective-permute-start.9) | collective-permute-done | bytes 8224 | tf_op jit(solution)/shard_map/ppermute | solution.py:373
  109.3 14.9 %all_to_all.48.slots_ref = f32[32,5,4,128]{3,2,1,0:T(4,128)S(1)} all-to-all(f32[32,5,4,128]{3,2,1,0:T(4,128)S(1)} %shard_map.121), channel_id=1, replica_groups=mesh['gx'=8,'gy'=4,'gz'=16] {'gx','gy'}, dimensions={0} | all-to-all | bytes 655360 | tf_op jit(solution)/shard_map/all_to_all | solution.py:377
  124.2 0.7 shard_map.122
  124.9 18.1 %all_to_all.49.layers_ref = f32[16,5,4,128]{3,2,1,0:T(4,128)S(1)} all-to-all(f32[16,5,4,128]{3,2,1,0:T(4,128)S(1)} %get-tuple-element.93), channel_id=1, replica_groups=mesh['gx'=8,'gy'=4,'gz'=16] {'gz'}, dimensions={0} | all-to-all | bytes 327680 | tf_op jit(solution)/shard_map/all_to_all | solution.py:377
  143.0 0.1 shard_map.123
  143.1 16.7 %all_to_all.50.slots_ref = f32[32,5,4,128]{3,2,1,0:T(4,128)S(1)} all-to-all(f32[32,5,4,128]{3,2,1,0:T(4,128)S(1)} %shard_map.123), channel_id=1, replica_groups=mesh['gx'=8,'gy'=4,'gz'=16] {'gx','gy'}, dimensions={0} | all-to-all | bytes 655360 | tf_op jit(solution)/shard_map/all_to_all | solution.py:377
  159.8 1.6 shard_map.124
  161.4 2.8 %collective-permute-start.10 = (f32[16,128]{1,0:T(8,128)S(1)}, f32[16,128]{1,0:T(8,128)S(1)}, u32[]{:S(2)}, u32[]{:S(2)}) collective-permute-start(f32[16,128]{1,0:T(8,128)S(1)} %get-tuple-element.101), channel_id=1, source_target_pairs={{0,1},{1,2},{2,3},{3,4},{4,5},{5,6},{6,7},{7,8},{8,9},{9,10},{10,1... | collective-permute-start | bytes 24584 | tf_op jit(solution)/shard_map/ppermute | solution.py:373
  164.3 1.3 collective-permute-start.11
  165.6 0.7 shard_map.125
  166.3 0.0 collective-permute-done.10.below_ref
  166.3 2.3 %collective-permute-done.11.above_ref = f32[16,128]{1,0:T(8,128)S(1)} collective-permute-done((f32[16,128]{1,0:T(8,128)S(1)}, f32[16,128]{1,0:T(8,128)S(1)}, u32[]{:S(2)}, u32[]{:S(2)}) %collective-permute-start.11) | collective-permute-done | bytes 8224 | tf_op jit(solution)/shard_map/ppermute | solution.py:373
  168.7 14.9 %all_to_all.51.slots_ref = f32[32,5,4,128]{3,2,1,0:T(4,128)S(1)} all-to-all(f32[32,5,4,128]{3,2,1,0:T(4,128)S(1)} %shard_map.125), channel_id=1, replica_groups=mesh['gx'=8,'gy'=4,'gz'=16] {'gx','gy'}, dimensions={0} | all-to-all | bytes 655360 | tf_op jit(solution)/shard_map/all_to_all | solution.py:377
  183.6 0.7 shard_map.126
  184.3 18.1 %all_to_all.52.layers_ref = f32[16,5,4,128]{3,2,1,0:T(4,128)S(1)} all-to-all(f32[16,5,4,128]{3,2,1,0:T(4,128)S(1)} %get-tuple-element.108), channel_id=1, replica_groups=mesh['gx'=8,'gy'=4,'gz'=16] {'gz'}, dimensions={0} | all-to-all | bytes 327680 | tf_op jit(solution)/shard_map/all_to_all | solution.py:377
  202.4 0.1 shard_map.127
  202.5 16.7 %all_to_all.53.slots_ref = f32[32,5,4,128]{3,2,1,0:T(4,128)S(1)} all-to-all(f32[32,5,4,128]{3,2,1,0:T(4,128)S(1)} %shard_map.127), channel_id=1, replica_groups=mesh['gx'=8,'gy'=4,'gz'=16] {'gx','gy'}, dimensions={0} | all-to-all | bytes 655360 | tf_op jit(solution)/shard_map/all_to_all | solution.py:377
  219.2 1.7 shard_map.128
  (5 shorter events, 0.0 us)
Async XLA Ops:
  1.3 0.9 copy-start.5
  2.2 0.7 copy-start.7
  2.9 0.7 copy-start.8
  4.3 14.6 %collective-permute-start.3 = (f32[32,128]{1,0:T(8,128)S(1)}, f32[32,128]{1,0:T(8,128)S(1)}, u32[]{:S(2)}, u32[]{:S(2)}) collective-permute-start(f32[32,128]{1,0:T(8,128)S(1)} %get-tuple-element.62), channel_id=1, source_target_pairs={{64,0},{128,64},{192,128},{256,192},{320,256},{384,320},{448,384},... | collective-permute-start | bytes 49160 | tf_op jit(solution)/shard_map/ppermute | solution.py:373
  13.1 10.9 %collective-permute-start = (f32[56,128]{1,0:T(8,128)S(1)}, f32[56,128]{1,0:T(8,128)S(1)}, u32[]{:S(2)}, u32[]{:S(2)}) collective-permute-start(f32[56,128]{1,0:T(8,128)S(1)} %get-tuple-element.59.ux_ref), channel_id=1, source_target_pairs={{0,64},{64,128},{128,192},{192,256},{256,320},{320,384},{384,448},... | collective-permute-start | bytes 86024 | tf_op jit(solution)/shard_map/ppermute | solution.py:373
  15.0 9.0 %collective-permute-start.1 = (f32[56,128]{1,0:T(8,128)S(1)}, f32[56,128]{1,0:T(8,128)S(1)}, u32[]{:S(2)}, u32[]{:S(2)}) collective-permute-start(f32[56,128]{1,0:T(8,128)S(1)} %get-tuple-element.60.uy_ref), channel_id=1, source_target_pairs={{0,16},{16,32},{32,48},{1,17},{17,33},{33,49},{2,18},{18,34},{34,5... | collective-permute-start | bytes 86024 | tf_op jit(solution)/shard_map/ppermute | solution.py:373
  16.3 7.7 %collective-permute-start.2 = (f32[56,128]{1,0:T(8,128)S(1)}, f32[56,128]{1,0:T(8,128)S(1)}, u32[]{:S(2)}, u32[]{:S(2)}) collective-permute-start(f32[56,128]{1,0:T(8,128)S(1)} %get-tuple-element.61.uz_ref), channel_id=1, source_target_pairs={{0,1},{1,2},{2,3},{3,4},{4,5},{5,6},{6,7},{7,8},{8,9},{9,10},{10,1... | collective-permute-start | bytes 86024 | tf_op jit(solution)/shard_map/ppermute | solution.py:373
  17.6 6.4 %collective-permute-start.4 = (f32[32,128]{1,0:T(8,128)S(1)}, f32[32,128]{1,0:T(8,128)S(1)}, u32[]{:S(2)}, u32[]{:S(2)}) collective-permute-start(f32[32,128]{1,0:T(8,128)S(1)} %get-tuple-element.63), channel_id=1, source_target_pairs={{16,0},{32,16},{48,32},{17,1},{33,17},{49,33},{18,2},{34,18},{50,3... | collective-permute-start | bytes 49160 | tf_op jit(solution)/shard_map/ppermute | solution.py:373
  18.9 5.1 %collective-permute-start.5 = (f32[32,128]{1,0:T(8,128)S(1)}, f32[32,128]{1,0:T(8,128)S(1)}, u32[]{:S(2)}, u32[]{:S(2)}) collective-permute-start(f32[32,128]{1,0:T(8,128)S(1)} %get-tuple-element.64), channel_id=1, source_target_pairs={{1,0},{2,1},{3,2},{4,3},{5,4},{6,5},{7,6},{8,7},{9,8},{10,9},{11,1... | collective-permute-start | bytes 49160 | tf_op jit(solution)/shard_map/ppermute | solution.py:373
  21.0 1.0 copy-start.3
  22.0 1.0 copy-start.4
  24.1 0.9 copy-start.6
  25.6 28.4 %copy-start = (f32[576,576]{1,0:T(8,128)S(1)}, f32[576,576]{1,0:T(8,128)}, u32[]{:S(2)}) copy-start(f32[576,576]{1,0:T(8,128)} %inverse_ref.1) | copy-start | bytes 3981316
  25.6 28.4 %copy-start.1 = (f32[1,1,1,6,128,128]{5,4,3,2,1,0:T(8,128)S(1)}, f32[1,1,1,6,128,128]{5,4,3,2,1,0:T(8,128)}, u32[]{:S(2)}) copy-start(f32[1,1,1,6,128,128]{5,4,3,2,1,0:T(8,128)} %param.11) | copy-start | bytes 1179652
  25.6 28.4 %copy-start.2 = (f32[1,1,1,6,128,128]{5,4,3,2,1,0:T(8,128)S(1)}, f32[1,1,1,6,128,128]{5,4,3,2,1,0:T(8,128)}, u32[]{:S(2)}) copy-start(f32[1,1,1,6,128,128]{5,4,3,2,1,0:T(8,128)} %param.12) | copy-start | bytes 1179652
  25.6 6.2 %collective-permute-start.6 = (f32[16,128]{1,0:T(8,128)S(1)}, f32[16,128]{1,0:T(8,128)S(1)}, u32[]{:S(2)}, u32[]{:S(2)}) collective-permute-start(f32[16,128]{1,0:T(8,128)S(1)} %get-tuple-element.72), channel_id=1, source_target_pairs={{0,1},{1,2},{2,3},{3,4},{4,5},{5,6},{6,7},{7,8},{8,9},{9,10},{10,1... | collective-permute-start | bytes 24584 | tf_op jit(solution)/shard_map/ppermute | solution.py:373
  29.8 5.1 %collective-permute-start.7 = (f32[16,128]{1,0:T(8,128)S(1)}, f32[16,128]{1,0:T(8,128)S(1)}, u32[]{:S(2)}, u32[]{:S(2)}) collective-permute-start(f32[16,128]{1,0:T(8,128)S(1)} %get-tuple-element.73), channel_id=1, source_target_pairs={{1,0},{2,1},{3,2},{4,3},{5,4},{6,5},{7,6},{8,7},{9,8},{10,9},{11,1... | collective-permute-start | bytes 24584 | tf_op jit(solution)/shard_map/ppermute | solution.py:373
  102.0 4.9 %collective-permute-start.8 = (f32[16,128]{1,0:T(8,128)S(1)}, f32[16,128]{1,0:T(8,128)S(1)}, u32[]{:S(2)}, u32[]{:S(2)}) collective-permute-start(f32[16,128]{1,0:T(8,128)S(1)} %get-tuple-element.86), channel_id=1, source_target_pairs={{0,1},{1,2},{2,3},{3,4},{4,5},{5,6},{6,7},{7,8},{8,9},{9,10},{10,1... | collective-permute-start | bytes 24584 | tf_op jit(solution)/shard_map/ppermute | solution.py:373
  104.9 4.4 %collective-permute-start.9 = (f32[16,128]{1,0:T(8,128)S(1)}, f32[16,128]{1,0:T(8,128)S(1)}, u32[]{:S(2)}, u32[]{:S(2)}) collective-permute-start(f32[16,128]{1,0:T(8,128)S(1)} %get-tuple-element.87), channel_id=1, source_target_pairs={{1,0},{2,1},{3,2},{4,3},{5,4},{6,5},{7,6},{8,7},{9,8},{10,9},{11,1... | collective-permute-start | bytes 24584 | tf_op jit(solution)/shard_map/ppermute | solution.py:373
  161.4 4.9 %collective-permute-start.10 = (f32[16,128]{1,0:T(8,128)S(1)}, f32[16,128]{1,0:T(8,128)S(1)}, u32[]{:S(2)}, u32[]{:S(2)}) collective-permute-start(f32[16,128]{1,0:T(8,128)S(1)} %get-tuple-element.101), channel_id=1, source_target_pairs={{0,1},{1,2},{2,3},{3,4},{4,5},{5,6},{6,7},{7,8},{8,9},{9,10},{10,1... | collective-permute-start | bytes 24584 | tf_op jit(solution)/shard_map/ppermute | solution.py:373
  164.3 4.4 %collective-permute-start.11 = (f32[16,128]{1,0:T(8,128)S(1)}, f32[16,128]{1,0:T(8,128)S(1)}, u32[]{:S(2)}, u32[]{:S(2)}) collective-permute-start(f32[16,128]{1,0:T(8,128)S(1)} %get-tuple-element.102), channel_id=1, source_target_pairs={{1,0},{2,1},{3,2},{4,3},{5,4},{6,5},{7,6},{8,7},{9,8},{10,9},{11,1... | collective-permute-start | bytes 24584 | tf_op jit(solution)/shard_map/ppermute | solution.py:373

commit v7 on v6

--- a/solution.py
+++ b/solution.py
@@ -126,7 +126,7 @@
     target = target_rows(ids)
     for d in range(3):
         up_ref, down_ref = message_refs[d], message_refs[3 + d]
-        row = partner_ref[0, 0, 0, d:d + 1, :]
+        row = partner_ref[0, 0, d, :, :]
         up_ref[0:CASES, :] = rhs_ref[d] * there[2 * d + 1].astype(F32)
         wanted = lax.broadcasted_iota(jnp.int32, (FD, FD), 0)
         hits = (wanted == jnp.broadcast_to(row, (FD, FD))).astype(F32).astype(BF16)
@@ -152,8 +152,8 @@
     for f in range(6):
         put(f * FD, f * FD, diag_ref[f])
     for k in range(6):
-        first = pl.multiple_of(pairs[0, 0, 0, k, 0] * FD, FD)
-        second = pl.multiple_of(pairs[0, 0, 0, k, 1] * FD, FD)
+        first = pl.multiple_of(pairs[0, 0, 0, 0, k] * FD, FD)
+        second = pl.multiple_of(pairs[0, 0, 0, 1, k] * FD, FD)
         block = couple_ref[k]
         put(second, first, block)
         put(first, second, block.T)
@@ -163,11 +163,9 @@
     put_dense(pairs, diag_ref, couple_ref, high_ref, low_ref)
 
 
-def start_kernel(ux_ref, uy_ref, uz_ref, mx_ref, my_ref, mz_ref, nx_ref, ny_ref, nz_ref, dh_ref,
-                 dl_ref, coupling_ref, field_ref, shown_ref, gh_ref, gl_ref, pick_ref, down_ref,
-                 up_ref, pad):
-    _, _, there = position()
-    own, messages, above = (ux_ref, uy_ref, uz_ref), (mx_ref, my_ref, mz_ref), (nx_ref, ny_ref, nz_ref)
+def start_kernel(ux_ref, uy_ref, uz_ref, mx_ref, my_ref, mz_ref, dz_ref, dh_ref, dl_ref, field_ref,
+                 shown_ref, down_ref, up_ref):
+    own, messages = (ux_ref, uy_ref, uz_ref), (mx_ref, my_ref, mz_ref)
     parts = []
     for d in range(3):
         parts += [messages[d][0:CASES, :], own[d][0:CASES, :]]
@@ -175,20 +173,30 @@
     field_ref[...] = field
     _, shown = apply_dense(field, messages, dh_ref, dl_ref)
     shown_ref[...] = shown
-    down_ref[...] = face(shown, 4)
+    down_ref[0:CASES, :] = face(shown, 4)
+    down_ref[CASES:CASES + 32, :] = dz_ref[...]
     up_ref[...] = face(shown, 5)
+
+
+def joint_kernel(ux_ref, uy_ref, uz_ref, mx_ref, my_ref, mz_ref, dx_ref, dy_ref, dz_ref, nx_ref, ny_ref,
+                 over_ref, shown_ref, residual_ref, gh_ref, gl_ref, pick_ref, out_ref, pad):
+    _, _, there = position()
+    own, messages, lower = (ux_ref, uy_ref, uz_ref), (mx_ref, my_ref, mz_ref), (dx_ref, dy_ref, dz_ref)
+    above = (nx_ref[...], ny_ref[...], over_ref[CASES:CASES + 32, :])
     pad[...] = jnp.zeros_like(pad)
-    pad[0:24, :] = lower_changed(coupling_ref[...], partner_rows(messages))
     targets = [own[0][48:56, :]]
     for d in range(3):
         row = own[d][CASES:CASES + 1, :]
+        low, high = slice(2 * d * FD, (2 * d + 1) * FD), slice((2 * d + 1) * FD, (2 * d + 2) * FD)
+        pad[0:24, low] = -take(lower[d][0:24, :], messages[d][CASES:CASES + 1, :])
+        pad[0:24, high] = own[d][24:48, :]
         sides = (
-            (messages[d][24:48, :], messages[d][48:56, :]),
-            (-take(above[d][0:24, :], row), above[d][24:32, :]),
+            (low, messages[d][24:48, :], messages[d][48:56, :]),
+            (high, -take(above[d][0:24, :], row), above[d][24:32, :]),
         )
-        for f, (rows, target) in zip((2 * d, 2 * d + 1), sides):
+        for f, (lanes, rows, target) in zip((2 * d, 2 * d + 1), sides):
             exists = there[f].astype(F32)
-            pad[SUBS * (f + 1):SUBS * (f + 1) + 24, f * FD:(f + 1) * FD] = rows * exists
+            pad[SUBS * (f + 1):SUBS * (f + 1) + 24, lanes] = rows * exists
             targets.append(target * exists)
     high, low = halves(pad[...])
     gh_ref[...] = high
@@ -201,6 +209,7 @@
             wanted = jnp.where(lanes // SUBS == n % 4, targets[n], wanted)
         wanted = jnp.broadcast_to(wanted[0:1, :].astype(jnp.int32), (3 * QPAD, FD))
         pick_ref[:, half * FD:(half + 1) * FD] = (rows == wanted).astype(F32).astype(BF16)
+    sum_kernel(shown_ref, residual_ref, gh_ref, gl_ref, pick_ref, out_ref)
 
 
 def late_kernel(pairs, diag_ref, couple_ref, inverse_ref, _, fh_ref, fl_ref, kh_ref, kl_ref, square):
@@ -273,7 +282,7 @@
     across = []
     for f, by in enumerate(steps()):
         across.append(take_rows(slots_ref, jnp.where(there[f], here + by, here)))
-    across += [below_ref[...], above_ref[...]]
+    across += [below_ref[...], above_ref[0:CASES, :]]
     z = 0.25 * (shown_ref[...] + jnp.concatenate(across, axis=1)) * mask_row(there)
     z_ref[...] = z
     _, flexed = apply_dense(z, (mx_ref, my_ref, mz_ref), fh_ref, fl_ref)
@@ -398,20 +407,19 @@
 
     *ups, dx, dy, dz = call(
         prep_kernel, [((56, FD), F32)] * 3 + [((32, FD), F32)] * 3,
-        [coarse_ids, rhs, partner, coupling], specs=[SMEM],
+        [coarse_ids, rhs, jnp.swapaxes(partner, 2, 3), coupling], specs=[SMEM],
     )
     messages = [passed_along(m, a, 1) for m, a in zip(ups, AXES)]
-    above = [passed_along(m, a, -1) for m, a in zip((dx, dy, dz), AXES)]
+    above = [passed_along(m, a, -1) for m, a in zip((dx, dy), AXES)]
+    pairs = jnp.swapaxes(face_pairs, 3, 4)
     blocks = [b.reshape(6, FD, FD) for b in (dirichlet_diag, dirichlet_couple, flex_diag, flex_couple)]
     dirichlet = call(
-        dense_kernel, [(square, BF16)] * 2, [face_pairs] + blocks[:2], specs=[SMEM]
+        dense_kernel, [(square, BF16)] * 2, [pairs] + blocks[:2], specs=[SMEM]
     )
-    residual, shown, *joint, down, up = call(
+    residual, shown, down, up = call(
         start_kernel,
-        [(wide, F32)] * 2 + [((QPAD, WIDE), BF16)] * 2 + [((3 * QPAD, QPAD), BF16)]
-        + [((CASES, FD), F32)] * 2,
-        [*ups, *messages, *above, *dirichlet, coupling],
-        scratch=[pltpu.VMEM((QPAD, WIDE), F32)],
+        [(wide, F32)] * 2 + [((CASES + 32, FD), F32), ((CASES, FD), F32)],
+        [*ups, *messages, dz, *dirichlet],
     )
     stacked = (plane, 5, 4, FD)
 
@@ -420,13 +428,21 @@
         first, last = iteration == 0, iteration + 1 == ITERS
         below = passed_along(up, "gz", 1)
         over = passed_along(down, "gz", -1)
-        (slots,) = call(sum_kernel, [(stacked, F32)], [shown, residual, *joint])
+        if first:
+            *joint, slots = call(
+                joint_kernel,
+                [((QPAD, WIDE), BF16)] * 2 + [((3 * QPAD, QPAD), BF16), (stacked, F32)],
+                [*ups, *messages, dx, dy, dz, *above, over, shown, residual],
+                scratch=[pltpu.VMEM((QPAD, WIDE), F32)],
+            )
+        else:
+            (slots,) = call(sum_kernel, [(stacked, F32)], [shown, residual, *joint])
         slots, below, over = lax.optimization_barrier((slots, below, over))
         slots = swapped(slots, PLANE)
         if first:
             late = call(
                 late_kernel, [(square, BF16)] * 4,
-                [face_pairs] + blocks[2:] + [coarse_inverse, slots],
+                [pairs] + blocks[2:] + [coarse_inverse, slots],
                 specs=[SMEM] + [VMEM] * 3 + [pl.BlockSpec(memory_space=pl.ANY)],
                 scratch=[pltpu.VMEM(square, F32)],
             )

time: 222 us -> 219 us (0.986)
  waiting for transfers between devices: 7.79 us -> 4.71 us
    ppermute x12 -> x11, waiting for transfers between devices: 7.79 us -> 4.71 us  [passed_along(): return lax.ppermute(shard, axis, pairs)]
    ppermute x12 -> x11, starting transfers between devices: 29.6 us -> 28.4 us  [passed_along(): return lax.ppermute(shard, axis, pairs)]
  transfers between devices with their start and end apart: 12 -> 11, of which waited for: 3 -> 2; matrix products, arithmetic and copies ran while one was open for 0% -> 0% of each run, Pallas kernels for 1% -> 1%
where the time goes in v7:
time: 219 us; the launch traced here: 218 us
  blocking collectives  165 us (75%)
  starting transfers between devices  28.4 us (13%)
  Pallas kernels  13.2 us (6%)
  local copies, waits for them, and re-layouts  5.63 us (3%)
  waiting for transfers between devices  4.71 us (2%)
    all_to_all x9, blocking collectives, swapped(): return lax.all_to_all(slots, axes, 0, 0)  165 us
    ppermute x11, starting transfers between devices, passed_along(): return lax.ppermute(shard, axis, pairs)  28.4 us
    pallas_call x16, Pallas kernels, call(): pl.pallas_call(kernel, out_shape=[jax.ShapeDtypeStruct(shape, dtype) for...  13.2 us
    unnamed x20, local copies, waits for them, and re-layouts  5.63 us
    ppermute x11, waiting for transfers between devices, passed_along(): return lax.ppermute(shard, axis, pairs)  4.71 us
  transfers between devices with their start and end apart: 11, of which 2 were waited for; matrix products, arithmetic and copies ran while one was open for 0% of the time, Pallas kernels for 1%

profile of v7, /device:TPU:1, one launch (start us, length us, event | category | flops | bytes accessed | tf_op | source)
XLA Modules:
  0.0 217.7 jit_solution(3668663342454509751)
XLA Ops:
  0.6 0.0 copy-start.5
  0.6 0.9 copy-done.5
  1.5 0.0 copy-start.6
  1.5 0.7 copy-done.6
  2.3 0.0 copy-start.8
  2.3 0.7 copy-done.8
  2.9 0.7 copy-done.9
  3.6 0.7 shard_map.113
  4.3 4.6 %collective-permute-start = (f32[56,128]{1,0:T(8,128)S(1)}, f32[56,128]{1,0:T(8,128)S(1)}, u32[]{:S(2)}, u32[]{:S(2)}) collective-permute-start(f32[56,128]{1,0:T(8,128)S(1)} %get-tuple-element.60.ux_ref), channel_id=1, source_target_pairs={{0,64},{64,128},{128,192},{192,256},{256,320},{320,384},{384,448},... | collective-permute-start | bytes 86024 | tf_op jit(solution)/shard_map/ppermute | solution.py:382
  8.9 3.1 %collective-permute-start.1 = (f32[56,128]{1,0:T(8,128)S(1)}, f32[56,128]{1,0:T(8,128)S(1)}, u32[]{:S(2)}, u32[]{:S(2)}) collective-permute-start(f32[56,128]{1,0:T(8,128)S(1)} %get-tuple-element.61.uy_ref), channel_id=1, source_target_pairs={{0,16},{16,32},{32,48},{1,17},{17,33},{33,49},{2,18},{18,34},{34,5... | collective-permute-start | bytes 86024 | tf_op jit(solution)/shard_map/ppermute | solution.py:382
  12.0 3.5 %collective-permute-start.2 = (f32[56,128]{1,0:T(8,128)S(1)}, f32[56,128]{1,0:T(8,128)S(1)}, u32[]{:S(2)}, u32[]{:S(2)}) collective-permute-start(f32[56,128]{1,0:T(8,128)S(1)} %get-tuple-element.62.uz_ref), channel_id=1, source_target_pairs={{0,1},{1,2},{2,3},{3,4},{4,5},{5,6},{6,7},{7,8},{8,9},{9,10},{10,1... | collective-permute-start | bytes 86024 | tf_op jit(solution)/shard_map/ppermute | solution.py:382
  15.6 0.0 copy-start.3
  15.6 1.0 copy-done.3
  16.6 1.0 copy-done.4
  17.6 0.7 copy-done.7
  18.3 1.0 shard_map.114
  19.2 0.0 collective-permute-done.mx_ref.rest_0_
  19.2 0.0 collective-permute-done.1.my_ref.rest_1_
  19.3 0.0 collective-permute-done.2.mz_ref.rest_2_
  19.3 0.0 copy-start
  19.3 0.0 copy-start.1
  19.3 0.0 copy-start.2
  19.3 0.6 shard_map.115
  19.9 1.4 collective-permute-start.5
  21.3 1.9 collective-permute-start.3
  23.2 1.3 collective-permute-start.4
  24.5 4.2 %collective-permute-start.6 = (f32[16,128]{1,0:T(8,128)S(1)}, f32[16,128]{1,0:T(8,128)S(1)}, u32[]{:S(2)}, u32[]{:S(2)}) collective-permute-start(f32[16,128]{1,0:T(8,128)S(1)} %get-tuple-element.72), channel_id=1, source_target_pairs={{0,1},{1,2},{2,3},{3,4},{4,5},{5,6},{6,7},{7,8},{8,9},{9,10},{10,1... | collective-permute-start | bytes 24584 | tf_op jit(solution)/shard_map/ppermute | solution.py:382
  28.7 0.0 collective-permute-done.3.nx_ref
  28.7 0.0 collective-permute-done.4.ny_ref
  28.7 0.0 collective-permute-done.5.over_ref.above_ref
  28.7 0.8 shard_map.116
  29.6 0.0 collective-permute-done.6.below_ref
  29.6 18.9 %all_to_all.45._.slots_ref = f32[32,5,4,128]{3,2,1,0:T(4,128)S(1)} all-to-all(f32[32,5,4,128]{3,2,1,0:T(4,128)S(1)} %get-tuple-element.73), channel_id=1, replica_groups=mesh['gx'=8,'gy'=4,'gz'=16] {'gx','gy'}, dimensions={0} | all-to-all | bytes 655360 | tf_op jit(solution)/shard_map/all_to_all | solution.py:386
  48.4 0.0 copy-done
  48.4 0.0 copy-done.1
  48.4 0.0 copy-done.2
  48.4 1.6 shard_map.117
  50.0 0.7 shard_map.118
  50.7 29.7 %all_to_all.46.layers_ref = f32[16,5,4,128]{3,2,1,0:T(4,128)S(1)} all-to-all(f32[16,5,4,128]{3,2,1,0:T(4,128)S(1)} %get-tuple-element.78), channel_id=1, replica_groups=mesh['gx'=8,'gy'=4,'gz'=16] {'gz'}, dimensions={0} | all-to-all | bytes 327680 | tf_op jit(solution)/shard_map/all_to_all | solution.py:386
  80.4 0.1 shard_map.119
  80.5 16.7 %all_to_all.47.slots_ref = f32[32,5,4,128]{3,2,1,0:T(4,128)S(1)} all-to-all(f32[32,5,4,128]{3,2,1,0:T(4,128)S(1)} %shard_map.119), channel_id=1, replica_groups=mesh['gx'=8,'gy'=4,'gz'=16] {'gx','gy'}, dimensions={0} | all-to-all | bytes 655360 | tf_op jit(solution)/shard_map/all_to_all | solution.py:386
  97.3 1.5 shard_map.120
  98.8 2.8 %collective-permute-start.7 = (f32[16,128]{1,0:T(8,128)S(1)}, f32[16,128]{1,0:T(8,128)S(1)}, u32[]{:S(2)}, u32[]{:S(2)}) collective-permute-start(f32[16,128]{1,0:T(8,128)S(1)} %get-tuple-element.88), channel_id=1, source_target_pairs={{0,1},{1,2},{2,3},{3,4},{4,5},{5,6},{6,7},{7,8},{8,9},{9,10},{10,1... | collective-permute-start | bytes 24584 | tf_op jit(solution)/shard_map/ppermute | solution.py:382
  101.6 1.3 collective-permute-start.8
  102.9 0.7 shard_map.121
  103.7 0.0 collective-permute-done.7.below_ref
  103.7 2.3 %collective-permute-done.8.above_ref = f32[16,128]{1,0:T(8,128)S(1)} collective-permute-done((f32[16,128]{1,0:T(8,128)S(1)}, f32[16,128]{1,0:T(8,128)S(1)}, u32[]{:S(2)}, u32[]{:S(2)}) %collective-permute-start.8) | collective-permute-done | bytes 8224 | tf_op jit(solution)/shard_map/ppermute | solution.py:382
  106.0 14.9 %all_to_all.48.slots_ref = f32[32,5,4,128]{3,2,1,0:T(4,128)S(1)} all-to-all(f32[32,5,4,128]{3,2,1,0:T(4,128)S(1)} %shard_map.121), channel_id=1, replica_groups=mesh['gx'=8,'gy'=4,'gz'=16] {'gx','gy'}, dimensions={0} | all-to-all | bytes 655360 | tf_op jit(solution)/shard_map/all_to_all | solution.py:386
  120.9 0.7 shard_map.122
  121.6 18.1 %all_to_all.49.layers_ref = f32[16,5,4,128]{3,2,1,0:T(4,128)S(1)} all-to-all(f32[16,5,4,128]{3,2,1,0:T(4,128)S(1)} %get-tuple-element.95), channel_id=1, replica_groups=mesh['gx'=8,'gy'=4,'gz'=16] {'gz'}, dimensions={0} | all-to-all | bytes 327680 | tf_op jit(solution)/shard_map/all_to_all | solution.py:386
  139.7 0.1 shard_map.123
  139.8 16.8 %all_to_all.50.slots_ref = f32[32,5,4,128]{3,2,1,0:T(4,128)S(1)} all-to-all(f32[32,5,4,128]{3,2,1,0:T(4,128)S(1)} %shard_map.123), channel_id=1, replica_groups=mesh['gx'=8,'gy'=4,'gz'=16] {'gx','gy'}, dimensions={0} | all-to-all | bytes 655360 | tf_op jit(solution)/shard_map/all_to_all | solution.py:386
  156.6 1.6 shard_map.124
  158.2 2.9 %collective-permute-start.9 = (f32[16,128]{1,0:T(8,128)S(1)}, f32[16,128]{1,0:T(8,128)S(1)}, u32[]{:S(2)}, u32[]{:S(2)}) collective-permute-start(f32[16,128]{1,0:T(8,128)S(1)} %get-tuple-element.103), channel_id=1, source_target_pairs={{0,1},{1,2},{2,3},{3,4},{4,5},{5,6},{6,7},{7,8},{8,9},{9,10},{10,1... | collective-permute-start | bytes 24584 | tf_op jit(solution)/shard_map/ppermute | solution.py:382
  161.1 1.3 collective-permute-start.10
  162.4 0.7 shard_map.125
  163.1 0.0 collective-permute-done.9.below_ref
  163.1 2.3 %collective-permute-done.10.above_ref = f32[16,128]{1,0:T(8,128)S(1)} collective-permute-done((f32[16,128]{1,0:T(8,128)S(1)}, f32[16,128]{1,0:T(8,128)S(1)}, u32[]{:S(2)}, u32[]{:S(2)}) %collective-permute-start.10) | collective-permute-done | bytes 8224 | tf_op jit(solution)/shard_map/ppermute | solution.py:382
  165.5 14.9 %all_to_all.51.slots_ref = f32[32,5,4,128]{3,2,1,0:T(4,128)S(1)} all-to-all(f32[32,5,4,128]{3,2,1,0:T(4,128)S(1)} %shard_map.125), channel_id=1, replica_groups=mesh['gx'=8,'gy'=4,'gz'=16] {'gx','gy'}, dimensions={0} | all-to-all | bytes 655360 | tf_op jit(solution)/shard_map/all_to_all | solution.py:386
  180.4 0.7 shard_map.126
  181.1 18.1 %all_to_all.52.layers_ref = f32[16,5,4,128]{3,2,1,0:T(4,128)S(1)} all-to-all(f32[16,5,4,128]{3,2,1,0:T(4,128)S(1)} %get-tuple-element.110), channel_id=1, replica_groups=mesh['gx'=8,'gy'=4,'gz'=16] {'gz'}, dimensions={0} | all-to-all | bytes 327680 | tf_op jit(solution)/shard_map/all_to_all | solution.py:386
  199.2 0.1 shard_map.127
  199.2 16.7 %all_to_all.53.slots_ref = f32[32,5,4,128]{3,2,1,0:T(4,128)S(1)} all-to-all(f32[32,5,4,128]{3,2,1,0:T(4,128)S(1)} %shard_map.127), channel_id=1, replica_groups=mesh['gx'=8,'gy'=4,'gz'=16] {'gx','gy'}, dimensions={0} | all-to-all | bytes 655360 | tf_op jit(solution)/shard_map/all_to_all | solution.py:386
  216.0 1.7 shard_map.128
  (3 shorter events, 0.0 us)
Async XLA Ops:
  0.6 0.9 copy-start.5
  1.5 0.7 copy-start.6
  2.3 0.7 copy-start.8
  2.9 0.7 copy-start.9
  4.3 14.9 %collective-permute-start = (f32[56,128]{1,0:T(8,128)S(1)}, f32[56,128]{1,0:T(8,128)S(1)}, u32[]{:S(2)}, u32[]{:S(2)}) collective-permute-start(f32[56,128]{1,0:T(8,128)S(1)} %get-tuple-element.60.ux_ref), channel_id=1, source_target_pairs={{0,64},{64,128},{128,192},{192,256},{256,320},{320,384},{384,448},... | collective-permute-start | bytes 86024 | tf_op jit(solution)/shard_map/ppermute | solution.py:382
  8.9 10.3 %collective-permute-start.1 = (f32[56,128]{1,0:T(8,128)S(1)}, f32[56,128]{1,0:T(8,128)S(1)}, u32[]{:S(2)}, u32[]{:S(2)}) collective-permute-start(f32[56,128]{1,0:T(8,128)S(1)} %get-tuple-element.61.uy_ref), channel_id=1, source_target_pairs={{0,16},{16,32},{32,48},{1,17},{17,33},{33,49},{2,18},{18,34},{34,5... | collective-permute-start | bytes 86024 | tf_op jit(solution)/shard_map/ppermute | solution.py:382
  12.0 7.2 %collective-permute-start.2 = (f32[56,128]{1,0:T(8,128)S(1)}, f32[56,128]{1,0:T(8,128)S(1)}, u32[]{:S(2)}, u32[]{:S(2)}) collective-permute-start(f32[56,128]{1,0:T(8,128)S(1)} %get-tuple-element.62.uz_ref), channel_id=1, source_target_pairs={{0,1},{1,2},{2,3},{3,4},{4,5},{5,6},{6,7},{7,8},{8,9},{9,10},{10,1... | collective-permute-start | bytes 86024 | tf_op jit(solution)/shard_map/ppermute | solution.py:382
  15.6 1.0 copy-start.3
  16.6 1.0 copy-start.4
  17.6 0.7 copy-start.7
  19.3 29.2 %copy-start = (f32[576,576]{1,0:T(8,128)S(1)}, f32[576,576]{1,0:T(8,128)}, u32[]{:S(2)}) copy-start(f32[576,576]{1,0:T(8,128)} %inverse_ref.1) | copy-start | bytes 3981316
  19.3 29.2 %copy-start.1 = (f32[1,1,1,6,128,128]{5,4,3,2,1,0:T(8,128)S(1)}, f32[1,1,1,6,128,128]{5,4,3,2,1,0:T(8,128)}, u32[]{:S(2)}) copy-start(f32[1,1,1,6,128,128]{5,4,3,2,1,0:T(8,128)} %param.11) | copy-start | bytes 1179652
  19.3 29.2 %copy-start.2 = (f32[1,1,1,6,128,128]{5,4,3,2,1,0:T(8,128)S(1)}, f32[1,1,1,6,128,128]{5,4,3,2,1,0:T(8,128)}, u32[]{:S(2)}) copy-start(f32[1,1,1,6,128,128]{5,4,3,2,1,0:T(8,128)} %param.12) | copy-start | bytes 1179652
  19.9 8.9 %collective-permute-start.5 = (f32[48,128]{1,0:T(8,128)S(1)}, f32[48,128]{1,0:T(8,128)S(1)}, u32[]{:S(2)}, u32[]{:S(2)}) collective-permute-start(f32[48,128]{1,0:T(8,128)S(1)} %get-tuple-element.69), channel_id=1, source_target_pairs={{1,0},{2,1},{3,2},{4,3},{5,4},{6,5},{7,6},{8,7},{9,8},{10,9},{11,1... | collective-permute-start | bytes 73736 | tf_op jit(solution)/shard_map/ppermute | solution.py:382
  21.3 7.4 %collective-permute-start.3 = (f32[32,128]{1,0:T(8,128)S(1)}, f32[32,128]{1,0:T(8,128)S(1)}, u32[]{:S(2)}, u32[]{:S(2)}) collective-permute-start(f32[32,128]{1,0:T(8,128)S(1)} %get-tuple-element.67.dx_ref), channel_id=1, source_target_pairs={{64,0},{128,64},{192,128},{256,192},{320,256},{384,320},{448,384},... | collective-permute-start | bytes 49160 | tf_op jit(solution)/shard_map/ppermute | solution.py:382
  23.2 5.5 %collective-permute-start.4 = (f32[32,128]{1,0:T(8,128)S(1)}, f32[32,128]{1,0:T(8,128)S(1)}, u32[]{:S(2)}, u32[]{:S(2)}) collective-permute-start(f32[32,128]{1,0:T(8,128)S(1)} %get-tuple-element.68.dy_ref), channel_id=1, source_target_pairs={{16,0},{32,16},{48,32},{17,1},{33,17},{49,33},{18,2},{34,18},{50,3... | collective-permute-start | bytes 49160 | tf_op jit(solution)/shard_map/ppermute | solution.py:382
  24.5 5.1 %collective-permute-start.6 = (f32[16,128]{1,0:T(8,128)S(1)}, f32[16,128]{1,0:T(8,128)S(1)}, u32[]{:S(2)}, u32[]{:S(2)}) collective-permute-start(f32[16,128]{1,0:T(8,128)S(1)} %get-tuple-element.72), channel_id=1, source_target_pairs={{0,1},{1,2},{2,3},{3,4},{4,5},{5,6},{6,7},{7,8},{8,9},{9,10},{10,1... | collective-permute-start | bytes 24584 | tf_op jit(solution)/shard_map/ppermute | solution.py:382
  98.8 4.9 %collective-permute-start.7 = (f32[16,128]{1,0:T(8,128)S(1)}, f32[16,128]{1,0:T(8,128)S(1)}, u32[]{:S(2)}, u32[]{:S(2)}) collective-permute-start(f32[16,128]{1,0:T(8,128)S(1)} %get-tuple-element.88), channel_id=1, source_target_pairs={{0,1},{1,2},{2,3},{3,4},{4,5},{5,6},{6,7},{7,8},{8,9},{9,10},{10,1... | collective-permute-start | bytes 24584 | tf_op jit(solution)/shard_map/ppermute | solution.py:382
  101.6 4.4 %collective-permute-start.8 = (f32[16,128]{1,0:T(8,128)S(1)}, f32[16,128]{1,0:T(8,128)S(1)}, u32[]{:S(2)}, u32[]{:S(2)}) collective-permute-start(f32[16,128]{1,0:T(8,128)S(1)} %get-tuple-element.89), channel_id=1, source_target_pairs={{1,0},{2,1},{3,2},{4,3},{5,4},{6,5},{7,6},{8,7},{9,8},{10,9},{11,1... | collective-permute-start | bytes 24584 | tf_op jit(solution)/shard_map/ppermute | solution.py:382
  158.2 4.9 %collective-permute-start.9 = (f32[16,128]{1,0:T(8,128)S(1)}, f32[16,128]{1,0:T(8,128)S(1)}, u32[]{:S(2)}, u32[]{:S(2)}) collective-permute-start(f32[16,128]{1,0:T(8,128)S(1)} %get-tuple-element.103), channel_id=1, source_target_pairs={{0,1},{1,2},{2,3},{3,4},{4,5},{5,6},{6,7},{7,8},{8,9},{9,10},{10,1... | collective-permute-start | bytes 24584 | tf_op jit(solution)/shard_map/ppermute | solution.py:382
  161.1 4.4 %collective-permute-start.10 = (f32[16,128]{1,0:T(8,128)S(1)}, f32[16,128]{1,0:T(8,128)S(1)}, u32[]{:S(2)}, u32[]{:S(2)}) collective-permute-start(f32[16,128]{1,0:T(8,128)S(1)} %get-tuple-element.104), channel_id=1, source_target_pairs={{1,0},{2,1},{3,2},{4,3},{5,4},{6,5},{7,6},{8,7},{9,8},{10,9},{11,1... | collective-permute-start | bytes 24584 | tf_op jit(solution)/shard_map/ppermute | solution.py:382

commit v8 on v7

--- a/solution.py
+++ b/solution.py
@@ -73,17 +73,17 @@
     return jnp.concatenate(parts, axis=1)
 
 
-def partner_rows(messages):
-    return [m[CASES:CASES + 1, :] for m in messages]
-
-
-def inverse_rows(messages):
-    return [m[CASES + 1:CASES + 2, :] for m in messages]
-
-
-def apply_dense(field, messages, high_ref, low_ref):
-    loads = lower_changed(field, inverse_rows(messages))
-    return loads, lower_changed(dot_split(loads, high_ref, low_ref), partner_rows(messages))
+RESIDUAL, SHOWN, SEARCH, APPLIED, LOAD, REST = (slice(CASES * i, CASES * (i + 1)) for i in range(6))
+ORDERS = 6 * CASES
+STATE = (ORDERS + 8, WIDE)
+
+
+def apply_dense(field, state_ref, high_ref, low_ref):
+    orders = state_ref[ORDERS:ORDERS + 8, :]
+    partner = [face(orders[0:1, :], d) for d in range(3)]
+    inverse = [face(orders[1:2, :], d) for d in range(3)]
+    loads = lower_changed(field, inverse)
+    return lower_changed(dot_split(loads, high_ref, low_ref), partner)
 
 
 def position():
@@ -113,20 +113,18 @@
     return jnp.concatenate([slots_ref[spot, q] for q in range(4)], axis=0)
 
 
-def target_rows(ids):
-    lanes = lax.broadcasted_iota(jnp.int32, (8, FD), 1) % SUBS
-    target = jnp.full((8, FD), -1, jnp.int32)
-    for r in range(24):
-        target = jnp.where(lanes == r, (r % 3) * QPAD + ids[0, 0, 0, r // 3], target)
-    return target.astype(F32)
-
-
-def prep_kernel(ids, rhs_ref, partner_ref, coupling_ref, *message_refs):
+def target_rows(ids_row):
+    row = lax.broadcasted_iota(jnp.int32, (8, FD), 1) % SUBS
+    ids = take(jnp.broadcast_to(ids_row.astype(F32), (8, FD)), jnp.minimum(row // 3, 7))
+    return jnp.where(row < 24, ids + (row % 3 * QPAD).astype(F32), -1.0)
+
+
+def prep_kernel(table_ref, rhs_ref, coupling_ref, *message_refs):
     _, _, there = position()
-    target = target_rows(ids)
+    target = target_rows(table_ref[0, 0, 3])
     for d in range(3):
         up_ref, down_ref = message_refs[d], message_refs[3 + d]
-        row = partner_ref[0, 0, d, :, :]
+        row = table_ref[0, 0, d]
         up_ref[0:CASES, :] = rhs_ref[d] * there[2 * d + 1].astype(F32)
         wanted = lax.broadcasted_iota(jnp.int32, (FD, FD), 0)
         hits = (wanted == jnp.broadcast_to(row, (FD, FD))).astype(F32).astype(BF16)
@@ -140,7 +138,7 @@
         down_ref[24:32, :] = target
 
 
-def put_dense(pairs, diag_ref, couple_ref, high_ref, low_ref):
+def put_dense(table, diag_ref, couple_ref, high_ref, low_ref):
     high_ref[...] = jnp.zeros_like(high_ref)
     low_ref[...] = jnp.zeros_like(low_ref)
 
@@ -152,34 +150,36 @@
     for f in range(6):
         put(f * FD, f * FD, diag_ref[f])
     for k in range(6):
-        first = pl.multiple_of(pairs[0, 0, 0, 0, k] * FD, FD)
-        second = pl.multiple_of(pairs[0, 0, 0, 1, k] * FD, FD)
+        first = pl.multiple_of(table[0, 0, 4, 0, k] * FD, FD)
+        second = pl.multiple_of(table[0, 0, 5, 0, k] * FD, FD)
         block = couple_ref[k]
         put(second, first, block)
         put(first, second, block.T)
 
 
-def dense_kernel(pairs, diag_ref, couple_ref, high_ref, low_ref):
-    put_dense(pairs, diag_ref, couple_ref, high_ref, low_ref)
-
-
-def start_kernel(ux_ref, uy_ref, uz_ref, mx_ref, my_ref, mz_ref, dz_ref, dh_ref, dl_ref, field_ref,
-                 shown_ref, down_ref, up_ref):
+def dense_kernel(table, diag_ref, couple_ref, high_ref, low_ref):
+    put_dense(table, diag_ref, couple_ref, high_ref, low_ref)
+
+
+def start_kernel(ux_ref, uy_ref, uz_ref, mx_ref, my_ref, mz_ref, dz_ref, dh_ref, dl_ref, state_ref,
+                 down_ref, up_ref):
     own, messages = (ux_ref, uy_ref, uz_ref), (mx_ref, my_ref, mz_ref)
+    state_ref[...] = jnp.zeros_like(state_ref)
     parts = []
     for d in range(3):
         parts += [messages[d][0:CASES, :], own[d][0:CASES, :]]
+        state_ref[ORDERS:ORDERS + 8, d * FD:(d + 1) * FD] = messages[d][CASES:CASES + 8, :]
     field = jnp.concatenate(parts, axis=1)
-    field_ref[...] = field
-    _, shown = apply_dense(field, messages, dh_ref, dl_ref)
-    shown_ref[...] = shown
+    state_ref[RESIDUAL, :] = field
+    shown = apply_dense(field, state_ref, dh_ref, dl_ref)
+    state_ref[SHOWN, :] = shown
     down_ref[0:CASES, :] = face(shown, 4)
     down_ref[CASES:CASES + 32, :] = dz_ref[...]
     up_ref[...] = face(shown, 5)
 
 
 def joint_kernel(ux_ref, uy_ref, uz_ref, mx_ref, my_ref, mz_ref, dx_ref, dy_ref, dz_ref, nx_ref, ny_ref,
-                 over_ref, shown_ref, residual_ref, gh_ref, gl_ref, pick_ref, out_ref, pad):
+                 over_ref, state_ref, gh_ref, gl_ref, pick_ref, out_ref, pad):
     _, _, there = position()
     own, messages, lower = (ux_ref, uy_ref, uz_ref), (mx_ref, my_ref, mz_ref), (dx_ref, dy_ref, dz_ref)
     above = (nx_ref[...], ny_ref[...], over_ref[CASES:CASES + 32, :])
@@ -209,11 +209,11 @@
             wanted = jnp.where(lanes // SUBS == n % 4, targets[n], wanted)
         wanted = jnp.broadcast_to(wanted[0:1, :].astype(jnp.int32), (3 * QPAD, FD))
         pick_ref[:, half * FD:(half + 1) * FD] = (rows == wanted).astype(F32).astype(BF16)
-    sum_kernel(shown_ref, residual_ref, gh_ref, gl_ref, pick_ref, out_ref)
-
-
-def late_kernel(pairs, diag_ref, couple_ref, inverse_ref, _, fh_ref, fl_ref, kh_ref, kl_ref, square):
-    put_dense(pairs, diag_ref, couple_ref, fh_ref, fl_ref)
+    sum_kernel(state_ref, gh_ref, gl_ref, pick_ref, out_ref)
+
+
+def late_kernel(table, diag_ref, couple_ref, inverse_ref, _, fh_ref, fl_ref, kh_ref, kl_ref, square):
+    put_dense(table, diag_ref, couple_ref, fh_ref, fl_ref)
     square[...] = jnp.zeros_like(square)
     for p in range(3):
         for q in range(3):
@@ -243,16 +243,16 @@
             out_ref[2 * c + b // 3, 4, b % 3:b % 3 + 1, :] = block[c:c + 1, :]
 
 
-def sum_kernel(shown_ref, residual_ref, gh_ref, gl_ref, pick_ref, out_ref):
+def sum_kernel(state_ref, gh_ref, gl_ref, pick_ref, out_ref):
     here, _, there = position()
-    shown = shown_ref[...]
+    shown = state_ref[SHOWN, :]
     share = 0.25 * shown * mask_row(there)
     high, low = halves(share)
     both = dot_across(jnp.concatenate([high, low], 0), gh_ref[...])
     corner = both[:CASES] + both[CASES:] + dot_across(high, gl_ref[...])
     high, low = halves(corner)
     both = dot_across(jnp.concatenate([high, low], 0), pick_ref[...])
-    norm = jnp.sum(face_sum(share * residual_ref[...]), axis=1, keepdims=True)
+    norm = jnp.sum(face_sum(share * state_ref[RESIDUAL, :]), axis=1, keepdims=True)
     out_ref[...] = jnp.zeros_like(out_ref)
     put_payload(out_ref, both[:CASES] + both[CASES:], [norm])
     for f, by in enumerate(steps()):
@@ -271,27 +271,23 @@
             put_rows(out_ref, layer + by, flexed_ref[:, f * FD:(f + 1) * FD])
 
 
-def flex_kernel(first, mx_ref, my_ref, mz_ref, shown_ref, slots_ref, below_ref, above_ref, fh_ref,
-                fl_ref, *rest):
-    rest = list(rest)
-    if not first:
-        search_ref, applied_ref = rest[:2]
-        rest = rest[2:]
-    z_ref, flexed_ref, out_ref, turn = rest
+def flex_kernel(first, state_ref, slots_ref, below_ref, above_ref, fh_ref, fl_ref, z_ref, flexed_ref,
+                out_ref, turn):
     here, layer, there = position()
     across = []
     for f, by in enumerate(steps()):
         across.append(take_rows(slots_ref, jnp.where(there[f], here + by, here)))
     across += [below_ref[...], above_ref[0:CASES, :]]
-    z = 0.25 * (shown_ref[...] + jnp.concatenate(across, axis=1)) * mask_row(there)
+    z = 0.25 * (state_ref[SHOWN, :] + jnp.concatenate(across, axis=1)) * mask_row(there)
     z_ref[...] = z
-    _, flexed = apply_dense(z, (mx_ref, my_ref, mz_ref), fh_ref, fl_ref)
+    flexed = apply_dense(z, state_ref, fh_ref, fl_ref)
     flexed_ref[...] = flexed
     turn[...] = jnp.zeros_like(turn)
     turn[0:CASES, :] = face_sum(z * flexed)
     if not first:
         turn[CASES:2 * CASES, :] = (
-            face_sum(z * applied_ref[...], (1, 3, 5)) + face_sum(search_ref[...] * flexed)
+            face_sum(z * state_ref[APPLIED, :], (1, 3, 5))
+            + face_sum(state_ref[SEARCH, :] * flexed)
         )
     sums = jnp.sum(turn[...].T, axis=0, keepdims=True)
     total = jnp.sum(slots_ref[:, 4], axis=0)
@@ -312,15 +308,9 @@
             put_rows(out_ref, here + by, flexed_ref[:, f * FD:(f + 1) * FD])
 
 
-def step_kernel(first, last, slots_ref, layers_ref, flexed_ref, z_ref,
-                residual_ref, kh_ref, kl_ref, gh_ref, gl_ref, pick_ref, *rest):
-    rest, whole = list(rest[:-1]), rest[-1]
-    if not last:
-        mx_ref, my_ref, mz_ref, dh_ref, dl_ref = rest[:5]
-        rest = rest[5:]
-    if not first:
-        search_ref, applied_ref, load_ref, scale_ref, iterate_ref = rest[:5]
-        rest = rest[5:]
+def step_kernel(first, last, slots_ref, layers_ref, flexed_ref, z_ref, state_ref, kh_ref, kl_ref,
+                gh_ref, gl_ref, pick_ref, *rest):
+    rest, whole = rest[:-1], rest[-1]
     here, layer, there = position()
     across = []
     for f, by in enumerate(steps()):
@@ -342,38 +332,41 @@
     lanes = lax.broadcasted_iota(jnp.int32, load.shape, 1) % QPAD
     load = jnp.where(lanes < 192, load, 0.0)
     if not first:
-        beta = norm / scale_ref[:, 0:1]
-        energy = energy + beta * cross + beta * beta * scale_ref[:, 1:2]
-        applied = applied + beta * applied_ref[...]
-        search = search + beta * search_ref[...]
-        load = load + beta * load_ref[...]
+        scale = state_ref[REST, 0:FD]
+        beta = norm / scale[:, 0:1]
+        energy = energy + beta * cross + beta * beta * scale[:, 1:2]
+        applied = applied + beta * state_ref[APPLIED, :]
+        search = search + beta * state_ref[SEARCH, :]
+        load = load + beta * state_ref[LOAD, :]
     coarse = dot_split(load, kh_ref, kl_ref)
     step = norm / (energy + jnp.sum(load * coarse, axis=1, keepdims=True))
     corner = dot_exact(coarse, pick_ref[...])
     correction = dot_split(corner, gh_ref, gl_ref) * mask
-    residual = residual_ref[...] - step * (applied + correction)
+    residual = state_ref[RESIDUAL, :] - step * (applied + correction)
     moved = step * search
     if last:
         multipliers_ref, left_ref = rest
         for d in range(3):
-            multipliers_ref[d] = iterate_ref[d] + face(moved, 2 * d + 1)
+            before = state_ref[REST, (d + 1) * FD:(d + 2) * FD]
+            multipliers_ref[d] = before + face(moved, 2 * d + 1)
             left_ref[d] = face(residual, 2 * d + 1)
         return
-    search_out, applied_out, load_out, scale_out, iterate_out, residual_out, shown_ref = rest[:7]
-    down_ref, up_ref = rest[7:]
-    search_out[...] = search
-    applied_out[...] = applied
-    load_out[...] = load
-    residual_out[...] = residual
-    lanes = lax.broadcasted_iota(jnp.int32, (CASES, FD), 1)
-    scale_out[...] = jnp.where(lanes == 0, norm, energy)
-    for d in range(3):
-        moved_face = face(moved, 2 * d + 1)
-        iterate_out[d] = moved_face if first else iterate_ref[d] + moved_face
-    _, shown = apply_dense(residual, (mx_ref, my_ref, mz_ref), dh_ref, dl_ref)
-    shown_ref[...] = shown
+    dh_ref, dl_ref, new_ref, down_ref, up_ref = rest
+    new_ref[RESIDUAL, :] = residual
+    shown = apply_dense(residual, state_ref, dh_ref, dl_ref)
+    new_ref[SHOWN, :] = shown
     down_ref[...] = face(shown, 4)
     up_ref[...] = face(shown, 5)
+    new_ref[SEARCH, :] = search
+    new_ref[APPLIED, :] = applied
+    new_ref[LOAD, :] = load
+    lanes = lax.broadcasted_iota(jnp.int32, (CASES, FD), 1)
+    scale = jnp.where(lanes == 0, norm, energy)
+    parts = [scale]
+    for d in range(3):
+        parts.append(state_ref[REST, (d + 1) * FD:(d + 2) * FD] + face(moved, 2 * d + 1))
+    new_ref[REST, :] = jnp.concatenate(parts + [scale, scale], axis=1)
+    new_ref[ORDERS:ORDERS + 8, :] = state_ref[ORDERS:ORDERS + 8, :]
 
 
 def passed_along(shard, axis, by):
@@ -405,25 +398,32 @@
     square = (WIDE, WIDE)
     wide = (CASES, WIDE)
 
+    width = ((0, 0),) * 4
+    table = jnp.concatenate(
+        [
+            jnp.swapaxes(partner, 2, 3),
+            jnp.pad(coarse_ids[:, :, :, None, :], width + ((0, FD - 8),)),
+            jnp.pad(jnp.transpose(face_pairs, (0, 1, 4, 2, 3)), width + ((0, FD - 6),)),
+        ],
+        axis=2,
+    )
     *ups, dx, dy, dz = call(
         prep_kernel, [((56, FD), F32)] * 3 + [((32, FD), F32)] * 3,
-        [coarse_ids, rhs, jnp.swapaxes(partner, 2, 3), coupling], specs=[SMEM],
+        [table, rhs, coupling],
     )
     messages = [passed_along(m, a, 1) for m, a in zip(ups, AXES)]
     above = [passed_along(m, a, -1) for m, a in zip((dx, dy), AXES)]
-    pairs = jnp.swapaxes(face_pairs, 3, 4)
     blocks = [b.reshape(6, FD, FD) for b in (dirichlet_diag, dirichlet_couple, flex_diag, flex_couple)]
     dirichlet = call(
-        dense_kernel, [(square, BF16)] * 2, [pairs] + blocks[:2], specs=[SMEM]
-    )
-    residual, shown, down, up = call(
+        dense_kernel, [(square, BF16)] * 2, [table] + blocks[:2], specs=[SMEM]
+    )
+    state, down, up = call(
         start_kernel,
-        [(wide, F32)] * 2 + [((CASES + 32, FD), F32), ((CASES, FD), F32)],
+        [(STATE, F32), ((CASES + 32, FD), F32), ((CASES, FD), F32)],
         [*ups, *messages, dz, *dirichlet],
     )
     stacked = (plane, 5, 4, FD)
 
-    kept = []
     for iteration in range(ITERS):
         first, last = iteration == 0, iteration + 1 == ITERS
         below = passed_along(up, "gz", 1)
@@ -432,17 +432,17 @@
             *joint, slots = call(
                 joint_kernel,
                 [((QPAD, WIDE), BF16)] * 2 + [((3 * QPAD, QPAD), BF16), (stacked, F32)],
-                [*ups, *messages, dx, dy, dz, *above, over, shown, residual],
+                [*ups, *messages, dx, dy, dz, *above, over, state],
                 scratch=[pltpu.VMEM((QPAD, WIDE), F32)],
             )
         else:
-            (slots,) = call(sum_kernel, [(stacked, F32)], [shown, residual, *joint])
+            (slots,) = call(sum_kernel, [(stacked, F32)], [state, *joint])
         slots, below, over = lax.optimization_barrier((slots, below, over))
         slots = swapped(slots, PLANE)
         if first:
             late = call(
                 late_kernel, [(square, BF16)] * 4,
-                [pairs] + blocks[2:] + [coarse_inverse, slots],
+                [table] + blocks[2:] + [coarse_inverse, slots],
                 specs=[SMEM] + [VMEM] * 3 + [pl.BlockSpec(memory_space=pl.ANY)],
                 scratch=[pltpu.VMEM(square, F32)],
             )
@@ -450,25 +450,20 @@
         z, flexed, layers = call(
             functools.partial(flex_kernel, first),
             [(wide, F32), (wide, F32), ((gz, 5, 4, FD), F32)],
-            [*messages, shown, slots, below, over, *flex, *kept[:2]],
+            [state, slots, below, over, *flex],
             scratch=[pltpu.VMEM((FD, FD), F32)],
         )
         layers = swapped(layers, "gz")
         (slots,) = call(share_kernel, [(stacked, F32)], [layers, flexed])
         slots = swapped(slots, PLANE)
-        common = [slots, layers, flexed, z, residual, *inverse, *joint]
+        common = [slots, layers, flexed, z, state, *inverse, *joint]
         kernel = functools.partial(step_kernel, first, last)
         scratch = [pltpu.VMEM(wide, F32)]
         if last:
-            multipliers, left = call(
-                kernel, [((3, CASES, FD), F32)] * 2, common + kept, scratch=scratch
-            )
+            multipliers, left = call(kernel, [((3, CASES, FD), F32)] * 2, common, scratch=scratch)
             break
-        *kept, residual, shown, down, up = call(
-            kernel,
-            [(wide, F32)] * 3 + [((CASES, FD), F32), ((3, CASES, FD), F32), (wide, F32), (wide, F32)]
-            + [((CASES, FD), F32)] * 2,
-            common + [*messages, *dirichlet] + kept, scratch=scratch,
+        state, down, up = call(
+            kernel, [(STATE, F32)] + [((CASES, FD), F32)] * 2, common + [*dirichlet], scratch=scratch
         )
     return multipliers.reshape(jump_rhs.shape), left.reshape(jump_rhs.shape)
 

time: 219 us -> 217 us (level)
    unnamed x20 -> x14, local copies, waits for them, and re-layouts: 5.63 us -> 3.62 us
  transfers between devices with their start and end apart: 11 -> 11, of which waited for: 2 -> 2; matrix products, arithmetic and copies ran while one was open for 0% -> 0% of each run, Pallas kernels for 1% -> 2%
where the time goes in v8:
time: 217 us; the launch traced here: 216 us
  blocking collectives  165 us (76%)
  starting transfers between devices  28.4 us (13%)
  Pallas kernels  12.8 us (6%)
  waiting for transfers between devices  4.72 us (2%)
  local copies, waits for them, and re-layouts  3.62 us (2%)
    all_to_all x9, blocking collectives, swapped(): return lax.all_to_all(slots, axes, 0, 0)  165 us
    ppermute x11, starting transfers between devices, passed_along(): return lax.ppermute(shard, axis, pairs)  28.4 us
    pallas_call x16, Pallas kernels, call(): pl.pallas_call(kernel, out_shape=[jax.ShapeDtypeStruct(shape, dtype) for...  12.8 us
    ppermute x11, waiting for transfers between devices, passed_along(): return lax.ppermute(shard, axis, pairs)  4.72 us
  transfers between devices with their start and end apart: 11, of which 2 were waited for; matrix products, arithmetic and copies ran while one was open for 0% of the time, Pallas kernels for 2%

profile of v8, /device:TPU:1, one launch (start us, length us, event | category | flops | bytes accessed | tf_op | source)
XLA Modules:
  0.0 215.9 jit_solution(15072840511356282176)
XLA Ops:
  0.6 0.7 pad_add_fusion.table_ref.table
  1.3 0.0 copy-start.5
  1.4 0.9 copy-done.5
  2.2 0.0 copy-start.6
  2.2 0.7 copy-done.6
  3.0 0.2 shard_map.113
  3.1 4.6 %collective-permute-start = (f32[56,128]{1,0:T(8,128)S(1)}, f32[56,128]{1,0:T(8,128)S(1)}, u32[]{:S(2)}, u32[]{:S(2)}) collective-permute-start(f32[56,128]{1,0:T(8,128)S(1)} %get-tuple-element.47.ux_ref), channel_id=1, source_target_pairs={{0,64},{64,128},{128,192},{192,256},{256,320},{320,384},{384,448},... | collective-permute-start | bytes 86024 | tf_op jit(solution)/shard_map/ppermute | solution.py:375
  7.8 3.1 %collective-permute-start.1 = (f32[56,128]{1,0:T(8,128)S(1)}, f32[56,128]{1,0:T(8,128)S(1)}, u32[]{:S(2)}, u32[]{:S(2)}) collective-permute-start(f32[56,128]{1,0:T(8,128)S(1)} %get-tuple-element.48.uy_ref), channel_id=1, source_target_pairs={{0,16},{16,32},{32,48},{1,17},{17,33},{33,49},{2,18},{18,34},{34,5... | collective-permute-start | bytes 86024 | tf_op jit(solution)/shard_map/ppermute | solution.py:375
  10.9 3.5 %collective-permute-start.2 = (f32[56,128]{1,0:T(8,128)S(1)}, f32[56,128]{1,0:T(8,128)S(1)}, u32[]{:S(2)}, u32[]{:S(2)}) collective-permute-start(f32[56,128]{1,0:T(8,128)S(1)} %get-tuple-element.49.uz_ref), channel_id=1, source_target_pairs={{0,1},{1,2},{2,3},{3,4},{4,5},{5,6},{6,7},{7,8},{8,9},{9,10},{10,1... | collective-permute-start | bytes 86024 | tf_op jit(solution)/shard_map/ppermute | solution.py:375
  14.4 0.0 copy-start.1
  14.4 1.0 copy-done.1
  15.4 0.0 copy-start.2
  15.4 1.0 copy-done.2
  16.4 1.0 shard_map.114
  17.4 0.0 collective-permute-done.mx_ref
  17.4 0.0 collective-permute-done.1.my_ref
  17.4 0.0 collective-permute-done.2.mz_ref
  17.5 0.0 copy-start
  17.5 0.6 shard_map.115
  18.0 0.0 copy-start.3
  18.0 0.0 copy-start.4
  18.0 1.4 collective-permute-start.5
  19.5 1.9 collective-permute-start.3
  21.4 1.3 collective-permute-start.4
  22.7 4.2 %collective-permute-start.6 = (f32[16,128]{1,0:T(8,128)S(1)}, f32[16,128]{1,0:T(8,128)S(1)}, u32[]{:S(2)}, u32[]{:S(2)}) collective-permute-start(f32[16,128]{1,0:T(8,128)S(1)} %get-tuple-element.58), channel_id=1, source_target_pairs={{0,1},{1,2},{2,3},{3,4},{4,5},{5,6},{6,7},{7,8},{8,9},{9,10},{10,1... | collective-permute-start | bytes 24584 | tf_op jit(solution)/shard_map/ppermute | solution.py:375
  26.9 0.0 collective-permute-done.3.nx_ref
  26.9 0.0 collective-permute-done.4.ny_ref
  26.9 0.0 collective-permute-done.5.over_ref.above_ref
  26.9 0.8 shard_map.116
  27.8 0.0 collective-permute-done.6.below_ref
  27.8 18.9 %all_to_all.45._.slots_ref = f32[32,5,4,128]{3,2,1,0:T(4,128)S(1)} all-to-all(f32[32,5,4,128]{3,2,1,0:T(4,128)S(1)} %get-tuple-element.59), channel_id=1, replica_groups=mesh['gx'=8,'gy'=4,'gz'=16] {'gx','gy'}, dimensions={0} | all-to-all | bytes 655360 | tf_op jit(solution)/shard_map/all_to_all | solution.py:379
  46.6 0.0 copy-done
  46.6 0.0 copy-done.3
  46.6 0.0 copy-done.4
  46.6 1.6 shard_map.117
  48.2 0.7 shard_map.118
  48.9 29.7 %all_to_all.46.layers_ref = f32[16,5,4,128]{3,2,1,0:T(4,128)S(1)} all-to-all(f32[16,5,4,128]{3,2,1,0:T(4,128)S(1)} %get-tuple-element.64), channel_id=1, replica_groups=mesh['gx'=8,'gy'=4,'gz'=16] {'gz'}, dimensions={0} | all-to-all | bytes 327680 | tf_op jit(solution)/shard_map/all_to_all | solution.py:379
  78.7 0.1 shard_map.119
  78.7 16.7 %all_to_all.47.slots_ref = f32[32,5,4,128]{3,2,1,0:T(4,128)S(1)} all-to-all(f32[32,5,4,128]{3,2,1,0:T(4,128)S(1)} %shard_map.119), channel_id=1, replica_groups=mesh['gx'=8,'gy'=4,'gz'=16] {'gx','gy'}, dimensions={0} | all-to-all | bytes 655360 | tf_op jit(solution)/shard_map/all_to_all | solution.py:379
  95.5 1.5 shard_map.120
  97.0 2.8 %collective-permute-start.7 = (f32[16,128]{1,0:T(8,128)S(1)}, f32[16,128]{1,0:T(8,128)S(1)}, u32[]{:S(2)}, u32[]{:S(2)}) collective-permute-start(f32[16,128]{1,0:T(8,128)S(1)} %get-tuple-element.73), channel_id=1, source_target_pairs={{0,1},{1,2},{2,3},{3,4},{4,5},{5,6},{6,7},{7,8},{8,9},{9,10},{10,1... | collective-permute-start | bytes 24584 | tf_op jit(solution)/shard_map/ppermute | solution.py:375
  99.9 1.3 collective-permute-start.8
  101.2 0.7 shard_map.121
  101.9 0.0 collective-permute-done.7.below_ref
  101.9 2.3 %collective-permute-done.8.above_ref = f32[16,128]{1,0:T(8,128)S(1)} collective-permute-done((f32[16,128]{1,0:T(8,128)S(1)}, f32[16,128]{1,0:T(8,128)S(1)}, u32[]{:S(2)}, u32[]{:S(2)}) %collective-permute-start.8) | collective-permute-done | bytes 8224 | tf_op jit(solution)/shard_map/ppermute | solution.py:375
  104.3 14.9 %all_to_all.48.slots_ref = f32[32,5,4,128]{3,2,1,0:T(4,128)S(1)} all-to-all(f32[32,5,4,128]{3,2,1,0:T(4,128)S(1)} %shard_map.121), channel_id=1, replica_groups=mesh['gx'=8,'gy'=4,'gz'=16] {'gx','gy'}, dimensions={0} | all-to-all | bytes 655360 | tf_op jit(solution)/shard_map/all_to_all | solution.py:379
  119.2 0.7 shard_map.122
  119.9 18.1 %all_to_all.49.layers_ref = f32[16,5,4,128]{3,2,1,0:T(4,128)S(1)} all-to-all(f32[16,5,4,128]{3,2,1,0:T(4,128)S(1)} %get-tuple-element.78), channel_id=1, replica_groups=mesh['gx'=8,'gy'=4,'gz'=16] {'gz'}, dimensions={0} | all-to-all | bytes 327680 | tf_op jit(solution)/shard_map/all_to_all | solution.py:379
  138.0 0.1 shard_map.123
  138.0 16.7 %all_to_all.50.slots_ref = f32[32,5,4,128]{3,2,1,0:T(4,128)S(1)} all-to-all(f32[32,5,4,128]{3,2,1,0:T(4,128)S(1)} %shard_map.123), channel_id=1, replica_groups=mesh['gx'=8,'gy'=4,'gz'=16] {'gx','gy'}, dimensions={0} | all-to-all | bytes 655360 | tf_op jit(solution)/shard_map/all_to_all | solution.py:379
  154.8 1.6 shard_map.124
  156.4 2.9 %collective-permute-start.9 = (f32[16,128]{1,0:T(8,128)S(1)}, f32[16,128]{1,0:T(8,128)S(1)}, u32[]{:S(2)}, u32[]{:S(2)}) collective-permute-start(f32[16,128]{1,0:T(8,128)S(1)} %get-tuple-element.82), channel_id=1, source_target_pairs={{0,1},{1,2},{2,3},{3,4},{4,5},{5,6},{6,7},{7,8},{8,9},{9,10},{10,1... | collective-permute-start | bytes 24584 | tf_op jit(solution)/shard_map/ppermute | solution.py:375
  159.3 1.3 collective-permute-start.10
  160.6 0.7 shard_map.125
  161.3 0.0 collective-permute-done.9.below_ref
  161.3 2.3 %collective-permute-done.10.above_ref = f32[16,128]{1,0:T(8,128)S(1)} collective-permute-done((f32[16,128]{1,0:T(8,128)S(1)}, f32[16,128]{1,0:T(8,128)S(1)}, u32[]{:S(2)}, u32[]{:S(2)}) %collective-permute-start.10) | collective-permute-done | bytes 8224 | tf_op jit(solution)/shard_map/ppermute | solution.py:375
  163.7 14.9 %all_to_all.51.slots_ref = f32[32,5,4,128]{3,2,1,0:T(4,128)S(1)} all-to-all(f32[32,5,4,128]{3,2,1,0:T(4,128)S(1)} %shard_map.125), channel_id=1, replica_groups=mesh['gx'=8,'gy'=4,'gz'=16] {'gx','gy'}, dimensions={0} | all-to-all | bytes 655360 | tf_op jit(solution)/shard_map/all_to_all | solution.py:379
  178.6 0.7 shard_map.126
  179.3 18.1 %all_to_all.52.layers_ref = f32[16,5,4,128]{3,2,1,0:T(4,128)S(1)} all-to-all(f32[16,5,4,128]{3,2,1,0:T(4,128)S(1)} %get-tuple-element.87), channel_id=1, replica_groups=mesh['gx'=8,'gy'=4,'gz'=16] {'gz'}, dimensions={0} | all-to-all | bytes 327680 | tf_op jit(solution)/shard_map/all_to_all | solution.py:379
  197.4 0.1 shard_map.127
  197.5 16.7 %all_to_all.53.slots_ref = f32[32,5,4,128]{3,2,1,0:T(4,128)S(1)} all-to-all(f32[32,5,4,128]{3,2,1,0:T(4,128)S(1)} %shard_map.127), channel_id=1, replica_groups=mesh['gx'=8,'gy'=4,'gz'=16] {'gx','gy'}, dimensions={0} | all-to-all | bytes 655360 | tf_op jit(solution)/shard_map/all_to_all | solution.py:379
  214.2 1.7 shard_map.128
Async XLA Ops:
  1.3 0.9 copy-start.5
  2.2 0.7 copy-start.6
  3.1 14.3 %collective-permute-start = (f32[56,128]{1,0:T(8,128)S(1)}, f32[56,128]{1,0:T(8,128)S(1)}, u32[]{:S(2)}, u32[]{:S(2)}) collective-permute-start(f32[56,128]{1,0:T(8,128)S(1)} %get-tuple-element.47.ux_ref), channel_id=1, source_target_pairs={{0,64},{64,128},{128,192},{192,256},{256,320},{320,384},{384,448},... | collective-permute-start | bytes 86024 | tf_op jit(solution)/shard_map/ppermute | solution.py:375
  7.8 9.7 %collective-permute-start.1 = (f32[56,128]{1,0:T(8,128)S(1)}, f32[56,128]{1,0:T(8,128)S(1)}, u32[]{:S(2)}, u32[]{:S(2)}) collective-permute-start(f32[56,128]{1,0:T(8,128)S(1)} %get-tuple-element.48.uy_ref), channel_id=1, source_target_pairs={{0,16},{16,32},{32,48},{1,17},{17,33},{33,49},{2,18},{18,34},{34,5... | collective-permute-start | bytes 86024 | tf_op jit(solution)/shard_map/ppermute | solution.py:375
  10.9 6.6 %collective-permute-start.2 = (f32[56,128]{1,0:T(8,128)S(1)}, f32[56,128]{1,0:T(8,128)S(1)}, u32[]{:S(2)}, u32[]{:S(2)}) collective-permute-start(f32[56,128]{1,0:T(8,128)S(1)} %get-tuple-element.49.uz_ref), channel_id=1, source_target_pairs={{0,1},{1,2},{2,3},{3,4},{4,5},{5,6},{6,7},{7,8},{8,9},{9,10},{10,1... | collective-permute-start | bytes 86024 | tf_op jit(solution)/shard_map/ppermute | solution.py:375
  14.4 1.0 copy-start.1
  15.4 1.0 copy-start.2
  17.5 29.2 %copy-start = (f32[576,576]{1,0:T(8,128)S(1)}, f32[576,576]{1,0:T(8,128)}, u32[]{:S(2)}) copy-start(f32[576,576]{1,0:T(8,128)} %inverse_ref.1) | copy-start | bytes 3981316
  18.0 28.6 %copy-start.3 = (f32[1,1,1,6,128,128]{5,4,3,2,1,0:T(8,128)S(1)}, f32[1,1,1,6,128,128]{5,4,3,2,1,0:T(8,128)}, u32[]{:S(2)}) copy-start(f32[1,1,1,6,128,128]{5,4,3,2,1,0:T(8,128)} %param.11) | copy-start | bytes 1179652
  18.0 28.6 %copy-start.4 = (f32[1,1,1,6,128,128]{5,4,3,2,1,0:T(8,128)S(1)}, f32[1,1,1,6,128,128]{5,4,3,2,1,0:T(8,128)}, u32[]{:S(2)}) copy-start(f32[1,1,1,6,128,128]{5,4,3,2,1,0:T(8,128)} %param.12) | copy-start | bytes 1179652
  18.0 8.9 %collective-permute-start.5 = (f32[48,128]{1,0:T(8,128)S(1)}, f32[48,128]{1,0:T(8,128)S(1)}, u32[]{:S(2)}, u32[]{:S(2)}) collective-permute-start(f32[48,128]{1,0:T(8,128)S(1)} %get-tuple-element.56), channel_id=1, source_target_pairs={{1,0},{2,1},{3,2},{4,3},{5,4},{6,5},{7,6},{8,7},{9,8},{10,9},{11,1... | collective-permute-start | bytes 73736 | tf_op jit(solution)/shard_map/ppermute | solution.py:375
  19.5 7.4 %collective-permute-start.3 = (f32[32,128]{1,0:T(8,128)S(1)}, f32[32,128]{1,0:T(8,128)S(1)}, u32[]{:S(2)}, u32[]{:S(2)}) collective-permute-start(f32[32,128]{1,0:T(8,128)S(1)} %get-tuple-element.54.dx_ref), channel_id=1, source_target_pairs={{64,0},{128,64},{192,128},{256,192},{320,256},{384,320},{448,384},... | collective-permute-start | bytes 49160 | tf_op jit(solution)/shard_map/ppermute | solution.py:375
  21.4 5.5 %collective-permute-start.4 = (f32[32,128]{1,0:T(8,128)S(1)}, f32[32,128]{1,0:T(8,128)S(1)}, u32[]{:S(2)}, u32[]{:S(2)}) collective-permute-start(f32[32,128]{1,0:T(8,128)S(1)} %get-tuple-element.55.dy_ref), channel_id=1, source_target_pairs={{16,0},{32,16},{48,32},{17,1},{33,17},{49,33},{18,2},{34,18},{50,3... | collective-permute-start | bytes 49160 | tf_op jit(solution)/shard_map/ppermute | solution.py:375
  22.7 5.1 %collective-permute-start.6 = (f32[16,128]{1,0:T(8,128)S(1)}, f32[16,128]{1,0:T(8,128)S(1)}, u32[]{:S(2)}, u32[]{:S(2)}) collective-permute-start(f32[16,128]{1,0:T(8,128)S(1)} %get-tuple-element.58), channel_id=1, source_target_pairs={{0,1},{1,2},{2,3},{3,4},{4,5},{5,6},{6,7},{7,8},{8,9},{9,10},{10,1... | collective-permute-start | bytes 24584 | tf_op jit(solution)/shard_map/ppermute | solution.py:375
  97.0 4.9 %collective-permute-start.7 = (f32[16,128]{1,0:T(8,128)S(1)}, f32[16,128]{1,0:T(8,128)S(1)}, u32[]{:S(2)}, u32[]{:S(2)}) collective-permute-start(f32[16,128]{1,0:T(8,128)S(1)} %get-tuple-element.73), channel_id=1, source_target_pairs={{0,1},{1,2},{2,3},{3,4},{4,5},{5,6},{6,7},{7,8},{8,9},{9,10},{10,1... | collective-permute-start | bytes 24584 | tf_op jit(solution)/shard_map/ppermute | solution.py:375
  99.9 4.4 %collective-permute-start.8 = (f32[16,128]{1,0:T(8,128)S(1)}, f32[16,128]{1,0:T(8,128)S(1)}, u32[]{:S(2)}, u32[]{:S(2)}) collective-permute-start(f32[16,128]{1,0:T(8,128)S(1)} %get-tuple-element.74), channel_id=1, source_target_pairs={{1,0},{2,1},{3,2},{4,3},{5,4},{6,5},{7,6},{8,7},{9,8},{10,9},{11,1... | collective-permute-start | bytes 24584 | tf_op jit(solution)/shard_map/ppermute | solution.py:375
  156.4 4.9 %collective-permute-start.9 = (f32[16,128]{1,0:T(8,128)S(1)}, f32[16,128]{1,0:T(8,128)S(1)}, u32[]{:S(2)}, u32[]{:S(2)}) collective-permute-start(f32[16,128]{1,0:T(8,128)S(1)} %get-tuple-element.82), channel_id=1, source_target_pairs={{0,1},{1,2},{2,3},{3,4},{4,5},{5,6},{6,7},{7,8},{8,9},{9,10},{10,1... | collective-permute-start | bytes 24584 | tf_op jit(solution)/shard_map/ppermute | solution.py:375
  159.3 4.4 %collective-permute-start.10 = (f32[16,128]{1,0:T(8,128)S(1)}, f32[16,128]{1,0:T(8,128)S(1)}, u32[]{:S(2)}, u32[]{:S(2)}) collective-permute-start(f32[16,128]{1,0:T(8,128)S(1)} %get-tuple-element.83), channel_id=1, source_target_pairs={{1,0},{2,1},{3,2},{4,3},{5,4},{6,5},{7,6},{8,7},{9,8},{10,9},{11,1... | collective-permute-start | bytes 24584 | tf_op jit(solution)/shard_map/ppermute | solution.py:375

commit v9 on v8

--- a/solution.py
+++ b/solution.py
@@ -11,8 +11,10 @@
 CASES = 16
 FD = 128
 WIDE = 6 * FD
-QPAD = 256
+AGGREGATES = 192
+COARSE = 640
 SUBS = 32
+CORNERS = 256
 AXES = ("gx", "gy", "gz")
 PLANE = ("gx", "gy")
 F32 = jnp.float32
@@ -116,7 +118,7 @@
 def target_rows(ids_row):
     row = lax.broadcasted_iota(jnp.int32, (8, FD), 1) % SUBS
     ids = take(jnp.broadcast_to(ids_row.astype(F32), (8, FD)), jnp.minimum(row // 3, 7))
-    return jnp.where(row < 24, ids + (row % 3 * QPAD).astype(F32), -1.0)
+    return jnp.where(row < 24, ids + (row % 3 * AGGREGATES).astype(F32), -1.0)
 
 
 def prep_kernel(table_ref, rhs_ref, coupling_ref, *message_refs):
@@ -202,27 +204,23 @@
     gh_ref[...] = high
     gl_ref[...] = low
     lanes = lax.broadcasted_iota(jnp.int32, (8, FD), 1)
-    rows = lax.broadcasted_iota(jnp.int32, (3 * QPAD, FD), 0)
+    rows = lax.broadcasted_iota(jnp.int32, (COARSE, FD), 0)
     for half in range(2):
         wanted = jnp.full((8, FD), -1.0, F32)
         for n in range(4 * half, min(4 * half + 4, 7)):
             wanted = jnp.where(lanes // SUBS == n % 4, targets[n], wanted)
-        wanted = jnp.broadcast_to(wanted[0:1, :].astype(jnp.int32), (3 * QPAD, FD))
+        wanted = jnp.broadcast_to(wanted[0:1, :].astype(jnp.int32), (COARSE, FD))
         pick_ref[:, half * FD:(half + 1) * FD] = (rows == wanted).astype(F32).astype(BF16)
     sum_kernel(state_ref, gh_ref, gl_ref, pick_ref, out_ref)
 
 
-def late_kernel(table, diag_ref, couple_ref, inverse_ref, _, fh_ref, fl_ref, kh_ref, kl_ref, square):
+def late_kernel(table, diag_ref, couple_ref, inverse_ref, _, fh_ref, fl_ref, kh_ref, kl_ref):
     put_dense(table, diag_ref, couple_ref, fh_ref, fl_ref)
-    square[...] = jnp.zeros_like(square)
-    for p in range(3):
-        for q in range(3):
-            square[p * QPAD:p * QPAD + 192, q * QPAD:q * QPAD + 192] = inverse_ref[
-                p * 192:(p + 1) * 192, q * 192:(q + 1) * 192
-            ]
-    high, low = halves(square[...])
-    kh_ref[...] = high
-    kl_ref[...] = low
+    count = inverse_ref.shape[0]
+    high, low = halves(inverse_ref[...])
+    for ref, piece in ((kh_ref, high), (kl_ref, low)):
+        ref[...] = jnp.zeros_like(ref)
+        ref[0:count, 0:count] = piece
 
 
 def face_sum(x, faces=range(6)):
@@ -232,15 +230,19 @@
     return total
 
 
-def put_payload(out_ref, gathered, extras):
+def payload_places():
+    for c in range(CASES):
+        for b in range(COARSE // FD):
+            spot, row = divmod(c * (COARSE // FD) + b, 3)
+            yield c, b, spot, slice(row, row + 1)
+
+
+def put_payload(out_ref, gathered, norm):
     lanes = lax.broadcasted_iota(jnp.int32, (CASES, FD), 1)
-    for b in range(6):
-        block = face(gathered, b)
-        if b == 1:
-            for t, value in enumerate(extras):
-                block = jnp.where(lanes == 64 + t, value, block)
-        for c in range(CASES):
-            out_ref[2 * c + b // 3, 4, b % 3:b % 3 + 1, :] = block[c:c + 1, :]
+    blocks = [face(gathered, b) for b in range(COARSE // FD)]
+    blocks[-1] = jnp.where(lanes == 64, norm, blocks[-1])
+    for c, b, spot, row in payload_places():
+        out_ref[spot, 4, row, :] = blocks[b][c:c + 1, :]
 
 
 def sum_kernel(state_ref, gh_ref, gl_ref, pick_ref, out_ref):
@@ -254,7 +256,7 @@
     both = dot_across(jnp.concatenate([high, low], 0), pick_ref[...])
     norm = jnp.sum(face_sum(share * state_ref[RESIDUAL, :]), axis=1, keepdims=True)
     out_ref[...] = jnp.zeros_like(out_ref)
-    put_payload(out_ref, both[:CASES] + both[CASES:], [norm])
+    put_payload(out_ref, both[:CASES] + both[CASES:], norm)
     for f, by in enumerate(steps()):
         @pl.when(there[f])
         def _():
@@ -320,24 +322,22 @@
     mask = mask_row(there)
     applied = (flexed_ref[...] + jnp.concatenate(across, axis=1)) * mask
     search = z_ref[...]
-    for c in range(CASES):
-        for b in range(6):
-            row = slice(b % 3, b % 3 + 1)
-            whole[c:c + 1, b * FD:(b + 1) * FD] = slots_ref[2 * c + b // 3, 4, row, :]
+    for c, b, spot, row in payload_places():
+        whole[c:c + 1, b * FD:(b + 1) * FD] = slots_ref[spot, 4, row, :]
     load = whole[...]
-    norm = load[:, FD + 64:FD + 65]
+    norm = load[:, COARSE - 64:COARSE - 63]
     sums = jnp.sum(slots_ref[:, 4], axis=0)[3:4, :]
     sums = jnp.broadcast_to(sums, (FD, FD)).T
     energy, cross = sums[0:CASES, 0:1], sums[CASES:2 * CASES, 0:1]
-    lanes = lax.broadcasted_iota(jnp.int32, load.shape, 1) % QPAD
-    load = jnp.where(lanes < 192, load, 0.0)
+    lanes = lax.broadcasted_iota(jnp.int32, load.shape, 1)
+    load = jnp.where(lanes < 3 * AGGREGATES, load, 0.0)
     if not first:
         scale = state_ref[REST, 0:FD]
         beta = norm / scale[:, 0:1]
         energy = energy + beta * cross + beta * beta * scale[:, 1:2]
         applied = applied + beta * state_ref[APPLIED, :]
         search = search + beta * state_ref[SEARCH, :]
-        load = load + beta * state_ref[LOAD, :]
+        load = load + beta * state_ref[LOAD, 0:COARSE]
     coarse = dot_split(load, kh_ref, kl_ref)
     step = norm / (energy + jnp.sum(load * coarse, axis=1, keepdims=True))
     corner = dot_exact(coarse, pick_ref[...])
@@ -359,7 +359,8 @@
     up_ref[...] = face(shown, 5)
     new_ref[SEARCH, :] = search
     new_ref[APPLIED, :] = applied
-    new_ref[LOAD, :] = load
+    new_ref[LOAD, 0:COARSE] = load
+    new_ref[LOAD, COARSE:] = jnp.zeros((CASES, WIDE - COARSE), F32)
     lanes = lax.broadcasted_iota(jnp.int32, (CASES, FD), 1)
     scale = jnp.where(lanes == 0, norm, energy)
     parts = [scale]
@@ -431,9 +432,9 @@
         if first:
             *joint, slots = call(
                 joint_kernel,
-                [((QPAD, WIDE), BF16)] * 2 + [((3 * QPAD, QPAD), BF16), (stacked, F32)],
+                [((CORNERS, WIDE), BF16)] * 2 + [((COARSE, CORNERS), BF16), (stacked, F32)],
                 [*ups, *messages, dx, dy, dz, *above, over, state],
-                scratch=[pltpu.VMEM((QPAD, WIDE), F32)],
+                scratch=[pltpu.VMEM((CORNERS, WIDE), F32)],
             )
         else:
             (slots,) = call(sum_kernel, [(stacked, F32)], [state, *joint])
@@ -441,10 +442,9 @@
         slots = swapped(slots, PLANE)
         if first:
             late = call(
-                late_kernel, [(square, BF16)] * 4,
+                late_kernel, [(square, BF16)] * 2 + [((COARSE, COARSE), BF16)] * 2,
                 [table] + blocks[2:] + [coarse_inverse, slots],
                 specs=[SMEM] + [VMEM] * 3 + [pl.BlockSpec(memory_space=pl.ANY)],
-                scratch=[pltpu.VMEM(square, F32)],
             )
             flex, inverse = late[:2], late[2:]
         z, flexed, layers = call(
@@ -458,7 +458,7 @@
         slots = swapped(slots, PLANE)
         common = [slots, layers, flexed, z, state, *inverse, *joint]
         kernel = functools.partial(step_kernel, first, last)
-        scratch = [pltpu.VMEM(wide, F32)]
+        scratch = [pltpu.VMEM((CASES, COARSE), F32)]
         if last:
             multipliers, left = call(kernel, [((3, CASES, FD), F32)] * 2, common, scratch=scratch)
             break

time: 217 us -> 216 us (level)
  transfers between devices with their start and end apart: 11 -> 11, of which waited for: 2 -> 2; matrix products, arithmetic and copies ran while one was open for 0% -> 0% of each run, Pallas kernels for 2% -> 1%
where the time goes in v9:
time: 216 us; the launch traced here: 215 us
  blocking collectives  165 us (76%)
  starting transfers between devices  28.4 us (13%)
  Pallas kernels  11.8 us (5%)
  waiting for transfers between devices  5 us (2%)
  local copies, waits for them, and re-layouts  3.62 us (2%)
    all_to_all x9, blocking collectives, swapped(): return lax.all_to_all(slots, axes, 0, 0)  165 us
    ppermute x11, starting transfers between devices, passed_along(): return lax.ppermute(shard, axis, pairs)  28.4 us
    pallas_call x16, Pallas kernels, call(): pl.pallas_call(kernel, out_shape=[jax.ShapeDtypeStruct(shape, dtype) for...  11.8 us
    ppermute x11, waiting for transfers between devices, passed_along(): return lax.ppermute(shard, axis, pairs)  5 us
  transfers between devices with their start and end apart: 11, of which 2 were waited for; matrix products, arithmetic and copies ran while one was open for 0% of the time, Pallas kernels for 1%

profile of v9, /device:TPU:1, one launch (start us, length us, event | category | flops | bytes accessed | tf_op | source)
XLA Modules:
  0.0 215.3 jit_solution(8379277542092574951)
XLA Ops:
  0.6 0.7 pad_add_fusion.table_ref.table
  1.3 0.0 copy-start.5
  1.4 0.9 copy-done.5
  2.2 0.0 copy-start.6
  2.2 0.7 copy-done.6
  3.0 0.2 shard_map.113
  3.1 4.6 %collective-permute-start = (f32[56,128]{1,0:T(8,128)S(1)}, f32[56,128]{1,0:T(8,128)S(1)}, u32[]{:S(2)}, u32[]{:S(2)}) collective-permute-start(f32[56,128]{1,0:T(8,128)S(1)} %get-tuple-element.47.ux_ref), channel_id=1, source_target_pairs={{0,64},{64,128},{128,192},{192,256},{256,320},{320,384},{384,448},... | collective-permute-start | bytes 86024 | tf_op jit(solution)/shard_map/ppermute | solution.py:376
  7.8 3.1 %collective-permute-start.1 = (f32[56,128]{1,0:T(8,128)S(1)}, f32[56,128]{1,0:T(8,128)S(1)}, u32[]{:S(2)}, u32[]{:S(2)}) collective-permute-start(f32[56,128]{1,0:T(8,128)S(1)} %get-tuple-element.48.uy_ref), channel_id=1, source_target_pairs={{0,16},{16,32},{32,48},{1,17},{17,33},{33,49},{2,18},{18,34},{34,5... | collective-permute-start | bytes 86024 | tf_op jit(solution)/shard_map/ppermute | solution.py:376
  10.9 3.5 %collective-permute-start.2 = (f32[56,128]{1,0:T(8,128)S(1)}, f32[56,128]{1,0:T(8,128)S(1)}, u32[]{:S(2)}, u32[]{:S(2)}) collective-permute-start(f32[56,128]{1,0:T(8,128)S(1)} %get-tuple-element.49.uz_ref), channel_id=1, source_target_pairs={{0,1},{1,2},{2,3},{3,4},{4,5},{5,6},{6,7},{7,8},{8,9},{9,10},{10,1... | collective-permute-start | bytes 86024 | tf_op jit(solution)/shard_map/ppermute | solution.py:376
  14.4 0.0 copy-start.1
  14.4 1.0 copy-done.1
  15.4 0.0 copy-start.2
  15.4 1.0 copy-done.2
  16.4 1.0 shard_map.114
  17.4 0.0 collective-permute-done.mx_ref
  17.4 0.0 collective-permute-done.1.my_ref
  17.4 0.0 collective-permute-done.2.mz_ref
  17.5 0.0 copy-start
  17.5 0.6 shard_map.115
  18.0 0.0 copy-start.3
  18.0 0.0 copy-start.4
  18.0 1.4 collective-permute-start.5
  19.5 1.9 collective-permute-start.3
  21.4 1.3 collective-permute-start.4
  22.7 4.2 %collective-permute-start.6 = (f32[16,128]{1,0:T(8,128)S(1)}, f32[16,128]{1,0:T(8,128)S(1)}, u32[]{:S(2)}, u32[]{:S(2)}) collective-permute-start(f32[16,128]{1,0:T(8,128)S(1)} %get-tuple-element.58), channel_id=1, source_target_pairs={{0,1},{1,2},{2,3},{3,4},{4,5},{5,6},{6,7},{7,8},{8,9},{9,10},{10,1... | collective-permute-start | bytes 24584 | tf_op jit(solution)/shard_map/ppermute | solution.py:376
  26.9 0.0 collective-permute-done.3.nx_ref
  26.9 0.0 collective-permute-done.4.ny_ref
  26.9 0.0 collective-permute-done.5.over_ref.above_ref
  26.9 0.7 shard_map.116
  27.6 0.0 collective-permute-done.6.below_ref
  27.7 19.0 %all_to_all.45._.slots_ref = f32[32,5,4,128]{3,2,1,0:T(4,128)S(1)} all-to-all(f32[32,5,4,128]{3,2,1,0:T(4,128)S(1)} %get-tuple-element.59), channel_id=1, replica_groups=mesh['gx'=8,'gy'=4,'gz'=16] {'gx','gy'}, dimensions={0} | all-to-all | bytes 655360 | tf_op jit(solution)/shard_map/all_to_all | solution.py:380
  46.6 0.0 copy-done
  46.6 0.0 copy-done.3
  46.6 0.0 copy-done.4
  46.6 1.4 shard_map.117
  48.1 0.7 shard_map.118
  48.8 29.7 %all_to_all.46.layers_ref = f32[16,5,4,128]{3,2,1,0:T(4,128)S(1)} all-to-all(f32[16,5,4,128]{3,2,1,0:T(4,128)S(1)} %get-tuple-element.64), channel_id=1, replica_groups=mesh['gx'=8,'gy'=4,'gz'=16] {'gz'}, dimensions={0} | all-to-all | bytes 327680 | tf_op jit(solution)/shard_map/all_to_all | solution.py:380
  78.5 0.1 shard_map.119
  78.6 16.7 %all_to_all.47.slots_ref = f32[32,5,4,128]{3,2,1,0:T(4,128)S(1)} all-to-all(f32[32,5,4,128]{3,2,1,0:T(4,128)S(1)} %shard_map.119), channel_id=1, replica_groups=mesh['gx'=8,'gy'=4,'gz'=16] {'gx','gy'}, dimensions={0} | all-to-all | bytes 655360 | tf_op jit(solution)/shard_map/all_to_all | solution.py:380
  95.3 1.4 shard_map.120
  96.7 2.8 %collective-permute-start.7 = (f32[16,128]{1,0:T(8,128)S(1)}, f32[16,128]{1,0:T(8,128)S(1)}, u32[]{:S(2)}, u32[]{:S(2)}) collective-permute-start(f32[16,128]{1,0:T(8,128)S(1)} %get-tuple-element.73), channel_id=1, source_target_pairs={{0,1},{1,2},{2,3},{3,4},{4,5},{5,6},{6,7},{7,8},{8,9},{9,10},{10,1... | collective-permute-start | bytes 24584 | tf_op jit(solution)/shard_map/ppermute | solution.py:376
  99.5 1.3 collective-permute-start.8
  100.8 0.6 shard_map.121
  101.5 0.0 collective-permute-done.7.below_ref
  101.5 2.5 %collective-permute-done.8.above_ref = f32[16,128]{1,0:T(8,128)S(1)} collective-permute-done((f32[16,128]{1,0:T(8,128)S(1)}, f32[16,128]{1,0:T(8,128)S(1)}, u32[]{:S(2)}, u32[]{:S(2)}) %collective-permute-start.8) | collective-permute-done | bytes 8224 | tf_op jit(solution)/shard_map/ppermute | solution.py:376
  103.9 14.9 %all_to_all.48.slots_ref = f32[32,5,4,128]{3,2,1,0:T(4,128)S(1)} all-to-all(f32[32,5,4,128]{3,2,1,0:T(4,128)S(1)} %shard_map.121), channel_id=1, replica_groups=mesh['gx'=8,'gy'=4,'gz'=16] {'gx','gy'}, dimensions={0} | all-to-all | bytes 655360 | tf_op jit(solution)/shard_map/all_to_all | solution.py:380
  118.8 0.7 shard_map.122
  119.5 18.1 %all_to_all.49.layers_ref = f32[16,5,4,128]{3,2,1,0:T(4,128)S(1)} all-to-all(f32[16,5,4,128]{3,2,1,0:T(4,128)S(1)} %get-tuple-element.78), channel_id=1, replica_groups=mesh['gx'=8,'gy'=4,'gz'=16] {'gz'}, dimensions={0} | all-to-all | bytes 327680 | tf_op jit(solution)/shard_map/all_to_all | solution.py:380
  137.6 0.1 shard_map.123
  137.7 16.7 %all_to_all.50.slots_ref = f32[32,5,4,128]{3,2,1,0:T(4,128)S(1)} all-to-all(f32[32,5,4,128]{3,2,1,0:T(4,128)S(1)} %shard_map.123), channel_id=1, replica_groups=mesh['gx'=8,'gy'=4,'gz'=16] {'gx','gy'}, dimensions={0} | all-to-all | bytes 655360 | tf_op jit(solution)/shard_map/all_to_all | solution.py:380
  154.5 1.5 shard_map.124
  156.0 2.9 %collective-permute-start.9 = (f32[16,128]{1,0:T(8,128)S(1)}, f32[16,128]{1,0:T(8,128)S(1)}, u32[]{:S(2)}, u32[]{:S(2)}) collective-permute-start(f32[16,128]{1,0:T(8,128)S(1)} %get-tuple-element.82), channel_id=1, source_target_pairs={{0,1},{1,2},{2,3},{3,4},{4,5},{5,6},{6,7},{7,8},{8,9},{9,10},{10,1... | collective-permute-start | bytes 24584 | tf_op jit(solution)/shard_map/ppermute | solution.py:376
  158.8 1.3 collective-permute-start.10
  160.1 0.6 shard_map.125
  160.7 0.0 collective-permute-done.9.below_ref
  160.8 2.5 %collective-permute-done.10.above_ref = f32[16,128]{1,0:T(8,128)S(1)} collective-permute-done((f32[16,128]{1,0:T(8,128)S(1)}, f32[16,128]{1,0:T(8,128)S(1)}, u32[]{:S(2)}, u32[]{:S(2)}) %collective-permute-start.10) | collective-permute-done | bytes 8224 | tf_op jit(solution)/shard_map/ppermute | solution.py:376
  163.2 14.9 %all_to_all.51.slots_ref = f32[32,5,4,128]{3,2,1,0:T(4,128)S(1)} all-to-all(f32[32,5,4,128]{3,2,1,0:T(4,128)S(1)} %shard_map.125), channel_id=1, replica_groups=mesh['gx'=8,'gy'=4,'gz'=16] {'gx','gy'}, dimensions={0} | all-to-all | bytes 655360 | tf_op jit(solution)/shard_map/all_to_all | solution.py:380
  178.1 0.7 shard_map.126
  178.8 18.1 %all_to_all.52.layers_ref = f32[16,5,4,128]{3,2,1,0:T(4,128)S(1)} all-to-all(f32[16,5,4,128]{3,2,1,0:T(4,128)S(1)} %get-tuple-element.87), channel_id=1, replica_groups=mesh['gx'=8,'gy'=4,'gz'=16] {'gz'}, dimensions={0} | all-to-all | bytes 327680 | tf_op jit(solution)/shard_map/all_to_all | solution.py:380
  196.9 0.1 shard_map.127
  197.0 16.7 %all_to_all.53.slots_ref = f32[32,5,4,128]{3,2,1,0:T(4,128)S(1)} all-to-all(f32[32,5,4,128]{3,2,1,0:T(4,128)S(1)} %shard_map.127), channel_id=1, replica_groups=mesh['gx'=8,'gy'=4,'gz'=16] {'gx','gy'}, dimensions={0} | all-to-all | bytes 655360 | tf_op jit(solution)/shard_map/all_to_all | solution.py:380
  213.7 1.6 shard_map.128
Async XLA Ops:
  1.3 0.9 copy-start.5
  2.2 0.7 copy-start.6
  3.1 14.3 %collective-permute-start = (f32[56,128]{1,0:T(8,128)S(1)}, f32[56,128]{1,0:T(8,128)S(1)}, u32[]{:S(2)}, u32[]{:S(2)}) collective-permute-start(f32[56,128]{1,0:T(8,128)S(1)} %get-tuple-element.47.ux_ref), channel_id=1, source_target_pairs={{0,64},{64,128},{128,192},{192,256},{256,320},{320,384},{384,448},... | collective-permute-start | bytes 86024 | tf_op jit(solution)/shard_map/ppermute | solution.py:376
  7.8 9.7 %collective-permute-start.1 = (f32[56,128]{1,0:T(8,128)S(1)}, f32[56,128]{1,0:T(8,128)S(1)}, u32[]{:S(2)}, u32[]{:S(2)}) collective-permute-start(f32[56,128]{1,0:T(8,128)S(1)} %get-tuple-element.48.uy_ref), channel_id=1, source_target_pairs={{0,16},{16,32},{32,48},{1,17},{17,33},{33,49},{2,18},{18,34},{34,5... | collective-permute-start | bytes 86024 | tf_op jit(solution)/shard_map/ppermute | solution.py:376
  10.9 6.6 %collective-permute-start.2 = (f32[56,128]{1,0:T(8,128)S(1)}, f32[56,128]{1,0:T(8,128)S(1)}, u32[]{:S(2)}, u32[]{:S(2)}) collective-permute-start(f32[56,128]{1,0:T(8,128)S(1)} %get-tuple-element.49.uz_ref), channel_id=1, source_target_pairs={{0,1},{1,2},{2,3},{3,4},{4,5},{5,6},{6,7},{7,8},{8,9},{9,10},{10,1... | collective-permute-start | bytes 86024 | tf_op jit(solution)/shard_map/ppermute | solution.py:376
  14.4 1.0 copy-start.1
  15.4 1.0 copy-start.2
  17.5 29.2 %copy-start = (f32[576,576]{1,0:T(8,128)S(1)}, f32[576,576]{1,0:T(8,128)}, u32[]{:S(2)}) copy-start(f32[576,576]{1,0:T(8,128)} %inverse_ref.1) | copy-start | bytes 3981316
  18.0 28.6 %copy-start.3 = (f32[1,1,1,6,128,128]{5,4,3,2,1,0:T(8,128)S(1)}, f32[1,1,1,6,128,128]{5,4,3,2,1,0:T(8,128)}, u32[]{:S(2)}) copy-start(f32[1,1,1,6,128,128]{5,4,3,2,1,0:T(8,128)} %param.11) | copy-start | bytes 1179652
  18.0 28.6 %copy-start.4 = (f32[1,1,1,6,128,128]{5,4,3,2,1,0:T(8,128)S(1)}, f32[1,1,1,6,128,128]{5,4,3,2,1,0:T(8,128)}, u32[]{:S(2)}) copy-start(f32[1,1,1,6,128,128]{5,4,3,2,1,0:T(8,128)} %param.12) | copy-start | bytes 1179652
  18.0 8.9 %collective-permute-start.5 = (f32[48,128]{1,0:T(8,128)S(1)}, f32[48,128]{1,0:T(8,128)S(1)}, u32[]{:S(2)}, u32[]{:S(2)}) collective-permute-start(f32[48,128]{1,0:T(8,128)S(1)} %get-tuple-element.56), channel_id=1, source_target_pairs={{1,0},{2,1},{3,2},{4,3},{5,4},{6,5},{7,6},{8,7},{9,8},{10,9},{11,1... | collective-permute-start | bytes 73736 | tf_op jit(solution)/shard_map/ppermute | solution.py:376
  19.5 7.4 %collective-permute-start.3 = (f32[32,128]{1,0:T(8,128)S(1)}, f32[32,128]{1,0:T(8,128)S(1)}, u32[]{:S(2)}, u32[]{:S(2)}) collective-permute-start(f32[32,128]{1,0:T(8,128)S(1)} %get-tuple-element.54.dx_ref), channel_id=1, source_target_pairs={{64,0},{128,64},{192,128},{256,192},{320,256},{384,320},{448,384},... | collective-permute-start | bytes 49160 | tf_op jit(solution)/shard_map/ppermute | solution.py:376
  21.4 5.5 %collective-permute-start.4 = (f32[32,128]{1,0:T(8,128)S(1)}, f32[32,128]{1,0:T(8,128)S(1)}, u32[]{:S(2)}, u32[]{:S(2)}) collective-permute-start(f32[32,128]{1,0:T(8,128)S(1)} %get-tuple-element.55.dy_ref), channel_id=1, source_target_pairs={{16,0},{32,16},{48,32},{17,1},{33,17},{49,33},{18,2},{34,18},{50,3... | collective-permute-start | bytes 49160 | tf_op jit(solution)/shard_map/ppermute | solution.py:376
  22.7 5.0 %collective-permute-start.6 = (f32[16,128]{1,0:T(8,128)S(1)}, f32[16,128]{1,0:T(8,128)S(1)}, u32[]{:S(2)}, u32[]{:S(2)}) collective-permute-start(f32[16,128]{1,0:T(8,128)S(1)} %get-tuple-element.58), channel_id=1, source_target_pairs={{0,1},{1,2},{2,3},{3,4},{4,5},{5,6},{6,7},{7,8},{8,9},{9,10},{10,1... | collective-permute-start | bytes 24584 | tf_op jit(solution)/shard_map/ppermute | solution.py:376
  96.7 4.8 %collective-permute-start.7 = (f32[16,128]{1,0:T(8,128)S(1)}, f32[16,128]{1,0:T(8,128)S(1)}, u32[]{:S(2)}, u32[]{:S(2)}) collective-permute-start(f32[16,128]{1,0:T(8,128)S(1)} %get-tuple-element.73), channel_id=1, source_target_pairs={{0,1},{1,2},{2,3},{3,4},{4,5},{5,6},{6,7},{7,8},{8,9},{9,10},{10,1... | collective-permute-start | bytes 24584 | tf_op jit(solution)/shard_map/ppermute | solution.py:376
  99.5 4.4 %collective-permute-start.8 = (f32[16,128]{1,0:T(8,128)S(1)}, f32[16,128]{1,0:T(8,128)S(1)}, u32[]{:S(2)}, u32[]{:S(2)}) collective-permute-start(f32[16,128]{1,0:T(8,128)S(1)} %get-tuple-element.74), channel_id=1, source_target_pairs={{1,0},{2,1},{3,2},{4,3},{5,4},{6,5},{7,6},{8,7},{9,8},{10,9},{11,1... | collective-permute-start | bytes 24584 | tf_op jit(solution)/shard_map/ppermute | solution.py:376
  156.0 4.8 %collective-permute-start.9 = (f32[16,128]{1,0:T(8,128)S(1)}, f32[16,128]{1,0:T(8,128)S(1)}, u32[]{:S(2)}, u32[]{:S(2)}) collective-permute-start(f32[16,128]{1,0:T(8,128)S(1)} %get-tuple-element.82), channel_id=1, source_target_pairs={{0,1},{1,2},{2,3},{3,4},{4,5},{5,6},{6,7},{7,8},{8,9},{9,10},{10,1... | collective-permute-start | bytes 24584 | tf_op jit(solution)/shard_map/ppermute | solution.py:376
  158.8 4.4 %collective-permute-start.10 = (f32[16,128]{1,0:T(8,128)S(1)}, f32[16,128]{1,0:T(8,128)S(1)}, u32[]{:S(2)}, u32[]{:S(2)}) collective-permute-start(f32[16,128]{1,0:T(8,128)S(1)} %get-tuple-element.83), channel_id=1, source_target_pairs={{1,0},{2,1},{3,2},{4,3},{5,4},{6,5},{7,6},{8,7},{9,8},{10,9},{11,1... | collective-permute-start | bytes 24584 | tf_op jit(solution)/shard_map/ppermute | solution.py:376

commit v10 on v9

--- a/solution.py
+++ b/solution.py
@@ -438,7 +438,8 @@
             )
         else:
             (slots,) = call(sum_kernel, [(stacked, F32)], [state, *joint])
-        slots, below, over = lax.optimization_barrier((slots, below, over))
+        if not last:
+            slots, below, over = lax.optimization_barrier((slots, below, over))
         slots = swapped(slots, PLANE)
         if first:
             late = call(

time: 216 us -> 214 us (level)
  blocking collectives: 165 us -> 152 us
  starting transfers between devices: 28.4 us -> 32.9 us
  waiting for transfers between devices: 5 us -> 8.04 us
  local copies, waits for them, and re-layouts: 3.62 us -> 6.08 us
    all_to_all x9 -> x8, blocking collectives: 165 us -> 152 us  [swapped(): return lax.all_to_all(slots, axes, 0, 0)]
    all_to_all x0 -> x1, starting transfers between devices: none -> 4.59 us  [swapped(): return lax.all_to_all(slots, axes, 0, 0)]
    unnamed x14 -> x28, local copies, waits for them, and re-layouts: 3.62 us -> 6.08 us
  transfers between devices with their start and end apart: 11 -> 12, of which waited for: 2 -> 3; matrix products, arithmetic and copies ran while one was open for 0% -> 0% of each run, Pallas kernels for 1% -> 1%
where the time goes in v10:
time: 214 us; the launch traced here: 213 us
  blocking collectives  152 us (71%)
  starting transfers between devices  32.9 us (15%)
  Pallas kernels  12.9 us (6%)
  waiting for transfers between devices  8.04 us (4%)
  local copies, waits for them, and re-layouts  6.08 us (3%)
    all_to_all x8, blocking collectives, swapped(): return lax.all_to_all(slots, axes, 0, 0)  152 us
    ppermute x11, starting transfers between devices, passed_along(): return lax.ppermute(shard, axis, pairs)  28.4 us
    pallas_call x16, Pallas kernels, call(): pl.pallas_call(kernel, out_shape=[jax.ShapeDtypeStruct(shape, dtype) for...  12.9 us
    unnamed x28, local copies, waits for them, and re-layouts  6.08 us
    ppermute x11, waiting for transfers between devices, passed_along(): return lax.ppermute(shard, axis, pairs)  6.01 us
    all_to_all x1, starting transfers between devices, swapped(): return lax.all_to_all(slots, axes, 0, 0)  4.59 us
  transfers between devices with their start and end apart: 12, of which 3 were waited for; matrix products, arithmetic and copies ran while one was open for 0% of the time, Pallas kernels for 1%

profile of v10, /device:TPU:1, one launch (start us, length us, event | category | flops | bytes accessed | tf_op | source)
XLA Modules:
  0.0 213.3 jit_solution(10053836332500356475)
XLA Ops:
  0.6 0.7 pad_add_fusion.table_ref.table
  1.4 0.9 copy-done.12
  2.2 0.7 copy-done.13
  3.0 0.2 shard_map.113
  3.1 4.6 %collective-permute-start = (f32[56,128]{1,0:T(8,128)S(1)}, f32[56,128]{1,0:T(8,128)S(1)}, u32[]{:S(2)}, u32[]{:S(2)}) collective-permute-start(f32[56,128]{1,0:T(8,128)S(1)} %get-tuple-element.44.ux_ref), channel_id=1, source_target_pairs={{0,64},{64,128},{128,192},{192,256},{256,320},{320,384},{384,448},... | collective-permute-start | bytes 86024 | tf_op jit(solution)/shard_map/ppermute | solution.py:376
  7.7 3.1 %collective-permute-start.1 = (f32[56,128]{1,0:T(8,128)S(1)}, f32[56,128]{1,0:T(8,128)S(1)}, u32[]{:S(2)}, u32[]{:S(2)}) collective-permute-start(f32[56,128]{1,0:T(8,128)S(1)} %get-tuple-element.45.uy_ref), channel_id=1, source_target_pairs={{0,16},{16,32},{32,48},{1,17},{17,33},{33,49},{2,18},{18,34},{34,5... | collective-permute-start | bytes 86024 | tf_op jit(solution)/shard_map/ppermute | solution.py:376
  10.9 3.5 %collective-permute-start.2 = (f32[56,128]{1,0:T(8,128)S(1)}, f32[56,128]{1,0:T(8,128)S(1)}, u32[]{:S(2)}, u32[]{:S(2)}) collective-permute-start(f32[56,128]{1,0:T(8,128)S(1)} %get-tuple-element.46.uz_ref), channel_id=1, source_target_pairs={{0,1},{1,2},{2,3},{3,4},{4,5},{5,6},{6,7},{7,8},{8,9},{9,10},{10,1... | collective-permute-start | bytes 86024 | tf_op jit(solution)/shard_map/ppermute | solution.py:376
  14.4 0.0 copy-start.8
  14.4 1.0 copy-done.8
  15.4 1.0 copy-done.9
  16.4 1.0 shard_map.114
  17.4 0.0 collective-permute-done.mx_ref
  17.4 0.0 collective-permute-done.1.my_ref
  17.4 0.0 collective-permute-done.2.mz_ref
  17.5 0.0 copy-start.6
  17.5 0.6 shard_map.115
  18.0 0.0 copy-start.11
  18.0 1.4 collective-permute-start.5
  19.5 1.9 collective-permute-start.3
  21.4 1.3 collective-permute-start.4
  22.7 4.2 %collective-permute-start.6 = (f32[16,128]{1,0:T(8,128)S(1)}, f32[16,128]{1,0:T(8,128)S(1)}, u32[]{:S(2)}, u32[]{:S(2)}) collective-permute-start(f32[16,128]{1,0:T(8,128)S(1)} %get-tuple-element.55), channel_id=1, source_target_pairs={{0,1},{1,2},{2,3},{3,4},{4,5},{5,6},{6,7},{7,8},{8,9},{9,10},{10,1... | collective-permute-start | bytes 24584 | tf_op jit(solution)/shard_map/ppermute | solution.py:376
  26.9 0.0 collective-permute-done.3.nx_ref
  26.9 0.0 collective-permute-done.4.ny_ref
  26.9 0.0 collective-permute-done.5.over_ref.above_ref
  26.9 0.7 shard_map.116
  27.6 0.0 collective-permute-done.6.below_ref
  27.7 19.0 %all_to_all.45._.slots_ref = f32[32,5,4,128]{3,2,1,0:T(4,128)S(1)} all-to-all(f32[32,5,4,128]{3,2,1,0:T(4,128)S(1)} %get-tuple-element.56), channel_id=1, replica_groups=mesh['gx'=8,'gy'=4,'gz'=16] {'gx','gy'}, dimensions={0} | all-to-all | bytes 655360 | tf_op jit(solution)/shard_map/all_to_all | solution.py:380
  46.6 0.0 copy-done.6
  46.6 0.0 copy-done.10
  46.6 0.0 copy-done.11
  46.6 1.4 shard_map.117
  48.1 0.0 copy-start
  48.1 0.0 copy-start.2
  48.1 0.7 shard_map.118
  48.8 29.7 %all_to_all.46.layers_ref = f32[16,5,4,128]{3,2,1,0:T(4,128)S(1)} all-to-all(f32[16,5,4,128]{3,2,1,0:T(4,128)S(1)} %get-tuple-element.61), channel_id=1, replica_groups=mesh['gx'=8,'gy'=4,'gz'=16] {'gz'}, dimensions={0} | all-to-all | bytes 327680 | tf_op jit(solution)/shard_map/all_to_all | solution.py:380
  78.5 0.1 shard_map.119
  78.6 16.7 %all_to_all.47.slots_ref = f32[32,5,4,128]{3,2,1,0:T(4,128)S(1)} all-to-all(f32[32,5,4,128]{3,2,1,0:T(4,128)S(1)} %shard_map.119), channel_id=1, replica_groups=mesh['gx'=8,'gy'=4,'gz'=16] {'gx','gy'}, dimensions={0} | all-to-all | bytes 655360 | tf_op jit(solution)/shard_map/all_to_all | solution.py:380
  95.3 1.4 shard_map.120
  96.7 2.9 %collective-permute-start.7 = (f32[16,128]{1,0:T(8,128)S(1)}, f32[16,128]{1,0:T(8,128)S(1)}, u32[]{:S(2)}, u32[]{:S(2)}) collective-permute-start(f32[16,128]{1,0:T(8,128)S(1)} %get-tuple-element.70), channel_id=1, source_target_pairs={{0,1},{1,2},{2,3},{3,4},{4,5},{5,6},{6,7},{7,8},{8,9},{9,10},{10,1... | collective-permute-start | bytes 24584 | tf_op jit(solution)/shard_map/ppermute | solution.py:376
  99.6 1.3 collective-permute-start.8
  100.9 0.6 shard_map.121
  101.5 0.0 collective-permute-done.7.below_ref
  101.5 2.5 %collective-permute-done.8.above_ref = f32[16,128]{1,0:T(8,128)S(1)} collective-permute-done((f32[16,128]{1,0:T(8,128)S(1)}, f32[16,128]{1,0:T(8,128)S(1)}, u32[]{:S(2)}, u32[]{:S(2)}) %collective-permute-start.8) | collective-permute-done | bytes 8224 | tf_op jit(solution)/shard_map/ppermute | solution.py:376
  104.0 14.9 %all_to_all.48.slots_ref = f32[32,5,4,128]{3,2,1,0:T(4,128)S(1)} all-to-all(f32[32,5,4,128]{3,2,1,0:T(4,128)S(1)} %shard_map.121), channel_id=1, replica_groups=mesh['gx'=8,'gy'=4,'gz'=16] {'gx','gy'}, dimensions={0} | all-to-all | bytes 655360 | tf_op jit(solution)/shard_map/all_to_all | solution.py:380
  118.9 0.7 shard_map.122
  119.6 18.1 %all_to_all.49.layers_ref = f32[16,5,4,128]{3,2,1,0:T(4,128)S(1)} all-to-all(f32[16,5,4,128]{3,2,1,0:T(4,128)S(1)} %get-tuple-element.75), channel_id=1, replica_groups=mesh['gx'=8,'gy'=4,'gz'=16] {'gz'}, dimensions={0} | all-to-all | bytes 327680 | tf_op jit(solution)/shard_map/all_to_all | solution.py:380
  137.7 0.1 shard_map.123
  137.7 16.8 %all_to_all.50.slots_ref = f32[32,5,4,128]{3,2,1,0:T(4,128)S(1)} all-to-all(f32[32,5,4,128]{3,2,1,0:T(4,128)S(1)} %shard_map.123), channel_id=1, replica_groups=mesh['gx'=8,'gy'=4,'gz'=16] {'gx','gy'}, dimensions={0} | all-to-all | bytes 655360 | tf_op jit(solution)/shard_map/all_to_all | solution.py:380
  154.5 1.5 shard_map.124
  156.0 0.6 shard_map.125
  156.6 0.7 copy-done.4
  157.4 0.7 copy-done.7
  158.1 4.6 %all-to-all-start.6 = ((f32[32,5,4,128]{3,2,1,0:T(4,128)}), f32[32,5,4,128]{3,2,1,0:T(4,128)}, u32[]{:S(2)}, u32[]{:S(2)}) async-start(f32[32,5,4,128]{3,2,1,0:T(4,128)} %copy-done.7), calls=%async_computation.6 | async-start | bytes 655360 | tf_op jit(solution)/shard_map/all_to_all | solution.py:380
  162.7 2.8 %collective-permute-start.9 = (f32[16,128]{1,0:T(8,128)S(1)}, f32[16,128]{1,0:T(8,128)S(1)}, u32[]{:S(2)}, u32[]{:S(2)}) collective-permute-start(f32[16,128]{1,0:T(8,128)S(1)} %get-tuple-element.79), channel_id=1, source_target_pairs={{0,1},{1,2},{2,3},{3,4},{4,5},{5,6},{6,7},{7,8},{8,9},{9,10},{10,1... | collective-permute-start | bytes 24584 | tf_op jit(solution)/shard_map/ppermute | solution.py:376
  165.6 1.3 collective-permute-start.10
  166.9 0.0 collective-permute-done.9.below_ref
  166.9 3.5 %collective-permute-done.10.above_ref = f32[16,128]{1,0:T(8,128)S(1)} collective-permute-done((f32[16,128]{1,0:T(8,128)S(1)}, f32[16,128]{1,0:T(8,128)S(1)}, u32[]{:S(2)}, u32[]{:S(2)}) %collective-permute-start.10) | collective-permute-done | bytes 8224 | tf_op jit(solution)/shard_map/ppermute | solution.py:376
  170.3 2.0 all-to-all-done.6.slots_ref
  172.4 1.0 copy-done.5
  173.4 1.7 shard_map.126
  175.1 16.1 %all_to_all.51.layers_ref = f32[16,5,4,128]{3,2,1,0:T(4,128)S(1)} all-to-all(f32[16,5,4,128]{3,2,1,0:T(4,128)S(1)} %get-tuple-element.81), channel_id=1, replica_groups=mesh['gx'=8,'gy'=4,'gz'=16] {'gz'}, dimensions={0} | all-to-all | bytes 327680 | tf_op jit(solution)/shard_map/all_to_all | solution.py:380
  191.2 0.1 shard_map.127
  191.3 20.4 %all_to_all.52.slots_ref = f32[32,5,4,128]{3,2,1,0:T(4,128)S(1)} all-to-all(f32[32,5,4,128]{3,2,1,0:T(4,128)S(1)} %shard_map.127), channel_id=1, replica_groups=mesh['gx'=8,'gy'=4,'gz'=16] {'gx','gy'}, dimensions={0} | all-to-all | bytes 655360 | tf_op jit(solution)/shard_map/all_to_all | solution.py:380
  211.8 1.6 shard_map.128
  (13 shorter events, 0.0 us)
Async XLA Ops:
  1.3 0.9 copy-start.12
  2.2 0.7 copy-start.13
  3.1 14.3 %collective-permute-start = (f32[56,128]{1,0:T(8,128)S(1)}, f32[56,128]{1,0:T(8,128)S(1)}, u32[]{:S(2)}, u32[]{:S(2)}) collective-permute-start(f32[56,128]{1,0:T(8,128)S(1)} %get-tuple-element.44.ux_ref), channel_id=1, source_target_pairs={{0,64},{64,128},{128,192},{192,256},{256,320},{320,384},{384,448},... | collective-permute-start | bytes 86024 | tf_op jit(solution)/shard_map/ppermute | solution.py:376
  7.7 9.7 %collective-permute-start.1 = (f32[56,128]{1,0:T(8,128)S(1)}, f32[56,128]{1,0:T(8,128)S(1)}, u32[]{:S(2)}, u32[]{:S(2)}) collective-permute-start(f32[56,128]{1,0:T(8,128)S(1)} %get-tuple-element.45.uy_ref), channel_id=1, source_target_pairs={{0,16},{16,32},{32,48},{1,17},{17,33},{33,49},{2,18},{18,34},{34,5... | collective-permute-start | bytes 86024 | tf_op jit(solution)/shard_map/ppermute | solution.py:376
  10.9 6.6 %collective-permute-start.2 = (f32[56,128]{1,0:T(8,128)S(1)}, f32[56,128]{1,0:T(8,128)S(1)}, u32[]{:S(2)}, u32[]{:S(2)}) collective-permute-start(f32[56,128]{1,0:T(8,128)S(1)} %get-tuple-element.46.uz_ref), channel_id=1, source_target_pairs={{0,1},{1,2},{2,3},{3,4},{4,5},{5,6},{6,7},{7,8},{8,9},{9,10},{10,1... | collective-permute-start | bytes 86024 | tf_op jit(solution)/shard_map/ppermute | solution.py:376
  14.4 1.0 copy-start.8
  15.4 1.0 copy-start.9
  17.5 29.2 %copy-start.6 = (f32[576,576]{1,0:T(8,128)S(1)}, f32[576,576]{1,0:T(8,128)}, u32[]{:S(2)}) copy-start(f32[576,576]{1,0:T(8,128)} %inverse_ref.1) | copy-start | bytes 3981316
  18.0 28.6 %copy-start.10 = (f32[1,1,1,6,128,128]{5,4,3,2,1,0:T(8,128)S(1)}, f32[1,1,1,6,128,128]{5,4,3,2,1,0:T(8,128)}, u32[]{:S(2)}) copy-start(f32[1,1,1,6,128,128]{5,4,3,2,1,0:T(8,128)} %param.11) | copy-start | bytes 1179652
  18.0 28.6 %copy-start.11 = (f32[1,1,1,6,128,128]{5,4,3,2,1,0:T(8,128)S(1)}, f32[1,1,1,6,128,128]{5,4,3,2,1,0:T(8,128)}, u32[]{:S(2)}) copy-start(f32[1,1,1,6,128,128]{5,4,3,2,1,0:T(8,128)} %param.12) | copy-start | bytes 1179652
  18.0 8.9 %collective-permute-start.5 = (f32[48,128]{1,0:T(8,128)S(1)}, f32[48,128]{1,0:T(8,128)S(1)}, u32[]{:S(2)}, u32[]{:S(2)}) collective-permute-start(f32[48,128]{1,0:T(8,128)S(1)} %get-tuple-element.53), channel_id=1, source_target_pairs={{1,0},{2,1},{3,2},{4,3},{5,4},{6,5},{7,6},{8,7},{9,8},{10,9},{11,1... | collective-permute-start | bytes 73736 | tf_op jit(solution)/shard_map/ppermute | solution.py:376
  19.5 7.4 %collective-permute-start.3 = (f32[32,128]{1,0:T(8,128)S(1)}, f32[32,128]{1,0:T(8,128)S(1)}, u32[]{:S(2)}, u32[]{:S(2)}) collective-permute-start(f32[32,128]{1,0:T(8,128)S(1)} %get-tuple-element.51.dx_ref), channel_id=1, source_target_pairs={{64,0},{128,64},{192,128},{256,192},{320,256},{384,320},{448,384},... | collective-permute-start | bytes 49160 | tf_op jit(solution)/shard_map/ppermute | solution.py:376
  21.4 5.5 %collective-permute-start.4 = (f32[32,128]{1,0:T(8,128)S(1)}, f32[32,128]{1,0:T(8,128)S(1)}, u32[]{:S(2)}, u32[]{:S(2)}) collective-permute-start(f32[32,128]{1,0:T(8,128)S(1)} %get-tuple-element.52.dy_ref), channel_id=1, source_target_pairs={{16,0},{32,16},{48,32},{17,1},{33,17},{49,33},{18,2},{34,18},{50,3... | collective-permute-start | bytes 49160 | tf_op jit(solution)/shard_map/ppermute | solution.py:376
  22.7 5.0 %collective-permute-start.6 = (f32[16,128]{1,0:T(8,128)S(1)}, f32[16,128]{1,0:T(8,128)S(1)}, u32[]{:S(2)}, u32[]{:S(2)}) collective-permute-start(f32[16,128]{1,0:T(8,128)S(1)} %get-tuple-element.55), channel_id=1, source_target_pairs={{0,1},{1,2},{2,3},{3,4},{4,5},{5,6},{6,7},{7,8},{8,9},{9,10},{10,1... | collective-permute-start | bytes 24584 | tf_op jit(solution)/shard_map/ppermute | solution.py:376
  48.1 106.4 %copy-start = (bf16[640,640]{1,0:T(8,128)(2,1)}, bf16[640,640]{1,0:T(8,128)(2,1)S(1)}, u32[]{:S(2)}) copy-start(bf16[640,640]{1,0:T(8,128)(2,1)S(1)} %get-tuple-element.64.kh_ref) | copy-start | bytes 2457604
  48.1 106.4 %copy-start.2 = (bf16[640,640]{1,0:T(8,128)(2,1)}, bf16[640,640]{1,0:T(8,128)(2,1)S(1)}, u32[]{:S(2)}) copy-start(bf16[640,640]{1,0:T(8,128)(2,1)S(1)} %get-tuple-element.65.kl_ref) | copy-start | bytes 2457604
  96.7 4.8 %collective-permute-start.7 = (f32[16,128]{1,0:T(8,128)S(1)}, f32[16,128]{1,0:T(8,128)S(1)}, u32[]{:S(2)}, u32[]{:S(2)}) collective-permute-start(f32[16,128]{1,0:T(8,128)S(1)} %get-tuple-element.70), channel_id=1, source_target_pairs={{0,1},{1,2},{2,3},{3,4},{4,5},{5,6},{6,7},{7,8},{8,9},{9,10},{10,1... | collective-permute-start | bytes 24584 | tf_op jit(solution)/shard_map/ppermute | solution.py:376
  99.6 4.4 %collective-permute-start.8 = (f32[16,128]{1,0:T(8,128)S(1)}, f32[16,128]{1,0:T(8,128)S(1)}, u32[]{:S(2)}, u32[]{:S(2)}) collective-permute-start(f32[16,128]{1,0:T(8,128)S(1)} %get-tuple-element.71), channel_id=1, source_target_pairs={{1,0},{2,1},{3,2},{4,3},{5,4},{6,5},{7,6},{8,7},{9,8},{10,9},{11,1... | collective-permute-start | bytes 24584 | tf_op jit(solution)/shard_map/ppermute | solution.py:376
  156.6 0.7 copy-start.4
  157.4 0.7 copy-start.7
  158.1 14.3 %all-to-all-start.6 = ((f32[32,5,4,128]{3,2,1,0:T(4,128)}), f32[32,5,4,128]{3,2,1,0:T(4,128)}, u32[]{:S(2)}, u32[]{:S(2)}) async-start(f32[32,5,4,128]{3,2,1,0:T(4,128)} %copy-done.7), calls=%async_computation.6 | async-start | bytes 655360 | tf_op jit(solution)/shard_map/all_to_all | solution.py:380
  162.7 4.2 %collective-permute-start.9 = (f32[16,128]{1,0:T(8,128)S(1)}, f32[16,128]{1,0:T(8,128)S(1)}, u32[]{:S(2)}, u32[]{:S(2)}) collective-permute-start(f32[16,128]{1,0:T(8,128)S(1)} %get-tuple-element.79), channel_id=1, source_target_pairs={{0,1},{1,2},{2,3},{3,4},{4,5},{5,6},{6,7},{7,8},{8,9},{9,10},{10,1... | collective-permute-start | bytes 24584 | tf_op jit(solution)/shard_map/ppermute | solution.py:376
  165.6 4.8 %collective-permute-start.10 = (f32[16,128]{1,0:T(8,128)S(1)}, f32[16,128]{1,0:T(8,128)S(1)}, u32[]{:S(2)}, u32[]{:S(2)}) collective-permute-start(f32[16,128]{1,0:T(8,128)S(1)} %get-tuple-element.80), channel_id=1, source_target_pairs={{1,0},{2,1},{3,2},{4,3},{5,4},{6,5},{7,6},{8,7},{9,8},{10,9},{11,1... | collective-permute-start | bytes 24584 | tf_op jit(solution)/shard_map/ppermute | solution.py:376
  172.4 1.0 copy-start.5
  173.4 38.4 %copy-start.3 = (bf16[640,640]{1,0:T(8,128)(2,1)S(1)}, bf16[640,640]{1,0:T(8,128)(2,1)}, u32[]{:S(2)}) copy-start(bf16[640,640]{1,0:T(8,128)(2,1)} %copy-done.2) | copy-start | bytes 2457604
  175.1 36.7 %copy-start.1 = (bf16[640,640]{1,0:T(8,128)(2,1)S(1)}, bf16[640,640]{1,0:T(8,128)(2,1)}, u32[]{:S(2)}) copy-start(bf16[640,640]{1,0:T(8,128)(2,1)} %copy-done) | copy-start | bytes 2457604

commit v11 on v10

--- a/solution.py
+++ b/solution.py
@@ -214,7 +214,10 @@
     sum_kernel(state_ref, gh_ref, gl_ref, pick_ref, out_ref)
 
 
-def late_kernel(table, diag_ref, couple_ref, inverse_ref, _, fh_ref, fl_ref, kh_ref, kl_ref):
+def late_kernel(table, diag_ref, couple_ref, inverse_ref, gh_ref, gl_ref, pick_ref, _, fh_ref, fl_ref, kh_ref,
+                kl_ref, gh2_ref, gl2_ref, pick2_ref):
+    for ref, again_ref in ((gh_ref, gh2_ref), (gl_ref, gl2_ref), (pick_ref, pick2_ref)):
+        again_ref[...] = ref[...]
     put_dense(table, diag_ref, couple_ref, fh_ref, fl_ref)
     count = inverse_ref.shape[0]
     high, low = halves(inverse_ref[...])
@@ -443,11 +446,13 @@
         slots = swapped(slots, PLANE)
         if first:
             late = call(
-                late_kernel, [(square, BF16)] * 2 + [((COARSE, COARSE), BF16)] * 2,
-                [table] + blocks[2:] + [coarse_inverse, slots],
-                specs=[SMEM] + [VMEM] * 3 + [pl.BlockSpec(memory_space=pl.ANY)],
+                late_kernel,
+                [(square, BF16)] * 2 + [((COARSE, COARSE), BF16)] * 2
+                + [((CORNERS, WIDE), BF16)] * 2 + [((COARSE, CORNERS), BF16)],
+                [table] + blocks[2:] + [coarse_inverse, *joint, slots],
+                specs=[SMEM] + [VMEM] * 6 + [pl.BlockSpec(memory_space=pl.ANY)],
             )
-            flex, inverse = late[:2], late[2:]
+            flex, inverse, again = late[:2], late[2:4], late[4:]
         z, flexed, layers = call(
             functools.partial(flex_kernel, first),
             [(wide, F32), (wide, F32), ((gz, 5, 4, FD), F32)],
@@ -457,7 +462,7 @@
         layers = swapped(layers, "gz")
         (slots,) = call(share_kernel, [(stacked, F32)], [layers, flexed])
         slots = swapped(slots, PLANE)
-        common = [slots, layers, flexed, z, state, *inverse, *joint]
+        common = [slots, layers, flexed, z, state, *inverse, *(again if last else joint)]
         kernel = functools.partial(step_kernel, first, last)
         scratch = [pltpu.VMEM((CASES, COARSE), F32)]
         if last:

time: 214 us -> 213 us (level)
    unnamed x28 -> x32, local copies, waits for them, and re-layouts: 6.08 us -> 4.63 us
where the time goes in v11:
time: 213 us; the launch traced here: 212 us
  blocking collectives  152 us (71%)
  starting transfers between devices  32.9 us (15%)
  Pallas kernels  12.9 us (6%)
  waiting for transfers between devices  8.05 us (4%)
  local copies, waits for them, and re-layouts  4.63 us (2%)
    all_to_all x8, blocking collectives, swapped(): return lax.all_to_all(slots, axes, 0, 0)  152 us
    ppermute x11, starting transfers between devices, passed_along(): return lax.ppermute(shard, axis, pairs)  28.3 us
    pallas_call x16, Pallas kernels, call(): pl.pallas_call(kernel, out_shape=[jax.ShapeDtypeStruct(shape, dtype) for...  12.9 us
    ppermute x11, waiting for transfers between devices, passed_along(): return lax.ppermute(shard, axis, pairs)  6.01 us
    unnamed x32, local copies, waits for them, and re-layouts  4.63 us
    all_to_all x1, starting transfers between devices, swapped(): return lax.all_to_all(slots, axes, 0, 0)  4.59 us
  transfers between devices with their start and end apart: 12, of which 3 were waited for; matrix products, arithmetic and copies ran while one was open for 0% of the time, Pallas kernels for 1%

profile of v11, /device:TPU:1, one launch (start us, length us, event | category | flops | bytes accessed | tf_op | source)
XLA Modules:
  0.0 212.0 jit_solution(7707560418243945600)
XLA Ops:
  0.6 0.7 pad_add_fusion.table_ref.table
  1.4 0.9 copy-done.14
  2.2 0.7 copy-done.15
  3.0 0.2 shard_map.113
  3.1 4.6 %collective-permute-start = (f32[56,128]{1,0:T(8,128)S(1)}, f32[56,128]{1,0:T(8,128)S(1)}, u32[]{:S(2)}, u32[]{:S(2)}) collective-permute-start(f32[56,128]{1,0:T(8,128)S(1)} %get-tuple-element.47.ux_ref), channel_id=1, source_target_pairs={{0,64},{64,128},{128,192},{192,256},{256,320},{320,384},{384,448},... | collective-permute-start | bytes 86024 | tf_op jit(solution)/shard_map/ppermute | solution.py:379
  7.8 3.1 %collective-permute-start.1 = (f32[56,128]{1,0:T(8,128)S(1)}, f32[56,128]{1,0:T(8,128)S(1)}, u32[]{:S(2)}, u32[]{:S(2)}) collective-permute-start(f32[56,128]{1,0:T(8,128)S(1)} %get-tuple-element.48.uy_ref), channel_id=1, source_target_pairs={{0,16},{16,32},{32,48},{1,17},{17,33},{33,49},{2,18},{18,34},{34,5... | collective-permute-start | bytes 86024 | tf_op jit(solution)/shard_map/ppermute | solution.py:379
  10.9 3.5 %collective-permute-start.2 = (f32[56,128]{1,0:T(8,128)S(1)}, f32[56,128]{1,0:T(8,128)S(1)}, u32[]{:S(2)}, u32[]{:S(2)}) collective-permute-start(f32[56,128]{1,0:T(8,128)S(1)} %get-tuple-element.49.uz_ref), channel_id=1, source_target_pairs={{0,1},{1,2},{2,3},{3,4},{4,5},{5,6},{6,7},{7,8},{8,9},{9,10},{10,1... | collective-permute-start | bytes 86024 | tf_op jit(solution)/shard_map/ppermute | solution.py:379
  14.4 0.0 copy-start.8
  14.4 1.0 copy-done.8
  15.4 1.0 copy-done.9
  16.4 1.0 shard_map.114
  17.4 0.0 collective-permute-done.mx_ref
  17.4 0.0 collective-permute-done.1.my_ref
  17.4 0.0 collective-permute-done.2.mz_ref
  17.5 0.0 copy-start.2
  17.5 0.6 shard_map.115
  18.0 0.0 copy-start.11
  18.0 1.4 collective-permute-start.5
  19.5 1.9 collective-permute-start.3
  21.4 1.3 collective-permute-start.4
  22.7 4.2 %collective-permute-start.6 = (f32[16,128]{1,0:T(8,128)S(1)}, f32[16,128]{1,0:T(8,128)S(1)}, u32[]{:S(2)}, u32[]{:S(2)}) collective-permute-start(f32[16,128]{1,0:T(8,128)S(1)} %get-tuple-element.58), channel_id=1, source_target_pairs={{0,1},{1,2},{2,3},{3,4},{4,5},{5,6},{6,7},{7,8},{8,9},{9,10},{10,1... | collective-permute-start | bytes 24584 | tf_op jit(solution)/shard_map/ppermute | solution.py:379
  26.9 0.0 collective-permute-done.3.nx_ref
  26.9 0.0 collective-permute-done.4.ny_ref
  26.9 0.0 collective-permute-done.5.over_ref.above_ref
  26.9 0.7 shard_map.116
  27.6 0.0 collective-permute-done.6.below_ref
  27.7 19.0 %all_to_all.45._.slots_ref = f32[32,5,4,128]{3,2,1,0:T(4,128)S(1)} all-to-all(f32[32,5,4,128]{3,2,1,0:T(4,128)S(1)} %get-tuple-element.59), channel_id=1, replica_groups=mesh['gx'=8,'gy'=4,'gz'=16] {'gx','gy'}, dimensions={0} | all-to-all | bytes 655360 | tf_op jit(solution)/shard_map/all_to_all | solution.py:383
  46.6 0.0 copy-done.2
  46.6 0.0 copy-done.11
  46.6 1.5 shard_map.117
  48.2 0.7 shard_map.118
  48.9 0.0 copy-done.4
  48.9 0.1 copy-done.6
  49.1 0.1 copy-done.12
  49.2 29.7 %all_to_all.46.layers_ref = f32[16,5,4,128]{3,2,1,0:T(4,128)S(1)} all-to-all(f32[16,5,4,128]{3,2,1,0:T(4,128)S(1)} %get-tuple-element.67), channel_id=1, replica_groups=mesh['gx'=8,'gy'=4,'gz'=16] {'gz'}, dimensions={0} | all-to-all | bytes 327680 | tf_op jit(solution)/shard_map/all_to_all | solution.py:383
  78.9 0.1 shard_map.119
  78.9 16.7 %all_to_all.47.slots_ref = f32[32,5,4,128]{3,2,1,0:T(4,128)S(1)} all-to-all(f32[32,5,4,128]{3,2,1,0:T(4,128)S(1)} %shard_map.119), channel_id=1, replica_groups=mesh['gx'=8,'gy'=4,'gz'=16] {'gx','gy'}, dimensions={0} | all-to-all | bytes 655360 | tf_op jit(solution)/shard_map/all_to_all | solution.py:383
  95.7 1.4 shard_map.120
  97.0 2.8 %collective-permute-start.7 = (f32[16,128]{1,0:T(8,128)S(1)}, f32[16,128]{1,0:T(8,128)S(1)}, u32[]{:S(2)}, u32[]{:S(2)}) collective-permute-start(f32[16,128]{1,0:T(8,128)S(1)} %get-tuple-element.73), channel_id=1, source_target_pairs={{0,1},{1,2},{2,3},{3,4},{4,5},{5,6},{6,7},{7,8},{8,9},{9,10},{10,1... | collective-permute-start | bytes 24584 | tf_op jit(solution)/shard_map/ppermute | solution.py:379
  99.9 1.3 collective-permute-start.8
  101.2 0.6 shard_map.121
  101.8 0.0 collective-permute-done.7.below_ref
  101.8 2.5 %collective-permute-done.8.above_ref = f32[16,128]{1,0:T(8,128)S(1)} collective-permute-done((f32[16,128]{1,0:T(8,128)S(1)}, f32[16,128]{1,0:T(8,128)S(1)}, u32[]{:S(2)}, u32[]{:S(2)}) %collective-permute-start.8) | collective-permute-done | bytes 8224 | tf_op jit(solution)/shard_map/ppermute | solution.py:379
  104.3 14.9 %all_to_all.48.slots_ref = f32[32,5,4,128]{3,2,1,0:T(4,128)S(1)} all-to-all(f32[32,5,4,128]{3,2,1,0:T(4,128)S(1)} %shard_map.121), channel_id=1, replica_groups=mesh['gx'=8,'gy'=4,'gz'=16] {'gx','gy'}, dimensions={0} | all-to-all | bytes 655360 | tf_op jit(solution)/shard_map/all_to_all | solution.py:383
  119.2 0.7 shard_map.122
  119.9 18.1 %all_to_all.49.layers_ref = f32[16,5,4,128]{3,2,1,0:T(4,128)S(1)} all-to-all(f32[16,5,4,128]{3,2,1,0:T(4,128)S(1)} %get-tuple-element.78), channel_id=1, replica_groups=mesh['gx'=8,'gy'=4,'gz'=16] {'gz'}, dimensions={0} | all-to-all | bytes 327680 | tf_op jit(solution)/shard_map/all_to_all | solution.py:383
  138.0 0.1 shard_map.123
  138.1 16.7 %all_to_all.50.slots_ref = f32[32,5,4,128]{3,2,1,0:T(4,128)S(1)} all-to-all(f32[32,5,4,128]{3,2,1,0:T(4,128)S(1)} %shard_map.123), channel_id=1, replica_groups=mesh['gx'=8,'gy'=4,'gz'=16] {'gx','gy'}, dimensions={0} | all-to-all | bytes 655360 | tf_op jit(solution)/shard_map/all_to_all | solution.py:383
  154.8 1.5 shard_map.124
  156.3 0.6 shard_map.125
  157.0 0.7 copy-done.3
  157.7 4.6 %all-to-all-start.6 = ((f32[32,5,4,128]{3,2,1,0:T(4,128)}), f32[32,5,4,128]{3,2,1,0:T(4,128)}, u32[]{:S(2)}, u32[]{:S(2)}) async-start(f32[32,5,4,128]{3,2,1,0:T(4,128)} %copy-done.3), calls=%async_computation.6 | async-start | bytes 655360 | tf_op jit(solution)/shard_map/all_to_all | solution.py:383
  162.3 2.8 %collective-permute-start.9 = (f32[16,128]{1,0:T(8,128)S(1)}, f32[16,128]{1,0:T(8,128)S(1)}, u32[]{:S(2)}, u32[]{:S(2)}) collective-permute-start(f32[16,128]{1,0:T(8,128)S(1)} %get-tuple-element.82), channel_id=1, source_target_pairs={{0,1},{1,2},{2,3},{3,4},{4,5},{5,6},{6,7},{7,8},{8,9},{9,10},{10,1... | collective-permute-start | bytes 24584 | tf_op jit(solution)/shard_map/ppermute | solution.py:379
  165.2 1.3 collective-permute-start.10
  166.5 0.0 collective-permute-done.9.below_ref
  166.5 3.5 %collective-permute-done.10.above_ref = f32[16,128]{1,0:T(8,128)S(1)} collective-permute-done((f32[16,128]{1,0:T(8,128)S(1)}, f32[16,128]{1,0:T(8,128)S(1)}, u32[]{:S(2)}, u32[]{:S(2)}) %collective-permute-start.10) | collective-permute-done | bytes 8224 | tf_op jit(solution)/shard_map/ppermute | solution.py:379
  169.9 2.0 all-to-all-done.6.slots_ref
  172.0 1.7 shard_map.126
  173.7 16.1 %all_to_all.51.layers_ref = f32[16,5,4,128]{3,2,1,0:T(4,128)S(1)} all-to-all(f32[16,5,4,128]{3,2,1,0:T(4,128)S(1)} %get-tuple-element.84), channel_id=1, replica_groups=mesh['gx'=8,'gy'=4,'gz'=16] {'gz'}, dimensions={0} | all-to-all | bytes 327680 | tf_op jit(solution)/shard_map/all_to_all | solution.py:383
  189.9 0.1 shard_map.127
  190.0 20.4 %all_to_all.52.slots_ref = f32[32,5,4,128]{3,2,1,0:T(4,128)S(1)} all-to-all(f32[32,5,4,128]{3,2,1,0:T(4,128)S(1)} %shard_map.127), channel_id=1, replica_groups=mesh['gx'=8,'gy'=4,'gz'=16] {'gx','gy'}, dimensions={0} | all-to-all | bytes 655360 | tf_op jit(solution)/shard_map/all_to_all | solution.py:383
  210.4 0.0 copy-done.1
  210.4 0.0 copy-done.5
  210.4 1.6 shard_map.128
  (17 shorter events, 0.0 us)
Async XLA Ops:
  1.3 0.9 copy-start.14
  2.2 0.7 copy-start.15
  3.1 14.3 %collective-permute-start = (f32[56,128]{1,0:T(8,128)S(1)}, f32[56,128]{1,0:T(8,128)S(1)}, u32[]{:S(2)}, u32[]{:S(2)}) collective-permute-start(f32[56,128]{1,0:T(8,128)S(1)} %get-tuple-element.47.ux_ref), channel_id=1, source_target_pairs={{0,64},{64,128},{128,192},{192,256},{256,320},{320,384},{384,448},... | collective-permute-start | bytes 86024 | tf_op jit(solution)/shard_map/ppermute | solution.py:379
  7.8 9.7 %collective-permute-start.1 = (f32[56,128]{1,0:T(8,128)S(1)}, f32[56,128]{1,0:T(8,128)S(1)}, u32[]{:S(2)}, u32[]{:S(2)}) collective-permute-start(f32[56,128]{1,0:T(8,128)S(1)} %get-tuple-element.48.uy_ref), channel_id=1, source_target_pairs={{0,16},{16,32},{32,48},{1,17},{17,33},{33,49},{2,18},{18,34},{34,5... | collective-permute-start | bytes 86024 | tf_op jit(solution)/shard_map/ppermute | solution.py:379
  10.9 6.6 %collective-permute-start.2 = (f32[56,128]{1,0:T(8,128)S(1)}, f32[56,128]{1,0:T(8,128)S(1)}, u32[]{:S(2)}, u32[]{:S(2)}) collective-permute-start(f32[56,128]{1,0:T(8,128)S(1)} %get-tuple-element.49.uz_ref), channel_id=1, source_target_pairs={{0,1},{1,2},{2,3},{3,4},{4,5},{5,6},{6,7},{7,8},{8,9},{9,10},{10,1... | collective-permute-start | bytes 86024 | tf_op jit(solution)/shard_map/ppermute | solution.py:379
  14.4 1.0 copy-start.8
  15.4 1.0 copy-start.9
  17.5 29.2 %copy-start.2 = (f32[576,576]{1,0:T(8,128)S(1)}, f32[576,576]{1,0:T(8,128)}, u32[]{:S(2)}) copy-start(f32[576,576]{1,0:T(8,128)} %inverse_ref.1) | copy-start | bytes 3981316
  18.0 28.6 %copy-start.10 = (f32[1,1,1,6,128,128]{5,4,3,2,1,0:T(8,128)S(1)}, f32[1,1,1,6,128,128]{5,4,3,2,1,0:T(8,128)}, u32[]{:S(2)}) copy-start(f32[1,1,1,6,128,128]{5,4,3,2,1,0:T(8,128)} %param.11) | copy-start | bytes 1179652
  18.0 28.6 %copy-start.11 = (f32[1,1,1,6,128,128]{5,4,3,2,1,0:T(8,128)S(1)}, f32[1,1,1,6,128,128]{5,4,3,2,1,0:T(8,128)}, u32[]{:S(2)}) copy-start(f32[1,1,1,6,128,128]{5,4,3,2,1,0:T(8,128)} %param.12) | copy-start | bytes 1179652
  18.0 8.9 %collective-permute-start.5 = (f32[48,128]{1,0:T(8,128)S(1)}, f32[48,128]{1,0:T(8,128)S(1)}, u32[]{:S(2)}, u32[]{:S(2)}) collective-permute-start(f32[48,128]{1,0:T(8,128)S(1)} %get-tuple-element.56), channel_id=1, source_target_pairs={{1,0},{2,1},{3,2},{4,3},{5,4},{6,5},{7,6},{8,7},{9,8},{10,9},{11,1... | collective-permute-start | bytes 73736 | tf_op jit(solution)/shard_map/ppermute | solution.py:379
  19.5 7.4 %collective-permute-start.3 = (f32[32,128]{1,0:T(8,128)S(1)}, f32[32,128]{1,0:T(8,128)S(1)}, u32[]{:S(2)}, u32[]{:S(2)}) collective-permute-start(f32[32,128]{1,0:T(8,128)S(1)} %get-tuple-element.54.dx_ref), channel_id=1, source_target_pairs={{64,0},{128,64},{192,128},{256,192},{320,256},{384,320},{448,384},... | collective-permute-start | bytes 49160 | tf_op jit(solution)/shard_map/ppermute | solution.py:379
  21.4 5.5 %collective-permute-start.4 = (f32[32,128]{1,0:T(8,128)S(1)}, f32[32,128]{1,0:T(8,128)S(1)}, u32[]{:S(2)}, u32[]{:S(2)}) collective-permute-start(f32[32,128]{1,0:T(8,128)S(1)} %get-tuple-element.55.dy_ref), channel_id=1, source_target_pairs={{16,0},{32,16},{48,32},{17,1},{33,17},{49,33},{18,2},{34,18},{50,3... | collective-permute-start | bytes 49160 | tf_op jit(solution)/shard_map/ppermute | solution.py:379
  22.7 5.0 %collective-permute-start.6 = (f32[16,128]{1,0:T(8,128)S(1)}, f32[16,128]{1,0:T(8,128)S(1)}, u32[]{:S(2)}, u32[]{:S(2)}) collective-permute-start(f32[16,128]{1,0:T(8,128)S(1)} %get-tuple-element.58), channel_id=1, source_target_pairs={{0,1},{1,2},{2,3},{3,4},{4,5},{5,6},{6,7},{7,8},{8,9},{9,10},{10,1... | collective-permute-start | bytes 24584 | tf_op jit(solution)/shard_map/ppermute | solution.py:379
  48.2 0.7 copy-start.4
  48.2 0.9 copy-start.6
  48.2 1.0 copy-start.12
  48.2 106.6 %copy-start = (bf16[640,640]{1,0:T(8,128)(2,1)}, bf16[640,640]{1,0:T(8,128)(2,1)S(1)}, u32[]{:S(2)}) copy-start(bf16[640,640]{1,0:T(8,128)(2,1)S(1)} %get-tuple-element.71.kl_ref) | copy-start | bytes 2457604
  97.0 4.8 %collective-permute-start.7 = (f32[16,128]{1,0:T(8,128)S(1)}, f32[16,128]{1,0:T(8,128)S(1)}, u32[]{:S(2)}, u32[]{:S(2)}) collective-permute-start(f32[16,128]{1,0:T(8,128)S(1)} %get-tuple-element.73), channel_id=1, source_target_pairs={{0,1},{1,2},{2,3},{3,4},{4,5},{5,6},{6,7},{7,8},{8,9},{9,10},{10,1... | collective-permute-start | bytes 24584 | tf_op jit(solution)/shard_map/ppermute | solution.py:379
  99.9 4.4 %collective-permute-start.8 = (f32[16,128]{1,0:T(8,128)S(1)}, f32[16,128]{1,0:T(8,128)S(1)}, u32[]{:S(2)}, u32[]{:S(2)}) collective-permute-start(f32[16,128]{1,0:T(8,128)S(1)} %get-tuple-element.74), channel_id=1, source_target_pairs={{1,0},{2,1},{3,2},{4,3},{5,4},{6,5},{7,6},{8,7},{9,8},{10,9},{11,1... | collective-permute-start | bytes 24584 | tf_op jit(solution)/shard_map/ppermute | solution.py:379
  157.0 0.7 copy-start.3
  157.7 14.3 %all-to-all-start.6 = ((f32[32,5,4,128]{3,2,1,0:T(4,128)}), f32[32,5,4,128]{3,2,1,0:T(4,128)}, u32[]{:S(2)}, u32[]{:S(2)}) async-start(f32[32,5,4,128]{3,2,1,0:T(4,128)} %copy-done.3), calls=%async_computation.6 | async-start | bytes 655360 | tf_op jit(solution)/shard_map/all_to_all | solution.py:383
  162.3 4.2 %collective-permute-start.9 = (f32[16,128]{1,0:T(8,128)S(1)}, f32[16,128]{1,0:T(8,128)S(1)}, u32[]{:S(2)}, u32[]{:S(2)}) collective-permute-start(f32[16,128]{1,0:T(8,128)S(1)} %get-tuple-element.82), channel_id=1, source_target_pairs={{0,1},{1,2},{2,3},{3,4},{4,5},{5,6},{6,7},{7,8},{8,9},{9,10},{10,1... | collective-permute-start | bytes 24584 | tf_op jit(solution)/shard_map/ppermute | solution.py:379
  165.2 4.8 %collective-permute-start.10 = (f32[16,128]{1,0:T(8,128)S(1)}, f32[16,128]{1,0:T(8,128)S(1)}, u32[]{:S(2)}, u32[]{:S(2)}) collective-permute-start(f32[16,128]{1,0:T(8,128)S(1)} %get-tuple-element.83), channel_id=1, source_target_pairs={{1,0},{2,1},{3,2},{4,3},{5,4},{6,5},{7,6},{8,7},{9,8},{10,9},{11,1... | collective-permute-start | bytes 24584 | tf_op jit(solution)/shard_map/ppermute | solution.py:379
  172.0 38.4 %copy-start.7 = (bf16[256,768]{1,0:T(8,128)(2,1)S(1)}, bf16[256,768]{1,0:T(8,128)(2,1)}, u32[]{:S(2)}) copy-start(bf16[256,768]{1,0:T(8,128)(2,1)} %copy-done.6) | copy-start | bytes 1179652
  172.0 38.4 %copy-start.13 = (bf16[640,256]{1,0:T(8,128)(2,1)S(1)}, bf16[640,256]{1,0:T(8,128)(2,1)}, u32[]{:S(2)}) copy-start(bf16[640,256]{1,0:T(8,128)(2,1)} %copy-done.12) | copy-start | bytes 983044
  173.7 36.7 %copy-start.1 = (bf16[640,640]{1,0:T(8,128)(2,1)S(1)}, bf16[640,640]{1,0:T(8,128)(2,1)}, u32[]{:S(2)}) copy-start(bf16[640,640]{1,0:T(8,128)(2,1)} %copy-done) | copy-start | bytes 2457604
  173.7 36.7 %copy-start.5 = (bf16[256,768]{1,0:T(8,128)(2,1)S(1)}, bf16[256,768]{1,0:T(8,128)(2,1)}, u32[]{:S(2)}) copy-start(bf16[256,768]{1,0:T(8,128)(2,1)} %copy-done.4) | copy-start | bytes 1179652

commit v12 on v11

--- a/solution.py
+++ b/solution.py
@@ -276,12 +276,24 @@
             put_rows(out_ref, layer + by, flexed_ref[:, f * FD:(f + 1) * FD])
 
 
-def flex_kernel(first, state_ref, slots_ref, below_ref, above_ref, fh_ref, fl_ref, z_ref, flexed_ref,
-                out_ref, turn):
+def flex_kernel(first, last, state_ref, slots_ref, below_ref, above_ref, fh_ref, fl_ref, z_ref, flexed_ref,
+                out_ref, turn, *apart):
     here, layer, there = position()
-    across = []
-    for f, by in enumerate(steps()):
-        across.append(take_rows(slots_ref, jnp.where(there[f], here + by, here)))
+    spots = [jnp.where(there[f], here + by, here) for f, by in enumerate(steps())]
+    if last:
+        faces, shares, sems = apart
+        copies = [
+            pltpu.make_async_copy(slots_ref.at[spot, pl.ds(0, 4)], faces.at[f], sems.at[f])
+            for f, spot in enumerate(spots)
+        ]
+        copies.append(pltpu.make_async_copy(slots_ref.at[:, 4], shares, sems.at[4]))
+        for copy in copies:
+            copy.start()
+        for copy in copies:
+            copy.wait()
+        across = [take_rows(faces, f) for f in range(4)]
+    else:
+        across = [take_rows(slots_ref, spot) for spot in spots]
     across += [below_ref[...], above_ref[0:CASES, :]]
     z = 0.25 * (state_ref[SHOWN, :] + jnp.concatenate(across, axis=1)) * mask_row(there)
     z_ref[...] = z
@@ -295,7 +307,7 @@
             + face_sum(state_ref[SEARCH, :] * flexed)
         )
     sums = jnp.sum(turn[...].T, axis=0, keepdims=True)
-    total = jnp.sum(slots_ref[:, 4], axis=0)
+    total = jnp.sum(shares[...] if last else slots_ref[:, 4], axis=0)
     rows = lax.broadcasted_iota(jnp.int32, total.shape, 0)
     total = jnp.where(rows == 3, jnp.broadcast_to(sums, total.shape), total)
     put_layers(out_ref, total, flexed_ref, layer, there)
@@ -454,10 +466,13 @@
             )
             flex, inverse, again = late[:2], late[2:4], late[4:]
         z, flexed, layers = call(
-            functools.partial(flex_kernel, first),
+            functools.partial(flex_kernel, first, last),
             [(wide, F32), (wide, F32), ((gz, 5, 4, FD), F32)],
             [state, slots, below, over, *flex],
-            scratch=[pltpu.VMEM((FD, FD), F32)],
+            specs=[VMEM, pl.BlockSpec(memory_space=pl.ANY)] if last else (),
+            scratch=[pltpu.VMEM((FD, FD), F32)]
+            + [pltpu.VMEM((4, 4, 4, FD), F32), pltpu.VMEM((plane, 4, FD), F32),
+               pltpu.SemaphoreType.DMA((5,))] * last,
         )
         layers = swapped(layers, "gz")
         (slots,) = call(share_kernel, [(stacked, F32)], [layers, flexed])

time: 213 us -> 213 us (level)
  no operation moved by 1% of the time
where the time goes in v12:
time: 213 us; the launch traced here: 212 us
  blocking collectives  152 us (71%)
  starting transfers between devices  32.9 us (15%)
  Pallas kernels  12.9 us (6%)
  waiting for transfers between devices  8.05 us (4%)
  local copies, waits for them, and re-layouts  4.63 us (2%)
    all_to_all x8, blocking collectives, swapped(): return lax.all_to_all(slots, axes, 0, 0)  152 us
    ppermute x11, starting transfers between devices, passed_along(): return lax.ppermute(shard, axis, pairs)  28.3 us
    pallas_call x16, Pallas kernels, call(): pl.pallas_call(kernel, out_shape=[jax.ShapeDtypeStruct(shape, dtype) for...  12.9 us
    ppermute x11, waiting for transfers between devices, passed_along(): return lax.ppermute(shard, axis, pairs)  6.01 us
    unnamed x32, local copies, waits for them, and re-layouts  4.63 us
    all_to_all x1, starting transfers between devices, swapped(): return lax.all_to_all(slots, axes, 0, 0)  4.59 us
  transfers between devices with their start and end apart: 12, of which 3 were waited for; matrix products, arithmetic and copies ran while one was open for 0% of the time, Pallas kernels for 1%

profile of v12, /device:TPU:1, one launch (start us, length us, event | category | flops | bytes accessed | tf_op | source)
XLA Modules:
  0.0 212.0 jit_solution(12147400398710147230)
XLA Ops:
  0.6 0.7 pad_add_fusion.table_ref.table
  1.4 0.9 copy-done.14
  2.2 0.7 copy-done.15
  3.0 0.2 shard_map.113
  3.1 4.6 %collective-permute-start = (f32[56,128]{1,0:T(8,128)S(1)}, f32[56,128]{1,0:T(8,128)S(1)}, u32[]{:S(2)}, u32[]{:S(2)}) collective-permute-start(f32[56,128]{1,0:T(8,128)S(1)} %get-tuple-element.47.ux_ref), channel_id=1, source_target_pairs={{0,64},{64,128},{128,192},{192,256},{256,320},{320,384},{384,448},... | collective-permute-start | bytes 86024 | tf_op jit(solution)/shard_map/ppermute | solution.py:391
  7.8 3.1 %collective-permute-start.1 = (f32[56,128]{1,0:T(8,128)S(1)}, f32[56,128]{1,0:T(8,128)S(1)}, u32[]{:S(2)}, u32[]{:S(2)}) collective-permute-start(f32[56,128]{1,0:T(8,128)S(1)} %get-tuple-element.48.uy_ref), channel_id=1, source_target_pairs={{0,16},{16,32},{32,48},{1,17},{17,33},{33,49},{2,18},{18,34},{34,5... | collective-permute-start | bytes 86024 | tf_op jit(solution)/shard_map/ppermute | solution.py:391
  10.9 3.5 %collective-permute-start.2 = (f32[56,128]{1,0:T(8,128)S(1)}, f32[56,128]{1,0:T(8,128)S(1)}, u32[]{:S(2)}, u32[]{:S(2)}) collective-permute-start(f32[56,128]{1,0:T(8,128)S(1)} %get-tuple-element.49.uz_ref), channel_id=1, source_target_pairs={{0,1},{1,2},{2,3},{3,4},{4,5},{5,6},{6,7},{7,8},{8,9},{9,10},{10,1... | collective-permute-start | bytes 86024 | tf_op jit(solution)/shard_map/ppermute | solution.py:391
  14.4 0.0 copy-start.8
  14.4 1.0 copy-done.8
  15.4 1.0 copy-done.9
  16.4 1.0 shard_map.114
  17.4 0.0 collective-permute-done.mx_ref
  17.4 0.0 collective-permute-done.1.my_ref
  17.4 0.0 collective-permute-done.2.mz_ref
  17.5 0.0 copy-start.2
  17.5 0.6 shard_map.115
  18.0 0.0 copy-start.11
  18.0 1.4 collective-permute-start.5
  19.5 1.9 collective-permute-start.3
  21.4 1.3 collective-permute-start.4
  22.7 4.2 %collective-permute-start.6 = (f32[16,128]{1,0:T(8,128)S(1)}, f32[16,128]{1,0:T(8,128)S(1)}, u32[]{:S(2)}, u32[]{:S(2)}) collective-permute-start(f32[16,128]{1,0:T(8,128)S(1)} %get-tuple-element.58), channel_id=1, source_target_pairs={{0,1},{1,2},{2,3},{3,4},{4,5},{5,6},{6,7},{7,8},{8,9},{9,10},{10,1... | collective-permute-start | bytes 24584 | tf_op jit(solution)/shard_map/ppermute | solution.py:391
  26.9 0.0 collective-permute-done.3.nx_ref
  26.9 0.0 collective-permute-done.4.ny_ref
  26.9 0.0 collective-permute-done.5.over_ref.above_ref
  26.9 0.7 shard_map.116
  27.6 0.0 collective-permute-done.6.below_ref
  27.7 19.0 %all_to_all.45._.slots_ref = f32[32,5,4,128]{3,2,1,0:T(4,128)S(1)} all-to-all(f32[32,5,4,128]{3,2,1,0:T(4,128)S(1)} %get-tuple-element.59), channel_id=1, replica_groups=mesh['gx'=8,'gy'=4,'gz'=16] {'gx','gy'}, dimensions={0} | all-to-all | bytes 655360 | tf_op jit(solution)/shard_map/all_to_all | solution.py:395
  46.6 0.0 copy-done.2
  46.6 0.0 copy-done.10
  46.6 0.0 copy-done.11
  46.6 1.5 shard_map.117
  48.2 0.7 shard_map.118
  48.9 0.0 copy-done.4
  48.9 0.1 copy-done.6
  49.1 0.1 copy-done.12
  49.2 29.7 %all_to_all.46.layers_ref = f32[16,5,4,128]{3,2,1,0:T(4,128)S(1)} all-to-all(f32[16,5,4,128]{3,2,1,0:T(4,128)S(1)} %get-tuple-element.67), channel_id=1, replica_groups=mesh['gx'=8,'gy'=4,'gz'=16] {'gz'}, dimensions={0} | all-to-all | bytes 327680 | tf_op jit(solution)/shard_map/all_to_all | solution.py:395
  78.9 0.1 shard_map.119
  78.9 16.7 %all_to_all.47.slots_ref = f32[32,5,4,128]{3,2,1,0:T(4,128)S(1)} all-to-all(f32[32,5,4,128]{3,2,1,0:T(4,128)S(1)} %shard_map.119), channel_id=1, replica_groups=mesh['gx'=8,'gy'=4,'gz'=16] {'gx','gy'}, dimensions={0} | all-to-all | bytes 655360 | tf_op jit(solution)/shard_map/all_to_all | solution.py:395
  95.7 1.4 shard_map.120
  97.0 2.8 %collective-permute-start.7 = (f32[16,128]{1,0:T(8,128)S(1)}, f32[16,128]{1,0:T(8,128)S(1)}, u32[]{:S(2)}, u32[]{:S(2)}) collective-permute-start(f32[16,128]{1,0:T(8,128)S(1)} %get-tuple-element.73), channel_id=1, source_target_pairs={{0,1},{1,2},{2,3},{3,4},{4,5},{5,6},{6,7},{7,8},{8,9},{9,10},{10,1... | collective-permute-start | bytes 24584 | tf_op jit(solution)/shard_map/ppermute | solution.py:391
  99.9 1.3 collective-permute-start.8
  101.2 0.6 shard_map.121
  101.8 0.0 collective-permute-done.7.below_ref
  101.8 2.5 %collective-permute-done.8.above_ref = f32[16,128]{1,0:T(8,128)S(1)} collective-permute-done((f32[16,128]{1,0:T(8,128)S(1)}, f32[16,128]{1,0:T(8,128)S(1)}, u32[]{:S(2)}, u32[]{:S(2)}) %collective-permute-start.8) | collective-permute-done | bytes 8224 | tf_op jit(solution)/shard_map/ppermute | solution.py:391
  104.3 14.9 %all_to_all.48.slots_ref = f32[32,5,4,128]{3,2,1,0:T(4,128)S(1)} all-to-all(f32[32,5,4,128]{3,2,1,0:T(4,128)S(1)} %shard_map.121), channel_id=1, replica_groups=mesh['gx'=8,'gy'=4,'gz'=16] {'gx','gy'}, dimensions={0} | all-to-all | bytes 655360 | tf_op jit(solution)/shard_map/all_to_all | solution.py:395
  119.2 0.7 shard_map.122
  119.9 18.1 %all_to_all.49.layers_ref = f32[16,5,4,128]{3,2,1,0:T(4,128)S(1)} all-to-all(f32[16,5,4,128]{3,2,1,0:T(4,128)S(1)} %get-tuple-element.78), channel_id=1, replica_groups=mesh['gx'=8,'gy'=4,'gz'=16] {'gz'}, dimensions={0} | all-to-all | bytes 327680 | tf_op jit(solution)/shard_map/all_to_all | solution.py:395
  138.0 0.1 shard_map.123
  138.1 16.7 %all_to_all.50.slots_ref = f32[32,5,4,128]{3,2,1,0:T(4,128)S(1)} all-to-all(f32[32,5,4,128]{3,2,1,0:T(4,128)S(1)} %shard_map.123), channel_id=1, replica_groups=mesh['gx'=8,'gy'=4,'gz'=16] {'gx','gy'}, dimensions={0} | all-to-all | bytes 655360 | tf_op jit(solution)/shard_map/all_to_all | solution.py:395
  154.8 1.5 shard_map.124
  156.3 0.6 shard_map.125
  157.0 0.7 copy-done.3
  157.7 4.6 %all-to-all-start.6 = ((f32[32,5,4,128]{3,2,1,0:T(4,128)}), f32[32,5,4,128]{3,2,1,0:T(4,128)}, u32[]{:S(2)}, u32[]{:S(2)}) async-start(f32[32,5,4,128]{3,2,1,0:T(4,128)} %copy-done.3), calls=%async_computation.6 | async-start | bytes 655360 | tf_op jit(solution)/shard_map/all_to_all | solution.py:395
  162.3 2.8 %collective-permute-start.9 = (f32[16,128]{1,0:T(8,128)S(1)}, f32[16,128]{1,0:T(8,128)S(1)}, u32[]{:S(2)}, u32[]{:S(2)}) collective-permute-start(f32[16,128]{1,0:T(8,128)S(1)} %get-tuple-element.82), channel_id=1, source_target_pairs={{0,1},{1,2},{2,3},{3,4},{4,5},{5,6},{6,7},{7,8},{8,9},{9,10},{10,1... | collective-permute-start | bytes 24584 | tf_op jit(solution)/shard_map/ppermute | solution.py:391
  165.1 1.3 collective-permute-start.10
  166.4 0.0 collective-permute-done.9.below_ref
  166.5 3.5 %collective-permute-done.10.above_ref = f32[16,128]{1,0:T(8,128)S(1)} collective-permute-done((f32[16,128]{1,0:T(8,128)S(1)}, f32[16,128]{1,0:T(8,128)S(1)}, u32[]{:S(2)}, u32[]{:S(2)}) %collective-permute-start.10) | collective-permute-done | bytes 8224 | tf_op jit(solution)/shard_map/ppermute | solution.py:391
  169.9 2.0 all-to-all-done.6.slots_ref
  172.0 1.7 shard_map.126
  173.7 16.1 %all_to_all.51.layers_ref = f32[16,5,4,128]{3,2,1,0:T(4,128)S(1)} all-to-all(f32[16,5,4,128]{3,2,1,0:T(4,128)S(1)} %get-tuple-element.84), channel_id=1, replica_groups=mesh['gx'=8,'gy'=4,'gz'=16] {'gz'}, dimensions={0} | all-to-all | bytes 327680 | tf_op jit(solution)/shard_map/all_to_all | solution.py:395
  189.8 0.1 shard_map.127
  189.9 20.5 %all_to_all.52.slots_ref = f32[32,5,4,128]{3,2,1,0:T(4,128)S(1)} all-to-all(f32[32,5,4,128]{3,2,1,0:T(4,128)S(1)} %shard_map.127), channel_id=1, replica_groups=mesh['gx'=8,'gy'=4,'gz'=16] {'gx','gy'}, dimensions={0} | all-to-all | bytes 655360 | tf_op jit(solution)/shard_map/all_to_all | solution.py:395
  210.4 0.0 copy-done.13
  210.4 1.6 shard_map.128
  (17 shorter events, 0.0 us)
Async XLA Ops:
  1.3 0.9 copy-start.14
  2.2 0.7 copy-start.15
  3.1 14.3 %collective-permute-start = (f32[56,128]{1,0:T(8,128)S(1)}, f32[56,128]{1,0:T(8,128)S(1)}, u32[]{:S(2)}, u32[]{:S(2)}) collective-permute-start(f32[56,128]{1,0:T(8,128)S(1)} %get-tuple-element.47.ux_ref), channel_id=1, source_target_pairs={{0,64},{64,128},{128,192},{192,256},{256,320},{320,384},{384,448},... | collective-permute-start | bytes 86024 | tf_op jit(solution)/shard_map/ppermute | solution.py:391
  7.8 9.7 %collective-permute-start.1 = (f32[56,128]{1,0:T(8,128)S(1)}, f32[56,128]{1,0:T(8,128)S(1)}, u32[]{:S(2)}, u32[]{:S(2)}) collective-permute-start(f32[56,128]{1,0:T(8,128)S(1)} %get-tuple-element.48.uy_ref), channel_id=1, source_target_pairs={{0,16},{16,32},{32,48},{1,17},{17,33},{33,49},{2,18},{18,34},{34,5... | collective-permute-start | bytes 86024 | tf_op jit(solution)/shard_map/ppermute | solution.py:391
  10.9 6.6 %collective-permute-start.2 = (f32[56,128]{1,0:T(8,128)S(1)}, f32[56,128]{1,0:T(8,128)S(1)}, u32[]{:S(2)}, u32[]{:S(2)}) collective-permute-start(f32[56,128]{1,0:T(8,128)S(1)} %get-tuple-element.49.uz_ref), channel_id=1, source_target_pairs={{0,1},{1,2},{2,3},{3,4},{4,5},{5,6},{6,7},{7,8},{8,9},{9,10},{10,1... | collective-permute-start | bytes 86024 | tf_op jit(solution)/shard_map/ppermute | solution.py:391
  14.4 1.0 copy-start.8
  15.4 1.0 copy-start.9
  17.5 29.2 %copy-start.2 = (f32[576,576]{1,0:T(8,128)S(1)}, f32[576,576]{1,0:T(8,128)}, u32[]{:S(2)}) copy-start(f32[576,576]{1,0:T(8,128)} %inverse_ref.1) | copy-start | bytes 3981316
  18.0 28.6 %copy-start.10 = (f32[1,1,1,6,128,128]{5,4,3,2,1,0:T(8,128)S(1)}, f32[1,1,1,6,128,128]{5,4,3,2,1,0:T(8,128)}, u32[]{:S(2)}) copy-start(f32[1,1,1,6,128,128]{5,4,3,2,1,0:T(8,128)} %param.11) | copy-start | bytes 1179652
  18.0 28.6 %copy-start.11 = (f32[1,1,1,6,128,128]{5,4,3,2,1,0:T(8,128)S(1)}, f32[1,1,1,6,128,128]{5,4,3,2,1,0:T(8,128)}, u32[]{:S(2)}) copy-start(f32[1,1,1,6,128,128]{5,4,3,2,1,0:T(8,128)} %param.12) | copy-start | bytes 1179652
  18.0 8.9 %collective-permute-start.5 = (f32[48,128]{1,0:T(8,128)S(1)}, f32[48,128]{1,0:T(8,128)S(1)}, u32[]{:S(2)}, u32[]{:S(2)}) collective-permute-start(f32[48,128]{1,0:T(8,128)S(1)} %get-tuple-element.56), channel_id=1, source_target_pairs={{1,0},{2,1},{3,2},{4,3},{5,4},{6,5},{7,6},{8,7},{9,8},{10,9},{11,1... | collective-permute-start | bytes 73736 | tf_op jit(solution)/shard_map/ppermute | solution.py:391
  19.5 7.4 %collective-permute-start.3 = (f32[32,128]{1,0:T(8,128)S(1)}, f32[32,128]{1,0:T(8,128)S(1)}, u32[]{:S(2)}, u32[]{:S(2)}) collective-permute-start(f32[32,128]{1,0:T(8,128)S(1)} %get-tuple-element.54.dx_ref), channel_id=1, source_target_pairs={{64,0},{128,64},{192,128},{256,192},{320,256},{384,320},{448,384},... | collective-permute-start | bytes 49160 | tf_op jit(solution)/shard_map/ppermute | solution.py:391
  21.4 5.5 %collective-permute-start.4 = (f32[32,128]{1,0:T(8,128)S(1)}, f32[32,128]{1,0:T(8,128)S(1)}, u32[]{:S(2)}, u32[]{:S(2)}) collective-permute-start(f32[32,128]{1,0:T(8,128)S(1)} %get-tuple-element.55.dy_ref), channel_id=1, source_target_pairs={{16,0},{32,16},{48,32},{17,1},{33,17},{49,33},{18,2},{34,18},{50,3... | collective-permute-start | bytes 49160 | tf_op jit(solution)/shard_map/ppermute | solution.py:391
  22.7 5.0 %collective-permute-start.6 = (f32[16,128]{1,0:T(8,128)S(1)}, f32[16,128]{1,0:T(8,128)S(1)}, u32[]{:S(2)}, u32[]{:S(2)}) collective-permute-start(f32[16,128]{1,0:T(8,128)S(1)} %get-tuple-element.58), channel_id=1, source_target_pairs={{0,1},{1,2},{2,3},{3,4},{4,5},{5,6},{6,7},{7,8},{8,9},{9,10},{10,1... | collective-permute-start | bytes 24584 | tf_op jit(solution)/shard_map/ppermute | solution.py:391
  48.2 0.7 copy-start.4
  48.2 0.9 copy-start.6
  48.2 1.0 copy-start.12
  48.2 106.6 %copy-start = (bf16[640,640]{1,0:T(8,128)(2,1)}, bf16[640,640]{1,0:T(8,128)(2,1)S(1)}, u32[]{:S(2)}) copy-start(bf16[640,640]{1,0:T(8,128)(2,1)S(1)} %get-tuple-element.71.kl_ref) | copy-start | bytes 2457604
  97.0 4.8 %collective-permute-start.7 = (f32[16,128]{1,0:T(8,128)S(1)}, f32[16,128]{1,0:T(8,128)S(1)}, u32[]{:S(2)}, u32[]{:S(2)}) collective-permute-start(f32[16,128]{1,0:T(8,128)S(1)} %get-tuple-element.73), channel_id=1, source_target_pairs={{0,1},{1,2},{2,3},{3,4},{4,5},{5,6},{6,7},{7,8},{8,9},{9,10},{10,1... | collective-permute-start | bytes 24584 | tf_op jit(solution)/shard_map/ppermute | solution.py:391
  99.9 4.4 %collective-permute-start.8 = (f32[16,128]{1,0:T(8,128)S(1)}, f32[16,128]{1,0:T(8,128)S(1)}, u32[]{:S(2)}, u32[]{:S(2)}) collective-permute-start(f32[16,128]{1,0:T(8,128)S(1)} %get-tuple-element.74), channel_id=1, source_target_pairs={{1,0},{2,1},{3,2},{4,3},{5,4},{6,5},{7,6},{8,7},{9,8},{10,9},{11,1... | collective-permute-start | bytes 24584 | tf_op jit(solution)/shard_map/ppermute | solution.py:391
  157.0 0.7 copy-start.3
  157.7 14.3 %all-to-all-start.6 = ((f32[32,5,4,128]{3,2,1,0:T(4,128)}), f32[32,5,4,128]{3,2,1,0:T(4,128)}, u32[]{:S(2)}, u32[]{:S(2)}) async-start(f32[32,5,4,128]{3,2,1,0:T(4,128)} %copy-done.3), calls=%async_computation.6 | async-start | bytes 655360 | tf_op jit(solution)/shard_map/all_to_all | solution.py:395
  162.3 4.1 %collective-permute-start.9 = (f32[16,128]{1,0:T(8,128)S(1)}, f32[16,128]{1,0:T(8,128)S(1)}, u32[]{:S(2)}, u32[]{:S(2)}) collective-permute-start(f32[16,128]{1,0:T(8,128)S(1)} %get-tuple-element.82), channel_id=1, source_target_pairs={{0,1},{1,2},{2,3},{3,4},{4,5},{5,6},{6,7},{7,8},{8,9},{9,10},{10,1... | collective-permute-start | bytes 24584 | tf_op jit(solution)/shard_map/ppermute | solution.py:391
  165.1 4.8 %collective-permute-start.10 = (f32[16,128]{1,0:T(8,128)S(1)}, f32[16,128]{1,0:T(8,128)S(1)}, u32[]{:S(2)}, u32[]{:S(2)}) collective-permute-start(f32[16,128]{1,0:T(8,128)S(1)} %get-tuple-element.83), channel_id=1, source_target_pairs={{1,0},{2,1},{3,2},{4,3},{5,4},{6,5},{7,6},{8,7},{9,8},{10,9},{11,1... | collective-permute-start | bytes 24584 | tf_op jit(solution)/shard_map/ppermute | solution.py:391
  172.0 38.4 %copy-start.7 = (bf16[256,768]{1,0:T(8,128)(2,1)S(1)}, bf16[256,768]{1,0:T(8,128)(2,1)}, u32[]{:S(2)}) copy-start(bf16[256,768]{1,0:T(8,128)(2,1)} %copy-done.6) | copy-start | bytes 1179652
  172.0 38.4 %copy-start.13 = (bf16[640,256]{1,0:T(8,128)(2,1)S(1)}, bf16[640,256]{1,0:T(8,128)(2,1)}, u32[]{:S(2)}) copy-start(bf16[640,256]{1,0:T(8,128)(2,1)} %copy-done.12) | copy-start | bytes 983044
  173.7 36.7 %copy-start.1 = (bf16[640,640]{1,0:T(8,128)(2,1)S(1)}, bf16[640,640]{1,0:T(8,128)(2,1)}, u32[]{:S(2)}) copy-start(bf16[640,640]{1,0:T(8,128)(2,1)} %copy-done) | copy-start | bytes 2457604
  173.7 36.7 %copy-start.5 = (bf16[256,768]{1,0:T(8,128)(2,1)S(1)}, bf16[256,768]{1,0:T(8,128)(2,1)}, u32[]{:S(2)}) copy-start(bf16[256,768]{1,0:T(8,128)(2,1)} %copy-done.4) | copy-start | bytes 1179652

commit v13 on v12

--- a/solution.py
+++ b/solution.py
@@ -289,7 +289,7 @@
         copies.append(pltpu.make_async_copy(slots_ref.at[:, 4], shares, sems.at[4]))
         for copy in copies:
             copy.start()
-        for copy in copies:
+        for copy in copies[:4]:
             copy.wait()
         across = [take_rows(faces, f) for f in range(4)]
     else:
@@ -307,6 +307,8 @@
             + face_sum(state_ref[SEARCH, :] * flexed)
         )
     sums = jnp.sum(turn[...].T, axis=0, keepdims=True)
+    if last:
+        copies[4].wait()
     total = jnp.sum(shares[...] if last else slots_ref[:, 4], axis=0)
     rows = lax.broadcasted_iota(jnp.int32, total.shape, 0)
     total = jnp.where(rows == 3, jnp.broadcast_to(sums, total.shape), total)

time: 213 us -> 213 us (level)
  no operation moved by 1% of the time
where the time goes in v13:
time: 213 us; the launch traced here: 212 us
  blocking collectives  152 us (71%)
  starting transfers between devices  32.9 us (15%)
  Pallas kernels  12.8 us (6%)
  waiting for transfers between devices  8.05 us (4%)
  local copies, waits for them, and re-layouts  4.63 us (2%)
    all_to_all x8, blocking collectives, swapped(): return lax.all_to_all(slots, axes, 0, 0)  152 us
    ppermute x11, starting transfers between devices, passed_along(): return lax.ppermute(shard, axis, pairs)  28.3 us
    pallas_call x16, Pallas kernels, call(): pl.pallas_call(kernel, out_shape=[jax.ShapeDtypeStruct(shape, dtype) for...  12.8 us
    ppermute x11, waiting for transfers between devices, passed_along(): return lax.ppermute(shard, axis, pairs)  6.01 us
    unnamed x32, local copies, waits for them, and re-layouts  4.63 us
    all_to_all x1, starting transfers between devices, swapped(): return lax.all_to_all(slots, axes, 0, 0)  4.59 us
  transfers between devices with their start and end apart: 12, of which 3 were waited for; matrix products, arithmetic and copies ran while one was open for 0% of the time, Pallas kernels for 1%

profile of v13, /device:TPU:1, one launch (start us, length us, event | category | flops | bytes accessed | tf_op | source)
XLA Modules:
  0.0 211.9 jit_solution(4009152645099653377)
XLA Ops:
  0.6 0.7 pad_add_fusion.table_ref.table
  1.4 0.9 copy-done.14
  2.2 0.7 copy-done.15
  3.0 0.2 shard_map.113
  3.1 4.6 %collective-permute-start = (f32[56,128]{1,0:T(8,128)S(1)}, f32[56,128]{1,0:T(8,128)S(1)}, u32[]{:S(2)}, u32[]{:S(2)}) collective-permute-start(f32[56,128]{1,0:T(8,128)S(1)} %get-tuple-element.47.ux_ref), channel_id=1, source_target_pairs={{0,64},{64,128},{128,192},{192,256},{256,320},{320,384},{384,448},... | collective-permute-start | bytes 86024 | tf_op jit(solution)/shard_map/ppermute | solution.py:393
  7.8 3.1 %collective-permute-start.1 = (f32[56,128]{1,0:T(8,128)S(1)}, f32[56,128]{1,0:T(8,128)S(1)}, u32[]{:S(2)}, u32[]{:S(2)}) collective-permute-start(f32[56,128]{1,0:T(8,128)S(1)} %get-tuple-element.48.uy_ref), channel_id=1, source_target_pairs={{0,16},{16,32},{32,48},{1,17},{17,33},{33,49},{2,18},{18,34},{34,5... | collective-permute-start | bytes 86024 | tf_op jit(solution)/shard_map/ppermute | solution.py:393
  10.9 3.5 %collective-permute-start.2 = (f32[56,128]{1,0:T(8,128)S(1)}, f32[56,128]{1,0:T(8,128)S(1)}, u32[]{:S(2)}, u32[]{:S(2)}) collective-permute-start(f32[56,128]{1,0:T(8,128)S(1)} %get-tuple-element.49.uz_ref), channel_id=1, source_target_pairs={{0,1},{1,2},{2,3},{3,4},{4,5},{5,6},{6,7},{7,8},{8,9},{9,10},{10,1... | collective-permute-start | bytes 86024 | tf_op jit(solution)/shard_map/ppermute | solution.py:393
  14.4 0.0 copy-start.8
  14.4 1.0 copy-done.8
  15.4 1.0 copy-done.9
  16.4 1.0 shard_map.114
  17.4 0.0 collective-permute-done.mx_ref
  17.4 0.0 collective-permute-done.1.my_ref
  17.4 0.0 collective-permute-done.2.mz_ref
  17.5 0.0 copy-start.2
  17.5 0.6 shard_map.115
  18.0 0.0 copy-start.11
  18.0 1.4 collective-permute-start.5
  19.5 1.9 collective-permute-start.3
  21.4 1.3 collective-permute-start.4
  22.7 4.2 %collective-permute-start.6 = (f32[16,128]{1,0:T(8,128)S(1)}, f32[16,128]{1,0:T(8,128)S(1)}, u32[]{:S(2)}, u32[]{:S(2)}) collective-permute-start(f32[16,128]{1,0:T(8,128)S(1)} %get-tuple-element.58), channel_id=1, source_target_pairs={{0,1},{1,2},{2,3},{3,4},{4,5},{5,6},{6,7},{7,8},{8,9},{9,10},{10,1... | collective-permute-start | bytes 24584 | tf_op jit(solution)/shard_map/ppermute | solution.py:393
  26.9 0.0 collective-permute-done.3.nx_ref
  26.9 0.0 collective-permute-done.4.ny_ref
  26.9 0.0 collective-permute-done.5.over_ref.above_ref
  26.9 0.7 shard_map.116
  27.6 0.0 collective-permute-done.6.below_ref
  27.7 19.0 %all_to_all.45._.slots_ref = f32[32,5,4,128]{3,2,1,0:T(4,128)S(1)} all-to-all(f32[32,5,4,128]{3,2,1,0:T(4,128)S(1)} %get-tuple-element.59), channel_id=1, replica_groups=mesh['gx'=8,'gy'=4,'gz'=16] {'gx','gy'}, dimensions={0} | all-to-all | bytes 655360 | tf_op jit(solution)/shard_map/all_to_all | solution.py:397
  46.6 0.0 copy-done.10
  46.6 1.5 shard_map.117
  48.2 0.0 copy-start.4
  48.2 0.0 copy-start.6
  48.2 0.0 copy-start.12
  48.2 0.7 shard_map.118
  48.9 0.0 copy-done.4
  48.9 0.1 copy-done.6
  49.1 0.1 copy-done.12
  49.2 29.7 %all_to_all.46.layers_ref = f32[16,5,4,128]{3,2,1,0:T(4,128)S(1)} all-to-all(f32[16,5,4,128]{3,2,1,0:T(4,128)S(1)} %get-tuple-element.67), channel_id=1, replica_groups=mesh['gx'=8,'gy'=4,'gz'=16] {'gz'}, dimensions={0} | all-to-all | bytes 327680 | tf_op jit(solution)/shard_map/all_to_all | solution.py:397
  78.9 0.1 shard_map.119
  78.9 16.7 %all_to_all.47.slots_ref = f32[32,5,4,128]{3,2,1,0:T(4,128)S(1)} all-to-all(f32[32,5,4,128]{3,2,1,0:T(4,128)S(1)} %shard_map.119), channel_id=1, replica_groups=mesh['gx'=8,'gy'=4,'gz'=16] {'gx','gy'}, dimensions={0} | all-to-all | bytes 655360 | tf_op jit(solution)/shard_map/all_to_all | solution.py:397
  95.7 1.4 shard_map.120
  97.0 2.8 %collective-permute-start.7 = (f32[16,128]{1,0:T(8,128)S(1)}, f32[16,128]{1,0:T(8,128)S(1)}, u32[]{:S(2)}, u32[]{:S(2)}) collective-permute-start(f32[16,128]{1,0:T(8,128)S(1)} %get-tuple-element.73), channel_id=1, source_target_pairs={{0,1},{1,2},{2,3},{3,4},{4,5},{5,6},{6,7},{7,8},{8,9},{9,10},{10,1... | collective-permute-start | bytes 24584 | tf_op jit(solution)/shard_map/ppermute | solution.py:393
  99.9 1.3 collective-permute-start.8
  101.2 0.6 shard_map.121
  101.8 0.0 collective-permute-done.7.below_ref
  101.8 2.5 %collective-permute-done.8.above_ref = f32[16,128]{1,0:T(8,128)S(1)} collective-permute-done((f32[16,128]{1,0:T(8,128)S(1)}, f32[16,128]{1,0:T(8,128)S(1)}, u32[]{:S(2)}, u32[]{:S(2)}) %collective-permute-start.8) | collective-permute-done | bytes 8224 | tf_op jit(solution)/shard_map/ppermute | solution.py:393
  104.3 14.9 %all_to_all.48.slots_ref = f32[32,5,4,128]{3,2,1,0:T(4,128)S(1)} all-to-all(f32[32,5,4,128]{3,2,1,0:T(4,128)S(1)} %shard_map.121), channel_id=1, replica_groups=mesh['gx'=8,'gy'=4,'gz'=16] {'gx','gy'}, dimensions={0} | all-to-all | bytes 655360 | tf_op jit(solution)/shard_map/all_to_all | solution.py:397
  119.2 0.7 shard_map.122
  119.9 18.1 %all_to_all.49.layers_ref = f32[16,5,4,128]{3,2,1,0:T(4,128)S(1)} all-to-all(f32[16,5,4,128]{3,2,1,0:T(4,128)S(1)} %get-tuple-element.78), channel_id=1, replica_groups=mesh['gx'=8,'gy'=4,'gz'=16] {'gz'}, dimensions={0} | all-to-all | bytes 327680 | tf_op jit(solution)/shard_map/all_to_all | solution.py:397
  138.0 0.1 shard_map.123
  138.1 16.7 %all_to_all.50.slots_ref = f32[32,5,4,128]{3,2,1,0:T(4,128)S(1)} all-to-all(f32[32,5,4,128]{3,2,1,0:T(4,128)S(1)} %shard_map.123), channel_id=1, replica_groups=mesh['gx'=8,'gy'=4,'gz'=16] {'gx','gy'}, dimensions={0} | all-to-all | bytes 655360 | tf_op jit(solution)/shard_map/all_to_all | solution.py:397
  154.8 1.5 shard_map.124
  156.3 0.6 shard_map.125
  157.0 0.7 copy-done.3
  157.7 4.6 %all-to-all-start.6 = ((f32[32,5,4,128]{3,2,1,0:T(4,128)}), f32[32,5,4,128]{3,2,1,0:T(4,128)}, u32[]{:S(2)}, u32[]{:S(2)}) async-start(f32[32,5,4,128]{3,2,1,0:T(4,128)} %copy-done.3), calls=%async_computation.6 | async-start | bytes 655360 | tf_op jit(solution)/shard_map/all_to_all | solution.py:397
  162.3 2.8 %collective-permute-start.9 = (f32[16,128]{1,0:T(8,128)S(1)}, f32[16,128]{1,0:T(8,128)S(1)}, u32[]{:S(2)}, u32[]{:S(2)}) collective-permute-start(f32[16,128]{1,0:T(8,128)S(1)} %get-tuple-element.82), channel_id=1, source_target_pairs={{0,1},{1,2},{2,3},{3,4},{4,5},{5,6},{6,7},{7,8},{8,9},{9,10},{10,1... | collective-permute-start | bytes 24584 | tf_op jit(solution)/shard_map/ppermute | solution.py:393
  165.1 1.3 collective-permute-start.10
  166.4 0.0 collective-permute-done.9.below_ref
  166.5 3.5 %collective-permute-done.10.above_ref = f32[16,128]{1,0:T(8,128)S(1)} collective-permute-done((f32[16,128]{1,0:T(8,128)S(1)}, f32[16,128]{1,0:T(8,128)S(1)}, u32[]{:S(2)}, u32[]{:S(2)}) %collective-permute-start.10) | collective-permute-done | bytes 8224 | tf_op jit(solution)/shard_map/ppermute | solution.py:393
  169.9 2.0 all-to-all-done.6.slots_ref
  172.0 1.6 shard_map.126
  173.6 16.1 %all_to_all.51.layers_ref = f32[16,5,4,128]{3,2,1,0:T(4,128)S(1)} all-to-all(f32[16,5,4,128]{3,2,1,0:T(4,128)S(1)} %get-tuple-element.84), channel_id=1, replica_groups=mesh['gx'=8,'gy'=4,'gz'=16] {'gz'}, dimensions={0} | all-to-all | bytes 327680 | tf_op jit(solution)/shard_map/all_to_all | solution.py:397
  189.7 0.1 shard_map.127
  189.8 20.5 %all_to_all.52.slots_ref = f32[32,5,4,128]{3,2,1,0:T(4,128)S(1)} all-to-all(f32[32,5,4,128]{3,2,1,0:T(4,128)S(1)} %shard_map.127), channel_id=1, replica_groups=mesh['gx'=8,'gy'=4,'gz'=16] {'gx','gy'}, dimensions={0} | all-to-all | bytes 655360 | tf_op jit(solution)/shard_map/all_to_all | solution.py:397
  210.3 1.6 shard_map.128
  (17 shorter events, 0.0 us)
Async XLA Ops:
  1.3 0.9 copy-start.14
  2.2 0.7 copy-start.15
  3.1 14.3 %collective-permute-start = (f32[56,128]{1,0:T(8,128)S(1)}, f32[56,128]{1,0:T(8,128)S(1)}, u32[]{:S(2)}, u32[]{:S(2)}) collective-permute-start(f32[56,128]{1,0:T(8,128)S(1)} %get-tuple-element.47.ux_ref), channel_id=1, source_target_pairs={{0,64},{64,128},{128,192},{192,256},{256,320},{320,384},{384,448},... | collective-permute-start | bytes 86024 | tf_op jit(solution)/shard_map/ppermute | solution.py:393
  7.8 9.7 %collective-permute-start.1 = (f32[56,128]{1,0:T(8,128)S(1)}, f32[56,128]{1,0:T(8,128)S(1)}, u32[]{:S(2)}, u32[]{:S(2)}) collective-permute-start(f32[56,128]{1,0:T(8,128)S(1)} %get-tuple-element.48.uy_ref), channel_id=1, source_target_pairs={{0,16},{16,32},{32,48},{1,17},{17,33},{33,49},{2,18},{18,34},{34,5... | collective-permute-start | bytes 86024 | tf_op jit(solution)/shard_map/ppermute | solution.py:393
  10.9 6.6 %collective-permute-start.2 = (f32[56,128]{1,0:T(8,128)S(1)}, f32[56,128]{1,0:T(8,128)S(1)}, u32[]{:S(2)}, u32[]{:S(2)}) collective-permute-start(f32[56,128]{1,0:T(8,128)S(1)} %get-tuple-element.49.uz_ref), channel_id=1, source_target_pairs={{0,1},{1,2},{2,3},{3,4},{4,5},{5,6},{6,7},{7,8},{8,9},{9,10},{10,1... | collective-permute-start | bytes 86024 | tf_op jit(solution)/shard_map/ppermute | solution.py:393
  14.4 1.0 copy-start.8
  15.4 1.0 copy-start.9
  17.5 29.2 %copy-start.2 = (f32[576,576]{1,0:T(8,128)S(1)}, f32[576,576]{1,0:T(8,128)}, u32[]{:S(2)}) copy-start(f32[576,576]{1,0:T(8,128)} %inverse_ref.1) | copy-start | bytes 3981316
  18.0 28.6 %copy-start.10 = (f32[1,1,1,6,128,128]{5,4,3,2,1,0:T(8,128)S(1)}, f32[1,1,1,6,128,128]{5,4,3,2,1,0:T(8,128)}, u32[]{:S(2)}) copy-start(f32[1,1,1,6,128,128]{5,4,3,2,1,0:T(8,128)} %param.11) | copy-start | bytes 1179652
  18.0 28.6 %copy-start.11 = (f32[1,1,1,6,128,128]{5,4,3,2,1,0:T(8,128)S(1)}, f32[1,1,1,6,128,128]{5,4,3,2,1,0:T(8,128)}, u32[]{:S(2)}) copy-start(f32[1,1,1,6,128,128]{5,4,3,2,1,0:T(8,128)} %param.12) | copy-start | bytes 1179652
  18.0 8.9 %collective-permute-start.5 = (f32[48,128]{1,0:T(8,128)S(1)}, f32[48,128]{1,0:T(8,128)S(1)}, u32[]{:S(2)}, u32[]{:S(2)}) collective-permute-start(f32[48,128]{1,0:T(8,128)S(1)} %get-tuple-element.56), channel_id=1, source_target_pairs={{1,0},{2,1},{3,2},{4,3},{5,4},{6,5},{7,6},{8,7},{9,8},{10,9},{11,1... | collective-permute-start | bytes 73736 | tf_op jit(solution)/shard_map/ppermute | solution.py:393
  19.5 7.4 %collective-permute-start.3 = (f32[32,128]{1,0:T(8,128)S(1)}, f32[32,128]{1,0:T(8,128)S(1)}, u32[]{:S(2)}, u32[]{:S(2)}) collective-permute-start(f32[32,128]{1,0:T(8,128)S(1)} %get-tuple-element.54.dx_ref), channel_id=1, source_target_pairs={{64,0},{128,64},{192,128},{256,192},{320,256},{384,320},{448,384},... | collective-permute-start | bytes 49160 | tf_op jit(solution)/shard_map/ppermute | solution.py:393
  21.4 5.5 %collective-permute-start.4 = (f32[32,128]{1,0:T(8,128)S(1)}, f32[32,128]{1,0:T(8,128)S(1)}, u32[]{:S(2)}, u32[]{:S(2)}) collective-permute-start(f32[32,128]{1,0:T(8,128)S(1)} %get-tuple-element.55.dy_ref), channel_id=1, source_target_pairs={{16,0},{32,16},{48,32},{17,1},{33,17},{49,33},{18,2},{34,18},{50,3... | collective-permute-start | bytes 49160 | tf_op jit(solution)/shard_map/ppermute | solution.py:393
  22.7 5.0 %collective-permute-start.6 = (f32[16,128]{1,0:T(8,128)S(1)}, f32[16,128]{1,0:T(8,128)S(1)}, u32[]{:S(2)}, u32[]{:S(2)}) collective-permute-start(f32[16,128]{1,0:T(8,128)S(1)} %get-tuple-element.58), channel_id=1, source_target_pairs={{0,1},{1,2},{2,3},{3,4},{4,5},{5,6},{6,7},{7,8},{8,9},{9,10},{10,1... | collective-permute-start | bytes 24584 | tf_op jit(solution)/shard_map/ppermute | solution.py:393
  48.2 0.7 copy-start.4
  48.2 0.9 copy-start.6
  48.2 1.0 copy-start.12
  48.2 106.6 %copy-start = (bf16[640,640]{1,0:T(8,128)(2,1)}, bf16[640,640]{1,0:T(8,128)(2,1)S(1)}, u32[]{:S(2)}) copy-start(bf16[640,640]{1,0:T(8,128)(2,1)S(1)} %get-tuple-element.71.kl_ref) | copy-start | bytes 2457604
  97.0 4.8 %collective-permute-start.7 = (f32[16,128]{1,0:T(8,128)S(1)}, f32[16,128]{1,0:T(8,128)S(1)}, u32[]{:S(2)}, u32[]{:S(2)}) collective-permute-start(f32[16,128]{1,0:T(8,128)S(1)} %get-tuple-element.73), channel_id=1, source_target_pairs={{0,1},{1,2},{2,3},{3,4},{4,5},{5,6},{6,7},{7,8},{8,9},{9,10},{10,1... | collective-permute-start | bytes 24584 | tf_op jit(solution)/shard_map/ppermute | solution.py:393
  99.9 4.4 %collective-permute-start.8 = (f32[16,128]{1,0:T(8,128)S(1)}, f32[16,128]{1,0:T(8,128)S(1)}, u32[]{:S(2)}, u32[]{:S(2)}) collective-permute-start(f32[16,128]{1,0:T(8,128)S(1)} %get-tuple-element.74), channel_id=1, source_target_pairs={{1,0},{2,1},{3,2},{4,3},{5,4},{6,5},{7,6},{8,7},{9,8},{10,9},{11,1... | collective-permute-start | bytes 24584 | tf_op jit(solution)/shard_map/ppermute | solution.py:393
  157.0 0.7 copy-start.3
  157.7 14.3 %all-to-all-start.6 = ((f32[32,5,4,128]{3,2,1,0:T(4,128)}), f32[32,5,4,128]{3,2,1,0:T(4,128)}, u32[]{:S(2)}, u32[]{:S(2)}) async-start(f32[32,5,4,128]{3,2,1,0:T(4,128)} %copy-done.3), calls=%async_computation.6 | async-start | bytes 655360 | tf_op jit(solution)/shard_map/all_to_all | solution.py:397
  162.3 4.1 %collective-permute-start.9 = (f32[16,128]{1,0:T(8,128)S(1)}, f32[16,128]{1,0:T(8,128)S(1)}, u32[]{:S(2)}, u32[]{:S(2)}) collective-permute-start(f32[16,128]{1,0:T(8,128)S(1)} %get-tuple-element.82), channel_id=1, source_target_pairs={{0,1},{1,2},{2,3},{3,4},{4,5},{5,6},{6,7},{7,8},{8,9},{9,10},{10,1... | collective-permute-start | bytes 24584 | tf_op jit(solution)/shard_map/ppermute | solution.py:393
  165.1 4.8 %collective-permute-start.10 = (f32[16,128]{1,0:T(8,128)S(1)}, f32[16,128]{1,0:T(8,128)S(1)}, u32[]{:S(2)}, u32[]{:S(2)}) collective-permute-start(f32[16,128]{1,0:T(8,128)S(1)} %get-tuple-element.83), channel_id=1, source_target_pairs={{1,0},{2,1},{3,2},{4,3},{5,4},{6,5},{7,6},{8,7},{9,8},{10,9},{11,1... | collective-permute-start | bytes 24584 | tf_op jit(solution)/shard_map/ppermute | solution.py:393
  172.0 38.3 %copy-start.7 = (bf16[256,768]{1,0:T(8,128)(2,1)S(1)}, bf16[256,768]{1,0:T(8,128)(2,1)}, u32[]{:S(2)}) copy-start(bf16[256,768]{1,0:T(8,128)(2,1)} %copy-done.6) | copy-start | bytes 1179652
  172.0 38.3 %copy-start.13 = (bf16[640,256]{1,0:T(8,128)(2,1)S(1)}, bf16[640,256]{1,0:T(8,128)(2,1)}, u32[]{:S(2)}) copy-start(bf16[640,256]{1,0:T(8,128)(2,1)} %copy-done.12) | copy-start | bytes 983044
  173.6 36.7 %copy-start.1 = (bf16[640,640]{1,0:T(8,128)(2,1)S(1)}, bf16[640,640]{1,0:T(8,128)(2,1)}, u32[]{:S(2)}) copy-start(bf16[640,640]{1,0:T(8,128)(2,1)} %copy-done) | copy-start | bytes 2457604
  173.6 36.7 %copy-start.5 = (bf16[256,768]{1,0:T(8,128)(2,1)S(1)}, bf16[256,768]{1,0:T(8,128)(2,1)}, u32[]{:S(2)}) copy-start(bf16[256,768]{1,0:T(8,128)(2,1)} %copy-done.4) | copy-start | bytes 1179652
